TPU v7x, 256 devices: a whole 4x4x8 slice. The times are simulated.
256 devices in a mesh: dp: 4 (over z_lo), ctx: 64 (over z_hi, x, y, core).
Axes of the slice: x: 4, y: 4, z: 8 (z_hi: 2, z_lo: 4; z = z_hi * 4 + z_lo), core: 2. Of those that a mesh axis runs over, the one named last changes fastest.
Arguments:
- query_rows: bfloat16 [4, 8192, 2048], P('dp', 'ctx'), may hold values from -6 to 6
- key_rows: bfloat16 [4, 8192, 512], P('dp', 'ctx'), may hold values from -6 to 6
- value_head_rows: bfloat16 [4, 8192, 512], P('dp', 'ctx'), may hold values from -6 to 6
- grad_output: bfloat16 [4, 8192, 2048], P('dp', 'ctx'), may hold values from -6 to 6
- layer_inputs: bfloat16 [4, 8192, 4096], P('dp', 'ctx'), may hold values from -16 to 16
- stretch_order: int32 [4, 64, 2], P('dp'), may hold values from 0 to 1, each once within a row
- session_starts: int32 [4, 64], P('dp'), may hold values from 0 to 8192, as said below
Outputs:
- grad_query: bfloat16 [4, 8192, 2048], P('dp', 'ctx')
- grad_key: bfloat16 [4, 8192, 512], P('dp', 'ctx')
- grad_value: bfloat16 [4, 8192, 512], P('dp', 'ctx')
- grad_value_weight: float32 [4096, 512], P(('dp', 'ctx'))
Inputs may be any that keep to these rules, and one draw needn't show every extreme that they name: `session_starts`: in each pack the first start is 0 and starts rise; of the starts below 8192, consecutive ones differ by at least 128 and at most 384; one session that begins inside the pack has exactly 384 positions, and none has more; the last entry, and any entry that would lie past the pack's end, equals 8192 and marks an unused start.
All inputs are finite; a program needn't handle non-finite values.
Results may differ from a plain program's by a relative error of at most 0.013.
Values may be sent and summed in bfloat16 or wider, within the bound.
No kernel may reach another device: no remote copies, remote signals or barrier semaphores. Data moves between devices by JAX's collectives and lax.ppermute only.
A program may use at most 128 MiB of HBM per device.

v0:
```python
import functools

import jax
import jax.numpy as jnp
from jax import lax
from jax.sharding import PartitionSpec as P

HEAD_SIZE = 128
STRETCH = 64
SPAN = 4


masked_value = -1e30


def shifted(block, axis, distance):
    devices = range(lax.axis_size(axis))
    route = [(i - distance, i) for i in devices if i - distance in devices]
    return lax.ppermute(block, axis, route)


def session_ids(positions, starts_row):
    return jnp.sum((starts_row[None, :] <= positions[:, None]).astype(jnp.int32), axis=1)


def shard_positions(stretch_perm, shard_index, rows_dev):
    offsets = jnp.arange(STRETCH, dtype=jnp.int32)
    return (shard_index * rows_dev + stretch_perm[:, None] * STRETCH + offsets[None, :]).reshape(
        rows_dev
    )


def block_scores(query_group, keys_block, allowed):
    scores = jnp.einsum(
        "tjd,kd->jtk", query_group, keys_block, preferred_element_type=jnp.float32
    ) * HEAD_SIZE ** (-0.5)
    return jnp.where(allowed[None], scores, masked_value)


def block_back(
    probability, prob_half, keys_block, values_block, query_group, grad_group, row_delta
):
    grad_prob = jnp.einsum(
        "tjd,kd->jtk", grad_group, values_block, preferred_element_type=jnp.float32
    )
    grad_score = (probability * (grad_prob - row_delta[:, :, None])).astype(jnp.bfloat16)
    query_part = jnp.einsum(
        "jtk,kd->tjd", grad_score, keys_block, preferred_element_type=jnp.float32
    )
    key_part = jnp.einsum(
        "jtk,tjd->kd", grad_score, query_group, preferred_element_type=jnp.float32
    )
    value_part = jnp.einsum(
        "jtk,tjd->kd", prob_half, grad_group, preferred_element_type=jnp.float32
    )
    return (query_part, key_part, value_part)


def shards(
    query_rows, key_rows, value_head_rows, grad_output, layer_inputs, stretch_order, session_starts
):
    rows_dev = query_rows.shape[1]
    head_count = query_rows.shape[2] // HEAD_SIZE
    group_count = key_rows.shape[2] // HEAD_SIZE
    group_width = head_count // group_count
    score_scale = HEAD_SIZE ** (-0.5)
    shard_index = lax.axis_index("ctx")
    order_table = stretch_order[0]
    starts_row = session_starts[0]
    own_perm = lax.dynamic_index_in_dim(order_table, shard_index, 0, keepdims=False)
    query_pos = shard_positions(own_perm, shard_index, rows_dev)
    query_sess = session_ids(query_pos, starts_row)
    local_keys = key_rows[0]
    local_values = value_head_rows[0]
    blocks = [(local_keys, local_values)]
    for distance in range(1, SPAN):
        blocks.append(shifted((local_keys, local_values), "ctx", distance))
    allowed_list = []
    for distance in range(SPAN):
        source = shard_index - distance
        source_perm = lax.dynamic_index_in_dim(
            order_table, jnp.maximum(source, 0), 0, keepdims=False
        )
        key_pos = shard_positions(source_perm, source, rows_dev)
        key_sess = session_ids(key_pos, starts_row)
        allowed_list.append(
            (key_sess[None, :] == query_sess[:, None])
            & (key_pos[None, :] <= query_pos[:, None])
            & (source >= 0)
        )
    query_all = query_rows[0].reshape(rows_dev, head_count, HEAD_SIZE)
    grad_all = grad_output[0].reshape(rows_dev, head_count, HEAD_SIZE)
    query_groups = []
    key_terms = [[] for distance in range(SPAN)]
    value_terms = [[] for distance in range(SPAN)]
    for head_group in range(group_count):
        query_group = query_all[:, head_group * group_width : (head_group + 1) * group_width]
        grad_group = grad_all[:, head_group * group_width : (head_group + 1) * group_width]
        keys_list = [
            pair[0][:, head_group * HEAD_SIZE : (head_group + 1) * HEAD_SIZE] for pair in blocks
        ]
        values_list = [
            pair[1][:, head_group * HEAD_SIZE : (head_group + 1) * HEAD_SIZE] for pair in blocks
        ]
        score_list = []
        for distance in range(SPAN):
            block_score = block_scores(query_group, keys_list[distance], allowed_list[distance])
            score_list.append(block_score)
        row_max = functools.reduce(
            jnp.maximum, [jnp.max(block_score, axis=2) for block_score in score_list]
        )
        row_sum = functools.reduce(
            jnp.add,
            [
                jnp.sum(jnp.exp(block_score - row_max[:, :, None]), axis=2)
                for block_score in score_list
            ],
        )
        log_total = row_max + jnp.log(row_sum)
        prob_list = [jnp.exp(block_score - log_total[:, :, None]) for block_score in score_list]
        half_list = [probability.astype(jnp.bfloat16) for probability in prob_list]
        attended = functools.reduce(
            jnp.add,
            [
                jnp.einsum(
                    "jtk,kd->tjd",
                    half_list[distance],
                    values_list[distance],
                    preferred_element_type=jnp.float32,
                )
                for distance in range(SPAN)
            ],
        )
        attended = lax.optimization_barrier(attended.astype(jnp.bfloat16))
        row_delta = jnp.sum(grad_group.astype(jnp.float32) * attended.astype(jnp.float32), axis=2).T
        query_total = jnp.zeros(query_group.shape, jnp.float32)
        for distance in range(SPAN):
            operands = (
                prob_list[distance],
                half_list[distance],
                keys_list[distance],
                values_list[distance],
                query_group,
                grad_group,
                row_delta,
            )
            query_part, key_part, value_part = block_back(*operands)
            query_total = query_total + query_part
            key_terms[distance].append(key_part * score_scale)
            value_terms[distance].append(value_part)
        query_groups.append((query_total * score_scale).astype(jnp.bfloat16))
    key_blocks = [jnp.concatenate(key_terms[distance], axis=1) for distance in range(SPAN)]
    value_blocks = [jnp.concatenate(value_terms[distance], axis=1) for distance in range(SPAN)]
    key_total, value_total = (key_blocks[0], value_blocks[0])
    for distance in range(1, SPAN):
        returned = (
            shifted(key_blocks[distance].astype(jnp.bfloat16), "ctx", -distance).astype(
                jnp.float32
            ),
            shifted(value_blocks[distance].astype(jnp.bfloat16), "ctx", -distance).astype(
                jnp.float32
            ),
        )
        key_total = key_total + returned[0]
        value_total = value_total + returned[1]
    grad_query_local = jnp.concatenate(query_groups, axis=1).reshape(
        rows_dev, head_count * HEAD_SIZE
    )
    grad_key_local = key_total.astype(jnp.bfloat16)
    grad_value_local = value_total.astype(jnp.bfloat16)
    input_rows = layer_inputs[0]
    weight_grad = lax.psum_scatter(
        jnp.einsum("tc,tk->ck", input_rows, grad_value_local, preferred_element_type=jnp.float32),
        ("dp", "ctx"),
        scatter_dimension=0,
        tiled=True,
    )
    return (grad_query_local[None], grad_key_local[None], grad_value_local[None], weight_grad)


def solution(mesh):
    placed = (
        P("dp", "ctx", None),
        P("dp", "ctx", None),
        P("dp", "ctx", None),
        P("dp", "ctx", None),
        P("dp", "ctx", None),
        P("dp", None, None),
        P("dp", None),
    )
    return jax.shard_map(
        shards,
        mesh=mesh,
        in_specs=placed,
        out_specs=(
            P("dp", "ctx", None),
            P("dp", "ctx", None),
            P("dp", "ctx", None),
            P(("dp", "ctx"), None),
        ),
        check_vma=False,
    )
```

profile of v0, /device:TPU:7, one launch (start us, length us, event | category | flops | bytes accessed | tf_op | source)
XLA Modules:
  0.0 1692.6 jit_solution(15732472691750721449)
XLA Ops:
  7.2 5.5 collective-permute-start.2
  12.8 2.3 collective-permute-start.1
  15.1 2.2 collective-permute-start
  21.9 1.5 fusion.314
  23.5 1.5 fusion.310
  25.0 1.5 fusion.306
  45.6 5.2 collective-permute-start.11
  50.8 1.9 collective-permute-start.10
  52.8 2.5 collective-permute-start.9
  55.7 2.6 collective-permute-done.11
  61.0 4.5 convolution_bitcast_fusion
  65.5 9.0 copy.633
  74.5 5.4 collective-permute-start.5
  79.9 11.6 collective-permute-start.4
  91.5 3.7 collective-permute-start.3
  96.1 1.7 copy.636
  97.7 1.6 copy.640
  99.4 1.7 copy.638
  101.1 1.7 copy.642
  145.4 1.9 collective-permute-start.6
  148.1 1.9 collective-permute-start.7
  151.7 1.9 collective-permute-start.8
  156.1 3.9 collective-permute-done.8
  160.9 1524.8 %reduce-scatter.4.cloned.1.call-done = f32[16,512]{1,0:T(8,128)} async-done(((f32[4096,512]{1,0:T(8,128)}), f32[16,512]{1,0:T(8,128)}) %reduce-scatter.4.cloned.1.call-update) | async-done | bytes 32784
  (243 shorter events, 74.7 us)
Async XLA Ops:
  7.2 53.8 %copy-start = (bf16[1,128,4096]{2,1,0:T(8,128)(2,1)S(1)}, bf16[1,128,4096]{2,1,0:T(8,128)(2,1)}, u32[]{:S(2)}) copy-start(bf16[1,128,4096]{2,1,0:T(8,128)(2,1)} %param.11) | copy-start | bytes 3145732
  7.2 1678.6 %reduce-scatter.4.cloned.1.call-start = ((), (), s32[]{:S(2)}) async-start(), calls=%async_computation.1 | async-start | bytes 8421376
  7.2 24.2 %collective-permute-start.2 = (bf16[128,512]{1,0:T(8,128)(2,1)}, bf16[128,512]{1,0:T(8,128)(2,1)}, u32[]{:S(2)}, u32[]{:S(2)}) collective-permute-start(bf16[128,512]{1,0:T(8,128)(2,1)} %bitcast.658), channel_id=1, source_target_pairs={{0,3},{1,4},{2,5},{3,6},{4,7},{5,8},{6,9},{7,10},{8,11},{9,12},{10... | collective-permute-start | bytes 393224 | tf_op jit(solution)/shard_map/ppermute | solution.py:19
  12.8 17.7 %collective-permute-start.1 = (bf16[128,512]{1,0:T(8,128)(2,1)}, bf16[128,512]{1,0:T(8,128)(2,1)S(1)}, u32[]{:S(2)}, u32[]{:S(2)}) collective-permute-start(bf16[128,512]{1,0:T(8,128)(2,1)} %bitcast.659), channel_id=1, source_target_pairs={{0,2},{1,3},{2,4},{3,5},{4,6},{5,7},{6,8},{7,9},{8,10},{9,11},{10,... | collective-permute-start | bytes 393224 | tf_op jit(solution)/shard_map/ppermute | solution.py:19
  15.1 13.8 collective-permute-start
  30.5 25.3 %copy-start.30 = (bf16[128,512]{1,0:T(8,128)(2,1)}, bf16[128,512]{1,0:T(8,128)(2,1)S(1)}, u32[]{:S(2)}) copy-start(bf16[128,512]{1,0:T(8,128)(2,1)S(1)} %collective-permute-done.1) | copy-start | bytes 393220
  33.3 26.4 %copy-start.41 = (f32[4,128]{1,0:T(4,128)}, f32[4,128]{1,0:T(4,128)S(1)}, u32[]{:S(2)}) copy-start(f32[4,128]{1,0:T(4,128)S(1)} %log_add_fusion.3) | copy-start | bytes 6148
  37.7 23.2 %copy-start.43 = (f32[4,128]{1,0:T(4,128)}, f32[4,128]{1,0:T(4,128)S(1)}, u32[]{:S(2)}) copy-start(f32[4,128]{1,0:T(4,128)S(1)} %log_add_fusion.2) | copy-start | bytes 6148
  45.6 12.8 collective-permute-start.11
  50.8 8.9 collective-permute-start.10
  52.8 8.1 collective-permute-start.9
  74.5 28.3 %copy-start.42 = (f32[4,128]{1,0:T(4,128)S(1)}, f32[4,128]{1,0:T(4,128)}, u32[]{:S(2)}) copy-start(f32[4,128]{1,0:T(4,128)} %copy-done.41) | copy-start | bytes 6148
  74.5 32.9 %copy-start.44 = (f32[4,128]{1,0:T(4,128)S(1)}, f32[4,128]{1,0:T(4,128)}, u32[]{:S(2)}) copy-start(f32[4,128]{1,0:T(4,128)} %copy-done.43) | copy-start | bytes 6148
  74.5 42.3 %copy-start.46 = (f32[4,128]{1,0:T(4,128)S(1)}, f32[4,128]{1,0:T(4,128)}, u32[]{:S(2)}) copy-start(f32[4,128]{1,0:T(4,128)} %copy-done.45) | copy-start | bytes 6148
  74.5 30.4 %collective-permute-start.5 = (bf16[128,512]{1,0:T(8,128)(2,1)}, bf16[128,512]{1,0:T(8,128)(2,1)}, u32[]{:S(2)}, u32[]{:S(2)}) collective-permute-start(bf16[128,512]{1,0:T(8,128)(2,1)} %bitcast.647), channel_id=1, source_target_pairs={{0,3},{1,4},{2,5},{3,6},{4,7},{5,8},{6,9},{7,10},{8,11},{9,12},{10... | collective-permute-start | bytes 393224 | tf_op jit(solution)/shard_map/ppermute | solution.py:19
  79.9 26.2 %collective-permute-start.4 = (bf16[128,512]{1,0:T(8,128)(2,1)}, bf16[128,512]{1,0:T(8,128)(2,1)}, u32[]{:S(2)}, u32[]{:S(2)}) collective-permute-start(bf16[128,512]{1,0:T(8,128)(2,1)} %bitcast.648), channel_id=1, source_target_pairs={{0,2},{1,3},{2,4},{3,5},{4,6},{5,7},{6,8},{7,9},{8,10},{9,11},{10,... | collective-permute-start | bytes 393224 | tf_op jit(solution)/shard_map/ppermute | solution.py:19
  91.5 12.4 collective-permute-start.3
  109.6 21.6 %copy-start.16 = (f32[4,128,128]{1,2,0:T(8,128)S(1)}, f32[4,128,128]{1,2,0:T(8,128)}, u32[]{:S(2)}) copy-start(f32[4,128,128]{1,2,0:T(8,128)} %copy-done.15) | copy-start | bytes 786436
  112.0 22.0 %copy-start.2 = (f32[4,128,128]{1,2,0:T(8,128)S(1)}, f32[4,128,128]{1,2,0:T(8,128)}, u32[]{:S(2)}) copy-start(f32[4,128,128]{1,2,0:T(8,128)} %copy-done.1) | copy-start | bytes 786436
  113.0 22.0 %copy-start.18 = (f32[4,128,128]{1,2,0:T(8,128)S(1)}, f32[4,128,128]{1,2,0:T(8,128)}, u32[]{:S(2)}) copy-start(f32[4,128,128]{1,2,0:T(8,128)} %copy-done.17) | copy-start | bytes 786436
  114.3 21.7 %copy-start.6 = (f32[4,128,128]{1,2,0:T(8,128)S(1)}, f32[4,128,128]{1,2,0:T(8,128)}, u32[]{:S(2)}) copy-start(f32[4,128,128]{1,2,0:T(8,128)} %copy-done.5) | copy-start | bytes 786436
  145.4 10.8 collective-permute-start.6
  148.1 8.0 collective-permute-start.7
  151.7 8.3 collective-permute-start.8
  (37 other events, 412.4 us)
Sparse Core Ops, SparseCore 0:
  74.6 1611.0 reduce-scatter.3
where the time goes:
time: 1720 us; the launch traced here: 1690 us
  waiting for transfers between devices  1530 us (89%)
  matrix products  68 us (4%)
  starting transfers between devices  46.2 us (3%)
  local copies, waits for them, and re-layouts  22.9 us (1%)
    unnamed x2, waiting for transfers between devices  1520 us
    ppermute x12, starting transfers between devices, shifted(): return lax.ppermute(block, axis, route)  46.2 us
  transfers between devices with their start and end apart: 13, of which 5 were waited for; matrix products, arithmetic and copies ran while one was open for 4% of the time, Pallas kernels for 0%

commit v1 on v0

v1 whole, which is shorter than its diff:
```python
import math

import jax
import jax.numpy as jnp
from jax import lax
from jax.experimental import pallas as pl
from jax.experimental.pallas import tpu as pltpu
from jax.sharding import Mesh, PartitionSpec as P

HEAD = 128
STRETCH = 64
SPAN = 4
GROUPS = 4
PER_GROUP = 4
ROWS = 128
KEYS = SPAN * ROWS
WIDE = PER_GROUP * ROWS
MASKED = -1e30
SCALE = HEAD**-0.5
LOG2E = math.log2(math.e)
BF16 = jnp.bfloat16
F32 = jnp.float32
AXES = ("zl", "zh", "x", "y", "c")
CTX = ("zh", "x", "y", "c")
N_CTX = 64
NSTART = 64
MIB = 1024 * 1024


def nt(a, b):
    return lax.dot_general(a, b, (((1,), (1,)), ((), ())), preferred_element_type=F32)


def tn(a, b):
    return lax.dot_general(a, b, (((0,), (0,)), ((), ())), preferred_element_type=F32)


def nn(a, b):
    return lax.dot_general(a, b, (((1,), (0,)), ((), ())), preferred_element_type=F32)


def stack_heads(block):
    return jnp.concatenate([block[:, h * HEAD : (h + 1) * HEAD] for h in range(PER_GROUP)], axis=0)


def forward_kernel(
    ids, order, starts, q_ref, g_ref, k0, k1, k2, k3, prob_ref, own_ref, v1, v2, v3, bias_ref
):
    shard = ids[0]

    @pl.when(pl.program_id(0) == 0)
    def _():
        lane = lax.broadcasted_iota(jnp.int32, (1, ROWS), 1)
        first, second = order[2 * shard], order[2 * shard + 1]
        stretch = jnp.where(lane < STRETCH, first, second)
        query_pos = shard * ROWS + stretch * STRETCH + (lane & (STRETCH - 1))
        begin = jnp.zeros((1, ROWS), jnp.int32)
        for i in range(NSTART):
            begin = jnp.where(starts[i] <= query_pos, starts[i], begin)
        row = lax.broadcasted_iota(jnp.int32, (STRETCH, ROWS), 0)
        for d in range(SPAN):
            source = shard - d
            known = jnp.maximum(source, 0)
            for j in range(2):
                key_pos = source * ROWS + order[2 * known + j] * STRETCH + row
                allowed = (key_pos <= query_pos) & (key_pos >= begin)
                bias_ref[pl.ds((2 * d + j) * STRETCH, STRETCH), :] = jnp.where(
                    allowed, 0.0, MASKED
                )

    keys = jnp.concatenate([k0[...], k1[...], k2[...], k3[...]], axis=0)
    bias = bias_ref[...]
    for h in range(PER_GROUP):
        cols = pl.ds(h * HEAD, HEAD)
        score = nt(keys, q_ref[:, cols]) * (SCALE * LOG2E) + bias
        weight = jnp.exp2(score - jnp.max(score, axis=0, keepdims=True))
        total = jnp.sum(weight, axis=0, keepdims=True)
        prob_ref[0, :, cols] = (weight * (1.0 / total)).astype(BF16)
    value_grad = nn(prob_ref[0], stack_heads(g_ref[...]))
    own_ref[...] = value_grad[:ROWS]
    for d, ref in ((1, v1), (2, v2), (3, v3)):
        ref[...] = value_grad[d * ROWS : (d + 1) * ROWS].astype(BF16)


def backward_kernel(
    prob_ref, q_ref, g_ref, k0, k1, k2, k3, v0, v1, v2, v3, gq_ref, own_ref, d1, d2, d3
):
    keys = jnp.concatenate([k0[...], k1[...], k2[...], k3[...]], axis=0)
    values = jnp.concatenate([v0[...], v1[...], v2[...], v3[...]], axis=0)
    prob = prob_ref[0].astype(F32)
    grad_prob = nt(values, stack_heads(g_ref[...]))
    weighted = prob * grad_prob
    delta = jnp.sum(weighted, axis=0, keepdims=True)
    grad_score = (weighted - prob * delta).astype(BF16)
    key_grad = nn(grad_score, stack_heads(q_ref[...])) * SCALE
    own_ref[...] = key_grad[:ROWS]
    for d, ref in ((1, d1), (2, d2), (3, d3)):
        ref[...] = key_grad[d * ROWS : (d + 1) * ROWS].astype(BF16)
    query_grad = tn(grad_score, keys) * SCALE
    for h in range(PER_GROUP):
        gq_ref[:, h * HEAD : (h + 1) * HEAD] = query_grad[h * ROWS : (h + 1) * ROWS].astype(BF16)


def group_spec(width):
    return pl.BlockSpec((ROWS, width), lambda g, *_: (0, g))


def prob_spec():
    return pl.BlockSpec((1, KEYS, WIDE), lambda g, *_: (g, 0, 0))


def forward_call(ids, order, starts, query, grad, keys):
    narrow = jax.ShapeDtypeStruct((ROWS, GROUPS * HEAD), BF16)
    return pl.pallas_call(
        forward_kernel,
        grid_spec=pltpu.PrefetchScalarGridSpec(
            num_scalar_prefetch=3,
            grid=(GROUPS,),
            in_specs=[group_spec(PER_GROUP * HEAD)] * 2 + [group_spec(HEAD)] * SPAN,
            out_specs=[prob_spec()] + [group_spec(HEAD)] * SPAN,
            scratch_shapes=[pltpu.VMEM((KEYS, ROWS), F32)],
        ),
        out_shape=[
            jax.ShapeDtypeStruct((GROUPS, KEYS, WIDE), BF16),
            jax.ShapeDtypeStruct((ROWS, GROUPS * HEAD), F32),
            narrow,
            narrow,
            narrow,
        ],
        cost_estimate=pl.CostEstimate(
            flops=4 * 16 * ROWS * KEYS * HEAD, bytes_accessed=6 * MIB, transcendentals=MIB
        ),
        compiler_params=pltpu.CompilerParams(vmem_limit_bytes=24 * MIB),
        name="forward_and_value_gradient",
    )(ids, order, starts, query, grad, *keys)


def backward_call(prob, query, grad, keys, values):
    narrow = jax.ShapeDtypeStruct((ROWS, GROUPS * HEAD), BF16)
    return pl.pallas_call(
        backward_kernel,
        grid=(GROUPS,),
        in_specs=[prob_spec()] + [group_spec(PER_GROUP * HEAD)] * 2 + [group_spec(HEAD)] * 8,
        out_specs=[group_spec(PER_GROUP * HEAD)] + [group_spec(HEAD)] * SPAN,
        out_shape=[
            jax.ShapeDtypeStruct((ROWS, GROUPS * WIDE), BF16),
            jax.ShapeDtypeStruct((ROWS, GROUPS * HEAD), F32),
            narrow,
            narrow,
            narrow,
        ],
        cost_estimate=pl.CostEstimate(
            flops=6 * 16 * ROWS * KEYS * HEAD, bytes_accessed=6 * MIB, transcendentals=0
        ),
        compiler_params=pltpu.CompilerParams(vmem_limit_bytes=24 * MIB),
        name="query_and_key_gradient",
    )(prob, query, grad, *keys, *values)


def pack_kernel(ids, a0, a1, a2, a3, o0, o1, o2, o3):
    for a, o in ((a0, o0), (a1, o1), (a2, o2), (a3, o3)):
        o[...] = a[...]


def pack_call(ids, inputs):
    def taken(d):
        return pl.BlockSpec((ROWS, HEAD), lambda i, ids: (0, 4 * i + ((ids[1] + d) & 3)))

    return pl.pallas_call(
        pack_kernel,
        grid_spec=pltpu.PrefetchScalarGridSpec(
            num_scalar_prefetch=1,
            grid=(8,),
            in_specs=[taken(d) for d in range(4)],
            out_specs=[pl.BlockSpec((ROWS, HEAD), lambda i, ids: (0, i))] * 4,
        ),
        out_shape=[jax.ShapeDtypeStruct((ROWS, 8 * HEAD), BF16)] * 4,
        cost_estimate=pl.CostEstimate(flops=0, bytes_accessed=2 * MIB, transcendentals=0),
        name="pack_inputs",
    )(ids, inputs, inputs, inputs, inputs)


def weight_kernel(ids, grads, a0, a1, a2, a3, b0, b1, b2, b3, out_ref):
    x, core = ids[1], ids[2]
    total = jnp.zeros((8 * HEAD, 256), F32)
    for side, blocks in ((core, (a0, a1, a2, a3)), (1 - core, (b0, b1, b2, b3))):
        for d, block in enumerate(blocks):
            total += tn(block[...], grads[((x + 4 - d) & 3) * 2 + side])
    half = total.astype(BF16)
    for z in range(8):
        for y in range(4):
            out_ref[y, z * 32 : (z + 1) * 32, :] = half[z * 128 + y * 32 : z * 128 + y * 32 + 32]


def weight_call(ids, grads, own, other):
    whole = pl.BlockSpec(memory_space=pltpu.VMEM)
    return pl.pallas_call(
        weight_kernel,
        grid_spec=pltpu.PrefetchScalarGridSpec(
            num_scalar_prefetch=1,
            grid=(1,),
            in_specs=[whole] * 9,
            out_specs=whole,
        ),
        out_shape=jax.ShapeDtypeStruct((4, 256, 256), BF16),
        cost_estimate=pl.CostEstimate(
            flops=2 * 1024 * 1024 * 256, bytes_accessed=3 * MIB, transcendentals=0
        ),
        compiler_params=pltpu.CompilerParams(vmem_limit_bytes=32 * MIB),
        name="weight_gradient",
    )(ids, grads, *own, *other)


def shift_shards(block, distance):
    route = [(i - distance, i) for i in range(N_CTX) if 0 <= i - distance < N_CTX]
    return lax.ppermute(block, CTX, route)


def shift_x(block, distance):
    return lax.ppermute(block, "x", [(i, (i + distance) % 4) for i in range(4)])


def swap_core(block):
    return lax.ppermute(block, "c", [(0, 1), (1, 0)])


def shards(query, key, value, grad, inputs, stretch_order, session_starts):
    query, key, value, grad, inputs = query[0], key[0], value[0], grad[0], inputs[0]
    x, core = lax.axis_index("x"), lax.axis_index("c")
    ids = jnp.stack([lax.axis_index(CTX), x, core]).astype(jnp.int32)
    order = stretch_order.reshape(-1)
    starts = session_starts.reshape(-1)

    keys = [key] + [shift_shards(key, d) for d in range(1, SPAN)]
    values = [value] + [shift_shards(value, d) for d in range(1, SPAN)]
    packed = pack_call(ids, inputs)
    own = [packed[0]] + [shift_x(packed[d], d) for d in range(1, 4)]
    other = [swap_core(block) for block in own]

    prob, value_own, *value_terms = forward_call(ids, order, starts, query, grad, keys)
    grad_value = value_own
    for d in range(1, SPAN):
        grad_value = grad_value + shift_shards(value_terms[d - 1], -d).astype(F32)
    grad_value = grad_value.astype(BF16)

    grad_query, key_own, *key_terms = backward_call(prob, query, grad, keys, values)
    grad_key = key_own
    for d in range(1, SPAN):
        grad_key = grad_key + shift_shards(key_terms[d - 1], -d).astype(F32)
    grad_key = grad_key.astype(BF16)

    halves = jnp.stack([grad_value[:, :256], grad_value[:, 256:]])
    sent = jnp.broadcast_to(halves[None], (4, 2, ROWS, 256)).reshape(8, ROWS, 256)
    gathered = lax.all_to_all(sent, ("x", "c"), 0, 0, tiled=True)
    partial = weight_call(ids, gathered, own, other)
    partial = lax.all_to_all(partial, "y", 0, 0, tiled=True)
    partial = jnp.sum(partial.astype(F32), axis=0).astype(BF16).reshape(16, 16, 256)
    partial = lax.all_to_all(partial, ("zl", "zh", "c"), 0, 0, tiled=True)
    summed = jnp.sum(partial.reshape(8, 2, 16, 256).astype(F32), axis=0)
    weight_grad = jnp.concatenate([summed[0], summed[1]], axis=1)
    return grad_query[None], grad_key[None], grad_value[None], weight_grad


def solution(mesh):
    fine = Mesh(mesh.devices.reshape(4, 2, 4, 4, 2), AXES)
    rows = P("zl", CTX, None)
    return jax.shard_map(
        shards,
        mesh=fine,
        in_specs=(rows, rows, rows, rows, rows, P("zl", None, None), P("zl", None)),
        out_specs=(rows, rows, rows, P(AXES, None)),
        check_vma=False,
    )
```

time: 1720 us -> 146 us (0.08)
  the two profiles are of different devices: /device:TPU:7 before, /device:TPU:3 now
where the time goes in v1:
time: 146 us; the launch traced here: 144 us
  starting transfers between devices  80.6 us (55%)
  waiting for transfers between devices  23.5 us (16%)
  Pallas kernels  18.2 us (12%)
  local copies, waits for them, and re-layouts  16.8 us (12%)
  other arithmetic  4.22 us (3%)
    ppermute x12, starting transfers between devices, shift_shards(): return lax.ppermute(block, CTX, route)  38.8 us
    all_to_all x1, starting transfers between devices, shards(): partial = lax.all_to_all(partial, ('zl', 'zh', 'c'), 0, 0, tiled=True)  20.9 us
    unnamed x53, local copies, waits for them, and re-layouts  15.8 us
    ppermute x12, waiting for transfers between devices, shift_shards(): return lax.ppermute(block, CTX, route)  10.9 us
    all_to_all x1, waiting for transfers between devices, shards(): partial = lax.all_to_all(partial, ('zl', 'zh', 'c'), 0, 0, tiled=True)  8.31 us
    all_to_all x1, starting transfers between devices, shards(): partial = lax.all_to_all(partial, 'y', 0, 0, tiled=True)  6.28 us
    pallas_call x1, Pallas kernels, pack_call(): pl.pallas_call(pack_kernel, grid_spec=pltpu.PrefetchScalarGridSpec(num_sc...  5.55 us
    all_to_all x1, starting transfers between devices, shards(): gathered = lax.all_to_all(sent, ('x', 'c'), 0, 0, tiled=True)  5.48 us
  transfers between devices with their start and end apart: 22, of which 7 were waited for; matrix products, arithmetic and copies ran while one was open for 4% of the time, Pallas kernels for 7%

profile of v1, /device:TPU:3, one launch (start us, length us, event | category | flops | bytes accessed | tf_op | source)
XLA Modules:
  0.0 144.2 jit_solution(4069177954066265098)
XLA Ops:
  0.6 3.8 %collective-permute-start = (bf16[128,512]{1,0:T(8,128)(2,1)}, bf16[128,512]{1,0:T(8,128)(2,1)S(1)}, u32[]{:S(2)}, u32[]{:S(2)}) collective-permute-start(bf16[128,512]{1,0:T(8,128)(2,1)} %bitcast.29), channel_id=1, source_target_pairs={{0,1},{1,2},{2,3},{3,4},{4,5},{5,6},{6,7},{7,8},{8,9},{9,10},{10,1... | collective-permute-start | bytes 393224 | tf_op jit(solution)/shard_map/ppermute | solution.py:216
  4.4 3.2 %collective-permute-start.1 = (bf16[128,512]{1,0:T(8,128)(2,1)}, bf16[128,512]{1,0:T(8,128)(2,1)S(1)}, u32[]{:S(2)}, u32[]{:S(2)}) collective-permute-start(bf16[128,512]{1,0:T(8,128)(2,1)} %bitcast.30), channel_id=1, source_target_pairs={{0,2},{1,3},{2,4},{3,5},{4,6},{5,7},{6,8},{7,9},{8,10},{9,11},{10,... | collective-permute-start | bytes 393224 | tf_op jit(solution)/shard_map/ppermute | solution.py:216
  7.6 3.5 %collective-permute-start.2 = (bf16[128,512]{1,0:T(8,128)(2,1)}, bf16[128,512]{1,0:T(8,128)(2,1)S(1)}, u32[]{:S(2)}, u32[]{:S(2)}) collective-permute-start(bf16[128,512]{1,0:T(8,128)(2,1)} %bitcast.31), channel_id=1, source_target_pairs={{0,3},{1,4},{2,5},{3,6},{4,7},{5,8},{6,9},{7,10},{8,11},{9,12},{10... | collective-permute-start | bytes 393224 | tf_op jit(solution)/shard_map/ppermute | solution.py:216
  13.1 3.9 %collective-permute-done.2.k3 = bf16[128,512]{1,0:T(8,128)(2,1)S(1)} collective-permute-done((bf16[128,512]{1,0:T(8,128)(2,1)}, bf16[128,512]{1,0:T(8,128)(2,1)S(1)}, u32[]{:S(2)}, u32[]{:S(2)}) %collective-permute-start.2) | collective-permute-done | bytes 131104 | tf_op jit(solution)/shard_map/ppermute | solution.py:216
  20.8 4.5 %forward_and_value_gradient.1 = (bf16[4,512,512]{2,1,0:T(8,128)(2,1)S(1)}, f32[128,512]{1,0:T(8,128)S(1)}, bf16[128,512]{1,0:T(8,128)(2,1)S(1)}, bf16[128,512]{1,0:T(8,128)(2,1)S(1)}, bf16[128,512]{1,0:T(8,128)(2,1)S(1)}) custom-call(s32[3]{0:T(128)S(1)} %pad_add_fusion.ids, s32[128]{0:T(128)S(1)} %reshape.24.order, s32[64]{0:T(128)S(1)} %bitcast.38, ...), custom_call_target="tpu_custom_call" | custom-call | flops 536870912 | bytes 6291456 | tf_op jit(solution)/shard_map/forward_and_value_gradient/pallas_call | solution.py:114
  27.2 3.7 %collective-permute-start.10 = (bf16[128,512]{1,0:T(8,128)(2,1)S(1)}, bf16[128,512]{1,0:T(8,128)(2,1)S(1)}, u32[]{:S(2)}, u32[]{:S(2)}) collective-permute-start(bf16[128,512]{1,0:T(8,128)(2,1)S(1)} %get-tuple-element.26), channel_id=1, source_target_pairs={{2,0},{3,1},{4,2},{5,3},{6,4},{7,5},{8,6},{9,7},{10,8},{11,9},{12,... | collective-permute-start | bytes 393224 | tf_op jit(solution)/shard_map/ppermute | solution.py:216
  30.9 2.6 %collective-permute-start.9 = (bf16[128,512]{1,0:T(8,128)(2,1)S(1)}, bf16[128,512]{1,0:T(8,128)(2,1)}, u32[]{:S(2)}, u32[]{:S(2)}) collective-permute-start(bf16[128,512]{1,0:T(8,128)(2,1)S(1)} %get-tuple-element.25), channel_id=1, source_target_pairs={{1,0},{2,1},{3,2},{4,3},{5,4},{6,5},{7,6},{8,7},{9,8},{10,9},{11,1... | collective-permute-start | bytes 393224 | tf_op jit(solution)/shard_map/ppermute | solution.py:216
  33.5 5.5 %pack_inputs.1 = (bf16[128,1024]{1,0:T(8,128)(2,1)}, bf16[128,1024]{1,0:T(8,128)(2,1)}, bf16[128,1024]{1,0:T(8,128)(2,1)}, bf16[128,1024]{1,0:T(8,128)(2,1)}) custom-call(s32[3]{0:T(128)} %copy-done.22, bf16[128,4096]{1,0:T(8,128)(2,1)} %bitcast.39, bf16[128,4096]{1,0:T(8,128)(2,1)} %bitcast.40, bf16[128,4096]{1,0:T(8,128)(2,1)} %bitcast.41, ...), custom_call_target="tpu_custom_call" | custom-call | bytes 2097152 | tf_op jit(solution)/shard_map/pack_inputs/pallas_call | solution.py:169
  41.7 2.0 %collective-permute-start.14 = (bf16[128,1024]{1,0:T(8,128)(2,1)}, bf16[128,1024]{1,0:T(8,128)(2,1)}, u32[]{:S(2)}, u32[]{:S(2)}) collective-permute-start(bf16[128,1024]{1,0:T(8,128)(2,1)} %get-tuple-element.31), channel_id=1, source_target_pairs={{0,24},{8,0},{16,8},{24,16},{1,25},{9,1},{17,9},{25,17},{2,26},{10... | collective-permute-start | bytes 786440 | tf_op jit(solution)/shard_map/ppermute | solution.py:220
  45.5 5.5 %all-to-all-start = ((bf16[8,128,256]{2,1,0:T(8,128)(2,1)}), bf16[8,128,256]{2,1,0:T(8,128)(2,1)S(1)}, u32[]{:S(2)}, u32[]{:S(2)}) async-start(bf16[8,128,256]{2,1,0:T(8,128)(2,1)} %bitcast.13), calls=%async_computation | async-start | bytes 1048576 | tf_op jit(solution)/shard_map/all_to_all | solution.py:254
  51.5 2.2 %collective-permute-start.16 = (bf16[128,1024]{1,0:T(8,128)(2,1)}, bf16[128,1024]{1,0:T(8,128)(2,1)S(1)}, u32[]{:S(2)}, u32[]{:S(2)}) collective-permute-start(bf16[128,1024]{1,0:T(8,128)(2,1)} %collective-permute-done.12.a1), channel_id=1, source_target_pairs={{0,1},{1,0},{2,3},{3,2},{4,5},{5,4},{6,7},{7,6},{8,9},{9,8},{10,11... | collective-permute-start | bytes 786440 | tf_op jit(solution)/shard_map/ppermute | solution.py:224
  53.7 3.3 %collective-permute-done.14.a3 = bf16[128,1024]{1,0:T(8,128)(2,1)} collective-permute-done((bf16[128,1024]{1,0:T(8,128)(2,1)}, bf16[128,1024]{1,0:T(8,128)(2,1)}, u32[]{:S(2)}, u32[]{:S(2)}) %collective-permute-start.14) | collective-permute-done | bytes 262176 | tf_op jit(solution)/shard_map/ppermute | solution.py:220
  66.4 3.7 %weight_gradient.1 = bf16[4,256,256]{2,1,0:T(8,128)(2,1)} custom-call(s32[3]{0:T(128)S(1)} %copy-done.23, bf16[8,128,256]{2,1,0:T(8,128)(2,1)S(1)} %all-to-all-done.grads, bf16[128,1024]{1,0:T(8,128)(2,1)S(1)} %copy-done.4, bf16[128,1024]{1,0:T(8,128)(2,1)} %collective-permute-done.12.a1, bf16[128,1024]{1,0:T(8,128)(2,1)} %collective-permute-done.13.a2, ...), custom_call_target="tpu_custom_call" | custom-call | flops 536870912 | bytes 3145728 | tf_op jit(solution)/shard_map/weight_gradient/pallas_call | solution.py:197
  70.1 6.3 %all-to-all-start.1 = ((bf16[4,256,256]{2,1,0:T(8,128)(2,1)}), bf16[4,256,256]{2,1,0:T(8,128)(2,1)}, u32[]{:S(2)}, u32[]{:S(2)}) async-start(bf16[4,256,256]{2,1,0:T(8,128)(2,1)} %weight_gradient.1), calls=%async_computation.1 | async-start | bytes 1048576 | tf_op jit(solution)/shard_map/all_to_all | solution.py:256
  76.4 4.7 %collective-permute-start.3 = (bf16[128,512]{1,0:T(8,128)(2,1)}, bf16[128,512]{1,0:T(8,128)(2,1)S(1)}, u32[]{:S(2)}, u32[]{:S(2)}) collective-permute-start(bf16[128,512]{1,0:T(8,128)(2,1)} %bitcast.34), channel_id=1, source_target_pairs={{0,1},{1,2},{2,3},{3,4},{4,5},{5,6},{6,7},{7,8},{8,9},{9,10},{10,1... | collective-permute-start | bytes 393224 | tf_op jit(solution)/shard_map/ppermute | solution.py:216
  81.1 3.1 %collective-permute-start.4 = (bf16[128,512]{1,0:T(8,128)(2,1)}, bf16[128,512]{1,0:T(8,128)(2,1)S(1)}, u32[]{:S(2)}, u32[]{:S(2)}) collective-permute-start(bf16[128,512]{1,0:T(8,128)(2,1)} %bitcast.35), channel_id=1, source_target_pairs={{0,2},{1,3},{2,4},{3,5},{4,6},{5,7},{6,8},{7,9},{8,10},{9,11},{10,... | collective-permute-start | bytes 393224 | tf_op jit(solution)/shard_map/ppermute | solution.py:216
  84.2 3.4 %collective-permute-start.5 = (bf16[128,512]{1,0:T(8,128)(2,1)}, bf16[128,512]{1,0:T(8,128)(2,1)S(1)}, u32[]{:S(2)}, u32[]{:S(2)}) collective-permute-start(bf16[128,512]{1,0:T(8,128)(2,1)} %bitcast.36), channel_id=1, source_target_pairs={{0,3},{1,4},{2,5},{3,6},{4,7},{5,8},{6,9},{7,10},{8,11},{9,12},{10... | collective-permute-start | bytes 393224 | tf_op jit(solution)/shard_map/ppermute | solution.py:216
  87.6 2.3 %collective-permute-done.4.v2 = bf16[128,512]{1,0:T(8,128)(2,1)S(1)} collective-permute-done((bf16[128,512]{1,0:T(8,128)(2,1)}, bf16[128,512]{1,0:T(8,128)(2,1)S(1)}, u32[]{:S(2)}, u32[]{:S(2)}) %collective-permute-start.4) | collective-permute-done | bytes 131104 | tf_op jit(solution)/shard_map/ppermute | solution.py:216
  89.9 3.7 %collective-permute-done.5.v3 = bf16[128,512]{1,0:T(8,128)(2,1)S(1)} collective-permute-done((bf16[128,512]{1,0:T(8,128)(2,1)}, bf16[128,512]{1,0:T(8,128)(2,1)S(1)}, u32[]{:S(2)}, u32[]{:S(2)}) %collective-permute-start.5) | collective-permute-done | bytes 131104 | tf_op jit(solution)/shard_map/ppermute | solution.py:216
  98.3 4.4 %query_and_key_gradient.1 = (bf16[128,2048]{1,0:T(8,128)(2,1)}, f32[128,512]{1,0:T(8,128)S(1)}, bf16[128,512]{1,0:T(8,128)(2,1)S(1)}, bf16[128,512]{1,0:T(8,128)(2,1)S(1)}, bf16[128,512]{1,0:T(8,128)(2,1)S(1)}) custom-call(bf16[4,512,512]{2,1,0:T(8,128)(2,1)S(1)} %get-tuple-element.18.prob_ref, bf16[128,2048]{1,0:T(8,128)(2,1)S(1)} %bitcast.26, ...), custom_call_target="tpu_custom_call" | custom-call | flops 805306368 | bytes 6291456 | tf_op jit(solution)/shard_map/query_and_key_gradient/pallas_call | solution.py:140
  104.6 4.5 %collective-permute-start.7 = (bf16[128,512]{1,0:T(8,128)(2,1)S(1)}, bf16[128,512]{1,0:T(8,128)(2,1)S(1)}, u32[]{:S(2)}, u32[]{:S(2)}) collective-permute-start(bf16[128,512]{1,0:T(8,128)(2,1)S(1)} %get-tuple-element.22), channel_id=1, source_target_pairs={{2,0},{3,1},{4,2},{5,3},{6,4},{7,5},{8,6},{9,7},{10,8},{11,9},{12,... | collective-permute-start | bytes 393224 | tf_op jit(solution)/shard_map/ppermute | solution.py:216
  109.1 2.6 %collective-permute-start.6 = (bf16[128,512]{1,0:T(8,128)(2,1)S(1)}, bf16[128,512]{1,0:T(8,128)(2,1)S(1)}, u32[]{:S(2)}, u32[]{:S(2)}) collective-permute-start(bf16[128,512]{1,0:T(8,128)(2,1)S(1)} %get-tuple-element.21), channel_id=1, source_target_pairs={{1,0},{2,1},{3,2},{4,3},{5,4},{6,5},{7,6},{8,7},{9,8},{10,9},{11,1... | collective-permute-start | bytes 393224 | tf_op jit(solution)/shard_map/ppermute | solution.py:216
  113.5 20.9 %all-to-all-start.2 = ((bf16[16,16,256]{2,1,0:T(8,128)(2,1)}), bf16[16,16,256]{2,1,0:T(8,128)(2,1)S(1)}, u32[]{:S(2)}, u32[]{:S(2)}) async-start(bf16[16,16,256]{2,1,0:T(8,128)(2,1)} %bitcast.15), calls=%async_computation.2 | async-start | bytes 262144 | tf_op jit(solution)/shard_map/all_to_all | solution.py:258
  135.2 8.3 %all-to-all-done.2 = bf16[16,16,256]{2,1,0:T(8,128)(2,1)S(1)} async-done(((bf16[16,16,256]{2,1,0:T(8,128)(2,1)}), bf16[16,16,256]{2,1,0:T(8,128)(2,1)S(1)}, u32[]{:S(2)}, u32[]{:S(2)}) %all-to-all-start.2) | async-done | bytes 131104 | tf_op jit(solution)/shard_map/all_to_all | solution.py:258
  (88 shorter events, 31.6 us)
Async XLA Ops:
  0.6 11.5 %collective-permute-start = (bf16[128,512]{1,0:T(8,128)(2,1)}, bf16[128,512]{1,0:T(8,128)(2,1)S(1)}, u32[]{:S(2)}, u32[]{:S(2)}) collective-permute-start(bf16[128,512]{1,0:T(8,128)(2,1)} %bitcast.29), channel_id=1, source_target_pairs={{0,1},{1,2},{2,3},{3,4},{4,5},{5,6},{6,7},{7,8},{8,9},{9,10},{10,1... | collective-permute-start | bytes 393224 | tf_op jit(solution)/shard_map/ppermute | solution.py:216
  4.4 8.7 %collective-permute-start.1 = (bf16[128,512]{1,0:T(8,128)(2,1)}, bf16[128,512]{1,0:T(8,128)(2,1)S(1)}, u32[]{:S(2)}, u32[]{:S(2)}) collective-permute-start(bf16[128,512]{1,0:T(8,128)(2,1)} %bitcast.30), channel_id=1, source_target_pairs={{0,2},{1,3},{2,4},{3,5},{4,6},{5,7},{6,8},{7,9},{8,10},{9,11},{10,... | collective-permute-start | bytes 393224 | tf_op jit(solution)/shard_map/ppermute | solution.py:216
  7.6 9.4 %collective-permute-start.2 = (bf16[128,512]{1,0:T(8,128)(2,1)}, bf16[128,512]{1,0:T(8,128)(2,1)S(1)}, u32[]{:S(2)}, u32[]{:S(2)}) collective-permute-start(bf16[128,512]{1,0:T(8,128)(2,1)} %bitcast.31), channel_id=1, source_target_pairs={{0,3},{1,4},{2,5},{3,6},{4,7},{5,8},{6,9},{7,10},{8,11},{9,12},{10... | collective-permute-start | bytes 393224 | tf_op jit(solution)/shard_map/ppermute | solution.py:216
  25.3 16.4 %collective-permute-start.11 = (bf16[128,512]{1,0:T(8,128)(2,1)S(1)}, bf16[128,512]{1,0:T(8,128)(2,1)S(1)}, u32[]{:S(2)}, u32[]{:S(2)}) collective-permute-start(bf16[128,512]{1,0:T(8,128)(2,1)S(1)} %get-tuple-element.27), channel_id=1, source_target_pairs={{3,0},{4,1},{5,2},{6,3},{7,4},{8,5},{9,6},{10,7},{11,8},{12,9},{13... | collective-permute-start | bytes 393224 | tf_op jit(solution)/shard_map/ppermute | solution.py:216
  27.2 16.5 %collective-permute-start.10 = (bf16[128,512]{1,0:T(8,128)(2,1)S(1)}, bf16[128,512]{1,0:T(8,128)(2,1)S(1)}, u32[]{:S(2)}, u32[]{:S(2)}) collective-permute-start(bf16[128,512]{1,0:T(8,128)(2,1)S(1)} %get-tuple-element.26), channel_id=1, source_target_pairs={{2,0},{3,1},{4,2},{5,3},{6,4},{7,5},{8,6},{9,7},{10,8},{11,9},{12,... | collective-permute-start | bytes 393224 | tf_op jit(solution)/shard_map/ppermute | solution.py:216
  30.9 12.8 %collective-permute-start.9 = (bf16[128,512]{1,0:T(8,128)(2,1)S(1)}, bf16[128,512]{1,0:T(8,128)(2,1)}, u32[]{:S(2)}, u32[]{:S(2)}) collective-permute-start(bf16[128,512]{1,0:T(8,128)(2,1)S(1)} %get-tuple-element.25), channel_id=1, source_target_pairs={{1,0},{2,1},{3,2},{4,3},{5,4},{6,5},{7,6},{8,7},{9,8},{10,9},{11,1... | collective-permute-start | bytes 393224 | tf_op jit(solution)/shard_map/ppermute | solution.py:216
  39.1 12.4 %collective-permute-start.12 = (bf16[128,1024]{1,0:T(8,128)(2,1)}, bf16[128,1024]{1,0:T(8,128)(2,1)}, u32[]{:S(2)}, u32[]{:S(2)}) collective-permute-start(bf16[128,1024]{1,0:T(8,128)(2,1)} %get-tuple-element.29), channel_id=1, source_target_pairs={{0,8},{8,16},{16,24},{24,0},{1,9},{9,17},{17,25},{25,1},{2,10},{10... | collective-permute-start | bytes 786440 | tf_op jit(solution)/shard_map/ppermute | solution.py:220
  40.7 13.0 %collective-permute-start.13 = (bf16[128,1024]{1,0:T(8,128)(2,1)}, bf16[128,1024]{1,0:T(8,128)(2,1)}, u32[]{:S(2)}, u32[]{:S(2)}) collective-permute-start(bf16[128,1024]{1,0:T(8,128)(2,1)} %get-tuple-element.30), channel_id=1, source_target_pairs={{0,16},{8,24},{16,0},{24,8},{1,17},{9,25},{17,1},{25,9},{2,18},{10... | collective-permute-start | bytes 786440 | tf_op jit(solution)/shard_map/ppermute | solution.py:220
  41.7 15.3 %collective-permute-start.14 = (bf16[128,1024]{1,0:T(8,128)(2,1)}, bf16[128,1024]{1,0:T(8,128)(2,1)}, u32[]{:S(2)}, u32[]{:S(2)}) collective-permute-start(bf16[128,1024]{1,0:T(8,128)(2,1)} %get-tuple-element.31), channel_id=1, source_target_pairs={{0,24},{8,0},{16,8},{24,16},{1,25},{9,1},{17,9},{25,17},{2,26},{10... | collective-permute-start | bytes 786440 | tf_op jit(solution)/shard_map/ppermute | solution.py:220
  45.5 48.1 %copy-start.14 = (bf16[1,128,512]{2,1,0:T(8,128)(2,1)S(1)}, bf16[1,128,512]{2,1,0:T(8,128)(2,1)}, u32[]{:S(2)}) copy-start(bf16[1,128,512]{2,1,0:T(8,128)(2,1)} %param.8) | copy-start | bytes 393220
  45.5 17.0 %all-to-all-start = ((bf16[8,128,256]{2,1,0:T(8,128)(2,1)}), bf16[8,128,256]{2,1,0:T(8,128)(2,1)S(1)}, u32[]{:S(2)}, u32[]{:S(2)}) async-start(bf16[8,128,256]{2,1,0:T(8,128)(2,1)} %bitcast.13), calls=%async_computation | async-start | bytes 1048576 | tf_op jit(solution)/shard_map/all_to_all | solution.py:254
  51.0 42.6 %copy-start.1 = (bf16[1,128,2048]{2,1,0:T(8,128)(2,1)S(1)}, bf16[1,128,2048]{2,1,0:T(8,128)(2,1)}, u32[]{:S(2)}) copy-start(bf16[1,128,2048]{2,1,0:T(8,128)(2,1)} %param.7) | copy-start | bytes 1572868
  51.1 7.8 %collective-permute-start.15 = (bf16[128,1024]{1,0:T(8,128)(2,1)S(1)}, bf16[128,1024]{1,0:T(8,128)(2,1)S(1)}, u32[]{:S(2)}, u32[]{:S(2)}) collective-permute-start(bf16[128,1024]{1,0:T(8,128)(2,1)S(1)} %copy-done.4), channel_id=1, source_target_pairs={{0,1},{1,0},{2,3},{3,2},{4,5},{5,4},{6,7},{7,6},{8,9},{9,8},{10,11... | collective-permute-start | bytes 786440 | tf_op jit(solution)/shard_map/ppermute | solution.py:224
  51.5 8.0 %collective-permute-start.16 = (bf16[128,1024]{1,0:T(8,128)(2,1)}, bf16[128,1024]{1,0:T(8,128)(2,1)S(1)}, u32[]{:S(2)}, u32[]{:S(2)}) collective-permute-start(bf16[128,1024]{1,0:T(8,128)(2,1)} %collective-permute-done.12.a1), channel_id=1, source_target_pairs={{0,1},{1,0},{2,3},{3,2},{4,5},{5,4},{6,7},{7,6},{8,9},{9,8},{10,11... | collective-permute-start | bytes 786440 | tf_op jit(solution)/shard_map/ppermute | solution.py:224
  53.7 6.5 %collective-permute-start.17 = (bf16[128,1024]{1,0:T(8,128)(2,1)}, bf16[128,1024]{1,0:T(8,128)(2,1)S(1)}, u32[]{:S(2)}, u32[]{:S(2)}) collective-permute-start(bf16[128,1024]{1,0:T(8,128)(2,1)} %collective-permute-done.13.a2), channel_id=1, source_target_pairs={{0,1},{1,0},{2,3},{3,2},{4,5},{5,4},{6,7},{7,6},{8,9},{9,8},{10,11... | collective-permute-start | bytes 786440 | tf_op jit(solution)/shard_map/ppermute | solution.py:224
  57.0 4.0 %collective-permute-start.18 = (bf16[128,1024]{1,0:T(8,128)(2,1)}, bf16[128,1024]{1,0:T(8,128)(2,1)S(1)}, u32[]{:S(2)}, u32[]{:S(2)}) collective-permute-start(bf16[128,1024]{1,0:T(8,128)(2,1)} %collective-permute-done.14.a3), channel_id=1, source_target_pairs={{0,1},{1,0},{2,3},{3,2},{4,5},{5,4},{6,7},{7,6},{8,9},{9,8},{10,11... | collective-permute-start | bytes 786440 | tf_op jit(solution)/shard_map/ppermute | solution.py:224
  70.1 41.6 %all-to-all-start.1 = ((bf16[4,256,256]{2,1,0:T(8,128)(2,1)}), bf16[4,256,256]{2,1,0:T(8,128)(2,1)}, u32[]{:S(2)}, u32[]{:S(2)}) async-start(bf16[4,256,256]{2,1,0:T(8,128)(2,1)} %weight_gradient.1), calls=%async_computation.1 | async-start | bytes 1048576 | tf_op jit(solution)/shard_map/all_to_all | solution.py:256
  76.4 11.2 %collective-permute-start.3 = (bf16[128,512]{1,0:T(8,128)(2,1)}, bf16[128,512]{1,0:T(8,128)(2,1)S(1)}, u32[]{:S(2)}, u32[]{:S(2)}) collective-permute-start(bf16[128,512]{1,0:T(8,128)(2,1)} %bitcast.34), channel_id=1, source_target_pairs={{0,1},{1,2},{2,3},{3,4},{4,5},{5,6},{6,7},{7,8},{8,9},{9,10},{10,1... | collective-permute-start | bytes 393224 | tf_op jit(solution)/shard_map/ppermute | solution.py:216
  81.1 8.8 %collective-permute-start.4 = (bf16[128,512]{1,0:T(8,128)(2,1)}, bf16[128,512]{1,0:T(8,128)(2,1)S(1)}, u32[]{:S(2)}, u32[]{:S(2)}) collective-permute-start(bf16[128,512]{1,0:T(8,128)(2,1)} %bitcast.35), channel_id=1, source_target_pairs={{0,2},{1,3},{2,4},{3,5},{4,6},{5,7},{6,8},{7,9},{8,10},{9,11},{10,... | collective-permute-start | bytes 393224 | tf_op jit(solution)/shard_map/ppermute | solution.py:216
  84.2 9.4 %collective-permute-start.5 = (bf16[128,512]{1,0:T(8,128)(2,1)}, bf16[128,512]{1,0:T(8,128)(2,1)S(1)}, u32[]{:S(2)}, u32[]{:S(2)}) collective-permute-start(bf16[128,512]{1,0:T(8,128)(2,1)} %bitcast.36), channel_id=1, source_target_pairs={{0,3},{1,4},{2,5},{3,6},{4,7},{5,8},{6,9},{7,10},{8,11},{9,12},{10... | collective-permute-start | bytes 393224 | tf_op jit(solution)/shard_map/ppermute | solution.py:216
  102.7 31.7 %collective-permute-start.8 = (bf16[128,512]{1,0:T(8,128)(2,1)S(1)}, bf16[128,512]{1,0:T(8,128)(2,1)S(1)}, u32[]{:S(2)}, u32[]{:S(2)}) collective-permute-start(bf16[128,512]{1,0:T(8,128)(2,1)S(1)} %get-tuple-element.23), channel_id=1, source_target_pairs={{3,0},{4,1},{5,2},{6,3},{7,4},{8,5},{9,6},{10,7},{11,8},{12,9},{13... | collective-permute-start | bytes 393224 | tf_op jit(solution)/shard_map/ppermute | solution.py:216
  104.6 29.8 %collective-permute-start.7 = (bf16[128,512]{1,0:T(8,128)(2,1)S(1)}, bf16[128,512]{1,0:T(8,128)(2,1)S(1)}, u32[]{:S(2)}, u32[]{:S(2)}) collective-permute-start(bf16[128,512]{1,0:T(8,128)(2,1)S(1)} %get-tuple-element.22), channel_id=1, source_target_pairs={{2,0},{3,1},{4,2},{5,3},{6,4},{7,5},{8,6},{9,7},{10,8},{11,9},{12,... | collective-permute-start | bytes 393224 | tf_op jit(solution)/shard_map/ppermute | solution.py:216
  109.1 25.3 %collective-permute-start.6 = (bf16[128,512]{1,0:T(8,128)(2,1)S(1)}, bf16[128,512]{1,0:T(8,128)(2,1)S(1)}, u32[]{:S(2)}, u32[]{:S(2)}) collective-permute-start(bf16[128,512]{1,0:T(8,128)(2,1)S(1)} %get-tuple-element.21), channel_id=1, source_target_pairs={{1,0},{2,1},{3,2},{4,3},{5,4},{6,5},{7,6},{8,7},{9,8},{10,9},{11,1... | collective-permute-start | bytes 393224 | tf_op jit(solution)/shard_map/ppermute | solution.py:216
  113.5 30.0 %all-to-all-start.2 = ((bf16[16,16,256]{2,1,0:T(8,128)(2,1)}), bf16[16,16,256]{2,1,0:T(8,128)(2,1)S(1)}, u32[]{:S(2)}, u32[]{:S(2)}) async-start(bf16[16,16,256]{2,1,0:T(8,128)(2,1)} %bitcast.15), calls=%async_computation.2 | async-start | bytes 262144 | tf_op jit(solution)/shard_map/all_to_all | solution.py:258
  (24 other events, 141.9 us)

commit v2 on v1

v2 whole, which is shorter than its diff:
```python
import math

import jax
import jax.numpy as jnp
from jax import lax
from jax.experimental import pallas as pl
from jax.experimental.pallas import tpu as pltpu
from jax.sharding import Mesh, PartitionSpec as P

HEAD = 128
STRETCH = 64
SPAN = 4
GROUPS = 4
PER_GROUP = 4
ROWS = 128
KEYS = SPAN * ROWS
WIDE = PER_GROUP * ROWS
MASKED = -1e30
SCALE = HEAD**-0.5
LOG2E = math.log2(math.e)
BF16 = jnp.bfloat16
F32 = jnp.float32
AXES = ("zl", "zh", "x", "y", "c")
CTX = ("zh", "x", "y", "c")
N_CTX = 64
NSTART = 64
MIB = 1024 * 1024
VMEM = 24 * MIB
VMEM_F = 59 * MIB


def nt(a, b):
    return lax.dot_general(a, b, (((1,), (1,)), ((), ())), preferred_element_type=F32)


def tn(a, b):
    return lax.dot_general(a, b, (((0,), (0,)), ((), ())), preferred_element_type=F32)


def nn(a, b):
    return lax.dot_general(a, b, (((1,), (0,)), ((), ())), preferred_element_type=F32)


def stack_heads(block):
    return jnp.concatenate([block[:, h * HEAD : (h + 1) * HEAD] for h in range(PER_GROUP)], axis=0)


def forward_kernel(
    ids,
    order_in,
    starts_in,
    q_in,
    g_in,
    k_in,
    k1,
    k2,
    k3,
    prob_ref,
    own_ref,
    v1,
    v2,
    v3,
    bias_ref,
    q_ref,
    g_ref,
    k0,
    order,
    starts,
    sems,
):
    group = pl.program_id(0)
    shard = ids[0]
    copies = [
        pltpu.make_async_copy(q_in, q_ref, sems.at[0]),
        pltpu.make_async_copy(g_in, g_ref, sems.at[1]),
        pltpu.make_async_copy(k_in, k0, sems.at[2]),
        pltpu.make_async_copy(order_in, order, sems.at[3]),
        pltpu.make_async_copy(starts_in, starts, sems.at[4]),
    ]

    @pl.when(group == 0)
    def _():
        for copy in copies:
            copy.start()
        copies[3].wait()
        copies[4].wait()
        lane = lax.broadcasted_iota(jnp.int32, (1, ROWS), 1)
        stretch = jnp.where(lane < STRETCH, order[0, shard, 0], order[0, shard, 1])
        query_pos = shard * ROWS + stretch * STRETCH + (lane & (STRETCH - 1))
        begin = jnp.zeros((1, ROWS), jnp.int32)
        for i in range(NSTART):
            begin = jnp.where(starts[0, i] <= query_pos, starts[0, i], begin)
        row = lax.broadcasted_iota(jnp.int32, (STRETCH, ROWS), 0)
        for d in range(SPAN):
            source = shard - d
            known = jnp.maximum(source, 0)
            for j in range(2):
                key_pos = source * ROWS + order[0, known, j] * STRETCH + row
                allowed = (key_pos <= query_pos) & (key_pos >= begin)
                bias_ref[pl.ds((2 * d + j) * STRETCH, STRETCH), :] = jnp.where(
                    allowed, 0.0, MASKED
                )
        for copy in copies[:3]:
            copy.wait()

    wide = pl.ds(pl.multiple_of(group * PER_GROUP * HEAD, PER_GROUP * HEAD), PER_GROUP * HEAD)
    narrow = pl.ds(pl.multiple_of(group * HEAD, HEAD), HEAD)
    keys = jnp.concatenate([k0[:, narrow], k1[...], k2[...], k3[...]], axis=0)
    bias = bias_ref[...]
    queries = q_ref[:, wide]
    for h in range(PER_GROUP):
        cols = slice(h * HEAD, (h + 1) * HEAD)
        score = nt(keys, queries[:, cols]) * (SCALE * LOG2E) + bias
        weight = jnp.exp2(score - jnp.max(score, axis=0, keepdims=True))
        total = jnp.sum(weight, axis=0, keepdims=True)
        prob_ref[0, :, cols] = (weight * (1.0 / total)).astype(BF16)
    value_grad = nn(prob_ref[0], stack_heads(g_ref[:, wide]))
    own_ref[...] = value_grad[:ROWS]
    for d, ref in ((1, v1), (2, v2), (3, v3)):
        ref[...] = value_grad[d * ROWS : (d + 1) * ROWS].astype(BF16)


def backward_kernel(
    prob_ref,
    q_in,
    g_in,
    k_in,
    v_in,
    k1,
    k2,
    k3,
    v1,
    v2,
    v3,
    gq_ref,
    own_ref,
    d1,
    d2,
    d3,
    q_ref,
    g_ref,
    k0,
    v0,
    sems,
):
    group = pl.program_id(0)

    @pl.when(group == 0)
    def _():
        copies = [
            pltpu.make_async_copy(source, target, sems.at[i])
            for i, (source, target) in enumerate(
                ((q_in, q_ref), (g_in, g_ref), (k_in, k0), (v_in, v0))
            )
        ]
        for copy in copies:
            copy.start()
        for copy in copies:
            copy.wait()

    wide = pl.ds(pl.multiple_of(group * PER_GROUP * HEAD, PER_GROUP * HEAD), PER_GROUP * HEAD)
    narrow = pl.ds(pl.multiple_of(group * HEAD, HEAD), HEAD)
    keys = jnp.concatenate([k0[:, narrow], k1[...], k2[...], k3[...]], axis=0)
    values = jnp.concatenate([v0[:, narrow], v1[...], v2[...], v3[...]], axis=0)
    prob = prob_ref[0].astype(F32)
    grad_prob = nt(values, stack_heads(g_ref[:, wide]))
    weighted = prob * grad_prob
    delta = jnp.sum(weighted, axis=0, keepdims=True)
    grad_score = (weighted - prob * delta).astype(BF16)
    key_grad = nn(grad_score, stack_heads(q_ref[:, wide])) * SCALE
    own_ref[...] = key_grad[:ROWS]
    for d, ref in ((1, d1), (2, d2), (3, d3)):
        ref[...] = key_grad[d * ROWS : (d + 1) * ROWS].astype(BF16)
    query_grad = tn(grad_score, keys) * SCALE
    for h in range(PER_GROUP):
        gq_ref[:, h * HEAD : (h + 1) * HEAD] = query_grad[h * ROWS : (h + 1) * ROWS].astype(BF16)


HBM_SPEC = pl.BlockSpec(memory_space=pltpu.HBM)


def group_spec(width):
    return pl.BlockSpec((ROWS, width), lambda g, *_: (0, g))


def prob_spec():
    return pl.BlockSpec((1, KEYS, WIDE), lambda g, *_: (g, 0, 0))


def forward_call(ids, order, starts, query, grad, keys):
    narrow = jax.ShapeDtypeStruct((ROWS, GROUPS * HEAD), BF16)
    return pl.pallas_call(
        forward_kernel,
        grid_spec=pltpu.PrefetchScalarGridSpec(
            num_scalar_prefetch=1,
            grid=(GROUPS,),
            in_specs=[HBM_SPEC] * 5 + [group_spec(HEAD)] * 3,
            out_specs=[prob_spec()] + [group_spec(HEAD)] * SPAN,
            scratch_shapes=[
                pltpu.VMEM((KEYS, ROWS), F32),
                pltpu.VMEM((ROWS, GROUPS * WIDE), BF16),
                pltpu.VMEM((ROWS, GROUPS * WIDE), BF16),
                pltpu.VMEM((ROWS, GROUPS * HEAD), BF16),
                pltpu.SMEM((1, N_CTX, 2), jnp.int32),
                pltpu.SMEM((1, NSTART), jnp.int32),
                pltpu.SemaphoreType.DMA((5,)),
            ],
        ),
        out_shape=[
            jax.ShapeDtypeStruct((GROUPS, KEYS, WIDE), BF16),
            jax.ShapeDtypeStruct((ROWS, GROUPS * HEAD), F32),
            narrow,
            narrow,
            narrow,
        ],
        cost_estimate=pl.CostEstimate(
            flops=4 * 16 * ROWS * KEYS * HEAD, bytes_accessed=6 * MIB, transcendentals=MIB
        ),
        compiler_params=pltpu.CompilerParams(vmem_limit_bytes=VMEM_F),
        name="forward_and_value_gradient",
    )(ids, order, starts, query, grad, *keys)


def backward_call(prob, query, grad, keys, values):
    narrow = jax.ShapeDtypeStruct((ROWS, GROUPS * HEAD), BF16)
    return pl.pallas_call(
        backward_kernel,
        grid=(GROUPS,),
        in_specs=[prob_spec()] + [HBM_SPEC] * 4 + [group_spec(HEAD)] * 6,
        out_specs=[group_spec(PER_GROUP * HEAD)] + [group_spec(HEAD)] * SPAN,
        scratch_shapes=[
            pltpu.VMEM((ROWS, GROUPS * WIDE), BF16),
            pltpu.VMEM((ROWS, GROUPS * WIDE), BF16),
            pltpu.VMEM((ROWS, GROUPS * HEAD), BF16),
            pltpu.VMEM((ROWS, GROUPS * HEAD), BF16),
            pltpu.SemaphoreType.DMA((4,)),
        ],
        out_shape=[
            jax.ShapeDtypeStruct((ROWS, GROUPS * WIDE), BF16),
            jax.ShapeDtypeStruct((ROWS, GROUPS * HEAD), F32),
            narrow,
            narrow,
            narrow,
        ],
        cost_estimate=pl.CostEstimate(
            flops=6 * 16 * ROWS * KEYS * HEAD, bytes_accessed=6 * MIB, transcendentals=0
        ),
        compiler_params=pltpu.CompilerParams(vmem_limit_bytes=VMEM),
        name="query_and_key_gradient",
    )(prob, query, grad, keys[0], values[0], *keys[1:], *values[1:])


def pack_kernel(ids, source, o0, o1, o2, o3, in_ref, sem):
    copy = pltpu.make_async_copy(source, in_ref, sem)
    copy.start()
    copy.wait()
    for d, out_ref in enumerate((o0, o1, o2, o3)):
        x = (ids[1] + d) & 3
        for z in range(8):
            column = pl.multiple_of((4 * z + x) * HEAD, HEAD)
            out_ref[:, z * HEAD : (z + 1) * HEAD] = in_ref[:, pl.ds(column, HEAD)]


def pack_call(ids, inputs):
    whole = pl.BlockSpec(memory_space=pltpu.VMEM)
    return pl.pallas_call(
        pack_kernel,
        grid_spec=pltpu.PrefetchScalarGridSpec(
            num_scalar_prefetch=1,
            grid=(1,),
            in_specs=[HBM_SPEC],
            out_specs=[whole] * 4,
            scratch_shapes=[pltpu.VMEM((ROWS, 32 * HEAD), BF16), pltpu.SemaphoreType.DMA],
        ),
        out_shape=[jax.ShapeDtypeStruct((ROWS, 8 * HEAD), BF16)] * 4,
        cost_estimate=pl.CostEstimate(flops=0, bytes_accessed=2 * MIB, transcendentals=0),
        compiler_params=pltpu.CompilerParams(vmem_limit_bytes=VMEM),
        name="pack_inputs",
    )(ids, inputs)


def total_kernel(own, r1, r2, r3, out_ref, sent_ref):
    total = own[...] + r1[...].astype(F32) + r2[...].astype(F32) + r3[...].astype(F32)
    total = total.astype(BF16)
    out_ref[...] = total
    for x in range(4):
        for c in range(2):
            sent_ref[2 * x + c] = total[:, c * 256 : (c + 1) * 256]


def total_call(own, returned):
    return pl.pallas_call(
        total_kernel,
        out_shape=[
            jax.ShapeDtypeStruct((ROWS, GROUPS * HEAD), BF16),
            jax.ShapeDtypeStruct((8, ROWS, 256), BF16),
        ],
        compiler_params=pltpu.CompilerParams(vmem_limit_bytes=VMEM),
        name="value_gradient_total",
    )(own, *returned)


def weight_kernel(ids, grads, a0, a1, a2, a3, b0, b1, b2, b3, out_ref):
    x, core = ids[1], ids[2]
    left = [ref[...] for ref in (a0, a1, a2, a3, b0, b1, b2, b3)]
    right = [grads[2 * ((x + 4 - d) & 3) + side] for side in (core, 1 - core) for d in range(4)]
    left, right = jnp.concatenate(left, axis=0), jnp.concatenate(right, axis=0)
    out_ref[...] = tn(left, right).astype(BF16)


def weight_call(ids, grads, own, other):
    taken = pl.BlockSpec((ROWS, 256), lambda i, _: (0, i))
    return pl.pallas_call(
        weight_kernel,
        grid_spec=pltpu.PrefetchScalarGridSpec(
            num_scalar_prefetch=1,
            grid=(4,),
            in_specs=[pl.BlockSpec((8, ROWS, 256), lambda i, _: (0, 0, 0))] + [taken] * 8,
            out_specs=pl.BlockSpec((256, 256), lambda i, _: (i, 0)),
        ),
        out_shape=jax.ShapeDtypeStruct((1024, 256), BF16),
        cost_estimate=pl.CostEstimate(
            flops=2 * 1024 * 1024 * 256, bytes_accessed=3 * MIB, transcendentals=0
        ),
        compiler_params=pltpu.CompilerParams(vmem_limit_bytes=VMEM),
        name="weight_gradient",
    )(ids, grads, *own, *other)


def final_kernel(ids, in_ref, keep_ref, send_ref):
    core = ids[2]
    total = in_ref[0].astype(F32)
    for i in range(1, 32):
        total += in_ref[i].astype(F32)
    first, second = total[:16], total[16:]
    keep_ref[...] = jnp.where(core == 0, first, second)
    send_ref[...] = jnp.where(core == 0, second, first)


def final_call(ids, parts):
    whole = pl.BlockSpec(memory_space=pltpu.VMEM)
    return pl.pallas_call(
        final_kernel,
        grid_spec=pltpu.PrefetchScalarGridSpec(
            num_scalar_prefetch=1, grid=(1,), in_specs=[whole], out_specs=[whole] * 2
        ),
        out_shape=[jax.ShapeDtypeStruct((16, 256), F32)] * 2,
        compiler_params=pltpu.CompilerParams(vmem_limit_bytes=VMEM),
        name="weight_rows",
    )(ids, parts)


def shift_shards(block, distance):
    route = [(i - distance, i) for i in range(N_CTX) if 0 <= i - distance < N_CTX]
    return lax.ppermute(block, CTX, route)


def shift_x(block, distance):
    return lax.ppermute(block, "x", [(i, (i + distance) % 4) for i in range(4)])


def swap_core(block):
    return lax.ppermute(block, "c", [(0, 1), (1, 0)])


def shards(query, key, value, grad, inputs, stretch_order, session_starts):
    query, key, value, grad, inputs = query[0], key[0], value[0], grad[0], inputs[0]
    x, core = lax.axis_index("x"), lax.axis_index("c")
    ids = jnp.stack([lax.axis_index(CTX), x, core]).astype(jnp.int32)

    far = [shift_shards(key, d) for d in (3, 2, 1)]
    keys = [key] + far[::-1]
    far = [shift_shards(value, d) for d in (3, 2, 1)]
    values = [value] + far[::-1]

    prob, value_own, *value_terms = forward_call(ids, stretch_order, session_starts, query, grad, keys)
    returned = [shift_shards(value_terms[d - 1], -d) for d in (3, 2, 1)]
    grad_query, key_own, *key_terms = backward_call(prob, query, grad, keys, values)
    packed = pack_call(ids, inputs)
    own = [packed[0]] + [shift_x(packed[d], d) for d in range(1, 4)]
    other = [swap_core(block) for block in own]
    grad_value, sent = total_call(value_own, returned)
    sent, grad_query = lax.optimization_barrier((sent, grad_query))
    gathered = lax.all_to_all(sent, ("x", "c"), 0, 0, tiled=True)
    partial = weight_call(ids, gathered, own, other).reshape(32, 32, 256)
    partial = lax.all_to_all(partial, ("zl", "zh", "y"), 0, 0, tiled=True)

    grad_key = key_own
    for d in (3, 2, 1):
        grad_key = grad_key + shift_shards(key_terms[d - 1], -d).astype(F32)
    grad_key = grad_key.astype(BF16)

    keep, send = final_call(ids, partial)
    swapped = swap_core(send)
    first, second = jnp.where(core == 0, keep, swapped), jnp.where(core == 0, swapped, keep)
    weight_grad = jnp.concatenate([first, second], axis=1)
    return grad_query[None], grad_key[None], grad_value[None], weight_grad


def solution(mesh):
    fine = Mesh(mesh.devices.reshape(4, 2, 4, 4, 2), AXES)
    rows = P("zl", CTX, None)
    return jax.shard_map(
        shards,
        mesh=fine,
        in_specs=(rows, rows, rows, rows, rows, P("zl", None, None), P("zl", None)),
        out_specs=(rows, rows, rows, P(AXES, None)),
        check_vma=False,
    )
```

time: 146 us -> 129 us (0.88)
  the two profiles are of different devices: /device:TPU:3 before, /device:TPU:55 now
where the time goes in v2:
time: 129 us; the launch traced here: 128 us
  starting transfers between devices  60.6 us (47%)
  waiting for transfers between devices  36 us (28%)
  Pallas kernels  18.5 us (14%)
  local copies, waits for them, and re-layouts  10.1 us (8%)
  other arithmetic  2 us (2%)
    ppermute x12, starting transfers between devices, shift_shards(): return lax.ppermute(block, CTX, route)  40.7 us
    ppermute x12, waiting for transfers between devices, shift_shards(): return lax.ppermute(block, CTX, route)  22 us
    all_to_all x1, starting transfers between devices, shards(): partial = lax.all_to_all(partial, ('zl', 'zh', 'y'), 0, 0, tiled=True)  12.5 us
    unnamed x47, local copies, waits for them, and re-layouts  10.1 us
    pallas_call x1, Pallas kernels, forward_call(): pl.pallas_call(forward_kernel, grid_spec=pltpu.PrefetchScalarGridSpec(num...  7.24 us
    all_to_all x1, waiting for transfers between devices, shards(): partial = lax.all_to_all(partial, ('zl', 'zh', 'y'), 0, 0, tiled=True)  7.21 us
    all_to_all x1, waiting for transfers between devices, shards(): gathered = lax.all_to_all(sent, ('x', 'c'), 0, 0, tiled=True)  5.11 us
    pallas_call x1, Pallas kernels, backward_call(): pl.pallas_call(backward_kernel, grid=(GROUPS,), in_specs=[prob_spec()] +...  4.81 us
  transfers between devices with their start and end apart: 22, of which 8 were waited for; matrix products, arithmetic and copies ran while one was open for 2% of the time, Pallas kernels for 12%

profile of v2, /device:TPU:55, one launch (start us, length us, event | category | flops | bytes accessed | tf_op | source)
XLA Modules:
  0.0 128.3 jit_solution(11515969020795365840)
XLA Ops:
  0.7 3.6 %collective-permute-start = (bf16[128,512]{1,0:T(8,128)(2,1)}, bf16[128,512]{1,0:T(8,128)(2,1)S(1)}, u32[]{:S(2)}, u32[]{:S(2)}) collective-permute-start(bf16[128,512]{1,0:T(8,128)(2,1)} %bitcast.18), channel_id=1, source_target_pairs={{0,1},{1,2},{2,3},{3,4},{4,5},{5,6},{6,7},{7,8},{8,9},{9,10},{10,1... | collective-permute-start | bytes 393224 | tf_op jit(solution)/shard_map/ppermute | solution.py:355
  4.3 7.5 %collective-permute-start.1 = (bf16[128,512]{1,0:T(8,128)(2,1)}, bf16[128,512]{1,0:T(8,128)(2,1)S(1)}, u32[]{:S(2)}, u32[]{:S(2)}) collective-permute-start(bf16[128,512]{1,0:T(8,128)(2,1)} %bitcast.19), channel_id=1, source_target_pairs={{0,2},{1,3},{2,4},{3,5},{4,6},{5,7},{6,8},{7,9},{8,10},{9,11},{10,... | collective-permute-start | bytes 393224 | tf_op jit(solution)/shard_map/ppermute | solution.py:355
  11.8 2.6 %collective-permute-start.2 = (bf16[128,512]{1,0:T(8,128)(2,1)}, bf16[128,512]{1,0:T(8,128)(2,1)S(1)}, u32[]{:S(2)}, u32[]{:S(2)}) collective-permute-start(bf16[128,512]{1,0:T(8,128)(2,1)} %bitcast.20), channel_id=1, source_target_pairs={{0,3},{1,4},{2,5},{3,6},{4,7},{5,8},{6,9},{7,10},{8,11},{9,12},{10... | collective-permute-start | bytes 393224 | tf_op jit(solution)/shard_map/ppermute | solution.py:355
  14.4 4.1 %collective-permute-start.6 = (bf16[128,512]{1,0:T(8,128)(2,1)}, bf16[128,512]{1,0:T(8,128)(2,1)S(1)}, u32[]{:S(2)}, u32[]{:S(2)}) collective-permute-start(bf16[128,512]{1,0:T(8,128)(2,1)} %bitcast.23), channel_id=1, source_target_pairs={{0,1},{1,2},{2,3},{3,4},{4,5},{5,6},{6,7},{7,8},{8,9},{9,10},{10,1... | collective-permute-start | bytes 393224 | tf_op jit(solution)/shard_map/ppermute | solution.py:355
  18.5 2.9 %collective-permute-start.7 = (bf16[128,512]{1,0:T(8,128)(2,1)}, bf16[128,512]{1,0:T(8,128)(2,1)S(1)}, u32[]{:S(2)}, u32[]{:S(2)}) collective-permute-start(bf16[128,512]{1,0:T(8,128)(2,1)} %bitcast.24), channel_id=1, source_target_pairs={{0,2},{1,3},{2,4},{3,5},{4,6},{5,7},{6,8},{7,9},{8,10},{9,11},{10,... | collective-permute-start | bytes 393224 | tf_op jit(solution)/shard_map/ppermute | solution.py:355
  23.5 2.3 %collective-permute-start.8 = (bf16[128,512]{1,0:T(8,128)(2,1)}, bf16[128,512]{1,0:T(8,128)(2,1)S(1)}, u32[]{:S(2)}, u32[]{:S(2)}) collective-permute-start(bf16[128,512]{1,0:T(8,128)(2,1)} %bitcast.25), channel_id=1, source_target_pairs={{0,3},{1,4},{2,5},{3,6},{4,7},{5,8},{6,9},{7,10},{8,11},{9,12},{10... | collective-permute-start | bytes 393224 | tf_op jit(solution)/shard_map/ppermute | solution.py:355
  26.5 7.2 %forward_and_value_gradient.1 = (bf16[4,512,512]{2,1,0:T(8,128)(2,1)}, f32[128,512]{1,0:T(8,128)}, bf16[128,512]{1,0:T(8,128)(2,1)}, bf16[128,512]{1,0:T(8,128)(2,1)}, bf16[128,512]{1,0:T(8,128)(2,1)}) custom-call(s32[3]{0:T(128)} %pad_add_fusion.ids, s32[1,64,2]{2,1,0:T(8,128)} %copy.11.order_in, s32[1,64]{1,0:T(1,128)} %starts_in.1, ...), custom_call_target="tpu_custom_call" | custom-call | flops 536870912 | bytes 6291456 | tf_op jit(solution)/shard_map/forward_and_value_gradient/pallas_call | solution.py:192
  33.7 3.3 %collective-permute-start.3 = (bf16[128,512]{1,0:T(8,128)(2,1)}, bf16[128,512]{1,0:T(8,128)(2,1)S(1)}, u32[]{:S(2)}, u32[]{:S(2)}) collective-permute-start(bf16[128,512]{1,0:T(8,128)(2,1)} %get-tuple-element.25), channel_id=1, source_target_pairs={{3,0},{4,1},{5,2},{6,3},{7,4},{8,5},{9,6},{10,7},{11,8},{12,9},{13... | collective-permute-start | bytes 393224 | tf_op jit(solution)/shard_map/ppermute | solution.py:355
  37.0 2.4 %collective-permute-start.4 = (bf16[128,512]{1,0:T(8,128)(2,1)}, bf16[128,512]{1,0:T(8,128)(2,1)S(1)}, u32[]{:S(2)}, u32[]{:S(2)}) collective-permute-start(bf16[128,512]{1,0:T(8,128)(2,1)} %get-tuple-element.26), channel_id=1, source_target_pairs={{2,0},{3,1},{4,2},{5,3},{6,4},{7,5},{8,6},{9,7},{10,8},{11,9},{12,... | collective-permute-start | bytes 393224 | tf_op jit(solution)/shard_map/ppermute | solution.py:355
  40.1 3.7 %collective-permute-start.5 = (bf16[128,512]{1,0:T(8,128)(2,1)}, bf16[128,512]{1,0:T(8,128)(2,1)S(1)}, u32[]{:S(2)}, u32[]{:S(2)}) collective-permute-start(bf16[128,512]{1,0:T(8,128)(2,1)} %get-tuple-element.27), channel_id=1, source_target_pairs={{1,0},{2,1},{3,2},{4,3},{5,4},{6,5},{7,6},{8,7},{9,8},{10,9},{11,1... | collective-permute-start | bytes 393224 | tf_op jit(solution)/shard_map/ppermute | solution.py:355
  44.4 1.7 %pack_inputs.1 = (bf16[128,1024]{1,0:T(8,128)(2,1)S(1)}, bf16[128,1024]{1,0:T(8,128)(2,1)}, bf16[128,1024]{1,0:T(8,128)(2,1)}, bf16[128,1024]{1,0:T(8,128)(2,1)S(1)}) custom-call(s32[3]{0:T(128)S(1)} %copy-done.17, bf16[128,4096]{1,0:T(8,128)(2,1)S(1)} %bitcast.13), custom_call_target="tpu_custom_call" | custom-call | bytes 2097152 | tf_op jit(solution)/shard_map/pack_inputs/pallas_call | solution.py:266
  46.8 8.3 %collective-permute-done.3.r1 = bf16[128,512]{1,0:T(8,128)(2,1)S(1)} collective-permute-done((bf16[128,512]{1,0:T(8,128)(2,1)}, bf16[128,512]{1,0:T(8,128)(2,1)S(1)}, u32[]{:S(2)}, u32[]{:S(2)}) %collective-permute-start.3) | collective-permute-done | bytes 131104 | tf_op jit(solution)/shard_map/ppermute | solution.py:355
  55.1 1.6 %copy-done = bf16[4,512,512]{2,1,0:T(8,128)(2,1)S(1)} copy-done((bf16[4,512,512]{2,1,0:T(8,128)(2,1)S(1)}, bf16[4,512,512]{2,1,0:T(8,128)(2,1)}, u32[]{:S(2)}) %copy-start) | copy-done | bytes 2097176
  61.2 4.8 %query_and_key_gradient.1 = (bf16[128,2048]{1,0:T(8,128)(2,1)}, f32[128,512]{1,0:T(8,128)S(1)}, bf16[128,512]{1,0:T(8,128)(2,1)S(1)}, bf16[128,512]{1,0:T(8,128)(2,1)S(1)}, bf16[128,512]{1,0:T(8,128)(2,1)S(1)}) custom-call(bf16[4,512,512]{2,1,0:T(8,128)(2,1)S(1)} %copy-done, bf16[128,2048]{1,0:T(8,128)(2,1)S(1)} %bitcast.15, bf16[128,2048]{1,0:T(8,128)(2,1)S(1)} %bitcast.17, ...), custom_call_target="tpu_custom_call" | custom-call | flops 805306368 | bytes 6291456 | tf_op jit(solution)/shard_map/query_and_key_gradient/pallas_call | solution.py:226
  67.0 4.3 %all-to-all-start = ((bf16[8,128,256]{2,1,0:T(8,128)(2,1)}), bf16[8,128,256]{2,1,0:T(8,128)(2,1)S(1)}, u32[]{:S(2)}, u32[]{:S(2)}) async-start(bf16[8,128,256]{2,1,0:T(8,128)(2,1)} %get-tuple-element.37), calls=%async_computation | async-start | bytes 1048576 | tf_op jit(solution)/shard_map/all_to_all | solution.py:384
  74.0 5.1 %all-to-all-done.grads = bf16[8,128,256]{2,1,0:T(8,128)(2,1)S(1)} async-done(((bf16[8,128,256]{2,1,0:T(8,128)(2,1)}), bf16[8,128,256]{2,1,0:T(8,128)(2,1)S(1)}, u32[]{:S(2)}, u32[]{:S(2)}) %all-to-all-start) | async-done | bytes 524320 | tf_op jit(solution)/shard_map/all_to_all | solution.py:384
  79.1 3.2 %weight_gradient.1 = bf16[1024,256]{1,0:T(8,128)(2,1)} custom-call(s32[3]{0:T(128)S(1)} %copy-done.18, bf16[8,128,256]{2,1,0:T(8,128)(2,1)S(1)} %all-to-all-done.grads, bf16[128,1024]{1,0:T(8,128)(2,1)S(1)} %get-tuple-element.38.a0, bf16[128,1024]{1,0:T(8,128)(2,1)S(1)} %collective-permute-done.12.a1, bf16[128,1024]{1,0:T(8,128)(2,1)S(1)} %collective-permute-done.13.a2, ...), custom_call_target="tpu_custom_call" | custom-call | flops 536870912 | bytes 3145728 | tf_op jit(solution)/shard_map/weight_gradient/pallas_call | solution.py:313
  82.4 12.5 %all-to-all-start.1 = ((bf16[32,32,256]{2,1,0:T(8,128)(2,1)}), bf16[32,32,256]{2,1,0:T(8,128)(2,1)S(1)}, u32[]{:S(2)}, u32[]{:S(2)}) async-start(bf16[32,32,256]{2,1,0:T(8,128)(2,1)} %bitcast.11), calls=%async_computation.1 | async-start | bytes 1048576 | tf_op jit(solution)/shard_map/all_to_all | solution.py:386
  94.9 2.2 %collective-permute-start.10 = (bf16[128,512]{1,0:T(8,128)(2,1)S(1)}, bf16[128,512]{1,0:T(8,128)(2,1)S(1)}, u32[]{:S(2)}, u32[]{:S(2)}) collective-permute-start(bf16[128,512]{1,0:T(8,128)(2,1)S(1)} %copy-done.22), channel_id=1, source_target_pairs={{2,0},{3,1},{4,2},{5,3},{6,4},{7,5},{8,6},{9,7},{10,8},{11,9},{12,... | collective-permute-start | bytes 393224 | tf_op jit(solution)/shard_map/ppermute | solution.py:355
  97.1 3.6 %collective-permute-start.11 = (bf16[128,512]{1,0:T(8,128)(2,1)S(1)}, bf16[128,512]{1,0:T(8,128)(2,1)S(1)}, u32[]{:S(2)}, u32[]{:S(2)}) collective-permute-start(bf16[128,512]{1,0:T(8,128)(2,1)S(1)} %copy-done.20), channel_id=1, source_target_pairs={{1,0},{2,1},{3,2},{4,3},{5,4},{6,5},{7,6},{8,7},{9,8},{10,9},{11,1... | collective-permute-start | bytes 393224 | tf_op jit(solution)/shard_map/ppermute | solution.py:355
  100.7 2.6 %collective-permute-start.9 = (bf16[128,512]{1,0:T(8,128)(2,1)S(1)}, bf16[128,512]{1,0:T(8,128)(2,1)S(1)}, u32[]{:S(2)}, u32[]{:S(2)}) collective-permute-start(bf16[128,512]{1,0:T(8,128)(2,1)S(1)} %get-tuple-element.33), channel_id=1, source_target_pairs={{3,0},{4,1},{5,2},{6,3},{7,4},{8,5},{9,6},{10,7},{11,8},{12,9},{13... | collective-permute-start | bytes 393224 | tf_op jit(solution)/shard_map/ppermute | solution.py:355
  103.3 7.2 %all-to-all-done.1.in_ref = bf16[32,32,256]{2,1,0:T(8,128)(2,1)S(1)} async-done(((bf16[32,32,256]{2,1,0:T(8,128)(2,1)}), bf16[32,32,256]{2,1,0:T(8,128)(2,1)S(1)}, u32[]{:S(2)}, u32[]{:S(2)}) %all-to-all-start.1) | async-done | bytes 524320 | tf_op jit(solution)/shard_map/all_to_all | solution.py:386
  111.1 2.0 %collective-permute-start.19 = (f32[16,256]{1,0:T(8,128)S(1)}, f32[16,256]{1,0:T(8,128)S(1)}, u32[]{:S(2)}, u32[]{:S(2)}) collective-permute-start(f32[16,256]{1,0:T(8,128)S(1)} %get-tuple-element.43), channel_id=1, source_target_pairs={{0,1},{1,0},{2,3},{3,2},{4,5},{5,4},{6,7},{7,6},{8,9},{9,8},{10,11... | collective-permute-start | bytes 49160 | tf_op jit(solution)/shard_map/ppermute | solution.py:363
  113.2 13.7 %collective-permute-done.9 = bf16[128,512]{1,0:T(8,128)(2,1)S(1)} collective-permute-done((bf16[128,512]{1,0:T(8,128)(2,1)S(1)}, bf16[128,512]{1,0:T(8,128)(2,1)S(1)}, u32[]{:S(2)}, u32[]{:S(2)}) %collective-permute-start.9) | collective-permute-done | bytes 131104 | tf_op jit(solution)/shard_map/ppermute | solution.py:355
  (77 shorter events, 14.8 us)
Async XLA Ops:
  0.6 54.5 %copy-start.5 = (bf16[1,128,512]{2,1,0:T(8,128)(2,1)S(1)}, bf16[1,128,512]{2,1,0:T(8,128)(2,1)}, u32[]{:S(2)}) copy-start(bf16[1,128,512]{2,1,0:T(8,128)(2,1)} %param.8) | copy-start | bytes 393220
  0.6 54.5 %copy-start.6 = (bf16[1,128,512]{2,1,0:T(8,128)(2,1)S(1)}, bf16[1,128,512]{2,1,0:T(8,128)(2,1)}, u32[]{:S(2)}) copy-start(bf16[1,128,512]{2,1,0:T(8,128)(2,1)} %param.9) | copy-start | bytes 393220
  0.7 22.8 %collective-permute-start = (bf16[128,512]{1,0:T(8,128)(2,1)}, bf16[128,512]{1,0:T(8,128)(2,1)S(1)}, u32[]{:S(2)}, u32[]{:S(2)}) collective-permute-start(bf16[128,512]{1,0:T(8,128)(2,1)} %bitcast.18), channel_id=1, source_target_pairs={{0,1},{1,2},{2,3},{3,4},{4,5},{5,6},{6,7},{7,8},{8,9},{9,10},{10,1... | collective-permute-start | bytes 393224 | tf_op jit(solution)/shard_map/ppermute | solution.py:355
  4.3 21.5 %collective-permute-start.1 = (bf16[128,512]{1,0:T(8,128)(2,1)}, bf16[128,512]{1,0:T(8,128)(2,1)S(1)}, u32[]{:S(2)}, u32[]{:S(2)}) collective-permute-start(bf16[128,512]{1,0:T(8,128)(2,1)} %bitcast.19), channel_id=1, source_target_pairs={{0,2},{1,3},{2,4},{3,5},{4,6},{5,7},{6,8},{7,9},{8,10},{9,11},{10,... | collective-permute-start | bytes 393224 | tf_op jit(solution)/shard_map/ppermute | solution.py:355
  11.8 14.0 %collective-permute-start.2 = (bf16[128,512]{1,0:T(8,128)(2,1)}, bf16[128,512]{1,0:T(8,128)(2,1)S(1)}, u32[]{:S(2)}, u32[]{:S(2)}) collective-permute-start(bf16[128,512]{1,0:T(8,128)(2,1)} %bitcast.20), channel_id=1, source_target_pairs={{0,3},{1,4},{2,5},{3,6},{4,7},{5,8},{6,9},{7,10},{8,11},{9,12},{10... | collective-permute-start | bytes 393224 | tf_op jit(solution)/shard_map/ppermute | solution.py:355
  14.4 25.0 %collective-permute-start.6 = (bf16[128,512]{1,0:T(8,128)(2,1)}, bf16[128,512]{1,0:T(8,128)(2,1)S(1)}, u32[]{:S(2)}, u32[]{:S(2)}) collective-permute-start(bf16[128,512]{1,0:T(8,128)(2,1)} %bitcast.23), channel_id=1, source_target_pairs={{0,1},{1,2},{2,3},{3,4},{4,5},{5,6},{6,7},{7,8},{8,9},{9,10},{10,1... | collective-permute-start | bytes 393224 | tf_op jit(solution)/shard_map/ppermute | solution.py:355
  18.5 27.6 %collective-permute-start.7 = (bf16[128,512]{1,0:T(8,128)(2,1)}, bf16[128,512]{1,0:T(8,128)(2,1)S(1)}, u32[]{:S(2)}, u32[]{:S(2)}) collective-permute-start(bf16[128,512]{1,0:T(8,128)(2,1)} %bitcast.24), channel_id=1, source_target_pairs={{0,2},{1,3},{2,4},{3,5},{4,6},{5,7},{6,8},{7,9},{8,10},{9,11},{10,... | collective-permute-start | bytes 393224 | tf_op jit(solution)/shard_map/ppermute | solution.py:355
  23.5 23.3 %collective-permute-start.8 = (bf16[128,512]{1,0:T(8,128)(2,1)}, bf16[128,512]{1,0:T(8,128)(2,1)S(1)}, u32[]{:S(2)}, u32[]{:S(2)}) collective-permute-start(bf16[128,512]{1,0:T(8,128)(2,1)} %bitcast.25), channel_id=1, source_target_pairs={{0,3},{1,4},{2,5},{3,6},{4,7},{5,8},{6,9},{7,10},{8,11},{9,12},{10... | collective-permute-start | bytes 393224 | tf_op jit(solution)/shard_map/ppermute | solution.py:355
  33.7 21.4 %collective-permute-start.3 = (bf16[128,512]{1,0:T(8,128)(2,1)}, bf16[128,512]{1,0:T(8,128)(2,1)S(1)}, u32[]{:S(2)}, u32[]{:S(2)}) collective-permute-start(bf16[128,512]{1,0:T(8,128)(2,1)} %get-tuple-element.25), channel_id=1, source_target_pairs={{3,0},{4,1},{5,2},{6,3},{7,4},{8,5},{9,6},{10,7},{11,8},{12,9},{13... | collective-permute-start | bytes 393224 | tf_op jit(solution)/shard_map/ppermute | solution.py:355
  37.0 29.1 %collective-permute-start.4 = (bf16[128,512]{1,0:T(8,128)(2,1)}, bf16[128,512]{1,0:T(8,128)(2,1)S(1)}, u32[]{:S(2)}, u32[]{:S(2)}) collective-permute-start(bf16[128,512]{1,0:T(8,128)(2,1)} %get-tuple-element.26), channel_id=1, source_target_pairs={{2,0},{3,1},{4,2},{5,3},{6,4},{7,5},{8,6},{9,7},{10,8},{11,9},{12,... | collective-permute-start | bytes 393224 | tf_op jit(solution)/shard_map/ppermute | solution.py:355
  40.1 26.0 %collective-permute-start.5 = (bf16[128,512]{1,0:T(8,128)(2,1)}, bf16[128,512]{1,0:T(8,128)(2,1)S(1)}, u32[]{:S(2)}, u32[]{:S(2)}) collective-permute-start(bf16[128,512]{1,0:T(8,128)(2,1)} %get-tuple-element.27), channel_id=1, source_target_pairs={{1,0},{2,1},{3,2},{4,3},{5,4},{6,5},{7,6},{8,7},{9,8},{10,9},{11,1... | collective-permute-start | bytes 393224 | tf_op jit(solution)/shard_map/ppermute | solution.py:355
  46.8 25.0 %collective-permute-start.12 = (bf16[128,1024]{1,0:T(8,128)(2,1)}, bf16[128,1024]{1,0:T(8,128)(2,1)S(1)}, u32[]{:S(2)}, u32[]{:S(2)}) collective-permute-start(bf16[128,1024]{1,0:T(8,128)(2,1)} %get-tuple-element.39), channel_id=1, source_target_pairs={{0,8},{8,16},{16,24},{24,0},{1,9},{9,17},{17,25},{25,1},{2,10},{10... | collective-permute-start | bytes 786440 | tf_op jit(solution)/shard_map/ppermute | solution.py:359
  46.8 25.1 %collective-permute-start.13 = (bf16[128,1024]{1,0:T(8,128)(2,1)}, bf16[128,1024]{1,0:T(8,128)(2,1)S(1)}, u32[]{:S(2)}, u32[]{:S(2)}) collective-permute-start(bf16[128,1024]{1,0:T(8,128)(2,1)} %get-tuple-element.40), channel_id=1, source_target_pairs={{0,16},{8,24},{16,0},{24,8},{1,17},{9,25},{17,1},{25,9},{2,18},{10... | collective-permute-start | bytes 786440 | tf_op jit(solution)/shard_map/ppermute | solution.py:359
  55.1 17.2 %collective-permute-start.14 = (bf16[128,1024]{1,0:T(8,128)(2,1)S(1)}, bf16[128,1024]{1,0:T(8,128)(2,1)S(1)}, u32[]{:S(2)}, u32[]{:S(2)}) collective-permute-start(bf16[128,1024]{1,0:T(8,128)(2,1)S(1)} %get-tuple-element.41), channel_id=1, source_target_pairs={{0,24},{8,0},{16,8},{24,16},{1,25},{9,1},{17,9},{25,17},{2,26},{10... | collective-permute-start | bytes 786440 | tf_op jit(solution)/shard_map/ppermute | solution.py:359
  67.0 12.1 %all-to-all-start = ((bf16[8,128,256]{2,1,0:T(8,128)(2,1)}), bf16[8,128,256]{2,1,0:T(8,128)(2,1)S(1)}, u32[]{:S(2)}, u32[]{:S(2)}) async-start(bf16[8,128,256]{2,1,0:T(8,128)(2,1)} %get-tuple-element.37), calls=%async_computation | async-start | bytes 1048576 | tf_op jit(solution)/shard_map/all_to_all | solution.py:384
  71.4 1.5 %collective-permute-start.15 = (bf16[128,1024]{1,0:T(8,128)(2,1)S(1)}, bf16[128,1024]{1,0:T(8,128)(2,1)S(1)}, u32[]{:S(2)}, u32[]{:S(2)}) collective-permute-start(bf16[128,1024]{1,0:T(8,128)(2,1)S(1)} %get-tuple-element.38.a0), channel_id=1, source_target_pairs={{0,1},{1,0},{2,3},{3,2},{4,5},{5,4},{6,7},{7,6},{8,9},{9,8},{10,11... | collective-permute-start | bytes 786440 | tf_op jit(solution)/shard_map/ppermute | solution.py:363
  71.7 1.5 %collective-permute-start.16 = (bf16[128,1024]{1,0:T(8,128)(2,1)S(1)}, bf16[128,1024]{1,0:T(8,128)(2,1)S(1)}, u32[]{:S(2)}, u32[]{:S(2)}) collective-permute-start(bf16[128,1024]{1,0:T(8,128)(2,1)S(1)} %collective-permute-done.12.a1), channel_id=1, source_target_pairs={{0,1},{1,0},{2,3},{3,2},{4,5},{5,4},{6,7},{7,6},{8,9},{9,8},{10,11... | collective-permute-start | bytes 786440 | tf_op jit(solution)/shard_map/ppermute | solution.py:363
  71.9 1.8 %collective-permute-start.17 = (bf16[128,1024]{1,0:T(8,128)(2,1)S(1)}, bf16[128,1024]{1,0:T(8,128)(2,1)S(1)}, u32[]{:S(2)}, u32[]{:S(2)}) collective-permute-start(bf16[128,1024]{1,0:T(8,128)(2,1)S(1)} %collective-permute-done.13.a2), channel_id=1, source_target_pairs={{0,1},{1,0},{2,3},{3,2},{4,5},{5,4},{6,7},{7,6},{8,9},{9,8},{10,11... | collective-permute-start | bytes 786440 | tf_op jit(solution)/shard_map/ppermute | solution.py:363
  72.3 1.8 %collective-permute-start.18 = (bf16[128,1024]{1,0:T(8,128)(2,1)S(1)}, bf16[128,1024]{1,0:T(8,128)(2,1)S(1)}, u32[]{:S(2)}, u32[]{:S(2)}) collective-permute-start(bf16[128,1024]{1,0:T(8,128)(2,1)S(1)} %collective-permute-done.14.a3), channel_id=1, source_target_pairs={{0,1},{1,0},{2,3},{3,2},{4,5},{5,4},{6,7},{7,6},{8,9},{9,8},{10,11... | collective-permute-start | bytes 786440 | tf_op jit(solution)/shard_map/ppermute | solution.py:363
  82.4 28.1 %all-to-all-start.1 = ((bf16[32,32,256]{2,1,0:T(8,128)(2,1)}), bf16[32,32,256]{2,1,0:T(8,128)(2,1)S(1)}, u32[]{:S(2)}, u32[]{:S(2)}) async-start(bf16[32,32,256]{2,1,0:T(8,128)(2,1)} %bitcast.11), calls=%async_computation.1 | async-start | bytes 1048576 | tf_op jit(solution)/shard_map/all_to_all | solution.py:386
  94.9 18.3 %collective-permute-start.10 = (bf16[128,512]{1,0:T(8,128)(2,1)S(1)}, bf16[128,512]{1,0:T(8,128)(2,1)S(1)}, u32[]{:S(2)}, u32[]{:S(2)}) collective-permute-start(bf16[128,512]{1,0:T(8,128)(2,1)S(1)} %copy-done.22), channel_id=1, source_target_pairs={{2,0},{3,1},{4,2},{5,3},{6,4},{7,5},{8,6},{9,7},{10,8},{11,9},{12,... | collective-permute-start | bytes 393224 | tf_op jit(solution)/shard_map/ppermute | solution.py:355
  97.1 16.1 %collective-permute-start.11 = (bf16[128,512]{1,0:T(8,128)(2,1)S(1)}, bf16[128,512]{1,0:T(8,128)(2,1)S(1)}, u32[]{:S(2)}, u32[]{:S(2)}) collective-permute-start(bf16[128,512]{1,0:T(8,128)(2,1)S(1)} %copy-done.20), channel_id=1, source_target_pairs={{1,0},{2,1},{3,2},{4,3},{5,4},{6,5},{7,6},{8,7},{9,8},{10,9},{11,1... | collective-permute-start | bytes 393224 | tf_op jit(solution)/shard_map/ppermute | solution.py:355
  100.7 26.2 %collective-permute-start.9 = (bf16[128,512]{1,0:T(8,128)(2,1)S(1)}, bf16[128,512]{1,0:T(8,128)(2,1)S(1)}, u32[]{:S(2)}, u32[]{:S(2)}) collective-permute-start(bf16[128,512]{1,0:T(8,128)(2,1)S(1)} %get-tuple-element.33), channel_id=1, source_target_pairs={{3,0},{4,1},{5,2},{6,3},{7,4},{8,5},{9,6},{10,7},{11,8},{12,9},{13... | collective-permute-start | bytes 393224 | tf_op jit(solution)/shard_map/ppermute | solution.py:355
  111.1 16.5 %collective-permute-start.19 = (f32[16,256]{1,0:T(8,128)S(1)}, f32[16,256]{1,0:T(8,128)S(1)}, u32[]{:S(2)}, u32[]{:S(2)}) collective-permute-start(f32[16,256]{1,0:T(8,128)S(1)} %get-tuple-element.43), channel_id=1, source_target_pairs={{0,1},{1,0},{2,3},{3,2},{4,5},{5,4},{6,7},{7,6},{8,9},{9,8},{10,11... | collective-permute-start | bytes 49160 | tf_op jit(solution)/shard_map/ppermute | solution.py:363
  (21 other events, 237.6 us)

commit v3 on v1

v3 whole, which is shorter than its diff:
```python
import math

import jax
import jax.numpy as jnp
from jax import lax
from jax.experimental import pallas as pl
from jax.experimental.pallas import tpu as pltpu
from jax.sharding import Mesh, PartitionSpec as P

HEAD = 128
STRETCH = 64
SPAN = 4
PER_GROUP = 4
GROUPS = 2
ROWS = 128
KEYS = SPAN * ROWS
WIDE = PER_GROUP * HEAD
HALF = GROUPS * HEAD
MASKED = -1e30
SCALE = HEAD**-0.5
LOG2E = math.log2(math.e)
BF16 = jnp.bfloat16
F32 = jnp.float32
AXES = ("zl", "zh", "x", "y", "c")
CTX = ("zh", "x", "y", "c")
CHIP = ("zh", "x", "y")
N_CHIP = 32
NSTART = 64
MIB = 1024 * 1024
PARAMS = pltpu.CompilerParams(vmem_limit_bytes=8 * MIB)
LARGE = pltpu.CompilerParams(vmem_limit_bytes=24 * MIB)
WHOLE = pl.BlockSpec(memory_space=pltpu.VMEM)


def nt(a, b):
    return lax.dot_general(a, b, (((1,), (1,)), ((), ())), preferred_element_type=F32)


def tn(a, b):
    return lax.dot_general(a, b, (((0,), (0,)), ((), ())), preferred_element_type=F32)


def nn(a, b):
    return lax.dot_general(a, b, (((1,), (0,)), ((), ())), preferred_element_type=F32)


def shape(*dims, dtype=BF16):
    return jax.ShapeDtypeStruct(dims, dtype)


def cost(flops, mib):
    return pl.CostEstimate(flops=flops, bytes_accessed=int(mib * MIB), transcendentals=0)


def stack_heads(block):
    return jnp.concatenate([block[:, h * HEAD : (h + 1) * HEAD] for h in range(PER_GROUP)], axis=0)


def put_rows(out_ref, core, own, other):
    out_ref[pl.ds(pl.multiple_of(core * ROWS, ROWS), ROWS), :] = own[...]
    out_ref[pl.ds(pl.multiple_of((1 - core) * ROWS, ROWS), ROWS), :] = other[...]


def pick_kernel(ids, k_own, k_other, v_own, v_other, key_ref, value_ref, last_ref):
    put_rows(key_ref, ids[2], k_own, k_other)
    put_rows(value_ref, ids[2], v_own, v_other)
    last_ref[:, :HALF] = key_ref[ROWS:]
    last_ref[:, HALF:] = value_ref[ROWS:]


def pick_call(ids, *blocks):
    half = pl.BlockSpec((ROWS, HALF), lambda i, ids: (0, ids[2]))
    return pl.pallas_call(
        pick_kernel,
        grid_spec=pltpu.PrefetchScalarGridSpec(
            num_scalar_prefetch=1, grid=(1,), in_specs=[half] * 4, out_specs=[WHOLE] * 3
        ),
        out_shape=[shape(2 * ROWS, HALF)] * 2 + [shape(ROWS, 2 * HALF)],
        compiler_params=PARAMS,
        cost_estimate=cost(0, 0.5),
        name="pick_keys_and_values",
    )(ids, *blocks)


def prepare_kernel(
    ids, order, starts, q_own, q_other, g_own, g_other, bias_ref, queries_ref, grads_ref
):
    put_rows(queries_ref, ids[2], q_own, q_other)
    put_rows(grads_ref, ids[2], g_own, g_other)
    base = ids[0] - ids[2]
    lane = lax.broadcasted_iota(jnp.int32, (1, ROWS), 1)
    row = lax.broadcasted_iota(jnp.int32, (STRETCH, ROWS), 0)
    for s in range(2):
        shard = base + s
        stretch = jnp.where(lane < STRETCH, order[2 * shard], order[2 * shard + 1])
        query_pos = shard * ROWS + stretch * STRETCH + (lane & (STRETCH - 1))
        begin = jnp.zeros((1, ROWS), jnp.int32)
        for i in range(NSTART):
            begin = jnp.where(starts[i] <= query_pos, starts[i], begin)
        for d in range(SPAN):
            source = shard - (SPAN - 1) + d
            known = jnp.maximum(source, 0)
            for j in range(2):
                key_pos = source * ROWS + order[2 * known + j] * STRETCH + row
                allowed = (key_pos <= query_pos) & (key_pos >= begin)
                bias_ref[s, (2 * d + j) * STRETCH : (2 * d + j + 1) * STRETCH, :] = jnp.where(
                    allowed, 0.0, MASKED
                )


def prepare_call(ids, order, starts, *blocks):
    half = pl.BlockSpec((ROWS, GROUPS * WIDE), lambda i, ids, *_: (0, ids[2]))
    return pl.pallas_call(
        prepare_kernel,
        grid_spec=pltpu.PrefetchScalarGridSpec(
            num_scalar_prefetch=3, grid=(1,), in_specs=[half] * 4, out_specs=[WHOLE] * 3
        ),
        out_shape=[shape(2, KEYS, ROWS, dtype=F32)] + [shape(2 * ROWS, GROUPS * WIDE)] * 2,
        compiler_params=PARAMS,
        cost_estimate=cost(0, 2.5),
        name="prepare",
    )(ids, order, starts, *blocks)


def spread(out, far1, far2, s0, s1):
    out[:ROWS] = s0[3 * ROWS :] + s1[2 * ROWS : 3 * ROWS]
    out[ROWS:] = s1[3 * ROWS :]
    far1[:ROWS] = (s0[ROWS : 2 * ROWS] + s1[:ROWS]).astype(BF16)
    far1[ROWS:] = (s0[2 * ROWS : 3 * ROWS] + s1[ROWS : 2 * ROWS]).astype(BF16)
    far2[...] = s0[:ROWS].astype(BF16)


def forward_kernel(bias, q_ref, g_ref, k2, k1, k0, prob_ref, own_ref, far1, far2):
    keys = jnp.concatenate([k2[...], k1[...], k0[...]], axis=0)
    terms = []
    for s in range(2):
        rows = slice(s * ROWS, (s + 1) * ROWS)
        window = keys[s * ROWS : s * ROWS + KEYS]
        for h in range(PER_GROUP):
            cols = slice(h * HEAD, (h + 1) * HEAD)
            score = nt(window, q_ref[rows, cols]) * (SCALE * LOG2E) + bias[s]
            weight = jnp.exp2(score - jnp.max(score, axis=0, keepdims=True))
            total = jnp.sum(weight, axis=0, keepdims=True)
            prob_ref[0, s, :, cols] = (weight * (1.0 / total)).astype(BF16)
        terms.append(nn(prob_ref[0, s], stack_heads(g_ref[rows, :])))
    spread(own_ref, far1, far2, *terms)


def backward_kernel(
    ids,
    prob_ref,
    q_ref,
    g_ref,
    k2,
    k1,
    k0,
    v2,
    v1,
    v0,
    keep_ref,
    send_ref,
    own_ref,
    far1,
    far2,
    gq_ref,
):
    core = ids[2]
    keys = jnp.concatenate([k2[...], k1[...], k0[...]], axis=0)
    values = jnp.concatenate([v2[...], v1[...], v0[...]], axis=0)
    terms = []
    for s in range(2):
        rows = slice(s * ROWS, (s + 1) * ROWS)
        window = slice(s * ROWS, s * ROWS + KEYS)
        prob = prob_ref[0, s].astype(F32)
        weighted = prob * nt(values[window], stack_heads(g_ref[rows, :]))
        delta = jnp.sum(weighted, axis=0, keepdims=True)
        grad_score = (weighted - prob * delta).astype(BF16)
        terms.append(nn(grad_score, stack_heads(q_ref[rows, :])) * SCALE)
        query_grad = tn(grad_score, keys[window]) * SCALE
        for h in range(PER_GROUP):
            gq_ref[s, :, h * HEAD : (h + 1) * HEAD] = query_grad[h * ROWS : (h + 1) * ROWS].astype(
                BF16
            )
    spread(own_ref, far1, far2, *terms)
    keep_ref[...] = gq_ref[core]
    send_ref[...] = gq_ref[1 - core]


def narrow(rows, shift=0):
    return pl.BlockSpec((rows, HEAD), lambda j, *_: (0, j + shift))


def wide(rows):
    return pl.BlockSpec((rows, WIDE), lambda j, *_: (0, j))


WINDOW = [narrow(ROWS), narrow(2 * ROWS), narrow(2 * ROWS)]
VALUE_WINDOW = [narrow(ROWS, GROUPS)] + WINDOW[1:]
TERMS = [narrow(2 * ROWS), narrow(2 * ROWS), narrow(ROWS)]
PROB_SPEC = pl.BlockSpec((1, 2, KEYS, WIDE), lambda j, *_: (j, 0, 0, 0))


def term_shapes():
    return [shape(2 * ROWS, HALF, dtype=F32), shape(2 * ROWS, HALF), shape(ROWS, HALF)]


def forward_call(bias, queries, grads, keys):
    return pl.pallas_call(
        forward_kernel,
        grid=(GROUPS,),
        in_specs=[pl.BlockSpec((2, KEYS, ROWS), lambda j: (0, 0, 0))]
        + [wide(2 * ROWS)] * 2
        + WINDOW,
        out_specs=[PROB_SPEC] + TERMS,
        out_shape=[shape(GROUPS, 2, KEYS, WIDE)] + term_shapes(),
        compiler_params=LARGE,
        cost_estimate=cost(4 * 16 * ROWS * KEYS * HEAD, 6),
        name="forward_and_value_gradient",
    )(bias, queries, grads, *keys)


def backward_call(ids, prob, queries, grads, keys, values):
    return pl.pallas_call(
        backward_kernel,
        grid_spec=pltpu.PrefetchScalarGridSpec(
            num_scalar_prefetch=1,
            grid=(GROUPS,),
            in_specs=[PROB_SPEC] + [wide(2 * ROWS)] * 2 + WINDOW + VALUE_WINDOW,
            out_specs=[wide(ROWS)] * 2 + TERMS,
            scratch_shapes=[pltpu.VMEM((2, ROWS, WIDE), BF16)],
        ),
        out_shape=[shape(ROWS, GROUPS * WIDE)] * 2 + term_shapes(),
        compiler_params=LARGE,
        cost_estimate=cost(6 * 16 * ROWS * KEYS * HEAD, 6),
        name="query_and_key_gradient",
    )(ids, prob, queries, grads, *keys, *values)


def pack_kernel(ids, in_ref, o0, o1, o2, o3):
    for d, out_ref in enumerate((o0, o1, o2, o3)):
        x = (ids[1] + d) & 3
        for z in range(8):
            column = pl.multiple_of((4 * z + x) * HEAD, HEAD)
            out_ref[:, z * HEAD : (z + 1) * HEAD] = in_ref[:, pl.ds(column, HEAD)]


def pack_call(ids, inputs):
    return pl.pallas_call(
        pack_kernel,
        grid_spec=pltpu.PrefetchScalarGridSpec(
            num_scalar_prefetch=1, grid=(1,), in_specs=[WHOLE], out_specs=[WHOLE] * 4
        ),
        out_shape=[shape(ROWS, 8 * HEAD)] * 4,
        compiler_params=PARAMS,
        cost_estimate=cost(0, 2),
        name="pack_inputs",
    )(ids, inputs)


def add_terms(own, r1, r2):
    first = own[:ROWS] + r1[:ROWS].astype(F32)
    second = own[ROWS:] + r1[ROWS:].astype(F32) + r2[...].astype(F32)
    return first.astype(BF16), second.astype(BF16)


def value_total_kernel(ids, own, r1, r2, keep_ref, send_ref, copies_ref):
    core = ids[2]
    first, second = add_terms(own, r1, r2)
    for x in range(4):
        copies_ref[x, :ROWS], copies_ref[x, ROWS:] = first, second
    keep_ref[...] = copies_ref[0, pl.ds(pl.multiple_of(core * ROWS, ROWS), ROWS), :]
    send_ref[...] = copies_ref[0, pl.ds(pl.multiple_of((1 - core) * ROWS, ROWS), ROWS), :]


def key_total_kernel(ids, own, r1, r2, keep_ref, send_ref, both_ref):
    core = ids[2]
    both_ref[:ROWS], both_ref[ROWS:] = add_terms(own, r1, r2)
    keep_ref[...] = both_ref[pl.ds(pl.multiple_of(core * ROWS, ROWS), ROWS), :]
    send_ref[...] = both_ref[pl.ds(pl.multiple_of((1 - core) * ROWS, ROWS), ROWS), :]


def total_call(ids, own, r1, r2, copies):
    return pl.pallas_call(
        value_total_kernel if copies else key_total_kernel,
        grid_spec=pltpu.PrefetchScalarGridSpec(
            num_scalar_prefetch=1,
            grid=(1,),
            in_specs=[WHOLE] * 3,
            out_specs=[WHOLE] * (3 if copies else 2),
            scratch_shapes=[] if copies else [pltpu.VMEM((2 * ROWS, HALF), BF16)],
        ),
        out_shape=[shape(ROWS, HALF)] * 2 + ([shape(4, 2 * ROWS, HALF)] if copies else []),
        compiler_params=PARAMS,
        cost_estimate=cost(0, 1),
        name="value_gradient_total" if copies else "key_gradient_total",
    )(ids, own, r1, r2)


def join_kernel(ids, *refs):
    core = ids[2]
    count = len(refs) // 3
    for keep, other, out in zip(refs[:count], refs[count : 2 * count], refs[2 * count :]):
        width = keep.shape[1]
        out[:, pl.ds(pl.multiple_of(core * width, HEAD), width)] = keep[...]
        out[:, pl.ds(pl.multiple_of((1 - core) * width, HEAD), width)] = other[...]


def join_call(ids, keep, other, name):
    return pl.pallas_call(
        join_kernel,
        grid_spec=pltpu.PrefetchScalarGridSpec(
            num_scalar_prefetch=1,
            grid=(1,),
            in_specs=[WHOLE] * (2 * len(keep)),
            out_specs=[WHOLE] * len(keep),
        ),
        out_shape=[shape(a.shape[0], 2 * a.shape[1], dtype=a.dtype) for a in keep],
        compiler_params=PARAMS,
        cost_estimate=cost(0, 0.5),
        name=name,
    )(ids, *keep, *other)


def weight_kernel(ids, grads, a0, a1, a2, a3, b0, b1, b2, b3, out_ref):
    x, core = ids[1], ids[2]
    left = [ref[...] for ref in (a0, a1, a2, a3, b0, b1, b2, b3)]
    right = []
    for side in (core, 1 - core):
        rows = pl.ds(pl.multiple_of(side * ROWS, ROWS), ROWS)
        right += [grads[(x + 4 - d) & 3, rows, :] for d in range(4)]
    left, right = jnp.concatenate(left, axis=0), jnp.concatenate(right, axis=0)
    out_ref[...] = tn(left, right).astype(BF16)


def weight_call(ids, grads, own, other):
    taken = pl.BlockSpec((ROWS, 256), lambda i, _: (0, i))
    return pl.pallas_call(
        weight_kernel,
        grid_spec=pltpu.PrefetchScalarGridSpec(
            num_scalar_prefetch=1,
            grid=(4,),
            in_specs=[pl.BlockSpec((4, 2 * ROWS, HALF), lambda i, _: (0, 0, 0))] + [taken] * 8,
            out_specs=pl.BlockSpec((256, HALF), lambda i, _: (i, 0)),
        ),
        out_shape=shape(1024, HALF),
        compiler_params=LARGE,
        cost_estimate=cost(2 * 1024 * 1024 * 256, 3),
        name="weight_gradient",
    )(ids, grads, *own, *other)


def final_kernel(ids, in_ref, keep_ref, send_ref, total_ref):
    core = ids[2]
    total = in_ref[0].astype(F32)
    for i in range(1, 32):
        total += in_ref[i].astype(F32)
    total_ref[...] = total
    keep_ref[...] = total_ref[pl.ds(pl.multiple_of(core * 16, 16), 16), :]
    send_ref[...] = total_ref[pl.ds(pl.multiple_of((1 - core) * 16, 16), 16), :]


def final_call(ids, parts):
    return pl.pallas_call(
        final_kernel,
        grid_spec=pltpu.PrefetchScalarGridSpec(
            num_scalar_prefetch=1,
            grid=(1,),
            in_specs=[WHOLE],
            out_specs=[WHOLE] * 2,
            scratch_shapes=[pltpu.VMEM((32, HALF), F32)],
        ),
        out_shape=[shape(16, HALF, dtype=F32)] * 2,
        compiler_params=PARAMS,
        cost_estimate=cost(0, 0.5),
        name="weight_rows",
    )(ids, parts)


def shift_chips(block, distance):
    route = [(i - distance, i) for i in range(N_CHIP) if 0 <= i - distance < N_CHIP]
    return lax.ppermute(block, CHIP, route)


def shift_x(block, distance):
    return lax.ppermute(block, "x", [(i, (i + distance) % 4) for i in range(4)])


def swap_core(block):
    return lax.ppermute(block, "c", [(0, 1), (1, 0)])


def shards(query, key, value, grad, inputs, stretch_order, session_starts):
    query, key, value, grad, inputs = query[0], key[0], value[0], grad[0], inputs[0]
    core = lax.axis_index("c")
    ids = jnp.stack([lax.axis_index(CTX), lax.axis_index("x"), core]).astype(jnp.int32)

    key0, value0, last = pick_call(ids, key, swap_core(key), value, swap_core(value))
    far2 = shift_chips(last, 2)
    keys = [far2, shift_chips(key0, 1), key0]
    bias, queries, grads = prepare_call(
        ids,
        stretch_order.reshape(-1),
        session_starts.reshape(-1),
        query,
        swap_core(query),
        grad,
        swap_core(grad),
    )
    bias, value0 = lax.optimization_barrier((bias, value0))
    value1 = shift_chips(value0, 1)

    prob, value_own, value_t1, value_t2 = forward_call(bias, queries, grads, keys)
    value_r2 = shift_chips(value_t2, -2)
    value_r1 = shift_chips(value_t1, -1)
    values = [far2, value1, value0]
    query_keep, query_send, key_own, key_t1, key_t2 = backward_call(
        ids, prob, queries, grads, keys, values
    )
    inputs, query_send = lax.optimization_barrier((inputs, query_send))
    packed = pack_call(ids, inputs)
    own = [packed[0]] + [shift_x(packed[d], d) for d in range(1, 4)]
    other = [swap_core(block) for block in own]
    value_r1, query_send = lax.optimization_barrier((value_r1, query_send))
    value_keep, value_send, sent = total_call(ids, value_own, value_r1, value_r2, True)
    gathered = lax.all_to_all(sent, "x", 0, 0, tiled=True)
    partial = weight_call(ids, gathered, own, other).reshape(32, 32, HALF)
    partial = lax.all_to_all(partial, ("zl", "zh", "y"), 0, 0, tiled=True)

    key_r2 = shift_chips(key_t2, -2)
    key_r1 = shift_chips(key_t1, -1)
    key_keep, key_send = total_call(ids, key_own, key_r1, key_r2, False)
    grad_query, grad_value = join_call(
        ids,
        [query_keep, value_keep],
        [swap_core(query_send), swap_core(value_send)],
        "join_query_and_value",
    )
    (grad_key,) = join_call(ids, [key_keep], [swap_core(key_send)], "join_key")

    row_keep, row_send = final_call(ids, partial)
    (weight_grad,) = join_call(ids, [row_keep], [swap_core(row_send)], "join_weight")
    return grad_query[None], grad_key[None], grad_value[None], weight_grad


def solution(mesh):
    fine = Mesh(mesh.devices.reshape(4, 2, 4, 4, 2), AXES)
    rows = P("zl", CTX, None)
    return jax.shard_map(
        shards,
        mesh=fine,
        in_specs=(rows, rows, rows, rows, rows, P("zl", None, None), P("zl", None)),
        out_specs=(rows, rows, rows, P(AXES, None)),
        check_vma=False,
    )
```

time: 146 us -> 113 us (0.77)
  the two profiles are of different devices: /device:TPU:3 before, /device:TPU:55 now
where the time goes in v3:
time: 113 us; the launch traced here: 112 us
  starting transfers between devices  54.2 us (48%)
  waiting for transfers between devices  32.6 us (29%)
  Pallas kernels  18.7 us (17%)
  local copies, waits for them, and re-layouts  6.09 us (5%)
    ppermute x7, waiting for transfers between devices, shift_chips(): return lax.ppermute(block, CHIP, route)  28.7 us
    ppermute x7, starting transfers between devices, shift_chips(): return lax.ppermute(block, CHIP, route)  25.1 us
    ppermute x12, starting transfers between devices, swap_core(): return lax.ppermute(block, 'c', [(0, 1), (1, 0)])  13.9 us
    all_to_all x1, starting transfers between devices, shards(): partial = lax.all_to_all(partial, ('zl', 'zh', 'y'), 0, 0, tiled=True)  9.74 us
    unnamed x17, local copies, waits for them, and re-layouts  5.95 us
    all_to_all x1, starting transfers between devices, shards(): gathered = lax.all_to_all(sent, 'x', 0, 0, tiled=True)  3.94 us
    ppermute x12, waiting for transfers between devices, swap_core(): return lax.ppermute(block, 'c', [(0, 1), (1, 0)])  3.87 us
    pallas_call x3, Pallas kernels, join_call(): pl.pallas_call(join_kernel, grid_spec=pltpu.PrefetchScalarGridSpec(num_sc...  3.78 us
  transfers between devices with their start and end apart: 24, of which 8 were waited for; matrix products, arithmetic and copies ran while one was open for 1% of the time, Pallas kernels for 13%

profile of v3, /device:TPU:55, one launch (start us, length us, event | category | flops | bytes accessed | tf_op | source)
XLA Modules:
  0.0 112.5 jit_solution(2313053408325143703)
XLA Ops:
  2.1 2.0 %collective-permute-done.2.k_other = bf16[128,512]{1,0:T(8,128)(2,1)S(1)} collective-permute-done((bf16[128,512]{1,0:T(8,128)(2,1)}, bf16[128,512]{1,0:T(8,128)(2,1)S(1)}, u32[]{:S(2)}, u32[]{:S(2)}) %collective-permute-start.2) | collective-permute-done | bytes 131104 | tf_op jit(solution)/shard_map/ppermute | solution.py:389
  6.7 7.6 %collective-permute-start.4 = (bf16[128,512]{1,0:T(8,128)(2,1)S(1)}, bf16[128,512]{1,0:T(8,128)(2,1)S(1)}, u32[]{:S(2)}, u32[]{:S(2)}) collective-permute-start(bf16[128,512]{1,0:T(8,128)(2,1)S(1)} %get-tuple-element.43), channel_id=1, source_target_pairs={{0,4},{2,6},{4,8},{6,10},{8,12},{10,14},{12,16},{14,18},{16,20},{1... | collective-permute-start | bytes 393224 | tf_op jit(solution)/shard_map/ppermute | solution.py:381
  14.3 3.8 %collective-permute-start.5 = (bf16[256,256]{1,0:T(8,128)(2,1)S(1)}, bf16[256,256]{1,0:T(8,128)(2,1)S(1)}, u32[]{:S(2)}, u32[]{:S(2)}) collective-permute-start(bf16[256,256]{1,0:T(8,128)(2,1)S(1)} %get-tuple-element.44.k0), channel_id=1, source_target_pairs={{0,2},{2,4},{4,6},{6,8},{8,10},{10,12},{12,14},{14,16},{16,18},{18... | collective-permute-start | bytes 393224 | tf_op jit(solution)/shard_map/ppermute | solution.py:381
  19.0 1.0 copy-done.1
  20.1 1.0 copy-done.2
  22.5 3.8 %collective-permute-start.6 = (bf16[256,256]{1,0:T(8,128)(2,1)S(1)}, bf16[256,256]{1,0:T(8,128)(2,1)S(1)}, u32[]{:S(2)}, u32[]{:S(2)}) collective-permute-start(bf16[256,256]{1,0:T(8,128)(2,1)S(1)} %get-tuple-element.46.v0), channel_id=1, source_target_pairs={{0,2},{2,4},{4,6},{6,8},{8,10},{10,12},{12,14},{14,16},{16,18},{18... | collective-permute-start | bytes 393224 | tf_op jit(solution)/shard_map/ppermute | solution.py:381
  26.3 3.1 %forward_and_value_gradient.1 = (bf16[2,2,512,512]{3,2,1,0:T(8,128)(2,1)S(1)}, f32[256,256]{1,0:T(8,128)S(1)}, bf16[256,256]{1,0:T(8,128)(2,1)S(1)}, bf16[128,256]{1,0:T(8,128)(2,1)S(1)}) custom-call(f32[2,512,128]{2,1,0:T(8,128)S(1)} %get-tuple-element.40.bias, bf16[256,1024]{1,0:T(8,128)(2,1)S(1)} %get-tuple-element.41.q_ref, ...), custom_call_target="tpu_custom_call" | custom-call | flops 536870912 | bytes 6291456 | tf_op jit(solution)/shard_map/forward_and_value_gradient/pallas_call | solution.py:208
  29.5 2.1 %collective-permute-start.7 = (bf16[256,256]{1,0:T(8,128)(2,1)S(1)}, bf16[256,256]{1,0:T(8,128)(2,1)S(1)}, u32[]{:S(2)}, u32[]{:S(2)}) collective-permute-start(bf16[256,256]{1,0:T(8,128)(2,1)S(1)} %get-tuple-element.49), channel_id=1, source_target_pairs={{2,0},{4,2},{6,4},{8,6},{10,8},{12,10},{14,12},{16,14},{18,16},{20... | collective-permute-start | bytes 393224 | tf_op jit(solution)/shard_map/ppermute | solution.py:381
  31.6 3.7 %query_and_key_gradient.1 = (bf16[128,1024]{1,0:T(8,128)(2,1)S(1)}, bf16[128,1024]{1,0:T(8,128)(2,1)S(1)}, f32[256,256]{1,0:T(8,128)S(1)}, bf16[256,256]{1,0:T(8,128)(2,1)S(1)}, bf16[128,256]{1,0:T(8,128)(2,1)S(1)}) custom-call(s32[3]{0:T(128)S(1)} %pad_add_fusion.ids, bf16[2,2,512,512]{3,2,1,0:T(8,128)(2,1)S(1)} %get-tuple-element.45.prob_ref, ...), custom_call_target="tpu_custom_call" | custom-call | flops 805306368 | bytes 6291456 | tf_op jit(solution)/shard_map/query_and_key_gradient/pallas_call | solution.py:223
  36.4 1.4 %collective-permute-start.16 = (bf16[128,1024]{1,0:T(8,128)(2,1)S(1)}, bf16[128,1024]{1,0:T(8,128)(2,1)S(1)}, u32[]{:S(2)}, u32[]{:S(2)}) collective-permute-start(bf16[128,1024]{1,0:T(8,128)(2,1)S(1)} %get-tuple-element.69), channel_id=1, source_target_pairs={{0,24},{8,0},{16,8},{24,16},{1,25},{9,1},{17,9},{25,17},{2,26},{10... | collective-permute-start | bytes 786440 | tf_op jit(solution)/shard_map/ppermute | solution.py:385
  37.7 1.9 %collective-permute-start.8 = (bf16[128,256]{1,0:T(8,128)(2,1)S(1)}, bf16[128,256]{1,0:T(8,128)(2,1)S(1)}, u32[]{:S(2)}, u32[]{:S(2)}) collective-permute-start(bf16[128,256]{1,0:T(8,128)(2,1)S(1)} %get-tuple-element.53), channel_id=1, source_target_pairs={{4,0},{6,2},{8,4},{10,6},{12,8},{14,10},{16,12},{18,14},{20,16},{2... | collective-permute-start | bytes 196616 | tf_op jit(solution)/shard_map/ppermute | solution.py:381
  39.6 13.7 %collective-permute-done.8.r2 = bf16[128,256]{1,0:T(8,128)(2,1)S(1)} collective-permute-done((bf16[128,256]{1,0:T(8,128)(2,1)S(1)}, bf16[128,256]{1,0:T(8,128)(2,1)S(1)}, u32[]{:S(2)}, u32[]{:S(2)}) %collective-permute-start.8) | collective-permute-done | bytes 65568 | tf_op jit(solution)/shard_map/ppermute | solution.py:381
  53.3 1.4 %value_gradient_total.1 = (bf16[128,256]{1,0:T(8,128)(2,1)S(1)}, bf16[128,256]{1,0:T(8,128)(2,1)S(1)}, bf16[4,256,256]{2,1,0:T(8,128)(2,1)}) custom-call(s32[3]{0:T(128)S(1)} %pad_add_fusion.ids, f32[256,256]{1,0:T(8,128)S(1)} %get-tuple-element.48.own, bf16[256,256]{1,0:T(8,128)(2,1)S(1)} %collective-permute-done.7.r1, ...), custom_call_target="tpu_custom_call" | custom-call | bytes 1048576 | tf_op jit(solution)/shard_map/value_gradient_total/pallas_call | solution.py:283
  55.4 3.9 %all-to-all-start = ((bf16[4,256,256]{2,1,0:T(8,128)(2,1)}), bf16[4,256,256]{2,1,0:T(8,128)(2,1)S(1)}, u32[]{:S(2)}, u32[]{:S(2)}) async-start(bf16[4,256,256]{2,1,0:T(8,128)(2,1)} %get-tuple-element.64), calls=%async_computation | async-start | bytes 1048576 | tf_op jit(solution)/shard_map/all_to_all | solution.py:425
  59.3 6.0 %collective-permute-start.17 = (bf16[128,1024]{1,0:T(8,128)(2,1)S(1)}, bf16[128,1024]{1,0:T(8,128)(2,1)S(1)}, u32[]{:S(2)}, u32[]{:S(2)}) collective-permute-start(bf16[128,1024]{1,0:T(8,128)(2,1)S(1)} %get-tuple-element.66.a0), channel_id=1, source_target_pairs={{0,1},{1,0},{2,3},{3,2},{4,5},{5,4},{6,7},{7,6},{8,9},{9,8},{10,11... | collective-permute-start | bytes 786440 | tf_op jit(solution)/shard_map/ppermute | solution.py:389
  67.6 3.3 %weight_gradient.1 = bf16[1024,256]{1,0:T(8,128)(2,1)} custom-call(s32[3]{0:T(128)S(1)} %pad_add_fusion.ids, bf16[4,256,256]{2,1,0:T(8,128)(2,1)S(1)} %all-to-all-done.grads, bf16[128,1024]{1,0:T(8,128)(2,1)S(1)} %get-tuple-element.66.a0, bf16[128,1024]{1,0:T(8,128)(2,1)S(1)} %collective-permute-done.14.a1, ...), custom_call_target="tpu_custom_call" | custom-call | flops 536870912 | bytes 3145728 | tf_op jit(solution)/shard_map/weight_gradient/pallas_call | solution.py:337
  70.9 9.7 %all-to-all-start.1 = ((bf16[32,32,256]{2,1,0:T(8,128)(2,1)}), bf16[32,32,256]{2,1,0:T(8,128)(2,1)S(1)}, u32[]{:S(2)}, u32[]{:S(2)}) async-start(bf16[32,32,256]{2,1,0:T(8,128)(2,1)} %bitcast.12), calls=%async_computation.1 | async-start | bytes 1048576 | tf_op jit(solution)/shard_map/all_to_all | solution.py:427
  80.6 4.4 %collective-permute-start.9 = (bf16[128,1024]{1,0:T(8,128)(2,1)S(1)}, bf16[128,1024]{1,0:T(8,128)(2,1)S(1)}, u32[]{:S(2)}, u32[]{:S(2)}) collective-permute-start(bf16[128,1024]{1,0:T(8,128)(2,1)S(1)} %get-tuple-element.55), channel_id=1, source_target_pairs={{0,1},{1,0},{2,3},{3,2},{4,5},{5,4},{6,7},{7,6},{8,9},{9,8},{10,11... | collective-permute-start | bytes 786440 | tf_op jit(solution)/shard_map/ppermute | solution.py:389
  85.0 2.2 %collective-permute-start.11 = (bf16[256,256]{1,0:T(8,128)(2,1)}, bf16[256,256]{1,0:T(8,128)(2,1)S(1)}, u32[]{:S(2)}, u32[]{:S(2)}) collective-permute-start(bf16[256,256]{1,0:T(8,128)(2,1)} %copy-done.6), channel_id=1, source_target_pairs={{2,0},{4,2},{6,4},{8,6},{10,8},{12,10},{14,12},{16,14},{18,16},{20... | collective-permute-start | bytes 393224 | tf_op jit(solution)/shard_map/ppermute | solution.py:381
  87.2 3.7 %collective-permute-start.12 = (bf16[128,256]{1,0:T(8,128)(2,1)S(1)}, bf16[128,256]{1,0:T(8,128)(2,1)S(1)}, u32[]{:S(2)}, u32[]{:S(2)}) collective-permute-start(bf16[128,256]{1,0:T(8,128)(2,1)S(1)} %get-tuple-element.60), channel_id=1, source_target_pairs={{4,0},{6,2},{8,4},{10,6},{12,8},{14,10},{16,12},{18,14},{20,16},{2... | collective-permute-start | bytes 196616 | tf_op jit(solution)/shard_map/ppermute | solution.py:381
  90.9 15.1 %collective-permute-done.12.r2 = bf16[128,256]{1,0:T(8,128)(2,1)S(1)} collective-permute-done((bf16[128,256]{1,0:T(8,128)(2,1)S(1)}, bf16[128,256]{1,0:T(8,128)(2,1)S(1)}, u32[]{:S(2)}, u32[]{:S(2)}) %collective-permute-start.12) | collective-permute-done | bytes 65568 | tf_op jit(solution)/shard_map/ppermute | solution.py:381
  108.7 1.2 %join_key.1 = bf16[128,512]{1,0:T(8,128)(2,1)} custom-call(s32[3]{0:T(128)S(1)} %pad_add_fusion.ids, bf16[128,256]{1,0:T(8,128)(2,1)S(1)} %get-tuple-element.61.refs_0_, bf16[128,256]{1,0:T(8,128)(2,1)S(1)} %collective-permute-done.13.refs_1_), custom_call_target="tpu_custom_call" | custom-call | bytes 524288 | tf_op jit(solution)/shard_map/join_key/pallas_call | solution.py:309
  109.9 1.4 %join_query_and_value.1 = (bf16[128,2048]{1,0:T(8,128)(2,1)}, bf16[128,512]{1,0:T(8,128)(2,1)}) custom-call(s32[3]{0:T(128)S(1)} %pad_add_fusion.ids, bf16[128,1024]{1,0:T(8,128)(2,1)S(1)} %get-tuple-element.47.refs_0_, bf16[128,256]{1,0:T(8,128)(2,1)S(1)} %get-tuple-element.54.refs_1_, bf16[128,1024]{1,0:T(8,128)(2,1)S(1)} %collective-permute-done.9.refs_2_, ...), custom_call_target="tpu_custom_call" | custom-call | bytes 524288 | tf_op jit(solution)/shard_map/join_query_and_value/pallas_call | solution.py:309
  111.3 1.2 %join_weight.1 = f32[16,512]{1,0:T(8,128)} custom-call(s32[3]{0:T(128)S(1)} %pad_add_fusion.ids, f32[16,256]{1,0:T(8,128)S(1)} %get-tuple-element.70.refs_0_, f32[16,256]{1,0:T(8,128)S(1)} %collective-permute-done.21.refs_1_), custom_call_target="tpu_custom_call" | custom-call | bytes 524288 | tf_op jit(solution)/shard_map/join_weight/pallas_call | solution.py:309
  (55 shorter events, 13.0 us)
Async XLA Ops:
  0.6 18.4 %collective-permute-start = (bf16[128,2048]{1,0:T(8,128)(2,1)}, bf16[128,2048]{1,0:T(8,128)(2,1)S(1)}, u32[]{:S(2)}, u32[]{:S(2)}) collective-permute-start(bf16[128,2048]{1,0:T(8,128)(2,1)} %bitcast.14), channel_id=1, source_target_pairs={{0,1},{1,0},{2,3},{3,2},{4,5},{5,4},{6,7},{7,6},{8,9},{9,8},{10,11... | collective-permute-start | bytes 1572872 | tf_op jit(solution)/shard_map/ppermute | solution.py:389
  1.4 17.6 %collective-permute-start.1 = (bf16[128,2048]{1,0:T(8,128)(2,1)}, bf16[128,2048]{1,0:T(8,128)(2,1)S(1)}, u32[]{:S(2)}, u32[]{:S(2)}) collective-permute-start(bf16[128,2048]{1,0:T(8,128)(2,1)} %bitcast.16), channel_id=1, source_target_pairs={{0,1},{1,0},{2,3},{3,2},{4,5},{5,4},{6,7},{7,6},{8,9},{9,8},{10,11... | collective-permute-start | bytes 1572872 | tf_op jit(solution)/shard_map/ppermute | solution.py:389
  1.5 2.6 %collective-permute-start.2 = (bf16[128,512]{1,0:T(8,128)(2,1)}, bf16[128,512]{1,0:T(8,128)(2,1)S(1)}, u32[]{:S(2)}, u32[]{:S(2)}) collective-permute-start(bf16[128,512]{1,0:T(8,128)(2,1)} %bitcast.18), channel_id=1, source_target_pairs={{0,1},{1,0},{2,3},{3,2},{4,5},{5,4},{6,7},{7,6},{8,9},{9,8},{10,11... | collective-permute-start | bytes 393224 | tf_op jit(solution)/shard_map/ppermute | solution.py:389
  1.9 2.4 %collective-permute-start.3 = (bf16[128,512]{1,0:T(8,128)(2,1)}, bf16[128,512]{1,0:T(8,128)(2,1)S(1)}, u32[]{:S(2)}, u32[]{:S(2)}) collective-permute-start(bf16[128,512]{1,0:T(8,128)(2,1)} %bitcast.20), channel_id=1, source_target_pairs={{0,1},{1,0},{2,3},{3,2},{4,5},{5,4},{6,7},{7,6},{8,9},{9,8},{10,11... | collective-permute-start | bytes 393224 | tf_op jit(solution)/shard_map/ppermute | solution.py:389
  6.7 19.7 %collective-permute-start.4 = (bf16[128,512]{1,0:T(8,128)(2,1)S(1)}, bf16[128,512]{1,0:T(8,128)(2,1)S(1)}, u32[]{:S(2)}, u32[]{:S(2)}) collective-permute-start(bf16[128,512]{1,0:T(8,128)(2,1)S(1)} %get-tuple-element.43), channel_id=1, source_target_pairs={{0,4},{2,6},{4,8},{6,10},{8,12},{10,14},{12,16},{14,18},{16,20},{1... | collective-permute-start | bytes 393224 | tf_op jit(solution)/shard_map/ppermute | solution.py:381
  14.3 12.1 %collective-permute-start.5 = (bf16[256,256]{1,0:T(8,128)(2,1)S(1)}, bf16[256,256]{1,0:T(8,128)(2,1)S(1)}, u32[]{:S(2)}, u32[]{:S(2)}) collective-permute-start(bf16[256,256]{1,0:T(8,128)(2,1)S(1)} %get-tuple-element.44.k0), channel_id=1, source_target_pairs={{0,2},{2,4},{4,6},{6,8},{8,10},{10,12},{12,14},{14,16},{16,18},{18... | collective-permute-start | bytes 393224 | tf_op jit(solution)/shard_map/ppermute | solution.py:381
  22.5 9.1 %collective-permute-start.6 = (bf16[256,256]{1,0:T(8,128)(2,1)S(1)}, bf16[256,256]{1,0:T(8,128)(2,1)S(1)}, u32[]{:S(2)}, u32[]{:S(2)}) collective-permute-start(bf16[256,256]{1,0:T(8,128)(2,1)S(1)} %get-tuple-element.46.v0), channel_id=1, source_target_pairs={{0,2},{2,4},{4,6},{6,8},{8,10},{10,12},{12,14},{14,16},{16,18},{18... | collective-permute-start | bytes 393224 | tf_op jit(solution)/shard_map/ppermute | solution.py:381
  29.5 10.1 %collective-permute-start.7 = (bf16[256,256]{1,0:T(8,128)(2,1)S(1)}, bf16[256,256]{1,0:T(8,128)(2,1)S(1)}, u32[]{:S(2)}, u32[]{:S(2)}) collective-permute-start(bf16[256,256]{1,0:T(8,128)(2,1)S(1)} %get-tuple-element.49), channel_id=1, source_target_pairs={{2,0},{4,2},{6,4},{8,6},{10,8},{12,10},{14,12},{16,14},{18,16},{20... | collective-permute-start | bytes 393224 | tf_op jit(solution)/shard_map/ppermute | solution.py:381
  36.2 29.2 %collective-permute-start.14 = (bf16[128,1024]{1,0:T(8,128)(2,1)S(1)}, bf16[128,1024]{1,0:T(8,128)(2,1)S(1)}, u32[]{:S(2)}, u32[]{:S(2)}) collective-permute-start(bf16[128,1024]{1,0:T(8,128)(2,1)S(1)} %get-tuple-element.67), channel_id=1, source_target_pairs={{0,8},{8,16},{16,24},{24,0},{1,9},{9,17},{17,25},{25,1},{2,10},{10... | collective-permute-start | bytes 786440 | tf_op jit(solution)/shard_map/ppermute | solution.py:385
  36.3 29.1 %collective-permute-start.15 = (bf16[128,1024]{1,0:T(8,128)(2,1)S(1)}, bf16[128,1024]{1,0:T(8,128)(2,1)S(1)}, u32[]{:S(2)}, u32[]{:S(2)}) collective-permute-start(bf16[128,1024]{1,0:T(8,128)(2,1)S(1)} %get-tuple-element.68), channel_id=1, source_target_pairs={{0,16},{8,24},{16,0},{24,8},{1,17},{9,25},{17,1},{25,9},{2,18},{10... | collective-permute-start | bytes 786440 | tf_op jit(solution)/shard_map/ppermute | solution.py:385
  36.4 29.5 %collective-permute-start.16 = (bf16[128,1024]{1,0:T(8,128)(2,1)S(1)}, bf16[128,1024]{1,0:T(8,128)(2,1)S(1)}, u32[]{:S(2)}, u32[]{:S(2)}) collective-permute-start(bf16[128,1024]{1,0:T(8,128)(2,1)S(1)} %get-tuple-element.69), channel_id=1, source_target_pairs={{0,24},{8,0},{16,8},{24,16},{1,25},{9,1},{17,9},{25,17},{2,26},{10... | collective-permute-start | bytes 786440 | tf_op jit(solution)/shard_map/ppermute | solution.py:385
  37.7 15.6 %collective-permute-start.8 = (bf16[128,256]{1,0:T(8,128)(2,1)S(1)}, bf16[128,256]{1,0:T(8,128)(2,1)S(1)}, u32[]{:S(2)}, u32[]{:S(2)}) collective-permute-start(bf16[128,256]{1,0:T(8,128)(2,1)S(1)} %get-tuple-element.53), channel_id=1, source_target_pairs={{4,0},{6,2},{8,4},{10,6},{12,8},{14,10},{16,12},{18,14},{20,16},{2... | collective-permute-start | bytes 196616 | tf_op jit(solution)/shard_map/ppermute | solution.py:381
  55.4 11.1 %all-to-all-start = ((bf16[4,256,256]{2,1,0:T(8,128)(2,1)}), bf16[4,256,256]{2,1,0:T(8,128)(2,1)S(1)}, u32[]{:S(2)}, u32[]{:S(2)}) async-start(bf16[4,256,256]{2,1,0:T(8,128)(2,1)} %get-tuple-element.64), calls=%async_computation | async-start | bytes 1048576 | tf_op jit(solution)/shard_map/all_to_all | solution.py:425
  59.3 7.2 %collective-permute-start.17 = (bf16[128,1024]{1,0:T(8,128)(2,1)S(1)}, bf16[128,1024]{1,0:T(8,128)(2,1)S(1)}, u32[]{:S(2)}, u32[]{:S(2)}) collective-permute-start(bf16[128,1024]{1,0:T(8,128)(2,1)S(1)} %get-tuple-element.66.a0), channel_id=1, source_target_pairs={{0,1},{1,0},{2,3},{3,2},{4,5},{5,4},{6,7},{7,6},{8,9},{9,8},{10,11... | collective-permute-start | bytes 786440 | tf_op jit(solution)/shard_map/ppermute | solution.py:389
  65.3 1.5 %collective-permute-start.18 = (bf16[128,1024]{1,0:T(8,128)(2,1)S(1)}, bf16[128,1024]{1,0:T(8,128)(2,1)S(1)}, u32[]{:S(2)}, u32[]{:S(2)}) collective-permute-start(bf16[128,1024]{1,0:T(8,128)(2,1)S(1)} %collective-permute-done.14.a1), channel_id=1, source_target_pairs={{0,1},{1,0},{2,3},{3,2},{4,5},{5,4},{6,7},{7,6},{8,9},{9,8},{10,11... | collective-permute-start | bytes 786440 | tf_op jit(solution)/shard_map/ppermute | solution.py:389
  65.3 1.9 %collective-permute-start.19 = (bf16[128,1024]{1,0:T(8,128)(2,1)S(1)}, bf16[128,1024]{1,0:T(8,128)(2,1)S(1)}, u32[]{:S(2)}, u32[]{:S(2)}) collective-permute-start(bf16[128,1024]{1,0:T(8,128)(2,1)S(1)} %collective-permute-done.15.a2), channel_id=1, source_target_pairs={{0,1},{1,0},{2,3},{3,2},{4,5},{5,4},{6,7},{7,6},{8,9},{9,8},{10,11... | collective-permute-start | bytes 786440 | tf_op jit(solution)/shard_map/ppermute | solution.py:389
  65.9 1.8 %collective-permute-start.20 = (bf16[128,1024]{1,0:T(8,128)(2,1)S(1)}, bf16[128,1024]{1,0:T(8,128)(2,1)S(1)}, u32[]{:S(2)}, u32[]{:S(2)}) collective-permute-start(bf16[128,1024]{1,0:T(8,128)(2,1)S(1)} %collective-permute-done.16.a3), channel_id=1, source_target_pairs={{0,1},{1,0},{2,3},{3,2},{4,5},{5,4},{6,7},{7,6},{8,9},{9,8},{10,11... | collective-permute-start | bytes 786440 | tf_op jit(solution)/shard_map/ppermute | solution.py:389
  70.9 36.7 %all-to-all-start.1 = ((bf16[32,32,256]{2,1,0:T(8,128)(2,1)}), bf16[32,32,256]{2,1,0:T(8,128)(2,1)S(1)}, u32[]{:S(2)}, u32[]{:S(2)}) async-start(bf16[32,32,256]{2,1,0:T(8,128)(2,1)} %bitcast.12), calls=%async_computation.1 | async-start | bytes 1048576 | tf_op jit(solution)/shard_map/all_to_all | solution.py:427
  80.6 29.3 %collective-permute-start.9 = (bf16[128,1024]{1,0:T(8,128)(2,1)S(1)}, bf16[128,1024]{1,0:T(8,128)(2,1)S(1)}, u32[]{:S(2)}, u32[]{:S(2)}) collective-permute-start(bf16[128,1024]{1,0:T(8,128)(2,1)S(1)} %get-tuple-element.55), channel_id=1, source_target_pairs={{0,1},{1,0},{2,3},{3,2},{4,5},{5,4},{6,7},{7,6},{8,9},{9,8},{10,11... | collective-permute-start | bytes 786440 | tf_op jit(solution)/shard_map/ppermute | solution.py:389
  85.0 20.9 %collective-permute-start.11 = (bf16[256,256]{1,0:T(8,128)(2,1)}, bf16[256,256]{1,0:T(8,128)(2,1)S(1)}, u32[]{:S(2)}, u32[]{:S(2)}) collective-permute-start(bf16[256,256]{1,0:T(8,128)(2,1)} %copy-done.6), channel_id=1, source_target_pairs={{2,0},{4,2},{6,4},{8,6},{10,8},{12,10},{14,12},{16,14},{18,16},{20... | collective-permute-start | bytes 393224 | tf_op jit(solution)/shard_map/ppermute | solution.py:381
  87.2 18.8 %collective-permute-start.12 = (bf16[128,256]{1,0:T(8,128)(2,1)S(1)}, bf16[128,256]{1,0:T(8,128)(2,1)S(1)}, u32[]{:S(2)}, u32[]{:S(2)}) collective-permute-start(bf16[128,256]{1,0:T(8,128)(2,1)S(1)} %get-tuple-element.60), channel_id=1, source_target_pairs={{4,0},{6,2},{8,4},{10,6},{12,8},{14,10},{16,12},{18,14},{20,16},{2... | collective-permute-start | bytes 196616 | tf_op jit(solution)/shard_map/ppermute | solution.py:381
  106.6 2.1 %collective-permute-start.13 = (bf16[128,256]{1,0:T(8,128)(2,1)S(1)}, bf16[128,256]{1,0:T(8,128)(2,1)S(1)}, u32[]{:S(2)}, u32[]{:S(2)}) collective-permute-start(bf16[128,256]{1,0:T(8,128)(2,1)S(1)} %get-tuple-element.62), channel_id=1, source_target_pairs={{0,1},{1,0},{2,3},{3,2},{4,5},{5,4},{6,7},{7,6},{8,9},{9,8},{10,11... | collective-permute-start | bytes 196616 | tf_op jit(solution)/shard_map/ppermute | solution.py:389
  107.5 2.4 %collective-permute-start.10 = (bf16[128,256]{1,0:T(8,128)(2,1)}, bf16[128,256]{1,0:T(8,128)(2,1)S(1)}, u32[]{:S(2)}, u32[]{:S(2)}) collective-permute-start(bf16[128,256]{1,0:T(8,128)(2,1)} %copy-done.7), channel_id=1, source_target_pairs={{0,1},{1,0},{2,3},{3,2},{4,5},{5,4},{6,7},{7,6},{8,9},{9,8},{10,11... | collective-permute-start | bytes 196616 | tf_op jit(solution)/shard_map/ppermute | solution.py:389
  108.2 3.1 %collective-permute-start.21 = (f32[16,256]{1,0:T(8,128)S(1)}, f32[16,256]{1,0:T(8,128)S(1)}, u32[]{:S(2)}, u32[]{:S(2)}) collective-permute-start(f32[16,256]{1,0:T(8,128)S(1)} %get-tuple-element.71), channel_id=1, source_target_pairs={{0,1},{1,0},{2,3},{3,2},{4,5},{5,4},{6,7},{7,6},{8,9},{9,8},{10,11... | collective-permute-start | bytes 49160 | tf_op jit(solution)/shard_map/ppermute | solution.py:389
  (8 other events, 30.4 us)

commit v4 on v3

--- a/solution.py
+++ b/solution.py
@@ -61,25 +61,32 @@
     out_ref[pl.ds(pl.multiple_of((1 - core) * ROWS, ROWS), ROWS), :] = other[...]
 
 
-def pick_kernel(ids, k_own, k_other, v_own, v_other, key_ref, value_ref, last_ref):
-    put_rows(key_ref, ids[2], k_own, k_other)
-    put_rows(value_ref, ids[2], v_own, v_other)
-    last_ref[:, :HALF] = key_ref[ROWS:]
-    last_ref[:, HALF:] = value_ref[ROWS:]
-
-
-def pick_call(ids, *blocks):
+def pick_keys_kernel(ids, own, other, both_ref):
+    put_rows(both_ref, ids[2], own, other)
+
+
+def pick_values_kernel(ids, own, other, keys, both_ref, last_ref):
+    put_rows(both_ref, ids[2], own, other)
+    last_ref[:, :HALF] = keys[ROWS:]
+    last_ref[:, HALF:] = both_ref[ROWS:]
+
+
+def pick_call(ids, own, other, keys=None):
     half = pl.BlockSpec((ROWS, HALF), lambda i, ids: (0, ids[2]))
-    return pl.pallas_call(
-        pick_kernel,
-        grid_spec=pltpu.PrefetchScalarGridSpec(
-            num_scalar_prefetch=1, grid=(1,), in_specs=[half] * 4, out_specs=[WHOLE] * 3
-        ),
-        out_shape=[shape(2 * ROWS, HALF)] * 2 + [shape(ROWS, 2 * HALF)],
+    extra = [] if keys is None else [keys]
+    return pl.pallas_call(
+        pick_values_kernel if extra else pick_keys_kernel,
+        grid_spec=pltpu.PrefetchScalarGridSpec(
+            num_scalar_prefetch=1,
+            grid=(1,),
+            in_specs=[half] * 2 + [WHOLE] * len(extra),
+            out_specs=[WHOLE] * (1 + len(extra)),
+        ),
+        out_shape=[shape(2 * ROWS, HALF)] + [shape(ROWS, 2 * HALF)] * len(extra),
         compiler_params=PARAMS,
         cost_estimate=cost(0, 0.5),
-        name="pick_keys_and_values",
-    )(ids, *blocks)
+        name="pick_values" if extra else "pick_keys",
+    )(ids, own, other, *extra)
 
 
 def prepare_kernel(
@@ -127,7 +134,7 @@
     out[ROWS:] = s1[3 * ROWS :]
     far1[:ROWS] = (s0[ROWS : 2 * ROWS] + s1[:ROWS]).astype(BF16)
     far1[ROWS:] = (s0[2 * ROWS : 3 * ROWS] + s1[ROWS : 2 * ROWS]).astype(BF16)
-    far2[...] = s0[:ROWS].astype(BF16)
+    far2[...] = s0[:ROWS].astype(far2.dtype)
 
 
 def forward_kernel(bias, q_ref, g_ref, k2, k1, k0, prob_ref, own_ref, far1, far2):
@@ -200,8 +207,8 @@
 PROB_SPEC = pl.BlockSpec((1, 2, KEYS, WIDE), lambda j, *_: (j, 0, 0, 0))
 
 
-def term_shapes():
-    return [shape(2 * ROWS, HALF, dtype=F32), shape(2 * ROWS, HALF), shape(ROWS, HALF)]
+def term_shapes(last):
+    return [shape(2 * ROWS, HALF, dtype=F32), shape(2 * ROWS, HALF), shape(ROWS, HALF, dtype=last)]
 
 
 def forward_call(bias, queries, grads, keys):
@@ -212,7 +219,7 @@
         + [wide(2 * ROWS)] * 2
         + WINDOW,
         out_specs=[PROB_SPEC] + TERMS,
-        out_shape=[shape(GROUPS, 2, KEYS, WIDE)] + term_shapes(),
+        out_shape=[shape(GROUPS, 2, KEYS, WIDE)] + term_shapes(F32),
         compiler_params=LARGE,
         cost_estimate=cost(4 * 16 * ROWS * KEYS * HEAD, 6),
         name="forward_and_value_gradient",
@@ -229,7 +236,7 @@
             out_specs=[wide(ROWS)] * 2 + TERMS,
             scratch_shapes=[pltpu.VMEM((2, ROWS, WIDE), BF16)],
         ),
-        out_shape=[shape(ROWS, GROUPS * WIDE)] * 2 + term_shapes(),
+        out_shape=[shape(ROWS, GROUPS * WIDE)] * 2 + term_shapes(BF16),
         compiler_params=LARGE,
         cost_estimate=cost(6 * 16 * ROWS * KEYS * HEAD, 6),
         name="query_and_key_gradient",
@@ -394,9 +401,13 @@
     core = lax.axis_index("c")
     ids = jnp.stack([lax.axis_index(CTX), lax.axis_index("x"), core]).astype(jnp.int32)
 
-    key0, value0, last = pick_call(ids, key, swap_core(key), value, swap_core(value))
+    key_other, value = lax.optimization_barrier((swap_core(key), value))
+    (key0,) = pick_call(ids, key, key_other)
+    key0, query, grad, value = lax.optimization_barrier((key0, query, grad, value))
+    key1 = shift_chips(key0, 1)
+    value0, last = pick_call(ids, value, swap_core(value), key0)
     far2 = shift_chips(last, 2)
-    keys = [far2, shift_chips(key0, 1), key0]
+    keys = [far2, key1, key0]
     bias, queries, grads = prepare_call(
         ids,
         stretch_order.reshape(-1),
@@ -407,12 +418,11 @@
         swap_core(grad),
     )
     bias, value0 = lax.optimization_barrier((bias, value0))
-    value1 = shift_chips(value0, 1)
+    values = [far2, shift_chips(value0, 1), value0]
 
     prob, value_own, value_t1, value_t2 = forward_call(bias, queries, grads, keys)
     value_r2 = shift_chips(value_t2, -2)
     value_r1 = shift_chips(value_t1, -1)
-    values = [far2, value1, value0]
     query_keep, query_send, key_own, key_t1, key_t2 = backward_call(
         ids, prob, queries, grads, keys, values
     )
@@ -422,23 +432,25 @@
     other = [swap_core(block) for block in own]
     value_r1, query_send = lax.optimization_barrier((value_r1, query_send))
     value_keep, value_send, sent = total_call(ids, value_own, value_r1, value_r2, True)
-    gathered = lax.all_to_all(sent, "x", 0, 0, tiled=True)
-    partial = weight_call(ids, gathered, own, other).reshape(32, 32, HALF)
-    partial = lax.all_to_all(partial, ("zl", "zh", "y"), 0, 0, tiled=True)
-
     key_r2 = shift_chips(key_t2, -2)
     key_r1 = shift_chips(key_t1, -1)
+    gathered = lax.all_to_all(sent, "x", 0, 0, tiled=True)
+    partial = weight_call(ids, gathered, own, other)
+    partial, key_r1, key_r2 = lax.optimization_barrier((partial, key_r1, key_r2))
+    partial = lax.all_to_all(partial.reshape(32, 32, HALF), ("zl", "zh", "y"), 0, 0, tiled=True)
+
     key_keep, key_send = total_call(ids, key_own, key_r1, key_r2, False)
-    grad_query, grad_value = join_call(
+    grad_query, grad_key, grad_value = join_call(
         ids,
-        [query_keep, value_keep],
-        [swap_core(query_send), swap_core(value_send)],
-        "join_query_and_value",
+        [query_keep, key_keep, value_keep],
+        [swap_core(query_send), swap_core(key_send), swap_core(value_send)],
+        "join_outputs",
     )
-    (grad_key,) = join_call(ids, [key_keep], [swap_core(key_send)], "join_key")
-
+    partial, grad_query = lax.optimization_barrier((partial, grad_query))
     row_keep, row_send = final_call(ids, partial)
-    (weight_grad,) = join_call(ids, [row_keep], [swap_core(row_send)], "join_weight")
+    swapped = swap_core(row_send)
+    first, second = jnp.where(core == 0, row_keep, swapped), jnp.where(core == 0, swapped, row_keep)
+    weight_grad = jnp.concatenate([first, second], axis=1)
     return grad_query[None], grad_key[None], grad_value[None], weight_grad
 
 

time: 113 us -> 108 us (0.956)
  the two profiles are of different devices: /device:TPU:55 before, /device:TPU:7 now
where the time goes in v4:
time: 108 us; the launch traced here: 107 us
  starting transfers between devices  62.9 us (58%)
  waiting for transfers between devices  20.5 us (19%)
  Pallas kernels  16.9 us (16%)
  local copies, waits for them, and re-layouts  5.46 us (5%)
    ppermute x7, starting transfers between devices, shift_chips(): return lax.ppermute(block, CHIP, route)  25.7 us
    all_to_all x1, starting transfers between devices, shards(): lax.all_to_all(partial.reshape(32, 32, HALF), ('zl', 'zh', 'y'), 0, 0, ti...  16.1 us
    ppermute x12, starting transfers between devices, swap_core(): return lax.ppermute(block, 'c', [(0, 1), (1, 0)])  13.6 us
    all_to_all x1, waiting for transfers between devices, shards(): lax.all_to_all(partial.reshape(32, 32, HALF), ('zl', 'zh', 'y'), 0, 0, ti...  9.99 us
    ppermute x3, waiting for transfers between devices, shift_x(): return lax.ppermute(block, 'x', [(i, (i + distance) % 4) for i in range(4)])  7.59 us
    all_to_all x1, starting transfers between devices, shards(): gathered = lax.all_to_all(sent, 'x', 0, 0, tiled=True)  5.84 us
    unnamed x19, local copies, waits for them, and re-layouts  5.33 us
    pallas_call x1, Pallas kernels, backward_call(): pl.pallas_call(backward_kernel, grid_spec=pltpu.PrefetchScalarGridSpec(nu...  3.73 us
  transfers between devices with their start and end apart: 24, of which 7 were waited for; matrix products, arithmetic and copies ran while one was open for 1% of the time, Pallas kernels for 15%

profile of v4, /device:TPU:7, one launch (start us, length us, event | category | flops | bytes accessed | tf_op | source)
XLA Modules:
  0.0 107.3 jit_solution(18415614159381375303)
XLA Ops:
  1.5 1.1 %collective-permute-done.other = bf16[128,512]{1,0:T(8,128)(2,1)S(1)} collective-permute-done((bf16[128,512]{1,0:T(8,128)(2,1)}, bf16[128,512]{1,0:T(8,128)(2,1)S(1)}, u32[]{:S(2)}, u32[]{:S(2)}) %collective-permute-start) | collective-permute-done | bytes 131104 | tf_op jit(solution)/shard_map/ppermute | solution.py:396
  5.0 3.2 %collective-permute-start.5 = (bf16[256,256]{1,0:T(8,128)(2,1)S(1)}, bf16[256,256]{1,0:T(8,128)(2,1)S(1)}, u32[]{:S(2)}, u32[]{:S(2)}) collective-permute-start(bf16[256,256]{1,0:T(8,128)(2,1)S(1)} %pick_keys.1.keys.k0), channel_id=1, source_target_pairs={{0,2},{2,4},{4,6},{6,8},{8,10},{10,12},{12,14},{14,16},{16,18},{18... | collective-permute-start | bytes 393224 | tf_op jit(solution)/shard_map/ppermute | solution.py:388
  9.7 4.5 %collective-permute-start.4 = (bf16[128,512]{1,0:T(8,128)(2,1)S(1)}, bf16[128,512]{1,0:T(8,128)(2,1)S(1)}, u32[]{:S(2)}, u32[]{:S(2)}) collective-permute-start(bf16[128,512]{1,0:T(8,128)(2,1)S(1)} %get-tuple-element.60), channel_id=1, source_target_pairs={{0,4},{2,6},{4,8},{6,10},{8,12},{10,14},{12,16},{14,18},{16,20},{1... | collective-permute-start | bytes 393224 | tf_op jit(solution)/shard_map/ppermute | solution.py:388
  16.2 1.0 copy-done.2
  18.7 7.8 %collective-permute-start.7 = (bf16[256,256]{1,0:T(8,128)(2,1)S(1)}, bf16[256,256]{1,0:T(8,128)(2,1)S(1)}, u32[]{:S(2)}, u32[]{:S(2)}) collective-permute-start(bf16[256,256]{1,0:T(8,128)(2,1)S(1)} %get-tuple-element.64.v0), channel_id=1, source_target_pairs={{0,2},{2,4},{4,6},{6,8},{8,10},{10,12},{12,14},{14,16},{16,18},{18... | collective-permute-start | bytes 393224 | tf_op jit(solution)/shard_map/ppermute | solution.py:388
  26.5 3.2 %forward_and_value_gradient.1 = (bf16[2,2,512,512]{3,2,1,0:T(8,128)(2,1)S(1)}, f32[256,256]{1,0:T(8,128)S(1)}, bf16[256,256]{1,0:T(8,128)(2,1)S(1)}, f32[128,256]{1,0:T(8,128)S(1)}) custom-call(f32[2,512,128]{2,1,0:T(8,128)S(1)} %get-tuple-element.57.bias, bf16[256,1024]{1,0:T(8,128)(2,1)S(1)} %get-tuple-element.58.q_ref, ...), custom_call_target="tpu_custom_call" | custom-call | flops 536870912 | bytes 6291456 | tf_op jit(solution)/shard_map/forward_and_value_gradient/pallas_call | solution.py:215
  29.7 2.1 %collective-permute-start.6 = (bf16[256,256]{1,0:T(8,128)(2,1)S(1)}, bf16[256,256]{1,0:T(8,128)(2,1)S(1)}, u32[]{:S(2)}, u32[]{:S(2)}) collective-permute-start(bf16[256,256]{1,0:T(8,128)(2,1)S(1)} %get-tuple-element.62), channel_id=1, source_target_pairs={{2,0},{4,2},{6,4},{8,6},{10,8},{12,10},{14,12},{16,14},{18,16},{20... | collective-permute-start | bytes 393224 | tf_op jit(solution)/shard_map/ppermute | solution.py:388
  31.7 1.9 %collective-permute-start.8 = (f32[128,256]{1,0:T(8,128)S(1)}, f32[128,256]{1,0:T(8,128)S(1)}, u32[]{:S(2)}, u32[]{:S(2)}) collective-permute-start(f32[128,256]{1,0:T(8,128)S(1)} %get-tuple-element.68), channel_id=1, source_target_pairs={{4,0},{6,2},{8,4},{10,6},{12,8},{14,10},{16,12},{18,14},{20,16},{2... | collective-permute-start | bytes 393224 | tf_op jit(solution)/shard_map/ppermute | solution.py:388
  33.7 3.7 %query_and_key_gradient.1 = (bf16[128,1024]{1,0:T(8,128)(2,1)S(1)}, bf16[128,1024]{1,0:T(8,128)(2,1)S(1)}, f32[256,256]{1,0:T(8,128)S(1)}, bf16[256,256]{1,0:T(8,128)(2,1)S(1)}, bf16[128,256]{1,0:T(8,128)(2,1)S(1)}) custom-call(s32[3]{0:T(128)S(1)} %pad_add_fusion.ids, bf16[2,2,512,512]{3,2,1,0:T(8,128)(2,1)S(1)} %get-tuple-element.63.prob_ref, ...), custom_call_target="tpu_custom_call" | custom-call | flops 805306368 | bytes 6291456 | tf_op jit(solution)/shard_map/query_and_key_gradient/pallas_call | solution.py:230
  38.5 1.4 %collective-permute-start.11 = (bf16[128,1024]{1,0:T(8,128)(2,1)S(1)}, bf16[128,1024]{1,0:T(8,128)(2,1)S(1)}, u32[]{:S(2)}, u32[]{:S(2)}) collective-permute-start(bf16[128,1024]{1,0:T(8,128)(2,1)S(1)} %get-tuple-element.74), channel_id=1, source_target_pairs={{0,24},{8,0},{16,8},{24,16},{1,25},{9,1},{17,9},{25,17},{2,26},{10... | collective-permute-start | bytes 786440 | tf_op jit(solution)/shard_map/ppermute | solution.py:392
  39.8 1.4 %value_gradient_total.1 = (bf16[128,256]{1,0:T(8,128)(2,1)S(1)}, bf16[128,256]{1,0:T(8,128)(2,1)S(1)}, bf16[4,256,256]{2,1,0:T(8,128)(2,1)}) custom-call(s32[3]{0:T(128)S(1)} %pad_add_fusion.ids, f32[256,256]{1,0:T(8,128)S(1)} %get-tuple-element.61.own, bf16[256,256]{1,0:T(8,128)(2,1)S(1)} %collective-permute-done.6.r1, f32[128,256]{1,0:T(8,128)S(1)} %collective-permute-done.8.r2), custom_call_target="tpu_custom_call" | custom-call | bytes 1048576 | tf_op jit(solution)/shard_map/value_gradient_total/pallas_call | solution.py:290
  41.2 5.8 %all-to-all-start = ((bf16[4,256,256]{2,1,0:T(8,128)(2,1)}), bf16[4,256,256]{2,1,0:T(8,128)(2,1)S(1)}, u32[]{:S(2)}, u32[]{:S(2)}) async-start(bf16[4,256,256]{2,1,0:T(8,128)(2,1)} %get-tuple-element.69), calls=%async_computation | async-start | bytes 1048576 | tf_op jit(solution)/shard_map/all_to_all | solution.py:437
  47.1 1.8 %collective-permute-start.12 = (bf16[128,1024]{1,0:T(8,128)(2,1)S(1)}, bf16[128,1024]{1,0:T(8,128)(2,1)S(1)}, u32[]{:S(2)}, u32[]{:S(2)}) collective-permute-start(bf16[128,1024]{1,0:T(8,128)(2,1)S(1)} %get-tuple-element.71.a0), channel_id=1, source_target_pairs={{0,1},{1,0},{2,3},{3,2},{4,5},{5,4},{6,7},{7,6},{8,9},{9,8},{10,11... | collective-permute-start | bytes 786440 | tf_op jit(solution)/shard_map/ppermute | solution.py:396
  49.0 3.0 %collective-permute-done.10.a2 = bf16[128,1024]{1,0:T(8,128)(2,1)S(1)} collective-permute-done((bf16[128,1024]{1,0:T(8,128)(2,1)S(1)}, bf16[128,1024]{1,0:T(8,128)(2,1)S(1)}, u32[]{:S(2)}, u32[]{:S(2)}) %collective-permute-start.10) | collective-permute-done | bytes 262176 | tf_op jit(solution)/shard_map/ppermute | solution.py:392
  52.0 2.8 %collective-permute-start.14 = (bf16[128,1024]{1,0:T(8,128)(2,1)S(1)}, bf16[128,1024]{1,0:T(8,128)(2,1)S(1)}, u32[]{:S(2)}, u32[]{:S(2)}) collective-permute-start(bf16[128,1024]{1,0:T(8,128)(2,1)S(1)} %collective-permute-done.10.a2), channel_id=1, source_target_pairs={{0,1},{1,0},{2,3},{3,2},{4,5},{5,4},{6,7},{7,6},{8,9},{9,8},{10,11... | collective-permute-start | bytes 786440 | tf_op jit(solution)/shard_map/ppermute | solution.py:396
  54.8 4.6 %collective-permute-done.11.a3 = bf16[128,1024]{1,0:T(8,128)(2,1)S(1)} collective-permute-done((bf16[128,1024]{1,0:T(8,128)(2,1)S(1)}, bf16[128,1024]{1,0:T(8,128)(2,1)S(1)}, u32[]{:S(2)}, u32[]{:S(2)}) %collective-permute-start.11) | collective-permute-done | bytes 262176 | tf_op jit(solution)/shard_map/ppermute | solution.py:392
  60.0 2.1 %collective-permute-start.16 = (bf16[256,256]{1,0:T(8,128)(2,1)S(1)}, bf16[256,256]{1,0:T(8,128)(2,1)S(1)}, u32[]{:S(2)}, u32[]{:S(2)}) collective-permute-start(bf16[256,256]{1,0:T(8,128)(2,1)S(1)} %get-tuple-element.75), channel_id=1, source_target_pairs={{2,0},{4,2},{6,4},{8,6},{10,8},{12,10},{14,12},{16,14},{18,16},{20... | collective-permute-start | bytes 393224 | tf_op jit(solution)/shard_map/ppermute | solution.py:388
  62.2 4.1 %collective-permute-start.17 = (bf16[128,256]{1,0:T(8,128)(2,1)}, bf16[128,256]{1,0:T(8,128)(2,1)S(1)}, u32[]{:S(2)}, u32[]{:S(2)}) collective-permute-start(bf16[128,256]{1,0:T(8,128)(2,1)} %copy-done.7), channel_id=1, source_target_pairs={{4,0},{6,2},{8,4},{10,6},{12,8},{14,10},{16,12},{18,14},{20,16},{2... | collective-permute-start | bytes 196616 | tf_op jit(solution)/shard_map/ppermute | solution.py:388
  66.3 3.3 %weight_gradient.1 = bf16[1024,256]{1,0:T(8,128)(2,1)} custom-call(s32[3]{0:T(128)S(1)} %pad_add_fusion.ids, bf16[4,256,256]{2,1,0:T(8,128)(2,1)S(1)} %all-to-all-done.grads, bf16[128,1024]{1,0:T(8,128)(2,1)S(1)} %get-tuple-element.71.a0, bf16[128,1024]{1,0:T(8,128)(2,1)S(1)} %collective-permute-done.9.a1, bf16[128,1024]{1,0:T(8,128)(2,1)S(1)} %collective-permute-done.10.a2, ...), custom_call_target="tpu_custom_call" | custom-call | flops 536870912 | bytes 3145728 | tf_op jit(solution)/shard_map/weight_gradient/pallas_call | solution.py:344
  69.6 16.1 %all-to-all-start.1 = ((bf16[32,32,256]{2,1,0:T(8,128)(2,1)}), bf16[32,32,256]{2,1,0:T(8,128)(2,1)S(1)}, u32[]{:S(2)}, u32[]{:S(2)}) async-start(bf16[32,32,256]{2,1,0:T(8,128)(2,1)} %bitcast.9), calls=%async_computation.1 | async-start | bytes 1048576 | tf_op jit(solution)/shard_map/all_to_all | solution.py:440
  85.7 2.0 %collective-permute-start.18 = (bf16[128,1024]{1,0:T(8,128)(2,1)}, bf16[128,1024]{1,0:T(8,128)(2,1)S(1)}, u32[]{:S(2)}, u32[]{:S(2)}) collective-permute-start(bf16[128,1024]{1,0:T(8,128)(2,1)} %copy-done.6), channel_id=1, source_target_pairs={{0,1},{1,0},{2,3},{3,2},{4,5},{5,4},{6,7},{7,6},{8,9},{9,8},{10,11... | collective-permute-start | bytes 786440 | tf_op jit(solution)/shard_map/ppermute | solution.py:396
  89.8 1.5 %join_outputs.1 = (bf16[128,2048]{1,0:T(8,128)(2,1)}, bf16[128,512]{1,0:T(8,128)(2,1)}, bf16[128,512]{1,0:T(8,128)(2,1)}) custom-call(s32[3]{0:T(128)S(1)} %pad_add_fusion.ids, bf16[128,1024]{1,0:T(8,128)(2,1)S(1)} %get-tuple-element.78.refs_0_, bf16[128,256]{1,0:T(8,128)(2,1)S(1)} %get-tuple-element.82.refs_1_, ...), custom_call_target="tpu_custom_call" | custom-call | bytes 524288 | tf_op jit(solution)/shard_map/join_outputs/pallas_call | solution.py:316
  91.2 10.0 %all-to-all-done.1.in_ref = bf16[32,32,256]{2,1,0:T(8,128)(2,1)S(1)} async-done(((bf16[32,32,256]{2,1,0:T(8,128)(2,1)}), bf16[32,32,256]{2,1,0:T(8,128)(2,1)S(1)}, u32[]{:S(2)}, u32[]{:S(2)}) %all-to-all-start.1) | async-done | bytes 524320 | tf_op jit(solution)/shard_map/all_to_all | solution.py:440
  101.8 4.0 %collective-permute-start.21 = (f32[16,256]{1,0:T(8,128)S(1)}, f32[16,256]{1,0:T(8,128)S(1)}, u32[]{:S(2)}, u32[]{:S(2)}) collective-permute-start(f32[16,256]{1,0:T(8,128)S(1)} %get-tuple-element.93), channel_id=1, source_target_pairs={{0,1},{1,0},{2,3},{3,2},{4,5},{5,4},{6,7},{7,6},{8,9},{9,8},{10,11... | collective-permute-start | bytes 49160 | tf_op jit(solution)/shard_map/ppermute | solution.py:396
  (58 shorter events, 14.0 us)
Async XLA Ops:
  0.6 2.0 %collective-permute-start = (bf16[128,512]{1,0:T(8,128)(2,1)}, bf16[128,512]{1,0:T(8,128)(2,1)S(1)}, u32[]{:S(2)}, u32[]{:S(2)}) collective-permute-start(bf16[128,512]{1,0:T(8,128)(2,1)} %bitcast.18), channel_id=1, source_target_pairs={{0,1},{1,0},{2,3},{3,2},{4,5},{5,4},{6,7},{7,6},{8,9},{9,8},{10,11... | collective-permute-start | bytes 393224 | tf_op jit(solution)/shard_map/ppermute | solution.py:396
  4.1 11.1 %collective-permute-start.1 = (bf16[128,2048]{1,0:T(8,128)(2,1)}, bf16[128,2048]{1,0:T(8,128)(2,1)S(1)}, u32[]{:S(2)}, u32[]{:S(2)}) collective-permute-start(bf16[128,2048]{1,0:T(8,128)(2,1)} %bitcast.14), channel_id=1, source_target_pairs={{0,1},{1,0},{2,3},{3,2},{4,5},{5,4},{6,7},{7,6},{8,9},{9,8},{10,11... | collective-permute-start | bytes 1572872 | tf_op jit(solution)/shard_map/ppermute | solution.py:396
  4.5 10.7 %collective-permute-start.2 = (bf16[128,2048]{1,0:T(8,128)(2,1)}, bf16[128,2048]{1,0:T(8,128)(2,1)S(1)}, u32[]{:S(2)}, u32[]{:S(2)}) collective-permute-start(bf16[128,2048]{1,0:T(8,128)(2,1)} %bitcast.16), channel_id=1, source_target_pairs={{0,1},{1,0},{2,3},{3,2},{4,5},{5,4},{6,7},{7,6},{8,9},{9,8},{10,11... | collective-permute-start | bytes 1572872 | tf_op jit(solution)/shard_map/ppermute | solution.py:396
  4.7 3.6 %collective-permute-start.3 = (bf16[128,512]{1,0:T(8,128)(2,1)}, bf16[128,512]{1,0:T(8,128)(2,1)S(1)}, u32[]{:S(2)}, u32[]{:S(2)}) collective-permute-start(bf16[128,512]{1,0:T(8,128)(2,1)} %bitcast.20), channel_id=1, source_target_pairs={{0,1},{1,0},{2,3},{3,2},{4,5},{5,4},{6,7},{7,6},{8,9},{9,8},{10,11... | collective-permute-start | bytes 393224 | tf_op jit(solution)/shard_map/ppermute | solution.py:396
  5.0 21.4 %collective-permute-start.5 = (bf16[256,256]{1,0:T(8,128)(2,1)S(1)}, bf16[256,256]{1,0:T(8,128)(2,1)S(1)}, u32[]{:S(2)}, u32[]{:S(2)}) collective-permute-start(bf16[256,256]{1,0:T(8,128)(2,1)S(1)} %pick_keys.1.keys.k0), channel_id=1, source_target_pairs={{0,2},{2,4},{4,6},{6,8},{8,10},{10,12},{12,14},{14,16},{16,18},{18... | collective-permute-start | bytes 393224 | tf_op jit(solution)/shard_map/ppermute | solution.py:388
  9.7 16.8 %collective-permute-start.4 = (bf16[128,512]{1,0:T(8,128)(2,1)S(1)}, bf16[128,512]{1,0:T(8,128)(2,1)S(1)}, u32[]{:S(2)}, u32[]{:S(2)}) collective-permute-start(bf16[128,512]{1,0:T(8,128)(2,1)S(1)} %get-tuple-element.60), channel_id=1, source_target_pairs={{0,4},{2,6},{4,8},{6,10},{8,12},{10,14},{12,16},{14,18},{16,20},{1... | collective-permute-start | bytes 393224 | tf_op jit(solution)/shard_map/ppermute | solution.py:388
  18.7 15.0 %collective-permute-start.7 = (bf16[256,256]{1,0:T(8,128)(2,1)S(1)}, bf16[256,256]{1,0:T(8,128)(2,1)S(1)}, u32[]{:S(2)}, u32[]{:S(2)}) collective-permute-start(bf16[256,256]{1,0:T(8,128)(2,1)S(1)} %get-tuple-element.64.v0), channel_id=1, source_target_pairs={{0,2},{2,4},{4,6},{6,8},{8,10},{10,12},{12,14},{14,16},{16,18},{18... | collective-permute-start | bytes 393224 | tf_op jit(solution)/shard_map/ppermute | solution.py:388
  29.7 10.2 %collective-permute-start.6 = (bf16[256,256]{1,0:T(8,128)(2,1)S(1)}, bf16[256,256]{1,0:T(8,128)(2,1)S(1)}, u32[]{:S(2)}, u32[]{:S(2)}) collective-permute-start(bf16[256,256]{1,0:T(8,128)(2,1)S(1)} %get-tuple-element.62), channel_id=1, source_target_pairs={{2,0},{4,2},{6,4},{8,6},{10,8},{12,10},{14,12},{16,14},{18,16},{20... | collective-permute-start | bytes 393224 | tf_op jit(solution)/shard_map/ppermute | solution.py:388
  31.7 8.1 %collective-permute-start.8 = (f32[128,256]{1,0:T(8,128)S(1)}, f32[128,256]{1,0:T(8,128)S(1)}, u32[]{:S(2)}, u32[]{:S(2)}) collective-permute-start(f32[128,256]{1,0:T(8,128)S(1)} %get-tuple-element.68), channel_id=1, source_target_pairs={{4,0},{6,2},{8,4},{10,6},{12,8},{14,10},{16,12},{18,14},{20,16},{2... | collective-permute-start | bytes 393224 | tf_op jit(solution)/shard_map/ppermute | solution.py:388
  38.3 10.6 %collective-permute-start.9 = (bf16[128,1024]{1,0:T(8,128)(2,1)S(1)}, bf16[128,1024]{1,0:T(8,128)(2,1)S(1)}, u32[]{:S(2)}, u32[]{:S(2)}) collective-permute-start(bf16[128,1024]{1,0:T(8,128)(2,1)S(1)} %get-tuple-element.72), channel_id=1, source_target_pairs={{0,8},{8,16},{16,24},{24,0},{1,9},{9,17},{17,25},{25,1},{2,10},{10... | collective-permute-start | bytes 786440 | tf_op jit(solution)/shard_map/ppermute | solution.py:392
  38.4 13.6 %collective-permute-start.10 = (bf16[128,1024]{1,0:T(8,128)(2,1)S(1)}, bf16[128,1024]{1,0:T(8,128)(2,1)S(1)}, u32[]{:S(2)}, u32[]{:S(2)}) collective-permute-start(bf16[128,1024]{1,0:T(8,128)(2,1)S(1)} %get-tuple-element.73), channel_id=1, source_target_pairs={{0,16},{8,24},{16,0},{24,8},{1,17},{9,25},{17,1},{25,9},{2,18},{10... | collective-permute-start | bytes 786440 | tf_op jit(solution)/shard_map/ppermute | solution.py:392
  38.5 21.0 %collective-permute-start.11 = (bf16[128,1024]{1,0:T(8,128)(2,1)S(1)}, bf16[128,1024]{1,0:T(8,128)(2,1)S(1)}, u32[]{:S(2)}, u32[]{:S(2)}) collective-permute-start(bf16[128,1024]{1,0:T(8,128)(2,1)S(1)} %get-tuple-element.74), channel_id=1, source_target_pairs={{0,24},{8,0},{16,8},{24,16},{1,25},{9,1},{17,9},{25,17},{2,26},{10... | collective-permute-start | bytes 786440 | tf_op jit(solution)/shard_map/ppermute | solution.py:392
  41.2 25.1 %all-to-all-start = ((bf16[4,256,256]{2,1,0:T(8,128)(2,1)}), bf16[4,256,256]{2,1,0:T(8,128)(2,1)S(1)}, u32[]{:S(2)}, u32[]{:S(2)}) async-start(bf16[4,256,256]{2,1,0:T(8,128)(2,1)} %get-tuple-element.69), calls=%async_computation | async-start | bytes 1048576 | tf_op jit(solution)/shard_map/all_to_all | solution.py:437
  47.1 15.1 %collective-permute-start.12 = (bf16[128,1024]{1,0:T(8,128)(2,1)S(1)}, bf16[128,1024]{1,0:T(8,128)(2,1)S(1)}, u32[]{:S(2)}, u32[]{:S(2)}) collective-permute-start(bf16[128,1024]{1,0:T(8,128)(2,1)S(1)} %get-tuple-element.71.a0), channel_id=1, source_target_pairs={{0,1},{1,0},{2,3},{3,2},{4,5},{5,4},{6,7},{7,6},{8,9},{9,8},{10,11... | collective-permute-start | bytes 786440 | tf_op jit(solution)/shard_map/ppermute | solution.py:396
  48.9 17.4 %collective-permute-start.13 = (bf16[128,1024]{1,0:T(8,128)(2,1)S(1)}, bf16[128,1024]{1,0:T(8,128)(2,1)S(1)}, u32[]{:S(2)}, u32[]{:S(2)}) collective-permute-start(bf16[128,1024]{1,0:T(8,128)(2,1)S(1)} %collective-permute-done.9.a1), channel_id=1, source_target_pairs={{0,1},{1,0},{2,3},{3,2},{4,5},{5,4},{6,7},{7,6},{8,9},{9,8},{10,11... | collective-permute-start | bytes 786440 | tf_op jit(solution)/shard_map/ppermute | solution.py:396
  52.0 14.3 %collective-permute-start.14 = (bf16[128,1024]{1,0:T(8,128)(2,1)S(1)}, bf16[128,1024]{1,0:T(8,128)(2,1)S(1)}, u32[]{:S(2)}, u32[]{:S(2)}) collective-permute-start(bf16[128,1024]{1,0:T(8,128)(2,1)S(1)} %collective-permute-done.10.a2), channel_id=1, source_target_pairs={{0,1},{1,0},{2,3},{3,2},{4,5},{5,4},{6,7},{7,6},{8,9},{9,8},{10,11... | collective-permute-start | bytes 786440 | tf_op jit(solution)/shard_map/ppermute | solution.py:396
  59.4 6.9 %collective-permute-start.15 = (bf16[128,1024]{1,0:T(8,128)(2,1)S(1)}, bf16[128,1024]{1,0:T(8,128)(2,1)S(1)}, u32[]{:S(2)}, u32[]{:S(2)}) collective-permute-start(bf16[128,1024]{1,0:T(8,128)(2,1)S(1)} %collective-permute-done.11.a3), channel_id=1, source_target_pairs={{0,1},{1,0},{2,3},{3,2},{4,5},{5,4},{6,7},{7,6},{8,9},{9,8},{10,11... | collective-permute-start | bytes 786440 | tf_op jit(solution)/shard_map/ppermute | solution.py:396
  60.0 9.6 %collective-permute-start.16 = (bf16[256,256]{1,0:T(8,128)(2,1)S(1)}, bf16[256,256]{1,0:T(8,128)(2,1)S(1)}, u32[]{:S(2)}, u32[]{:S(2)}) collective-permute-start(bf16[256,256]{1,0:T(8,128)(2,1)S(1)} %get-tuple-element.75), channel_id=1, source_target_pairs={{2,0},{4,2},{6,4},{8,6},{10,8},{12,10},{14,12},{16,14},{18,16},{20... | collective-permute-start | bytes 393224 | tf_op jit(solution)/shard_map/ppermute | solution.py:388
  62.2 7.4 %collective-permute-start.17 = (bf16[128,256]{1,0:T(8,128)(2,1)}, bf16[128,256]{1,0:T(8,128)(2,1)S(1)}, u32[]{:S(2)}, u32[]{:S(2)}) collective-permute-start(bf16[128,256]{1,0:T(8,128)(2,1)} %copy-done.7), channel_id=1, source_target_pairs={{4,0},{6,2},{8,4},{10,6},{12,8},{14,10},{16,12},{18,14},{20,16},{2... | collective-permute-start | bytes 196616 | tf_op jit(solution)/shard_map/ppermute | solution.py:388
  69.6 31.6 %all-to-all-start.1 = ((bf16[32,32,256]{2,1,0:T(8,128)(2,1)}), bf16[32,32,256]{2,1,0:T(8,128)(2,1)S(1)}, u32[]{:S(2)}, u32[]{:S(2)}) async-start(bf16[32,32,256]{2,1,0:T(8,128)(2,1)} %bitcast.9), calls=%async_computation.1 | async-start | bytes 1048576 | tf_op jit(solution)/shard_map/all_to_all | solution.py:440
  85.7 3.5 %collective-permute-start.18 = (bf16[128,1024]{1,0:T(8,128)(2,1)}, bf16[128,1024]{1,0:T(8,128)(2,1)S(1)}, u32[]{:S(2)}, u32[]{:S(2)}) collective-permute-start(bf16[128,1024]{1,0:T(8,128)(2,1)} %copy-done.6), channel_id=1, source_target_pairs={{0,1},{1,0},{2,3},{3,2},{4,5},{5,4},{6,7},{7,6},{8,9},{9,8},{10,11... | collective-permute-start | bytes 786440 | tf_op jit(solution)/shard_map/ppermute | solution.py:396
  87.7 1.5 %collective-permute-start.20 = (bf16[128,256]{1,0:T(8,128)(2,1)}, bf16[128,256]{1,0:T(8,128)(2,1)S(1)}, u32[]{:S(2)}, u32[]{:S(2)}) collective-permute-start(bf16[128,256]{1,0:T(8,128)(2,1)} %copy-done.8), channel_id=1, source_target_pairs={{0,1},{1,0},{2,3},{3,2},{4,5},{5,4},{6,7},{7,6},{8,9},{9,8},{10,11... | collective-permute-start | bytes 196616 | tf_op jit(solution)/shard_map/ppermute | solution.py:396
  88.4 1.4 %collective-permute-start.19 = (bf16[128,256]{1,0:T(8,128)(2,1)S(1)}, bf16[128,256]{1,0:T(8,128)(2,1)S(1)}, u32[]{:S(2)}, u32[]{:S(2)}) collective-permute-start(bf16[128,256]{1,0:T(8,128)(2,1)S(1)} %get-tuple-element.85), channel_id=1, source_target_pairs={{0,1},{1,0},{2,3},{3,2},{4,5},{5,4},{6,7},{7,6},{8,9},{9,8},{10,11... | collective-permute-start | bytes 196616 | tf_op jit(solution)/shard_map/ppermute | solution.py:396
  101.8 4.8 %collective-permute-start.21 = (f32[16,256]{1,0:T(8,128)S(1)}, f32[16,256]{1,0:T(8,128)S(1)}, u32[]{:S(2)}, u32[]{:S(2)}) collective-permute-start(f32[16,256]{1,0:T(8,128)S(1)} %get-tuple-element.93), channel_id=1, source_target_pairs={{0,1},{1,0},{2,3},{3,2},{4,5},{5,4},{6,7},{7,6},{8,9},{9,8},{10,11... | collective-permute-start | bytes 49160 | tf_op jit(solution)/shard_map/ppermute | solution.py:396
  (9 other events, 24.7 us)

commit v5 on v4

--- a/solution.py
+++ b/solution.py
@@ -219,7 +219,7 @@
         + [wide(2 * ROWS)] * 2
         + WINDOW,
         out_specs=[PROB_SPEC] + TERMS,
-        out_shape=[shape(GROUPS, 2, KEYS, WIDE)] + term_shapes(F32),
+        out_shape=[shape(GROUPS, 2, KEYS, WIDE)] + term_shapes(BF16),
         compiler_params=LARGE,
         cost_estimate=cost(4 * 16 * ROWS * KEYS * HEAD, 6),
         name="forward_and_value_gradient",
@@ -417,19 +417,22 @@
         grad,
         swap_core(grad),
     )
-    bias, value0 = lax.optimization_barrier((bias, value0))
-    values = [far2, shift_chips(value0, 1), value0]
+
+    bias, inputs = lax.optimization_barrier((bias, inputs))
+    packed = pack_call(ids, inputs)
+    own = [packed[0]] + [shift_x(packed[d], d) for d in range(1, 4)]
 
     prob, value_own, value_t1, value_t2 = forward_call(bias, queries, grads, keys)
     value_r2 = shift_chips(value_t2, -2)
     value_r1 = shift_chips(value_t1, -1)
+    value_own, value0 = lax.optimization_barrier((value_own, value0))
+    values = [far2, shift_chips(value0, 1), value0]
+    prob, *far = lax.optimization_barrier((prob, *own[1:]))
+    own = [own[0]] + far
+    other = [swap_core(block) for block in own]
     query_keep, query_send, key_own, key_t1, key_t2 = backward_call(
         ids, prob, queries, grads, keys, values
     )
-    inputs, query_send = lax.optimization_barrier((inputs, query_send))
-    packed = pack_call(ids, inputs)
-    own = [packed[0]] + [shift_x(packed[d], d) for d in range(1, 4)]
-    other = [swap_core(block) for block in own]
     value_r1, query_send = lax.optimization_barrier((value_r1, query_send))
     value_keep, value_send, sent = total_call(ids, value_own, value_r1, value_r2, True)
     key_r2 = shift_chips(key_t2, -2)

time: 108 us -> 112 us (1.037)
  starting transfers between devices: 62.9 us -> 70.5 us
  waiting for transfers between devices: 20.5 us -> 16.5 us
    ppermute x7, starting transfers between devices: 25.7 us -> 35.3 us  [shift_chips(): return lax.ppermute(block, CHIP, route)]
    ppermute x3, waiting for transfers between devices: 7.59 us -> 0.01 us  [shift_x(): return lax.ppermute(block, 'x', [(i, (i + distance) % 4) for i in range(4)])]
    ppermute x7, waiting for transfers between devices: 0.02 us -> 4.18 us  [shift_chips(): return lax.ppermute(block, CHIP, route)]
    all_to_all x1, starting transfers between devices: 5.84 us -> 3.96 us  [shards(): gathered = lax.all_to_all(sent, 'x', 0, 0, tiled=True)]
    ppermute x12, starting transfers between devices: 13.6 us -> 12.2 us  [swap_core(): return lax.ppermute(block, 'c', [(0, 1), (1, 0)])]
  transfers between devices with their start and end apart: 24 -> 24, of which waited for: 7 -> 7; matrix products, arithmetic and copies ran while one was open for 1% -> 1% of each run, Pallas kernels for 15% -> 13%
where the time goes in v5:
time: 112 us; the launch traced here: 111 us
  starting transfers between devices  70.5 us (63%)
  Pallas kernels  16.9 us (15%)
  waiting for transfers between devices  16.5 us (15%)
  local copies, waits for them, and re-layouts  5.46 us (5%)
    ppermute x7, starting transfers between devices, shift_chips(): return lax.ppermute(block, CHIP, route)  35.3 us
    all_to_all x1, starting transfers between devices, shards(): lax.all_to_all(partial.reshape(32, 32, HALF), ('zl', 'zh', 'y'), 0, 0, ti...  16.6 us
    ppermute x12, starting transfers between devices, swap_core(): return lax.ppermute(block, 'c', [(0, 1), (1, 0)])  12.2 us
    all_to_all x1, waiting for transfers between devices, shards(): lax.all_to_all(partial.reshape(32, 32, HALF), ('zl', 'zh', 'y'), 0, 0, ti...  9.46 us
    unnamed x19, local copies, waits for them, and re-layouts  5.33 us
    ppermute x7, waiting for transfers between devices, shift_chips(): return lax.ppermute(block, CHIP, route)  4.18 us
    all_to_all x1, starting transfers between devices, shards(): gathered = lax.all_to_all(sent, 'x', 0, 0, tiled=True)  3.96 us
    pallas_call x1, Pallas kernels, backward_call(): pl.pallas_call(backward_kernel, grid_spec=pltpu.PrefetchScalarGridSpec(nu...  3.72 us
  transfers between devices with their start and end apart: 24, of which 7 were waited for; matrix products, arithmetic and copies ran while one was open for 1% of the time, Pallas kernels for 13%

profile of v5, /device:TPU:7, one launch (start us, length us, event | category | flops | bytes accessed | tf_op | source)
XLA Modules:
  0.0 111.0 jit_solution(17008501077218626956)
XLA Ops:
  1.5 1.1 %collective-permute-done.other = bf16[128,512]{1,0:T(8,128)(2,1)S(1)} collective-permute-done((bf16[128,512]{1,0:T(8,128)(2,1)}, bf16[128,512]{1,0:T(8,128)(2,1)S(1)}, u32[]{:S(2)}, u32[]{:S(2)}) %collective-permute-start) | collective-permute-done | bytes 131104 | tf_op jit(solution)/shard_map/ppermute | solution.py:396
  5.0 3.2 %collective-permute-start.5 = (bf16[256,256]{1,0:T(8,128)(2,1)S(1)}, bf16[256,256]{1,0:T(8,128)(2,1)S(1)}, u32[]{:S(2)}, u32[]{:S(2)}) collective-permute-start(bf16[256,256]{1,0:T(8,128)(2,1)S(1)} %pick_keys.1.keys.k0), channel_id=1, source_target_pairs={{0,2},{2,4},{4,6},{6,8},{8,10},{10,12},{12,14},{14,16},{16,18},{18... | collective-permute-start | bytes 393224 | tf_op jit(solution)/shard_map/ppermute | solution.py:388
  9.7 4.5 %collective-permute-start.4 = (bf16[128,512]{1,0:T(8,128)(2,1)S(1)}, bf16[128,512]{1,0:T(8,128)(2,1)S(1)}, u32[]{:S(2)}, u32[]{:S(2)}) collective-permute-start(bf16[128,512]{1,0:T(8,128)(2,1)S(1)} %get-tuple-element.63), channel_id=1, source_target_pairs={{0,4},{2,6},{4,8},{6,10},{8,12},{10,14},{12,16},{14,18},{16,20},{1... | collective-permute-start | bytes 393224 | tf_op jit(solution)/shard_map/ppermute | solution.py:388
  15.2 1.0 copy-done.1
  16.2 1.0 copy-done.2
  19.8 2.1 %collective-permute-start.8 = (bf16[128,1024]{1,0:T(8,128)(2,1)S(1)}, bf16[128,1024]{1,0:T(8,128)(2,1)S(1)}, u32[]{:S(2)}, u32[]{:S(2)}) collective-permute-start(bf16[128,1024]{1,0:T(8,128)(2,1)S(1)} %get-tuple-element.71), channel_id=1, source_target_pairs={{0,16},{8,24},{16,0},{24,8},{1,17},{9,25},{17,1},{25,9},{2,18},{10... | collective-permute-start | bytes 786440 | tf_op jit(solution)/shard_map/ppermute | solution.py:392
  21.9 3.1 %forward_and_value_gradient.1 = (bf16[2,2,512,512]{3,2,1,0:T(8,128)(2,1)S(1)}, f32[256,256]{1,0:T(8,128)S(1)}, bf16[256,256]{1,0:T(8,128)(2,1)S(1)}, bf16[128,256]{1,0:T(8,128)(2,1)S(1)}) custom-call(f32[2,512,128]{2,1,0:T(8,128)S(1)} %get-tuple-element.58.bias, bf16[256,1024]{1,0:T(8,128)(2,1)S(1)} %get-tuple-element.59.q_ref, ...), custom_call_target="tpu_custom_call" | custom-call | flops 536870912 | bytes 6291456 | tf_op jit(solution)/shard_map/forward_and_value_gradient/pallas_call | solution.py:215
  25.1 6.9 %collective-permute-start.10 = (bf16[256,256]{1,0:T(8,128)(2,1)S(1)}, bf16[256,256]{1,0:T(8,128)(2,1)S(1)}, u32[]{:S(2)}, u32[]{:S(2)}) collective-permute-start(bf16[256,256]{1,0:T(8,128)(2,1)S(1)} %get-tuple-element.74.v0), channel_id=1, source_target_pairs={{0,2},{2,4},{4,6},{6,8},{8,10},{10,12},{12,14},{14,16},{16,18},{18... | collective-permute-start | bytes 393224 | tf_op jit(solution)/shard_map/ppermute | solution.py:388
  32.0 4.7 %collective-permute-start.6 = (bf16[256,256]{1,0:T(8,128)(2,1)S(1)}, bf16[256,256]{1,0:T(8,128)(2,1)S(1)}, u32[]{:S(2)}, u32[]{:S(2)}) collective-permute-start(bf16[256,256]{1,0:T(8,128)(2,1)S(1)} %get-tuple-element.67), channel_id=1, source_target_pairs={{2,0},{4,2},{6,4},{8,6},{10,8},{12,10},{14,12},{16,14},{18,16},{20... | collective-permute-start | bytes 393224 | tf_op jit(solution)/shard_map/ppermute | solution.py:388
  36.7 3.1 %collective-permute-start.11 = (bf16[128,256]{1,0:T(8,128)(2,1)S(1)}, bf16[128,256]{1,0:T(8,128)(2,1)S(1)}, u32[]{:S(2)}, u32[]{:S(2)}) collective-permute-start(bf16[128,256]{1,0:T(8,128)(2,1)S(1)} %get-tuple-element.77), channel_id=1, source_target_pairs={{4,0},{6,2},{8,4},{10,6},{12,8},{14,10},{16,12},{18,14},{20,16},{2... | collective-permute-start | bytes 196616 | tf_op jit(solution)/shard_map/ppermute | solution.py:388
  39.8 2.7 %collective-permute-done.10.v1 = bf16[256,256]{1,0:T(8,128)(2,1)S(1)} collective-permute-done((bf16[256,256]{1,0:T(8,128)(2,1)S(1)}, bf16[256,256]{1,0:T(8,128)(2,1)S(1)}, u32[]{:S(2)}, u32[]{:S(2)}) %collective-permute-start.10) | collective-permute-done | bytes 131104 | tf_op jit(solution)/shard_map/ppermute | solution.py:388
  42.5 3.7 %query_and_key_gradient.1 = (bf16[128,1024]{1,0:T(8,128)(2,1)S(1)}, bf16[128,1024]{1,0:T(8,128)(2,1)S(1)}, f32[256,256]{1,0:T(8,128)S(1)}, bf16[256,256]{1,0:T(8,128)(2,1)S(1)}, bf16[128,256]{1,0:T(8,128)(2,1)S(1)}) custom-call(s32[3]{0:T(128)S(1)} %pad_add_fusion.ids, bf16[2,2,512,512]{3,2,1,0:T(8,128)(2,1)S(1)} %get-tuple-element.73.prob_ref, ...), custom_call_target="tpu_custom_call" | custom-call | flops 805306368 | bytes 6291456 | tf_op jit(solution)/shard_map/query_and_key_gradient/pallas_call | solution.py:230
  46.2 1.4 %value_gradient_total.1 = (bf16[128,256]{1,0:T(8,128)(2,1)S(1)}, bf16[128,256]{1,0:T(8,128)(2,1)}, bf16[4,256,256]{2,1,0:T(8,128)(2,1)}) custom-call(s32[3]{0:T(128)S(1)} %pad_add_fusion.ids, f32[256,256]{1,0:T(8,128)S(1)} %get-tuple-element.66.own, bf16[256,256]{1,0:T(8,128)(2,1)S(1)} %collective-permute-done.6.r1, ...), custom_call_target="tpu_custom_call" | custom-call | bytes 1048576 | tf_op jit(solution)/shard_map/value_gradient_total/pallas_call | solution.py:290
  47.7 4.0 %all-to-all-start = ((bf16[4,256,256]{2,1,0:T(8,128)(2,1)}), bf16[4,256,256]{2,1,0:T(8,128)(2,1)S(1)}, u32[]{:S(2)}, u32[]{:S(2)}) async-start(bf16[4,256,256]{2,1,0:T(8,128)(2,1)} %get-tuple-element.78), calls=%async_computation | async-start | bytes 1048576 | tf_op jit(solution)/shard_map/all_to_all | solution.py:440
  51.6 2.9 %collective-permute-start.12 = (bf16[128,1024]{1,0:T(8,128)(2,1)S(1)}, bf16[128,1024]{1,0:T(8,128)(2,1)S(1)}, u32[]{:S(2)}, u32[]{:S(2)}) collective-permute-start(bf16[128,1024]{1,0:T(8,128)(2,1)S(1)} %get-tuple-element.79.a0), channel_id=1, source_target_pairs={{0,1},{1,0},{2,3},{3,2},{4,5},{5,4},{6,7},{7,6},{8,9},{9,8},{10,11... | collective-permute-start | bytes 786440 | tf_op jit(solution)/shard_map/ppermute | solution.py:396
  55.0 11.0 %collective-permute-start.16 = (bf16[256,256]{1,0:T(8,128)(2,1)}, bf16[256,256]{1,0:T(8,128)(2,1)S(1)}, u32[]{:S(2)}, u32[]{:S(2)}) collective-permute-start(bf16[256,256]{1,0:T(8,128)(2,1)} %copy-done.7), channel_id=1, source_target_pairs={{2,0},{4,2},{6,4},{8,6},{10,8},{12,10},{14,12},{16,14},{18,16},{20... | collective-permute-start | bytes 393224 | tf_op jit(solution)/shard_map/ppermute | solution.py:388
  66.0 1.9 %collective-permute-start.17 = (bf16[128,256]{1,0:T(8,128)(2,1)}, bf16[128,256]{1,0:T(8,128)(2,1)S(1)}, u32[]{:S(2)}, u32[]{:S(2)}) collective-permute-start(bf16[128,256]{1,0:T(8,128)(2,1)} %copy-done.8), channel_id=1, source_target_pairs={{4,0},{6,2},{8,4},{10,6},{12,8},{14,10},{16,12},{18,14},{20,16},{2... | collective-permute-start | bytes 196616 | tf_op jit(solution)/shard_map/ppermute | solution.py:388
  68.0 3.3 %weight_gradient.1 = bf16[1024,256]{1,0:T(8,128)(2,1)} custom-call(s32[3]{0:T(128)S(1)} %pad_add_fusion.ids, bf16[4,256,256]{2,1,0:T(8,128)(2,1)S(1)} %all-to-all-done.grads, bf16[128,1024]{1,0:T(8,128)(2,1)S(1)} %get-tuple-element.79.a0, bf16[128,1024]{1,0:T(8,128)(2,1)S(1)} %collective-permute-done.7.a1, bf16[128,1024]{1,0:T(8,128)(2,1)S(1)} %collective-permute-done.8.a2, ...), custom_call_target="tpu_custom_call" | custom-call | flops 536870912 | bytes 3145728 | tf_op jit(solution)/shard_map/weight_gradient/pallas_call | solution.py:344
  71.3 1.5 %collective-permute-done.17.r2 = bf16[128,256]{1,0:T(8,128)(2,1)S(1)} collective-permute-done((bf16[128,256]{1,0:T(8,128)(2,1)}, bf16[128,256]{1,0:T(8,128)(2,1)S(1)}, u32[]{:S(2)}, u32[]{:S(2)}) %collective-permute-start.17) | collective-permute-done | bytes 65568 | tf_op jit(solution)/shard_map/ppermute | solution.py:388
  72.8 16.6 %all-to-all-start.1 = ((bf16[32,32,256]{2,1,0:T(8,128)(2,1)}), bf16[32,32,256]{2,1,0:T(8,128)(2,1)S(1)}, u32[]{:S(2)}, u32[]{:S(2)}) async-start(bf16[32,32,256]{2,1,0:T(8,128)(2,1)} %bitcast.9), calls=%async_computation.1 | async-start | bytes 1048576 | tf_op jit(solution)/shard_map/all_to_all | solution.py:443
  89.4 2.3 %collective-permute-start.18 = (bf16[128,1024]{1,0:T(8,128)(2,1)}, bf16[128,1024]{1,0:T(8,128)(2,1)S(1)}, u32[]{:S(2)}, u32[]{:S(2)}) collective-permute-start(bf16[128,1024]{1,0:T(8,128)(2,1)} %copy-done.6), channel_id=1, source_target_pairs={{0,1},{1,0},{2,3},{3,2},{4,5},{5,4},{6,7},{7,6},{8,9},{9,8},{10,11... | collective-permute-start | bytes 786440 | tf_op jit(solution)/shard_map/ppermute | solution.py:396
  93.8 1.5 %join_outputs.1 = (bf16[128,2048]{1,0:T(8,128)(2,1)}, bf16[128,512]{1,0:T(8,128)(2,1)}, bf16[128,512]{1,0:T(8,128)(2,1)}) custom-call(s32[3]{0:T(128)S(1)} %pad_add_fusion.ids, bf16[128,1024]{1,0:T(8,128)(2,1)S(1)} %get-tuple-element.86.refs_0_, bf16[128,256]{1,0:T(8,128)(2,1)S(1)} %get-tuple-element.90.refs_1_, ...), custom_call_target="tpu_custom_call" | custom-call | bytes 524288 | tf_op jit(solution)/shard_map/join_outputs/pallas_call | solution.py:316
  95.3 9.5 %all-to-all-done.1.in_ref = bf16[32,32,256]{2,1,0:T(8,128)(2,1)S(1)} async-done(((bf16[32,32,256]{2,1,0:T(8,128)(2,1)}), bf16[32,32,256]{2,1,0:T(8,128)(2,1)S(1)}, u32[]{:S(2)}, u32[]{:S(2)}) %all-to-all-start.1) | async-done | bytes 524320 | tf_op jit(solution)/shard_map/all_to_all | solution.py:443
  105.3 4.2 %collective-permute-start.21 = (f32[16,256]{1,0:T(8,128)S(1)}, f32[16,256]{1,0:T(8,128)S(1)}, u32[]{:S(2)}, u32[]{:S(2)}) collective-permute-start(f32[16,256]{1,0:T(8,128)S(1)} %get-tuple-element.101), channel_id=1, source_target_pairs={{0,1},{1,0},{2,3},{3,2},{4,5},{5,4},{6,7},{7,6},{8,9},{9,8},{10,11... | collective-permute-start | bytes 49160 | tf_op jit(solution)/shard_map/ppermute | solution.py:396
  (58 shorter events, 12.9 us)
Async XLA Ops:
  0.6 2.0 %collective-permute-start = (bf16[128,512]{1,0:T(8,128)(2,1)}, bf16[128,512]{1,0:T(8,128)(2,1)S(1)}, u32[]{:S(2)}, u32[]{:S(2)}) collective-permute-start(bf16[128,512]{1,0:T(8,128)(2,1)} %bitcast.18), channel_id=1, source_target_pairs={{0,1},{1,0},{2,3},{3,2},{4,5},{5,4},{6,7},{7,6},{8,9},{9,8},{10,11... | collective-permute-start | bytes 393224 | tf_op jit(solution)/shard_map/ppermute | solution.py:396
  4.1 11.1 %collective-permute-start.1 = (bf16[128,2048]{1,0:T(8,128)(2,1)}, bf16[128,2048]{1,0:T(8,128)(2,1)S(1)}, u32[]{:S(2)}, u32[]{:S(2)}) collective-permute-start(bf16[128,2048]{1,0:T(8,128)(2,1)} %bitcast.14), channel_id=1, source_target_pairs={{0,1},{1,0},{2,3},{3,2},{4,5},{5,4},{6,7},{7,6},{8,9},{9,8},{10,11... | collective-permute-start | bytes 1572872 | tf_op jit(solution)/shard_map/ppermute | solution.py:396
  4.5 10.7 %collective-permute-start.2 = (bf16[128,2048]{1,0:T(8,128)(2,1)}, bf16[128,2048]{1,0:T(8,128)(2,1)S(1)}, u32[]{:S(2)}, u32[]{:S(2)}) collective-permute-start(bf16[128,2048]{1,0:T(8,128)(2,1)} %bitcast.16), channel_id=1, source_target_pairs={{0,1},{1,0},{2,3},{3,2},{4,5},{5,4},{6,7},{7,6},{8,9},{9,8},{10,11... | collective-permute-start | bytes 1572872 | tf_op jit(solution)/shard_map/ppermute | solution.py:396
  4.7 3.6 %collective-permute-start.3 = (bf16[128,512]{1,0:T(8,128)(2,1)}, bf16[128,512]{1,0:T(8,128)(2,1)S(1)}, u32[]{:S(2)}, u32[]{:S(2)}) collective-permute-start(bf16[128,512]{1,0:T(8,128)(2,1)} %bitcast.20), channel_id=1, source_target_pairs={{0,1},{1,0},{2,3},{3,2},{4,5},{5,4},{6,7},{7,6},{8,9},{9,8},{10,11... | collective-permute-start | bytes 393224 | tf_op jit(solution)/shard_map/ppermute | solution.py:396
  5.0 16.9 %collective-permute-start.5 = (bf16[256,256]{1,0:T(8,128)(2,1)S(1)}, bf16[256,256]{1,0:T(8,128)(2,1)S(1)}, u32[]{:S(2)}, u32[]{:S(2)}) collective-permute-start(bf16[256,256]{1,0:T(8,128)(2,1)S(1)} %pick_keys.1.keys.k0), channel_id=1, source_target_pairs={{0,2},{2,4},{4,6},{6,8},{8,10},{10,12},{12,14},{14,16},{16,18},{18... | collective-permute-start | bytes 393224 | tf_op jit(solution)/shard_map/ppermute | solution.py:388
  9.7 12.2 %collective-permute-start.4 = (bf16[128,512]{1,0:T(8,128)(2,1)S(1)}, bf16[128,512]{1,0:T(8,128)(2,1)S(1)}, u32[]{:S(2)}, u32[]{:S(2)}) collective-permute-start(bf16[128,512]{1,0:T(8,128)(2,1)S(1)} %get-tuple-element.63), channel_id=1, source_target_pairs={{0,4},{2,6},{4,8},{6,10},{8,12},{10,14},{12,16},{14,18},{16,20},{1... | collective-permute-start | bytes 393224 | tf_op jit(solution)/shard_map/ppermute | solution.py:388
  19.5 17.2 %collective-permute-start.7 = (bf16[128,1024]{1,0:T(8,128)(2,1)S(1)}, bf16[128,1024]{1,0:T(8,128)(2,1)S(1)}, u32[]{:S(2)}, u32[]{:S(2)}) collective-permute-start(bf16[128,1024]{1,0:T(8,128)(2,1)S(1)} %get-tuple-element.70), channel_id=1, source_target_pairs={{0,8},{8,16},{16,24},{24,0},{1,9},{9,17},{17,25},{25,1},{2,10},{10... | collective-permute-start | bytes 786440 | tf_op jit(solution)/shard_map/ppermute | solution.py:392
  19.8 20.0 %collective-permute-start.8 = (bf16[128,1024]{1,0:T(8,128)(2,1)S(1)}, bf16[128,1024]{1,0:T(8,128)(2,1)S(1)}, u32[]{:S(2)}, u32[]{:S(2)}) collective-permute-start(bf16[128,1024]{1,0:T(8,128)(2,1)S(1)} %get-tuple-element.71), channel_id=1, source_target_pairs={{0,16},{8,24},{16,0},{24,8},{1,17},{9,25},{17,1},{25,9},{2,18},{10... | collective-permute-start | bytes 786440 | tf_op jit(solution)/shard_map/ppermute | solution.py:392
  21.9 17.9 %collective-permute-start.9 = (bf16[128,1024]{1,0:T(8,128)(2,1)S(1)}, bf16[128,1024]{1,0:T(8,128)(2,1)S(1)}, u32[]{:S(2)}, u32[]{:S(2)}) collective-permute-start(bf16[128,1024]{1,0:T(8,128)(2,1)S(1)} %get-tuple-element.72), channel_id=1, source_target_pairs={{0,24},{8,0},{16,8},{24,16},{1,25},{9,1},{17,9},{25,17},{2,26},{10... | collective-permute-start | bytes 786440 | tf_op jit(solution)/shard_map/ppermute | solution.py:392
  25.1 17.4 %collective-permute-start.10 = (bf16[256,256]{1,0:T(8,128)(2,1)S(1)}, bf16[256,256]{1,0:T(8,128)(2,1)S(1)}, u32[]{:S(2)}, u32[]{:S(2)}) collective-permute-start(bf16[256,256]{1,0:T(8,128)(2,1)S(1)} %get-tuple-element.74.v0), channel_id=1, source_target_pairs={{0,2},{2,4},{4,6},{6,8},{8,10},{10,12},{12,14},{14,16},{16,18},{18... | collective-permute-start | bytes 393224 | tf_op jit(solution)/shard_map/ppermute | solution.py:388
  32.0 14.2 %collective-permute-start.6 = (bf16[256,256]{1,0:T(8,128)(2,1)S(1)}, bf16[256,256]{1,0:T(8,128)(2,1)S(1)}, u32[]{:S(2)}, u32[]{:S(2)}) collective-permute-start(bf16[256,256]{1,0:T(8,128)(2,1)S(1)} %get-tuple-element.67), channel_id=1, source_target_pairs={{2,0},{4,2},{6,4},{8,6},{10,8},{12,10},{14,12},{16,14},{18,16},{20... | collective-permute-start | bytes 393224 | tf_op jit(solution)/shard_map/ppermute | solution.py:388
  36.7 9.6 %collective-permute-start.11 = (bf16[128,256]{1,0:T(8,128)(2,1)S(1)}, bf16[128,256]{1,0:T(8,128)(2,1)S(1)}, u32[]{:S(2)}, u32[]{:S(2)}) collective-permute-start(bf16[128,256]{1,0:T(8,128)(2,1)S(1)} %get-tuple-element.77), channel_id=1, source_target_pairs={{4,0},{6,2},{8,4},{10,6},{12,8},{14,10},{16,12},{18,14},{20,16},{2... | collective-permute-start | bytes 196616 | tf_op jit(solution)/shard_map/ppermute | solution.py:388
  47.7 20.3 %all-to-all-start = ((bf16[4,256,256]{2,1,0:T(8,128)(2,1)}), bf16[4,256,256]{2,1,0:T(8,128)(2,1)S(1)}, u32[]{:S(2)}, u32[]{:S(2)}) async-start(bf16[4,256,256]{2,1,0:T(8,128)(2,1)} %get-tuple-element.78), calls=%async_computation | async-start | bytes 1048576 | tf_op jit(solution)/shard_map/all_to_all | solution.py:440
  51.6 14.4 %collective-permute-start.12 = (bf16[128,1024]{1,0:T(8,128)(2,1)S(1)}, bf16[128,1024]{1,0:T(8,128)(2,1)S(1)}, u32[]{:S(2)}, u32[]{:S(2)}) collective-permute-start(bf16[128,1024]{1,0:T(8,128)(2,1)S(1)} %get-tuple-element.79.a0), channel_id=1, source_target_pairs={{0,1},{1,0},{2,3},{3,2},{4,5},{5,4},{6,7},{7,6},{8,9},{9,8},{10,11... | collective-permute-start | bytes 786440 | tf_op jit(solution)/shard_map/ppermute | solution.py:396
  54.5 13.5 %collective-permute-start.13 = (bf16[128,1024]{1,0:T(8,128)(2,1)S(1)}, bf16[128,1024]{1,0:T(8,128)(2,1)S(1)}, u32[]{:S(2)}, u32[]{:S(2)}) collective-permute-start(bf16[128,1024]{1,0:T(8,128)(2,1)S(1)} %collective-permute-done.7.a1), channel_id=1, source_target_pairs={{0,1},{1,0},{2,3},{3,2},{4,5},{5,4},{6,7},{7,6},{8,9},{9,8},{10,11... | collective-permute-start | bytes 786440 | tf_op jit(solution)/shard_map/ppermute | solution.py:396
  54.5 13.5 %collective-permute-start.14 = (bf16[128,1024]{1,0:T(8,128)(2,1)S(1)}, bf16[128,1024]{1,0:T(8,128)(2,1)S(1)}, u32[]{:S(2)}, u32[]{:S(2)}) collective-permute-start(bf16[128,1024]{1,0:T(8,128)(2,1)S(1)} %collective-permute-done.8.a2), channel_id=1, source_target_pairs={{0,1},{1,0},{2,3},{3,2},{4,5},{5,4},{6,7},{7,6},{8,9},{9,8},{10,11... | collective-permute-start | bytes 786440 | tf_op jit(solution)/shard_map/ppermute | solution.py:396
  55.0 13.0 %collective-permute-start.15 = (bf16[128,1024]{1,0:T(8,128)(2,1)S(1)}, bf16[128,1024]{1,0:T(8,128)(2,1)S(1)}, u32[]{:S(2)}, u32[]{:S(2)}) collective-permute-start(bf16[128,1024]{1,0:T(8,128)(2,1)S(1)} %collective-permute-done.9.a3), channel_id=1, source_target_pairs={{0,1},{1,0},{2,3},{3,2},{4,5},{5,4},{6,7},{7,6},{8,9},{9,8},{10,11... | collective-permute-start | bytes 786440 | tf_op jit(solution)/shard_map/ppermute | solution.py:396
  55.0 17.8 %collective-permute-start.16 = (bf16[256,256]{1,0:T(8,128)(2,1)}, bf16[256,256]{1,0:T(8,128)(2,1)S(1)}, u32[]{:S(2)}, u32[]{:S(2)}) collective-permute-start(bf16[256,256]{1,0:T(8,128)(2,1)} %copy-done.7), channel_id=1, source_target_pairs={{2,0},{4,2},{6,4},{8,6},{10,8},{12,10},{14,12},{16,14},{18,16},{20... | collective-permute-start | bytes 393224 | tf_op jit(solution)/shard_map/ppermute | solution.py:388
  66.0 6.7 %collective-permute-start.17 = (bf16[128,256]{1,0:T(8,128)(2,1)}, bf16[128,256]{1,0:T(8,128)(2,1)S(1)}, u32[]{:S(2)}, u32[]{:S(2)}) collective-permute-start(bf16[128,256]{1,0:T(8,128)(2,1)} %copy-done.8), channel_id=1, source_target_pairs={{4,0},{6,2},{8,4},{10,6},{12,8},{14,10},{16,12},{18,14},{20,16},{2... | collective-permute-start | bytes 196616 | tf_op jit(solution)/shard_map/ppermute | solution.py:388
  72.8 32.0 %all-to-all-start.1 = ((bf16[32,32,256]{2,1,0:T(8,128)(2,1)}), bf16[32,32,256]{2,1,0:T(8,128)(2,1)S(1)}, u32[]{:S(2)}, u32[]{:S(2)}) async-start(bf16[32,32,256]{2,1,0:T(8,128)(2,1)} %bitcast.9), calls=%async_computation.1 | async-start | bytes 1048576 | tf_op jit(solution)/shard_map/all_to_all | solution.py:443
  89.4 3.8 %collective-permute-start.18 = (bf16[128,1024]{1,0:T(8,128)(2,1)}, bf16[128,1024]{1,0:T(8,128)(2,1)S(1)}, u32[]{:S(2)}, u32[]{:S(2)}) collective-permute-start(bf16[128,1024]{1,0:T(8,128)(2,1)} %copy-done.6), channel_id=1, source_target_pairs={{0,1},{1,0},{2,3},{3,2},{4,5},{5,4},{6,7},{7,6},{8,9},{9,8},{10,11... | collective-permute-start | bytes 786440 | tf_op jit(solution)/shard_map/ppermute | solution.py:396
  91.7 1.5 %collective-permute-start.20 = (bf16[128,256]{1,0:T(8,128)(2,1)}, bf16[128,256]{1,0:T(8,128)(2,1)S(1)}, u32[]{:S(2)}, u32[]{:S(2)}) collective-permute-start(bf16[128,256]{1,0:T(8,128)(2,1)} %get-tuple-element.94), channel_id=1, source_target_pairs={{0,1},{1,0},{2,3},{3,2},{4,5},{5,4},{6,7},{7,6},{8,9},{9,8},{10,11... | collective-permute-start | bytes 196616 | tf_op jit(solution)/shard_map/ppermute | solution.py:396
  92.4 1.4 %collective-permute-start.19 = (bf16[128,256]{1,0:T(8,128)(2,1)S(1)}, bf16[128,256]{1,0:T(8,128)(2,1)S(1)}, u32[]{:S(2)}, u32[]{:S(2)}) collective-permute-start(bf16[128,256]{1,0:T(8,128)(2,1)S(1)} %get-tuple-element.93), channel_id=1, source_target_pairs={{0,1},{1,0},{2,3},{3,2},{4,5},{5,4},{6,7},{7,6},{8,9},{9,8},{10,11... | collective-permute-start | bytes 196616 | tf_op jit(solution)/shard_map/ppermute | solution.py:396
  105.3 5.1 %collective-permute-start.21 = (f32[16,256]{1,0:T(8,128)S(1)}, f32[16,256]{1,0:T(8,128)S(1)}, u32[]{:S(2)}, u32[]{:S(2)}) collective-permute-start(f32[16,256]{1,0:T(8,128)S(1)} %get-tuple-element.101), channel_id=1, source_target_pairs={{0,1},{1,0},{2,3},{3,2},{4,5},{5,4},{6,7},{7,6},{8,9},{9,8},{10,11... | collective-permute-start | bytes 49160 | tf_op jit(solution)/shard_map/ppermute | solution.py:396
  (9 other events, 27.0 us)

commit v6 on v5

--- a/solution.py
+++ b/solution.py
@@ -61,32 +61,24 @@
     out_ref[pl.ds(pl.multiple_of((1 - core) * ROWS, ROWS), ROWS), :] = other[...]
 
 
-def pick_keys_kernel(ids, own, other, both_ref):
-    put_rows(both_ref, ids[2], own, other)
-
-
-def pick_values_kernel(ids, own, other, keys, both_ref, last_ref):
-    put_rows(both_ref, ids[2], own, other)
-    last_ref[:, :HALF] = keys[ROWS:]
-    last_ref[:, HALF:] = both_ref[ROWS:]
-
-
-def pick_call(ids, own, other, keys=None):
+def pick_kernel(ids, k_own, k_other, v_own, v_other, both_ref, last_ref):
+    put_rows(both_ref.at[:, :HALF], ids[2], k_own, k_other)
+    put_rows(both_ref.at[:, HALF:], ids[2], v_own, v_other)
+    last_ref[...] = both_ref[ROWS:]
+
+
+def pick_call(ids, *blocks):
     half = pl.BlockSpec((ROWS, HALF), lambda i, ids: (0, ids[2]))
-    extra = [] if keys is None else [keys]
-    return pl.pallas_call(
-        pick_values_kernel if extra else pick_keys_kernel,
-        grid_spec=pltpu.PrefetchScalarGridSpec(
-            num_scalar_prefetch=1,
-            grid=(1,),
-            in_specs=[half] * 2 + [WHOLE] * len(extra),
-            out_specs=[WHOLE] * (1 + len(extra)),
-        ),
-        out_shape=[shape(2 * ROWS, HALF)] + [shape(ROWS, 2 * HALF)] * len(extra),
+    return pl.pallas_call(
+        pick_kernel,
+        grid_spec=pltpu.PrefetchScalarGridSpec(
+            num_scalar_prefetch=1, grid=(1,), in_specs=[half] * 4, out_specs=[WHOLE] * 2
+        ),
+        out_shape=[shape(2 * ROWS, 2 * HALF), shape(ROWS, 2 * HALF)],
         compiler_params=PARAMS,
         cost_estimate=cost(0, 0.5),
-        name="pick_values" if extra else "pick_keys",
-    )(ids, own, other, *extra)
+        name="pick_keys_and_values",
+    )(ids, *blocks)
 
 
 def prepare_kernel(
@@ -202,7 +194,7 @@
 
 
 WINDOW = [narrow(ROWS), narrow(2 * ROWS), narrow(2 * ROWS)]
-VALUE_WINDOW = [narrow(ROWS, GROUPS)] + WINDOW[1:]
+VALUE_WINDOW = [narrow(ROWS, GROUPS), narrow(2 * ROWS, GROUPS), narrow(2 * ROWS, GROUPS)]
 TERMS = [narrow(2 * ROWS), narrow(2 * ROWS), narrow(ROWS)]
 PROB_SPEC = pl.BlockSpec((1, 2, KEYS, WIDE), lambda j, *_: (j, 0, 0, 0))
 
@@ -211,7 +203,7 @@
     return [shape(2 * ROWS, HALF, dtype=F32), shape(2 * ROWS, HALF), shape(ROWS, HALF, dtype=last)]
 
 
-def forward_call(bias, queries, grads, keys):
+def forward_call(bias, queries, grads, blocks):
     return pl.pallas_call(
         forward_kernel,
         grid=(GROUPS,),
@@ -223,10 +215,10 @@
         compiler_params=LARGE,
         cost_estimate=cost(4 * 16 * ROWS * KEYS * HEAD, 6),
         name="forward_and_value_gradient",
-    )(bias, queries, grads, *keys)
-
-
-def backward_call(ids, prob, queries, grads, keys, values):
+    )(bias, queries, grads, *blocks)
+
+
+def backward_call(ids, prob, queries, grads, blocks):
     return pl.pallas_call(
         backward_kernel,
         grid_spec=pltpu.PrefetchScalarGridSpec(
@@ -240,7 +232,7 @@
         compiler_params=LARGE,
         cost_estimate=cost(6 * 16 * ROWS * KEYS * HEAD, 6),
         name="query_and_key_gradient",
-    )(ids, prob, queries, grads, *keys, *values)
+    )(ids, prob, queries, grads, *blocks, *blocks)
 
 
 def pack_kernel(ids, in_ref, o0, o1, o2, o3):
@@ -401,13 +393,9 @@
     core = lax.axis_index("c")
     ids = jnp.stack([lax.axis_index(CTX), lax.axis_index("x"), core]).astype(jnp.int32)
 
-    key_other, value = lax.optimization_barrier((swap_core(key), value))
-    (key0,) = pick_call(ids, key, key_other)
-    key0, query, grad, value = lax.optimization_barrier((key0, query, grad, value))
-    key1 = shift_chips(key0, 1)
-    value0, last = pick_call(ids, value, swap_core(value), key0)
-    far2 = shift_chips(last, 2)
-    keys = [far2, key1, key0]
+    key_other, value_other = swap_core(key), swap_core(value)
+    both, last = pick_call(ids, key, key_other, value, value_other)
+    blocks = [shift_chips(last, 2), shift_chips(both, 1), both]
     bias, queries, grads = prepare_call(
         ids,
         stretch_order.reshape(-1),
@@ -422,18 +410,15 @@
     packed = pack_call(ids, inputs)
     own = [packed[0]] + [shift_x(packed[d], d) for d in range(1, 4)]
 
-    prob, value_own, value_t1, value_t2 = forward_call(bias, queries, grads, keys)
+    prob, value_own, value_t1, value_t2 = forward_call(bias, queries, grads, blocks)
     value_r2 = shift_chips(value_t2, -2)
     value_r1 = shift_chips(value_t1, -1)
-    value_own, value0 = lax.optimization_barrier((value_own, value0))
-    values = [far2, shift_chips(value0, 1), value0]
-    prob, *far = lax.optimization_barrier((prob, *own[1:]))
+    query_keep, query_send, key_own, key_t1, key_t2 = backward_call(
+        ids, prob, queries, grads, blocks
+    )
+    value_r1, query_send, *far = lax.optimization_barrier((value_r1, query_send, *own[1:]))
     own = [own[0]] + far
     other = [swap_core(block) for block in own]
-    query_keep, query_send, key_own, key_t1, key_t2 = backward_call(
-        ids, prob, queries, grads, keys, values
-    )
-    value_r1, query_send = lax.optimization_barrier((value_r1, query_send))
     value_keep, value_send, sent = total_call(ids, value_own, value_r1, value_r2, True)
     key_r2 = shift_chips(key_t2, -2)
     key_r1 = shift_chips(key_t1, -1)

time: 112 us -> 108 us (0.964)
  starting transfers between devices: 70.5 us -> 66.7 us
  local copies, waits for them, and re-layouts: 5.46 us -> 6.71 us
    ppermute x7 -> x6, starting transfers between devices: 35.3 us -> 27.5 us  [shift_chips(): return lax.ppermute(block, CHIP, route)]
    all_to_all x1, starting transfers between devices: 16.6 us -> 20 us  [shards(): lax.all_to_all(partial.reshape(32, 32, HALF), ('zl', 'zh', 'y'), 0, 0, ti...]
    ppermute x7 -> x6, waiting for transfers between devices: 4.18 us -> 1.33 us  [shift_chips(): return lax.ppermute(block, CHIP, route)]
    all_to_all x1, starting transfers between devices: 3.96 us -> 5.65 us  [shards(): gathered = lax.all_to_all(sent, 'x', 0, 0, tiled=True)]
    all_to_all x1, waiting for transfers between devices: 9.46 us -> 11 us  [shards(): lax.all_to_all(partial.reshape(32, 32, HALF), ('zl', 'zh', 'y'), 0, 0, ti...]
    unnamed x19, local copies, waits for them, and re-layouts: 5.33 us -> 6.57 us
  transfers between devices with their start and end apart: 24 -> 23, of which waited for: 7 -> 8; matrix products, arithmetic and copies ran while one was open for 1% -> 1% of each run, Pallas kernels for 13% -> 13%
where the time goes in v6:
time: 108 us
  starting transfers between devices  66.7 us (62%)
  Pallas kernels  16.3 us (15%)
  waiting for transfers between devices  16.2 us (15%)
  local copies, waits for them, and re-layouts  6.71 us (6%)
    ppermute x6, starting transfers between devices, shift_chips(): return lax.ppermute(block, CHIP, route)  27.5 us
    all_to_all x1, starting transfers between devices, shards(): lax.all_to_all(partial.reshape(32, 32, HALF), ('zl', 'zh', 'y'), 0, 0, ti...  20 us
    ppermute x12, starting transfers between devices, swap_core(): return lax.ppermute(block, 'c', [(0, 1), (1, 0)])  11.2 us
    all_to_all x1, waiting for transfers between devices, shards(): lax.all_to_all(partial.reshape(32, 32, HALF), ('zl', 'zh', 'y'), 0, 0, ti...  11 us
    unnamed x19, local copies, waits for them, and re-layouts  6.57 us
    all_to_all x1, starting transfers between devices, shards(): gathered = lax.all_to_all(sent, 'x', 0, 0, tiled=True)  5.65 us
    ppermute x12, waiting for transfers between devices, swap_core(): return lax.ppermute(block, 'c', [(0, 1), (1, 0)])  3.94 us
    pallas_call x1, Pallas kernels, backward_call(): pl.pallas_call(backward_kernel, grid_spec=pltpu.PrefetchScalarGridSpec(nu...  3.73 us
  transfers between devices with their start and end apart: 23, of which 8 were waited for; matrix products, arithmetic and copies ran while one was open for 1% of the time, Pallas kernels for 13%

profile of v6, /device:TPU:7, one launch (start us, length us, event | category | flops | bytes accessed | tf_op | source)
XLA Modules:
  0.0 107.5 jit_solution(14626202466794577084)
XLA Ops:
  2.1 2.0 %collective-permute-done.2.k_other = bf16[128,512]{1,0:T(8,128)(2,1)S(1)} collective-permute-done((bf16[128,512]{1,0:T(8,128)(2,1)}, bf16[128,512]{1,0:T(8,128)(2,1)S(1)}, u32[]{:S(2)}, u32[]{:S(2)}) %collective-permute-start.2) | collective-permute-done | bytes 131104 | tf_op jit(solution)/shard_map/ppermute | solution.py:388
  4.3 0.9 copy-done.3
  5.2 0.9 copy-done.4
  6.7 3.2 %collective-permute-start.5 = (bf16[256,512]{1,0:T(8,128)(2,1)S(1)}, bf16[256,512]{1,0:T(8,128)(2,1)S(1)}, u32[]{:S(2)}, u32[]{:S(2)}) collective-permute-start(bf16[256,512]{1,0:T(8,128)(2,1)S(1)} %get-tuple-element.49.k0.v0), channel_id=1, source_target_pairs={{0,2},{2,4},{4,6},{6,8},{8,10},{10,12},{12,14},{14,16},{16,18},{18... | collective-permute-start | bytes 786440 | tf_op jit(solution)/shard_map/ppermute | solution.py:380
  9.9 4.5 %collective-permute-start.4 = (bf16[128,512]{1,0:T(8,128)(2,1)S(1)}, bf16[128,512]{1,0:T(8,128)(2,1)S(1)}, u32[]{:S(2)}, u32[]{:S(2)}) collective-permute-start(bf16[128,512]{1,0:T(8,128)(2,1)S(1)} %get-tuple-element.48), channel_id=1, source_target_pairs={{0,4},{2,6},{4,8},{6,10},{8,12},{10,14},{12,16},{14,18},{16,20},{1... | collective-permute-start | bytes 393224 | tf_op jit(solution)/shard_map/ppermute | solution.py:380
  15.4 1.0 copy-done.1
  16.4 1.0 copy-done.2
  20.0 2.1 %collective-permute-start.8 = (bf16[128,1024]{1,0:T(8,128)(2,1)S(1)}, bf16[128,1024]{1,0:T(8,128)(2,1)S(1)}, u32[]{:S(2)}, u32[]{:S(2)}) collective-permute-start(bf16[128,1024]{1,0:T(8,128)(2,1)S(1)} %get-tuple-element.56), channel_id=1, source_target_pairs={{0,16},{8,24},{16,0},{24,8},{1,17},{9,25},{17,1},{25,9},{2,18},{10... | collective-permute-start | bytes 786440 | tf_op jit(solution)/shard_map/ppermute | solution.py:384
  22.1 3.1 %forward_and_value_gradient.1 = (bf16[2,2,512,512]{3,2,1,0:T(8,128)(2,1)S(1)}, f32[256,256]{1,0:T(8,128)S(1)}, bf16[256,256]{1,0:T(8,128)(2,1)S(1)}, bf16[128,256]{1,0:T(8,128)(2,1)S(1)}) custom-call(f32[2,512,128]{2,1,0:T(8,128)S(1)} %get-tuple-element.45.bias, bf16[256,1024]{1,0:T(8,128)(2,1)S(1)} %get-tuple-element.46.q_ref, ...), custom_call_target="tpu_custom_call" | custom-call | flops 536870912 | bytes 6291456 | tf_op jit(solution)/shard_map/forward_and_value_gradient/pallas_call | solution.py:207
  25.3 9.6 %collective-permute-start.6 = (bf16[256,256]{1,0:T(8,128)(2,1)S(1)}, bf16[256,256]{1,0:T(8,128)(2,1)S(1)}, u32[]{:S(2)}, u32[]{:S(2)}) collective-permute-start(bf16[256,256]{1,0:T(8,128)(2,1)S(1)} %get-tuple-element.51), channel_id=1, source_target_pairs={{2,0},{4,2},{6,4},{8,6},{10,8},{12,10},{14,12},{16,14},{18,16},{20... | collective-permute-start | bytes 393224 | tf_op jit(solution)/shard_map/ppermute | solution.py:380
  34.9 2.0 %collective-permute-start.10 = (bf16[128,256]{1,0:T(8,128)(2,1)S(1)}, bf16[128,256]{1,0:T(8,128)(2,1)S(1)}, u32[]{:S(2)}, u32[]{:S(2)}) collective-permute-start(bf16[128,256]{1,0:T(8,128)(2,1)S(1)} %get-tuple-element.59), channel_id=1, source_target_pairs={{4,0},{6,2},{8,4},{10,6},{12,8},{14,10},{16,12},{18,14},{20,16},{2... | collective-permute-start | bytes 196616 | tf_op jit(solution)/shard_map/ppermute | solution.py:380
  36.9 3.7 %query_and_key_gradient.1 = (bf16[128,1024]{1,0:T(8,128)(2,1)S(1)}, bf16[128,1024]{1,0:T(8,128)(2,1)S(1)}, f32[256,256]{1,0:T(8,128)S(1)}, bf16[256,256]{1,0:T(8,128)(2,1)S(1)}, bf16[128,256]{1,0:T(8,128)(2,1)S(1)}) custom-call(s32[3]{0:T(128)S(1)} %pad_add_fusion.ids, bf16[2,2,512,512]{3,2,1,0:T(8,128)(2,1)S(1)} %get-tuple-element.52.prob_ref, ...), custom_call_target="tpu_custom_call" | custom-call | flops 805306368 | bytes 6291456 | tf_op jit(solution)/shard_map/query_and_key_gradient/pallas_call | solution.py:222
  41.4 1.4 %value_gradient_total.1 = (bf16[128,256]{1,0:T(8,128)(2,1)S(1)}, bf16[128,256]{1,0:T(8,128)(2,1)S(1)}, bf16[4,256,256]{2,1,0:T(8,128)(2,1)}) custom-call(s32[3]{0:T(128)S(1)} %pad_add_fusion.ids, f32[256,256]{1,0:T(8,128)S(1)} %get-tuple-element.50.own, bf16[256,256]{1,0:T(8,128)(2,1)S(1)} %collective-permute-done.6.r1, ...), custom_call_target="tpu_custom_call" | custom-call | bytes 1048576 | tf_op jit(solution)/shard_map/value_gradient_total/pallas_call | solution.py:282
  43.4 5.6 %all-to-all-start = ((bf16[4,256,256]{2,1,0:T(8,128)(2,1)}), bf16[4,256,256]{2,1,0:T(8,128)(2,1)S(1)}, u32[]{:S(2)}, u32[]{:S(2)}) async-start(bf16[4,256,256]{2,1,0:T(8,128)(2,1)} %get-tuple-element.60), calls=%async_computation | async-start | bytes 1048576 | tf_op jit(solution)/shard_map/all_to_all | solution.py:425
  49.1 3.7 %collective-permute-start.11 = (bf16[128,1024]{1,0:T(8,128)(2,1)S(1)}, bf16[128,1024]{1,0:T(8,128)(2,1)S(1)}, u32[]{:S(2)}, u32[]{:S(2)}) collective-permute-start(bf16[128,1024]{1,0:T(8,128)(2,1)S(1)} %get-tuple-element.61.a0), channel_id=1, source_target_pairs={{0,1},{1,0},{2,3},{3,2},{4,5},{5,4},{6,7},{7,6},{8,9},{9,8},{10,11... | collective-permute-start | bytes 786440 | tf_op jit(solution)/shard_map/ppermute | solution.py:388
  53.3 5.9 %collective-permute-start.15 = (bf16[256,256]{1,0:T(8,128)(2,1)S(1)}, bf16[256,256]{1,0:T(8,128)(2,1)S(1)}, u32[]{:S(2)}, u32[]{:S(2)}) collective-permute-start(bf16[256,256]{1,0:T(8,128)(2,1)S(1)} %get-tuple-element.65), channel_id=1, source_target_pairs={{2,0},{4,2},{6,4},{8,6},{10,8},{12,10},{14,12},{16,14},{18,16},{20... | collective-permute-start | bytes 393224 | tf_op jit(solution)/shard_map/ppermute | solution.py:380
  59.3 2.2 %collective-permute-start.16 = (bf16[128,256]{1,0:T(8,128)(2,1)}, bf16[128,256]{1,0:T(8,128)(2,1)S(1)}, u32[]{:S(2)}, u32[]{:S(2)}) collective-permute-start(bf16[128,256]{1,0:T(8,128)(2,1)} %copy-done.7), channel_id=1, source_target_pairs={{4,0},{6,2},{8,4},{10,6},{12,8},{14,10},{16,12},{18,14},{20,16},{2... | collective-permute-start | bytes 196616 | tf_op jit(solution)/shard_map/ppermute | solution.py:380
  61.5 3.3 %weight_gradient.1 = bf16[1024,256]{1,0:T(8,128)(2,1)} custom-call(s32[3]{0:T(128)S(1)} %pad_add_fusion.ids, bf16[4,256,256]{2,1,0:T(8,128)(2,1)S(1)} %all-to-all-done.grads, bf16[128,1024]{1,0:T(8,128)(2,1)S(1)} %get-tuple-element.61.a0, bf16[128,1024]{1,0:T(8,128)(2,1)S(1)} %collective-permute-done.7.a1, bf16[128,1024]{1,0:T(8,128)(2,1)S(1)} %collective-permute-done.8.a2, ...), custom_call_target="tpu_custom_call" | custom-call | flops 536870912 | bytes 3145728 | tf_op jit(solution)/shard_map/weight_gradient/pallas_call | solution.py:336
  64.8 1.2 %collective-permute-done.16.r2 = bf16[128,256]{1,0:T(8,128)(2,1)S(1)} collective-permute-done((bf16[128,256]{1,0:T(8,128)(2,1)}, bf16[128,256]{1,0:T(8,128)(2,1)S(1)}, u32[]{:S(2)}, u32[]{:S(2)}) %collective-permute-start.16) | collective-permute-done | bytes 65568 | tf_op jit(solution)/shard_map/ppermute | solution.py:380
  66.0 20.0 %all-to-all-start.1 = ((bf16[32,32,256]{2,1,0:T(8,128)(2,1)}), bf16[32,32,256]{2,1,0:T(8,128)(2,1)S(1)}, u32[]{:S(2)}, u32[]{:S(2)}) async-start(bf16[32,32,256]{2,1,0:T(8,128)(2,1)} %bitcast.9), calls=%async_computation.1 | async-start | bytes 1048576 | tf_op jit(solution)/shard_map/all_to_all | solution.py:428
  86.0 1.4 %collective-permute-start.17 = (bf16[128,1024]{1,0:T(8,128)(2,1)}, bf16[128,1024]{1,0:T(8,128)(2,1)S(1)}, u32[]{:S(2)}, u32[]{:S(2)}) collective-permute-start(bf16[128,1024]{1,0:T(8,128)(2,1)} %copy-done.6), channel_id=1, source_target_pairs={{0,1},{1,0},{2,3},{3,2},{4,5},{5,4},{6,7},{7,6},{8,9},{9,8},{10,11... | collective-permute-start | bytes 786440 | tf_op jit(solution)/shard_map/ppermute | solution.py:388
  89.5 1.5 %join_outputs.1 = (bf16[128,2048]{1,0:T(8,128)(2,1)}, bf16[128,512]{1,0:T(8,128)(2,1)}, bf16[128,512]{1,0:T(8,128)(2,1)}) custom-call(s32[3]{0:T(128)S(1)} %pad_add_fusion.ids, bf16[128,1024]{1,0:T(8,128)(2,1)S(1)} %get-tuple-element.68.refs_0_, bf16[128,256]{1,0:T(8,128)(2,1)S(1)} %get-tuple-element.72.refs_1_, ...), custom_call_target="tpu_custom_call" | custom-call | bytes 524288 | tf_op jit(solution)/shard_map/join_outputs/pallas_call | solution.py:308
  90.9 11.0 %all-to-all-done.1.in_ref = bf16[32,32,256]{2,1,0:T(8,128)(2,1)S(1)} async-done(((bf16[32,32,256]{2,1,0:T(8,128)(2,1)}), bf16[32,32,256]{2,1,0:T(8,128)(2,1)S(1)}, u32[]{:S(2)}, u32[]{:S(2)}) %all-to-all-start.1) | async-done | bytes 524320 | tf_op jit(solution)/shard_map/all_to_all | solution.py:428
  102.5 3.5 %collective-permute-start.20 = (f32[16,256]{1,0:T(8,128)S(1)}, f32[16,256]{1,0:T(8,128)S(1)}, u32[]{:S(2)}, u32[]{:S(2)}) collective-permute-start(f32[16,256]{1,0:T(8,128)S(1)} %get-tuple-element.83), channel_id=1, source_target_pairs={{0,1},{1,0},{2,3},{3,2},{4,5},{5,4},{6,7},{7,6},{8,9},{9,8},{10,11... | collective-permute-start | bytes 49160 | tf_op jit(solution)/shard_map/ppermute | solution.py:388
  (55 shorter events, 11.7 us)
Async XLA Ops:
  0.6 18.2 %copy-start = (bf16[1,128,4096]{2,1,0:T(8,128)(2,1)S(1)}, bf16[1,128,4096]{2,1,0:T(8,128)(2,1)}, u32[]{:S(2)}) copy-start(bf16[1,128,4096]{2,1,0:T(8,128)(2,1)} %param.11) | copy-start | bytes 3145732
  0.6 14.7 %collective-permute-start = (bf16[128,2048]{1,0:T(8,128)(2,1)}, bf16[128,2048]{1,0:T(8,128)(2,1)S(1)}, u32[]{:S(2)}, u32[]{:S(2)}) collective-permute-start(bf16[128,2048]{1,0:T(8,128)(2,1)} %bitcast.14), channel_id=1, source_target_pairs={{0,1},{1,0},{2,3},{3,2},{4,5},{5,4},{6,7},{7,6},{8,9},{9,8},{10,11... | collective-permute-start | bytes 1572872 | tf_op jit(solution)/shard_map/ppermute | solution.py:388
  1.4 13.9 %collective-permute-start.1 = (bf16[128,2048]{1,0:T(8,128)(2,1)}, bf16[128,2048]{1,0:T(8,128)(2,1)S(1)}, u32[]{:S(2)}, u32[]{:S(2)}) collective-permute-start(bf16[128,2048]{1,0:T(8,128)(2,1)} %bitcast.16), channel_id=1, source_target_pairs={{0,1},{1,0},{2,3},{3,2},{4,5},{5,4},{6,7},{7,6},{8,9},{9,8},{10,11... | collective-permute-start | bytes 1572872 | tf_op jit(solution)/shard_map/ppermute | solution.py:388
  1.5 2.6 %collective-permute-start.2 = (bf16[128,512]{1,0:T(8,128)(2,1)}, bf16[128,512]{1,0:T(8,128)(2,1)S(1)}, u32[]{:S(2)}, u32[]{:S(2)}) collective-permute-start(bf16[128,512]{1,0:T(8,128)(2,1)} %bitcast.18), channel_id=1, source_target_pairs={{0,1},{1,0},{2,3},{3,2},{4,5},{5,4},{6,7},{7,6},{8,9},{9,8},{10,11... | collective-permute-start | bytes 393224 | tf_op jit(solution)/shard_map/ppermute | solution.py:388
  1.9 2.4 %collective-permute-start.3 = (bf16[128,512]{1,0:T(8,128)(2,1)}, bf16[128,512]{1,0:T(8,128)(2,1)S(1)}, u32[]{:S(2)}, u32[]{:S(2)}) collective-permute-start(bf16[128,512]{1,0:T(8,128)(2,1)} %bitcast.20), channel_id=1, source_target_pairs={{0,1},{1,0},{2,3},{3,2},{4,5},{5,4},{6,7},{7,6},{8,9},{9,8},{10,11... | collective-permute-start | bytes 393224 | tf_op jit(solution)/shard_map/ppermute | solution.py:388
  6.7 15.4 %collective-permute-start.5 = (bf16[256,512]{1,0:T(8,128)(2,1)S(1)}, bf16[256,512]{1,0:T(8,128)(2,1)S(1)}, u32[]{:S(2)}, u32[]{:S(2)}) collective-permute-start(bf16[256,512]{1,0:T(8,128)(2,1)S(1)} %get-tuple-element.49.k0.v0), channel_id=1, source_target_pairs={{0,2},{2,4},{4,6},{6,8},{8,10},{10,12},{12,14},{14,16},{16,18},{18... | collective-permute-start | bytes 786440 | tf_op jit(solution)/shard_map/ppermute | solution.py:380
  9.9 12.2 %collective-permute-start.4 = (bf16[128,512]{1,0:T(8,128)(2,1)S(1)}, bf16[128,512]{1,0:T(8,128)(2,1)S(1)}, u32[]{:S(2)}, u32[]{:S(2)}) collective-permute-start(bf16[128,512]{1,0:T(8,128)(2,1)S(1)} %get-tuple-element.48), channel_id=1, source_target_pairs={{0,4},{2,6},{4,8},{6,10},{8,12},{10,14},{12,16},{14,18},{16,20},{1... | collective-permute-start | bytes 393224 | tf_op jit(solution)/shard_map/ppermute | solution.py:380
  19.7 21.6 %collective-permute-start.7 = (bf16[128,1024]{1,0:T(8,128)(2,1)S(1)}, bf16[128,1024]{1,0:T(8,128)(2,1)S(1)}, u32[]{:S(2)}, u32[]{:S(2)}) collective-permute-start(bf16[128,1024]{1,0:T(8,128)(2,1)S(1)} %get-tuple-element.55), channel_id=1, source_target_pairs={{0,8},{8,16},{16,24},{24,0},{1,9},{9,17},{17,25},{25,1},{2,10},{10... | collective-permute-start | bytes 786440 | tf_op jit(solution)/shard_map/ppermute | solution.py:384
  20.0 21.3 %collective-permute-start.8 = (bf16[128,1024]{1,0:T(8,128)(2,1)S(1)}, bf16[128,1024]{1,0:T(8,128)(2,1)S(1)}, u32[]{:S(2)}, u32[]{:S(2)}) collective-permute-start(bf16[128,1024]{1,0:T(8,128)(2,1)S(1)} %get-tuple-element.56), channel_id=1, source_target_pairs={{0,16},{8,24},{16,0},{24,8},{1,17},{9,25},{17,1},{25,9},{2,18},{10... | collective-permute-start | bytes 786440 | tf_op jit(solution)/shard_map/ppermute | solution.py:384
  22.1 19.2 %collective-permute-start.9 = (bf16[128,1024]{1,0:T(8,128)(2,1)S(1)}, bf16[128,1024]{1,0:T(8,128)(2,1)S(1)}, u32[]{:S(2)}, u32[]{:S(2)}) collective-permute-start(bf16[128,1024]{1,0:T(8,128)(2,1)S(1)} %get-tuple-element.57), channel_id=1, source_target_pairs={{0,24},{8,0},{16,8},{24,16},{1,25},{9,1},{17,9},{25,17},{2,26},{10... | collective-permute-start | bytes 786440 | tf_op jit(solution)/shard_map/ppermute | solution.py:384
  25.3 16.0 %collective-permute-start.6 = (bf16[256,256]{1,0:T(8,128)(2,1)S(1)}, bf16[256,256]{1,0:T(8,128)(2,1)S(1)}, u32[]{:S(2)}, u32[]{:S(2)}) collective-permute-start(bf16[256,256]{1,0:T(8,128)(2,1)S(1)} %get-tuple-element.51), channel_id=1, source_target_pairs={{2,0},{4,2},{6,4},{8,6},{10,8},{12,10},{14,12},{16,14},{18,16},{20... | collective-permute-start | bytes 393224 | tf_op jit(solution)/shard_map/ppermute | solution.py:380
  34.9 6.5 %collective-permute-start.10 = (bf16[128,256]{1,0:T(8,128)(2,1)S(1)}, bf16[128,256]{1,0:T(8,128)(2,1)S(1)}, u32[]{:S(2)}, u32[]{:S(2)}) collective-permute-start(bf16[128,256]{1,0:T(8,128)(2,1)S(1)} %get-tuple-element.59), channel_id=1, source_target_pairs={{4,0},{6,2},{8,4},{10,6},{12,8},{14,10},{16,12},{18,14},{20,16},{2... | collective-permute-start | bytes 196616 | tf_op jit(solution)/shard_map/ppermute | solution.py:380
  43.4 18.1 %all-to-all-start = ((bf16[4,256,256]{2,1,0:T(8,128)(2,1)}), bf16[4,256,256]{2,1,0:T(8,128)(2,1)S(1)}, u32[]{:S(2)}, u32[]{:S(2)}) async-start(bf16[4,256,256]{2,1,0:T(8,128)(2,1)} %get-tuple-element.60), calls=%async_computation | async-start | bytes 1048576 | tf_op jit(solution)/shard_map/all_to_all | solution.py:425
  49.1 10.2 %collective-permute-start.11 = (bf16[128,1024]{1,0:T(8,128)(2,1)S(1)}, bf16[128,1024]{1,0:T(8,128)(2,1)S(1)}, u32[]{:S(2)}, u32[]{:S(2)}) collective-permute-start(bf16[128,1024]{1,0:T(8,128)(2,1)S(1)} %get-tuple-element.61.a0), channel_id=1, source_target_pairs={{0,1},{1,0},{2,3},{3,2},{4,5},{5,4},{6,7},{7,6},{8,9},{9,8},{10,11... | collective-permute-start | bytes 786440 | tf_op jit(solution)/shard_map/ppermute | solution.py:388
  52.8 8.7 %collective-permute-start.12 = (bf16[128,1024]{1,0:T(8,128)(2,1)S(1)}, bf16[128,1024]{1,0:T(8,128)(2,1)S(1)}, u32[]{:S(2)}, u32[]{:S(2)}) collective-permute-start(bf16[128,1024]{1,0:T(8,128)(2,1)S(1)} %collective-permute-done.7.a1), channel_id=1, source_target_pairs={{0,1},{1,0},{2,3},{3,2},{4,5},{5,4},{6,7},{7,6},{8,9},{9,8},{10,11... | collective-permute-start | bytes 786440 | tf_op jit(solution)/shard_map/ppermute | solution.py:388
  52.8 8.7 %collective-permute-start.13 = (bf16[128,1024]{1,0:T(8,128)(2,1)S(1)}, bf16[128,1024]{1,0:T(8,128)(2,1)S(1)}, u32[]{:S(2)}, u32[]{:S(2)}) collective-permute-start(bf16[128,1024]{1,0:T(8,128)(2,1)S(1)} %collective-permute-done.8.a2), channel_id=1, source_target_pairs={{0,1},{1,0},{2,3},{3,2},{4,5},{5,4},{6,7},{7,6},{8,9},{9,8},{10,11... | collective-permute-start | bytes 786440 | tf_op jit(solution)/shard_map/ppermute | solution.py:388
  53.3 8.2 %collective-permute-start.14 = (bf16[128,1024]{1,0:T(8,128)(2,1)S(1)}, bf16[128,1024]{1,0:T(8,128)(2,1)S(1)}, u32[]{:S(2)}, u32[]{:S(2)}) collective-permute-start(bf16[128,1024]{1,0:T(8,128)(2,1)S(1)} %collective-permute-done.9.a3), channel_id=1, source_target_pairs={{0,1},{1,0},{2,3},{3,2},{4,5},{5,4},{6,7},{7,6},{8,9},{9,8},{10,11... | collective-permute-start | bytes 786440 | tf_op jit(solution)/shard_map/ppermute | solution.py:388
  53.3 12.6 %collective-permute-start.15 = (bf16[256,256]{1,0:T(8,128)(2,1)S(1)}, bf16[256,256]{1,0:T(8,128)(2,1)S(1)}, u32[]{:S(2)}, u32[]{:S(2)}) collective-permute-start(bf16[256,256]{1,0:T(8,128)(2,1)S(1)} %get-tuple-element.65), channel_id=1, source_target_pairs={{2,0},{4,2},{6,4},{8,6},{10,8},{12,10},{14,12},{16,14},{18,16},{20... | collective-permute-start | bytes 393224 | tf_op jit(solution)/shard_map/ppermute | solution.py:380
  59.3 6.7 %collective-permute-start.16 = (bf16[128,256]{1,0:T(8,128)(2,1)}, bf16[128,256]{1,0:T(8,128)(2,1)S(1)}, u32[]{:S(2)}, u32[]{:S(2)}) collective-permute-start(bf16[128,256]{1,0:T(8,128)(2,1)} %copy-done.7), channel_id=1, source_target_pairs={{4,0},{6,2},{8,4},{10,6},{12,8},{14,10},{16,12},{18,14},{20,16},{2... | collective-permute-start | bytes 196616 | tf_op jit(solution)/shard_map/ppermute | solution.py:380
  66.0 35.9 %all-to-all-start.1 = ((bf16[32,32,256]{2,1,0:T(8,128)(2,1)}), bf16[32,32,256]{2,1,0:T(8,128)(2,1)S(1)}, u32[]{:S(2)}, u32[]{:S(2)}) async-start(bf16[32,32,256]{2,1,0:T(8,128)(2,1)} %bitcast.9), calls=%async_computation.1 | async-start | bytes 1048576 | tf_op jit(solution)/shard_map/all_to_all | solution.py:428
  86.0 2.9 %collective-permute-start.17 = (bf16[128,1024]{1,0:T(8,128)(2,1)}, bf16[128,1024]{1,0:T(8,128)(2,1)S(1)}, u32[]{:S(2)}, u32[]{:S(2)}) collective-permute-start(bf16[128,1024]{1,0:T(8,128)(2,1)} %copy-done.6), channel_id=1, source_target_pairs={{0,1},{1,0},{2,3},{3,2},{4,5},{5,4},{6,7},{7,6},{8,9},{9,8},{10,11... | collective-permute-start | bytes 786440 | tf_op jit(solution)/shard_map/ppermute | solution.py:388
  87.4 1.5 %collective-permute-start.19 = (bf16[128,256]{1,0:T(8,128)(2,1)}, bf16[128,256]{1,0:T(8,128)(2,1)S(1)}, u32[]{:S(2)}, u32[]{:S(2)}) collective-permute-start(bf16[128,256]{1,0:T(8,128)(2,1)} %copy-done.8), channel_id=1, source_target_pairs={{0,1},{1,0},{2,3},{3,2},{4,5},{5,4},{6,7},{7,6},{8,9},{9,8},{10,11... | collective-permute-start | bytes 196616 | tf_op jit(solution)/shard_map/ppermute | solution.py:388
  88.1 1.4 %collective-permute-start.18 = (bf16[128,256]{1,0:T(8,128)(2,1)S(1)}, bf16[128,256]{1,0:T(8,128)(2,1)S(1)}, u32[]{:S(2)}, u32[]{:S(2)}) collective-permute-start(bf16[128,256]{1,0:T(8,128)(2,1)S(1)} %get-tuple-element.75), channel_id=1, source_target_pairs={{0,1},{1,0},{2,3},{3,2},{4,5},{5,4},{6,7},{7,6},{8,9},{9,8},{10,11... | collective-permute-start | bytes 196616 | tf_op jit(solution)/shard_map/ppermute | solution.py:388
  102.5 4.4 %collective-permute-start.20 = (f32[16,256]{1,0:T(8,128)S(1)}, f32[16,256]{1,0:T(8,128)S(1)}, u32[]{:S(2)}, u32[]{:S(2)}) collective-permute-start(f32[16,256]{1,0:T(8,128)S(1)} %get-tuple-element.83), channel_id=1, source_target_pairs={{0,1},{1,0},{2,3},{3,2},{4,5},{5,4},{6,7},{7,6},{8,9},{9,8},{10,11... | collective-permute-start | bytes 49160 | tf_op jit(solution)/shard_map/ppermute | solution.py:388
  (8 other events, 7.4 us)

commit v7 on v5

--- a/solution.py
+++ b/solution.py
@@ -417,6 +417,8 @@
         grad,
         swap_core(grad),
     )
+    bias, value0 = lax.optimization_barrier((bias, value0))
+    values = [far2, shift_chips(value0, 1), value0]
 
     bias, inputs = lax.optimization_barrier((bias, inputs))
     packed = pack_call(ids, inputs)
@@ -425,15 +427,12 @@
     prob, value_own, value_t1, value_t2 = forward_call(bias, queries, grads, keys)
     value_r2 = shift_chips(value_t2, -2)
     value_r1 = shift_chips(value_t1, -1)
-    value_own, value0 = lax.optimization_barrier((value_own, value0))
-    values = [far2, shift_chips(value0, 1), value0]
-    prob, *far = lax.optimization_barrier((prob, *own[1:]))
-    own = [own[0]] + far
-    other = [swap_core(block) for block in own]
     query_keep, query_send, key_own, key_t1, key_t2 = backward_call(
         ids, prob, queries, grads, keys, values
     )
-    value_r1, query_send = lax.optimization_barrier((value_r1, query_send))
+    value_r1, query_send, *far = lax.optimization_barrier((value_r1, query_send, *own[1:]))
+    own = [own[0]] + far
+    other = [swap_core(block) for block in own]
     value_keep, value_send, sent = total_call(ids, value_own, value_r1, value_r2, True)
     key_r2 = shift_chips(key_t2, -2)
     key_r1 = shift_chips(key_t1, -1)

time: 112 us -> 110 us (0.982)
  starting transfers between devices: 70.5 us -> 62.1 us
  waiting for transfers between devices: 16.5 us -> 22.4 us
  local copies, waits for them, and re-layouts: 5.46 us -> 6.7 us
    ppermute x7, starting transfers between devices: 35.3 us -> 30.2 us  [shift_chips(): return lax.ppermute(block, CHIP, route)]
    all_to_all x1, waiting for transfers between devices: 9.46 us -> 12.5 us  [shards(): lax.all_to_all(partial.reshape(32, 32, HALF), ('zl', 'zh', 'y'), 0, 0, ti...]
    ppermute x7, waiting for transfers between devices: 4.18 us -> 7.01 us  [shift_chips(): return lax.ppermute(block, CHIP, route)]
    ppermute x12, starting transfers between devices: 12.2 us -> 9.41 us  [swap_core(): return lax.ppermute(block, 'c', [(0, 1), (1, 0)])]
    unnamed x19, local copies, waits for them, and re-layouts: 5.33 us -> 6.57 us
  transfers between devices with their start and end apart: 24 -> 24, of which waited for: 7 -> 8; matrix products, arithmetic and copies ran while one was open for 1% -> 1% of each run, Pallas kernels for 13% -> 13%
where the time goes in v7:
time: 110 us
  starting transfers between devices  62.1 us (56%)
  waiting for transfers between devices  22.4 us (20%)
  Pallas kernels  17 us (15%)
  local copies, waits for them, and re-layouts  6.7 us (6%)
    ppermute x7, starting transfers between devices, shift_chips(): return lax.ppermute(block, CHIP, route)  30.2 us
    all_to_all x1, starting transfers between devices, shards(): lax.all_to_all(partial.reshape(32, 32, HALF), ('zl', 'zh', 'y'), 0, 0, ti...  15.9 us
    all_to_all x1, waiting for transfers between devices, shards(): lax.all_to_all(partial.reshape(32, 32, HALF), ('zl', 'zh', 'y'), 0, 0, ti...  12.5 us
    ppermute x12, starting transfers between devices, swap_core(): return lax.ppermute(block, 'c', [(0, 1), (1, 0)])  9.41 us
    ppermute x7, waiting for transfers between devices, shift_chips(): return lax.ppermute(block, CHIP, route)  7.01 us
    unnamed x19, local copies, waits for them, and re-layouts  6.57 us
    all_to_all x1, starting transfers between devices, shards(): gathered = lax.all_to_all(sent, 'x', 0, 0, tiled=True)  3.94 us
    pallas_call x1, Pallas kernels, backward_call(): pl.pallas_call(backward_kernel, grid_spec=pltpu.PrefetchScalarGridSpec(nu...  3.75 us
  transfers between devices with their start and end apart: 24, of which 8 were waited for; matrix products, arithmetic and copies ran while one was open for 1% of the time, Pallas kernels for 13%

profile of v7, /device:TPU:7, one launch (start us, length us, event | category | flops | bytes accessed | tf_op | source)
XLA Modules:
  0.0 109.9 jit_solution(16633267891318537503)
XLA Ops:
  1.5 1.1 %collective-permute-done.other = bf16[128,512]{1,0:T(8,128)(2,1)S(1)} collective-permute-done((bf16[128,512]{1,0:T(8,128)(2,1)}, bf16[128,512]{1,0:T(8,128)(2,1)S(1)}, u32[]{:S(2)}, u32[]{:S(2)}) %collective-permute-start) | collective-permute-done | bytes 131104 | tf_op jit(solution)/shard_map/ppermute | solution.py:396
  2.6 0.9 copy-done.3
  5.0 3.2 %collective-permute-start.5 = (bf16[256,256]{1,0:T(8,128)(2,1)S(1)}, bf16[256,256]{1,0:T(8,128)(2,1)S(1)}, u32[]{:S(2)}, u32[]{:S(2)}) collective-permute-start(bf16[256,256]{1,0:T(8,128)(2,1)S(1)} %pick_keys.1.keys.k0), channel_id=1, source_target_pairs={{0,2},{2,4},{4,6},{6,8},{8,10},{10,12},{12,14},{14,16},{16,18},{18... | collective-permute-start | bytes 393224 | tf_op jit(solution)/shard_map/ppermute | solution.py:388
  9.7 4.5 %collective-permute-start.4 = (bf16[128,512]{1,0:T(8,128)(2,1)S(1)}, bf16[128,512]{1,0:T(8,128)(2,1)S(1)}, u32[]{:S(2)}, u32[]{:S(2)}) collective-permute-start(bf16[128,512]{1,0:T(8,128)(2,1)S(1)} %get-tuple-element.64), channel_id=1, source_target_pairs={{0,4},{2,6},{4,8},{6,10},{8,12},{10,14},{12,16},{14,18},{16,20},{1... | collective-permute-start | bytes 393224 | tf_op jit(solution)/shard_map/ppermute | solution.py:388
  15.2 1.0 copy-done.1
  16.2 1.0 copy-done.2
  20.1 2.1 %collective-permute-start.8 = (bf16[128,1024]{1,0:T(8,128)(2,1)S(1)}, bf16[128,1024]{1,0:T(8,128)(2,1)S(1)}, u32[]{:S(2)}, u32[]{:S(2)}) collective-permute-start(bf16[128,1024]{1,0:T(8,128)(2,1)S(1)} %get-tuple-element.71), channel_id=1, source_target_pairs={{0,8},{8,16},{16,24},{24,0},{1,9},{9,17},{17,25},{25,1},{2,10},{10... | collective-permute-start | bytes 786440 | tf_op jit(solution)/shard_map/ppermute | solution.py:392
  22.3 7.8 %collective-permute-start.7 = (bf16[256,256]{1,0:T(8,128)(2,1)S(1)}, bf16[256,256]{1,0:T(8,128)(2,1)S(1)}, u32[]{:S(2)}, u32[]{:S(2)}) collective-permute-start(bf16[256,256]{1,0:T(8,128)(2,1)S(1)} %get-tuple-element.68.v0), channel_id=1, source_target_pairs={{0,2},{2,4},{4,6},{6,8},{8,10},{10,12},{12,14},{14,16},{16,18},{18... | collective-permute-start | bytes 393224 | tf_op jit(solution)/shard_map/ppermute | solution.py:388
  30.1 3.3 %forward_and_value_gradient.1 = (bf16[2,2,512,512]{3,2,1,0:T(8,128)(2,1)S(1)}, f32[256,256]{1,0:T(8,128)S(1)}, bf16[256,256]{1,0:T(8,128)(2,1)S(1)}, bf16[128,256]{1,0:T(8,128)(2,1)S(1)}) custom-call(f32[2,512,128]{2,1,0:T(8,128)S(1)} %get-tuple-element.61.bias, bf16[256,1024]{1,0:T(8,128)(2,1)S(1)} %get-tuple-element.62.q_ref, ...), custom_call_target="tpu_custom_call" | custom-call | flops 536870912 | bytes 6291456 | tf_op jit(solution)/shard_map/forward_and_value_gradient/pallas_call | solution.py:215
  33.3 3.9 %collective-permute-start.6 = (bf16[256,256]{1,0:T(8,128)(2,1)S(1)}, bf16[256,256]{1,0:T(8,128)(2,1)S(1)}, u32[]{:S(2)}, u32[]{:S(2)}) collective-permute-start(bf16[256,256]{1,0:T(8,128)(2,1)S(1)} %get-tuple-element.66), channel_id=1, source_target_pairs={{2,0},{4,2},{6,4},{8,6},{10,8},{12,10},{14,12},{16,14},{18,16},{20... | collective-permute-start | bytes 393224 | tf_op jit(solution)/shard_map/ppermute | solution.py:388
  37.3 5.3 %collective-permute-done.7.v1 = bf16[256,256]{1,0:T(8,128)(2,1)S(1)} collective-permute-done((bf16[256,256]{1,0:T(8,128)(2,1)S(1)}, bf16[256,256]{1,0:T(8,128)(2,1)S(1)}, u32[]{:S(2)}, u32[]{:S(2)}) %collective-permute-start.7) | collective-permute-done | bytes 131104 | tf_op jit(solution)/shard_map/ppermute | solution.py:388
  42.6 1.9 %collective-permute-start.11 = (bf16[128,256]{1,0:T(8,128)(2,1)S(1)}, bf16[128,256]{1,0:T(8,128)(2,1)S(1)}, u32[]{:S(2)}, u32[]{:S(2)}) collective-permute-start(bf16[128,256]{1,0:T(8,128)(2,1)S(1)} %get-tuple-element.75), channel_id=1, source_target_pairs={{4,0},{6,2},{8,4},{10,6},{12,8},{14,10},{16,12},{18,14},{20,16},{2... | collective-permute-start | bytes 196616 | tf_op jit(solution)/shard_map/ppermute | solution.py:388
  44.5 3.8 %query_and_key_gradient.1 = (bf16[128,1024]{1,0:T(8,128)(2,1)S(1)}, bf16[128,1024]{1,0:T(8,128)(2,1)S(1)}, f32[256,256]{1,0:T(8,128)S(1)}, bf16[256,256]{1,0:T(8,128)(2,1)S(1)}, bf16[128,256]{1,0:T(8,128)(2,1)S(1)}) custom-call(s32[3]{0:T(128)S(1)} %pad_add_fusion.ids, bf16[2,2,512,512]{3,2,1,0:T(8,128)(2,1)S(1)} %get-tuple-element.67.prob_ref, ...), custom_call_target="tpu_custom_call" | custom-call | flops 805306368 | bytes 6291456 | tf_op jit(solution)/shard_map/query_and_key_gradient/pallas_call | solution.py:230
  49.1 1.4 %value_gradient_total.1 = (bf16[128,256]{1,0:T(8,128)(2,1)S(1)}, bf16[128,256]{1,0:T(8,128)(2,1)S(1)}, bf16[4,256,256]{2,1,0:T(8,128)(2,1)}) custom-call(s32[3]{0:T(128)S(1)} %pad_add_fusion.ids, f32[256,256]{1,0:T(8,128)S(1)} %get-tuple-element.65.own, bf16[256,256]{1,0:T(8,128)(2,1)S(1)} %collective-permute-done.6.r1, ...), custom_call_target="tpu_custom_call" | custom-call | bytes 1048576 | tf_op jit(solution)/shard_map/value_gradient_total/pallas_call | solution.py:290
  51.1 3.9 %all-to-all-start = ((bf16[4,256,256]{2,1,0:T(8,128)(2,1)}), bf16[4,256,256]{2,1,0:T(8,128)(2,1)S(1)}, u32[]{:S(2)}, u32[]{:S(2)}) async-start(bf16[4,256,256]{2,1,0:T(8,128)(2,1)} %get-tuple-element.76), calls=%async_computation | async-start | bytes 1048576 | tf_op jit(solution)/shard_map/all_to_all | solution.py:439
  55.1 3.3 %collective-permute-start.12 = (bf16[128,1024]{1,0:T(8,128)(2,1)S(1)}, bf16[128,1024]{1,0:T(8,128)(2,1)S(1)}, u32[]{:S(2)}, u32[]{:S(2)}) collective-permute-start(bf16[128,1024]{1,0:T(8,128)(2,1)S(1)} %get-tuple-element.77.a0), channel_id=1, source_target_pairs={{0,1},{1,0},{2,3},{3,2},{4,5},{5,4},{6,7},{7,6},{8,9},{9,8},{10,11... | collective-permute-start | bytes 786440 | tf_op jit(solution)/shard_map/ppermute | solution.py:396
  58.9 6.9 %collective-permute-start.16 = (bf16[256,256]{1,0:T(8,128)(2,1)S(1)}, bf16[256,256]{1,0:T(8,128)(2,1)S(1)}, u32[]{:S(2)}, u32[]{:S(2)}) collective-permute-start(bf16[256,256]{1,0:T(8,128)(2,1)S(1)} %get-tuple-element.81), channel_id=1, source_target_pairs={{2,0},{4,2},{6,4},{8,6},{10,8},{12,10},{14,12},{16,14},{18,16},{20... | collective-permute-start | bytes 393224 | tf_op jit(solution)/shard_map/ppermute | solution.py:388
  65.8 1.9 %collective-permute-start.17 = (bf16[128,256]{1,0:T(8,128)(2,1)}, bf16[128,256]{1,0:T(8,128)(2,1)S(1)}, u32[]{:S(2)}, u32[]{:S(2)}) collective-permute-start(bf16[128,256]{1,0:T(8,128)(2,1)} %copy-done.7), channel_id=1, source_target_pairs={{4,0},{6,2},{8,4},{10,6},{12,8},{14,10},{16,12},{18,14},{20,16},{2... | collective-permute-start | bytes 196616 | tf_op jit(solution)/shard_map/ppermute | solution.py:388
  67.8 3.2 %weight_gradient.1 = bf16[1024,256]{1,0:T(8,128)(2,1)} custom-call(s32[3]{0:T(128)S(1)} %pad_add_fusion.ids, bf16[4,256,256]{2,1,0:T(8,128)(2,1)S(1)} %all-to-all-done.grads, bf16[128,1024]{1,0:T(8,128)(2,1)S(1)} %get-tuple-element.77.a0, bf16[128,1024]{1,0:T(8,128)(2,1)S(1)} %collective-permute-done.8.a1, bf16[128,1024]{1,0:T(8,128)(2,1)S(1)} %collective-permute-done.9.a2, ...), custom_call_target="tpu_custom_call" | custom-call | flops 536870912 | bytes 3145728 | tf_op jit(solution)/shard_map/weight_gradient/pallas_call | solution.py:344
  71.0 1.5 %collective-permute-done.17.r2 = bf16[128,256]{1,0:T(8,128)(2,1)S(1)} collective-permute-done((bf16[128,256]{1,0:T(8,128)(2,1)}, bf16[128,256]{1,0:T(8,128)(2,1)S(1)}, u32[]{:S(2)}, u32[]{:S(2)}) %collective-permute-start.17) | collective-permute-done | bytes 65568 | tf_op jit(solution)/shard_map/ppermute | solution.py:388
  72.5 15.9 %all-to-all-start.1 = ((bf16[32,32,256]{2,1,0:T(8,128)(2,1)}), bf16[32,32,256]{2,1,0:T(8,128)(2,1)S(1)}, u32[]{:S(2)}, u32[]{:S(2)}) async-start(bf16[32,32,256]{2,1,0:T(8,128)(2,1)} %bitcast.9), calls=%async_computation.1 | async-start | bytes 1048576 | tf_op jit(solution)/shard_map/all_to_all | solution.py:442
  91.4 1.5 %join_outputs.1 = (bf16[128,2048]{1,0:T(8,128)(2,1)}, bf16[128,512]{1,0:T(8,128)(2,1)}, bf16[128,512]{1,0:T(8,128)(2,1)}) custom-call(s32[3]{0:T(128)S(1)} %pad_add_fusion.ids, bf16[128,1024]{1,0:T(8,128)(2,1)S(1)} %get-tuple-element.84.refs_0_, bf16[128,256]{1,0:T(8,128)(2,1)S(1)} %get-tuple-element.88.refs_1_, ...), custom_call_target="tpu_custom_call" | custom-call | bytes 524288 | tf_op jit(solution)/shard_map/join_outputs/pallas_call | solution.py:316
  92.8 12.5 %all-to-all-done.1.in_ref = bf16[32,32,256]{2,1,0:T(8,128)(2,1)S(1)} async-done(((bf16[32,32,256]{2,1,0:T(8,128)(2,1)}), bf16[32,32,256]{2,1,0:T(8,128)(2,1)S(1)}, u32[]{:S(2)}, u32[]{:S(2)}) %all-to-all-start.1) | async-done | bytes 524320 | tf_op jit(solution)/shard_map/all_to_all | solution.py:442
  106.0 2.4 %collective-permute-start.21 = (f32[16,256]{1,0:T(8,128)S(1)}, f32[16,256]{1,0:T(8,128)S(1)}, u32[]{:S(2)}, u32[]{:S(2)}) collective-permute-start(f32[16,256]{1,0:T(8,128)S(1)} %get-tuple-element.99), channel_id=1, source_target_pairs={{0,1},{1,0},{2,3},{3,2},{4,5},{5,4},{6,7},{7,6},{8,9},{9,8},{10,11... | collective-permute-start | bytes 49160 | tf_op jit(solution)/shard_map/ppermute | solution.py:396
  (58 shorter events, 14.6 us)
Async XLA Ops:
  0.6 2.0 %collective-permute-start = (bf16[128,512]{1,0:T(8,128)(2,1)}, bf16[128,512]{1,0:T(8,128)(2,1)S(1)}, u32[]{:S(2)}, u32[]{:S(2)}) collective-permute-start(bf16[128,512]{1,0:T(8,128)(2,1)} %bitcast.18), channel_id=1, source_target_pairs={{0,1},{1,0},{2,3},{3,2},{4,5},{5,4},{6,7},{7,6},{8,9},{9,8},{10,11... | collective-permute-start | bytes 393224 | tf_op jit(solution)/shard_map/ppermute | solution.py:396
  4.1 11.1 %collective-permute-start.1 = (bf16[128,2048]{1,0:T(8,128)(2,1)}, bf16[128,2048]{1,0:T(8,128)(2,1)S(1)}, u32[]{:S(2)}, u32[]{:S(2)}) collective-permute-start(bf16[128,2048]{1,0:T(8,128)(2,1)} %bitcast.14), channel_id=1, source_target_pairs={{0,1},{1,0},{2,3},{3,2},{4,5},{5,4},{6,7},{7,6},{8,9},{9,8},{10,11... | collective-permute-start | bytes 1572872 | tf_op jit(solution)/shard_map/ppermute | solution.py:396
  4.5 10.7 %collective-permute-start.2 = (bf16[128,2048]{1,0:T(8,128)(2,1)}, bf16[128,2048]{1,0:T(8,128)(2,1)S(1)}, u32[]{:S(2)}, u32[]{:S(2)}) collective-permute-start(bf16[128,2048]{1,0:T(8,128)(2,1)} %bitcast.16), channel_id=1, source_target_pairs={{0,1},{1,0},{2,3},{3,2},{4,5},{5,4},{6,7},{7,6},{8,9},{9,8},{10,11... | collective-permute-start | bytes 1572872 | tf_op jit(solution)/shard_map/ppermute | solution.py:396
  4.7 3.6 %collective-permute-start.3 = (bf16[128,512]{1,0:T(8,128)(2,1)}, bf16[128,512]{1,0:T(8,128)(2,1)S(1)}, u32[]{:S(2)}, u32[]{:S(2)}) collective-permute-start(bf16[128,512]{1,0:T(8,128)(2,1)} %bitcast.20), channel_id=1, source_target_pairs={{0,1},{1,0},{2,3},{3,2},{4,5},{5,4},{6,7},{7,6},{8,9},{9,8},{10,11... | collective-permute-start | bytes 393224 | tf_op jit(solution)/shard_map/ppermute | solution.py:396
  5.0 17.2 %collective-permute-start.5 = (bf16[256,256]{1,0:T(8,128)(2,1)S(1)}, bf16[256,256]{1,0:T(8,128)(2,1)S(1)}, u32[]{:S(2)}, u32[]{:S(2)}) collective-permute-start(bf16[256,256]{1,0:T(8,128)(2,1)S(1)} %pick_keys.1.keys.k0), channel_id=1, source_target_pairs={{0,2},{2,4},{4,6},{6,8},{8,10},{10,12},{12,14},{14,16},{16,18},{18... | collective-permute-start | bytes 393224 | tf_op jit(solution)/shard_map/ppermute | solution.py:388
  9.7 20.3 %collective-permute-start.4 = (bf16[128,512]{1,0:T(8,128)(2,1)S(1)}, bf16[128,512]{1,0:T(8,128)(2,1)S(1)}, u32[]{:S(2)}, u32[]{:S(2)}) collective-permute-start(bf16[128,512]{1,0:T(8,128)(2,1)S(1)} %get-tuple-element.64), channel_id=1, source_target_pairs={{0,4},{2,6},{4,8},{6,10},{8,12},{10,14},{12,16},{14,18},{16,20},{1... | collective-permute-start | bytes 393224 | tf_op jit(solution)/shard_map/ppermute | solution.py:388
  19.5 29.4 %collective-permute-start.10 = (bf16[128,1024]{1,0:T(8,128)(2,1)S(1)}, bf16[128,1024]{1,0:T(8,128)(2,1)S(1)}, u32[]{:S(2)}, u32[]{:S(2)}) collective-permute-start(bf16[128,1024]{1,0:T(8,128)(2,1)S(1)} %get-tuple-element.73), channel_id=1, source_target_pairs={{0,24},{8,0},{16,8},{24,16},{1,25},{9,1},{17,9},{25,17},{2,26},{10... | collective-permute-start | bytes 786440 | tf_op jit(solution)/shard_map/ppermute | solution.py:392
  20.1 28.8 %collective-permute-start.8 = (bf16[128,1024]{1,0:T(8,128)(2,1)S(1)}, bf16[128,1024]{1,0:T(8,128)(2,1)S(1)}, u32[]{:S(2)}, u32[]{:S(2)}) collective-permute-start(bf16[128,1024]{1,0:T(8,128)(2,1)S(1)} %get-tuple-element.71), channel_id=1, source_target_pairs={{0,8},{8,16},{16,24},{24,0},{1,9},{9,17},{17,25},{25,1},{2,10},{10... | collective-permute-start | bytes 786440 | tf_op jit(solution)/shard_map/ppermute | solution.py:392
  22.3 26.7 %collective-permute-start.9 = (bf16[128,1024]{1,0:T(8,128)(2,1)S(1)}, bf16[128,1024]{1,0:T(8,128)(2,1)S(1)}, u32[]{:S(2)}, u32[]{:S(2)}) collective-permute-start(bf16[128,1024]{1,0:T(8,128)(2,1)S(1)} %get-tuple-element.72), channel_id=1, source_target_pairs={{0,16},{8,24},{16,0},{24,8},{1,17},{9,25},{17,1},{25,9},{2,18},{10... | collective-permute-start | bytes 786440 | tf_op jit(solution)/shard_map/ppermute | solution.py:392
  22.3 20.3 %collective-permute-start.7 = (bf16[256,256]{1,0:T(8,128)(2,1)S(1)}, bf16[256,256]{1,0:T(8,128)(2,1)S(1)}, u32[]{:S(2)}, u32[]{:S(2)}) collective-permute-start(bf16[256,256]{1,0:T(8,128)(2,1)S(1)} %get-tuple-element.68.v0), channel_id=1, source_target_pairs={{0,2},{2,4},{4,6},{6,8},{8,10},{10,12},{12,14},{14,16},{16,18},{18... | collective-permute-start | bytes 393224 | tf_op jit(solution)/shard_map/ppermute | solution.py:388
  33.3 15.6 %collective-permute-start.6 = (bf16[256,256]{1,0:T(8,128)(2,1)S(1)}, bf16[256,256]{1,0:T(8,128)(2,1)S(1)}, u32[]{:S(2)}, u32[]{:S(2)}) collective-permute-start(bf16[256,256]{1,0:T(8,128)(2,1)S(1)} %get-tuple-element.66), channel_id=1, source_target_pairs={{2,0},{4,2},{6,4},{8,6},{10,8},{12,10},{14,12},{16,14},{18,16},{20... | collective-permute-start | bytes 393224 | tf_op jit(solution)/shard_map/ppermute | solution.py:388
  42.6 6.5 %collective-permute-start.11 = (bf16[128,256]{1,0:T(8,128)(2,1)S(1)}, bf16[128,256]{1,0:T(8,128)(2,1)S(1)}, u32[]{:S(2)}, u32[]{:S(2)}) collective-permute-start(bf16[128,256]{1,0:T(8,128)(2,1)S(1)} %get-tuple-element.75), channel_id=1, source_target_pairs={{4,0},{6,2},{8,4},{10,6},{12,8},{14,10},{16,12},{18,14},{20,16},{2... | collective-permute-start | bytes 196616 | tf_op jit(solution)/shard_map/ppermute | solution.py:388
  51.1 16.6 %all-to-all-start = ((bf16[4,256,256]{2,1,0:T(8,128)(2,1)}), bf16[4,256,256]{2,1,0:T(8,128)(2,1)S(1)}, u32[]{:S(2)}, u32[]{:S(2)}) async-start(bf16[4,256,256]{2,1,0:T(8,128)(2,1)} %get-tuple-element.76), calls=%async_computation | async-start | bytes 1048576 | tf_op jit(solution)/shard_map/all_to_all | solution.py:439
  55.1 10.7 %collective-permute-start.12 = (bf16[128,1024]{1,0:T(8,128)(2,1)S(1)}, bf16[128,1024]{1,0:T(8,128)(2,1)S(1)}, u32[]{:S(2)}, u32[]{:S(2)}) collective-permute-start(bf16[128,1024]{1,0:T(8,128)(2,1)S(1)} %get-tuple-element.77.a0), channel_id=1, source_target_pairs={{0,1},{1,0},{2,3},{3,2},{4,5},{5,4},{6,7},{7,6},{8,9},{9,8},{10,11... | collective-permute-start | bytes 786440 | tf_op jit(solution)/shard_map/ppermute | solution.py:396
  58.4 9.4 %collective-permute-start.13 = (bf16[128,1024]{1,0:T(8,128)(2,1)S(1)}, bf16[128,1024]{1,0:T(8,128)(2,1)S(1)}, u32[]{:S(2)}, u32[]{:S(2)}) collective-permute-start(bf16[128,1024]{1,0:T(8,128)(2,1)S(1)} %collective-permute-done.8.a1), channel_id=1, source_target_pairs={{0,1},{1,0},{2,3},{3,2},{4,5},{5,4},{6,7},{7,6},{8,9},{9,8},{10,11... | collective-permute-start | bytes 786440 | tf_op jit(solution)/shard_map/ppermute | solution.py:396
  58.4 9.4 %collective-permute-start.14 = (bf16[128,1024]{1,0:T(8,128)(2,1)S(1)}, bf16[128,1024]{1,0:T(8,128)(2,1)S(1)}, u32[]{:S(2)}, u32[]{:S(2)}) collective-permute-start(bf16[128,1024]{1,0:T(8,128)(2,1)S(1)} %collective-permute-done.9.a2), channel_id=1, source_target_pairs={{0,1},{1,0},{2,3},{3,2},{4,5},{5,4},{6,7},{7,6},{8,9},{9,8},{10,11... | collective-permute-start | bytes 786440 | tf_op jit(solution)/shard_map/ppermute | solution.py:396
  58.9 8.9 %collective-permute-start.15 = (bf16[128,1024]{1,0:T(8,128)(2,1)S(1)}, bf16[128,1024]{1,0:T(8,128)(2,1)S(1)}, u32[]{:S(2)}, u32[]{:S(2)}) collective-permute-start(bf16[128,1024]{1,0:T(8,128)(2,1)S(1)} %collective-permute-done.10.a3), channel_id=1, source_target_pairs={{0,1},{1,0},{2,3},{3,2},{4,5},{5,4},{6,7},{7,6},{8,9},{9,8},{10,11... | collective-permute-start | bytes 786440 | tf_op jit(solution)/shard_map/ppermute | solution.py:396
  58.9 13.6 %collective-permute-start.16 = (bf16[256,256]{1,0:T(8,128)(2,1)S(1)}, bf16[256,256]{1,0:T(8,128)(2,1)S(1)}, u32[]{:S(2)}, u32[]{:S(2)}) collective-permute-start(bf16[256,256]{1,0:T(8,128)(2,1)S(1)} %get-tuple-element.81), channel_id=1, source_target_pairs={{2,0},{4,2},{6,4},{8,6},{10,8},{12,10},{14,12},{16,14},{18,16},{20... | collective-permute-start | bytes 393224 | tf_op jit(solution)/shard_map/ppermute | solution.py:388
  65.8 6.7 %collective-permute-start.17 = (bf16[128,256]{1,0:T(8,128)(2,1)}, bf16[128,256]{1,0:T(8,128)(2,1)S(1)}, u32[]{:S(2)}, u32[]{:S(2)}) collective-permute-start(bf16[128,256]{1,0:T(8,128)(2,1)} %copy-done.7), channel_id=1, source_target_pairs={{4,0},{6,2},{8,4},{10,6},{12,8},{14,10},{16,12},{18,14},{20,16},{2... | collective-permute-start | bytes 196616 | tf_op jit(solution)/shard_map/ppermute | solution.py:388
  72.5 32.8 %all-to-all-start.1 = ((bf16[32,32,256]{2,1,0:T(8,128)(2,1)}), bf16[32,32,256]{2,1,0:T(8,128)(2,1)S(1)}, u32[]{:S(2)}, u32[]{:S(2)}) async-start(bf16[32,32,256]{2,1,0:T(8,128)(2,1)} %bitcast.9), calls=%async_computation.1 | async-start | bytes 1048576 | tf_op jit(solution)/shard_map/all_to_all | solution.py:442
  88.4 2.3 %collective-permute-start.18 = (bf16[128,1024]{1,0:T(8,128)(2,1)}, bf16[128,1024]{1,0:T(8,128)(2,1)S(1)}, u32[]{:S(2)}, u32[]{:S(2)}) collective-permute-start(bf16[128,1024]{1,0:T(8,128)(2,1)} %copy-done.6), channel_id=1, source_target_pairs={{0,1},{1,0},{2,3},{3,2},{4,5},{5,4},{6,7},{7,6},{8,9},{9,8},{10,11... | collective-permute-start | bytes 786440 | tf_op jit(solution)/shard_map/ppermute | solution.py:396
  89.3 1.5 %collective-permute-start.20 = (bf16[128,256]{1,0:T(8,128)(2,1)}, bf16[128,256]{1,0:T(8,128)(2,1)S(1)}, u32[]{:S(2)}, u32[]{:S(2)}) collective-permute-start(bf16[128,256]{1,0:T(8,128)(2,1)} %copy-done.8), channel_id=1, source_target_pairs={{0,1},{1,0},{2,3},{3,2},{4,5},{5,4},{6,7},{7,6},{8,9},{9,8},{10,11... | collective-permute-start | bytes 196616 | tf_op jit(solution)/shard_map/ppermute | solution.py:396
  90.0 1.4 %collective-permute-start.19 = (bf16[128,256]{1,0:T(8,128)(2,1)S(1)}, bf16[128,256]{1,0:T(8,128)(2,1)S(1)}, u32[]{:S(2)}, u32[]{:S(2)}) collective-permute-start(bf16[128,256]{1,0:T(8,128)(2,1)S(1)} %get-tuple-element.91), channel_id=1, source_target_pairs={{0,1},{1,0},{2,3},{3,2},{4,5},{5,4},{6,7},{7,6},{8,9},{9,8},{10,11... | collective-permute-start | bytes 196616 | tf_op jit(solution)/shard_map/ppermute | solution.py:396
  106.0 3.2 %collective-permute-start.21 = (f32[16,256]{1,0:T(8,128)S(1)}, f32[16,256]{1,0:T(8,128)S(1)}, u32[]{:S(2)}, u32[]{:S(2)}) collective-permute-start(f32[16,256]{1,0:T(8,128)S(1)} %get-tuple-element.99), channel_id=1, source_target_pairs={{0,1},{1,0},{2,3},{3,2},{4,5},{5,4},{6,7},{7,6},{8,9},{9,8},{10,11... | collective-permute-start | bytes 49160 | tf_op jit(solution)/shard_map/ppermute | solution.py:396
  (9 other events, 25.4 us)

commit v8 on v4

--- a/solution.py
+++ b/solution.py
@@ -25,6 +25,7 @@
 CTX = ("zh", "x", "y", "c")
 CHIP = ("zh", "x", "y")
 N_CHIP = 32
+N_SHARD = 64
 NSTART = 64
 MIB = 1024 * 1024
 PARAMS = pltpu.CompilerParams(vmem_limit_bytes=8 * MIB)
@@ -73,13 +74,14 @@
 
 def pick_call(ids, own, other, keys=None):
     half = pl.BlockSpec((ROWS, HALF), lambda i, ids: (0, ids[2]))
+    whole = pl.BlockSpec((ROWS, HALF), lambda i, ids: (0, 0))
     extra = [] if keys is None else [keys]
     return pl.pallas_call(
         pick_values_kernel if extra else pick_keys_kernel,
         grid_spec=pltpu.PrefetchScalarGridSpec(
             num_scalar_prefetch=1,
             grid=(1,),
-            in_specs=[half] * 2 + [WHOLE] * len(extra),
+            in_specs=[whole, half] + [WHOLE] * len(extra),
             out_specs=[WHOLE] * (1 + len(extra)),
         ),
         out_shape=[shape(2 * ROWS, HALF)] + [shape(ROWS, 2 * HALF)] * len(extra),
@@ -90,7 +92,7 @@
 
 
 def prepare_kernel(
-    ids, order, starts, q_own, q_other, g_own, g_other, bias_ref, queries_ref, grads_ref
+    ids, table, q_own, q_other, g_own, g_other, bias_ref, queries_ref, grads_ref
 ):
     put_rows(queries_ref, ids[2], q_own, q_other)
     put_rows(grads_ref, ids[2], g_own, g_other)
@@ -99,34 +101,40 @@
     row = lax.broadcasted_iota(jnp.int32, (STRETCH, ROWS), 0)
     for s in range(2):
         shard = base + s
-        stretch = jnp.where(lane < STRETCH, order[2 * shard], order[2 * shard + 1])
+        stretch = jnp.where(lane < STRETCH, table[2 * shard], table[2 * shard + 1])
         query_pos = shard * ROWS + stretch * STRETCH + (lane & (STRETCH - 1))
         begin = jnp.zeros((1, ROWS), jnp.int32)
         for i in range(NSTART):
-            begin = jnp.where(starts[i] <= query_pos, starts[i], begin)
+            start = table[2 * N_SHARD + i]
+            begin = jnp.where(start <= query_pos, start, begin)
         for d in range(SPAN):
             source = shard - (SPAN - 1) + d
             known = jnp.maximum(source, 0)
             for j in range(2):
-                key_pos = source * ROWS + order[2 * known + j] * STRETCH + row
+                key_pos = source * ROWS + table[2 * known + j] * STRETCH + row
                 allowed = (key_pos <= query_pos) & (key_pos >= begin)
                 bias_ref[s, (2 * d + j) * STRETCH : (2 * d + j + 1) * STRETCH, :] = jnp.where(
                     allowed, 0.0, MASKED
                 )
 
 
-def prepare_call(ids, order, starts, *blocks):
-    half = pl.BlockSpec((ROWS, GROUPS * WIDE), lambda i, ids, *_: (0, ids[2]))
+def prepare_call(ids, table, *blocks):
+    width = GROUPS * WIDE
+    own = pl.BlockSpec((ROWS, width), lambda i, *_: (0, 0))
+    other = pl.BlockSpec((ROWS, width), lambda i, ids, *_: (0, ids[2]))
     return pl.pallas_call(
         prepare_kernel,
         grid_spec=pltpu.PrefetchScalarGridSpec(
-            num_scalar_prefetch=3, grid=(1,), in_specs=[half] * 4, out_specs=[WHOLE] * 3
-        ),
-        out_shape=[shape(2, KEYS, ROWS, dtype=F32)] + [shape(2 * ROWS, GROUPS * WIDE)] * 2,
+            num_scalar_prefetch=2,
+            grid=(1,),
+            in_specs=[own, other] * 2,
+            out_specs=[WHOLE] * 3,
+        ),
+        out_shape=[shape(2, KEYS, ROWS, dtype=F32)] + [shape(2 * ROWS, width)] * 2,
         compiler_params=PARAMS,
         cost_estimate=cost(0, 2.5),
         name="prepare",
-    )(ids, order, starts, *blocks)
+    )(ids, table, *blocks)
 
 
 def spread(out, far1, far2, s0, s1):
@@ -396,25 +404,32 @@
     return lax.ppermute(block, "c", [(0, 1), (1, 0)])
 
 
+def own_half(block, core):
+    width = block.shape[1] // 2
+    return lax.dynamic_slice(block, (0, core * width), (ROWS, width))
+
+
 def shards(query, key, value, grad, inputs, stretch_order, session_starts):
     query, key, value, grad, inputs = query[0], key[0], value[0], grad[0], inputs[0]
     core = lax.axis_index("c")
     ids = jnp.stack([lax.axis_index(CTX), lax.axis_index("x"), core]).astype(jnp.int32)
 
-    key_other, value = lax.optimization_barrier((swap_core(key), value))
-    (key0,) = pick_call(ids, key, key_other)
+    table = jnp.concatenate([stretch_order.reshape(-1), session_starts.reshape(-1)])
+    key_other, value, table, value_half, key_half = lax.optimization_barrier(
+        (swap_core(key), value, table, own_half(value, core), own_half(key, core))
+    )
+    (key0,) = pick_call(ids, key_half, key_other)
     key0, query, grad, value = lax.optimization_barrier((key0, query, grad, value))
     key1 = shift_chips(key0, 1)
-    value0, last = pick_call(ids, value, swap_core(value), key0)
+    value0, last = pick_call(ids, value_half, swap_core(value), key0)
     far2 = shift_chips(last, 2)
     keys = [far2, key1, key0]
     bias, queries, grads = prepare_call(
         ids,
-        stretch_order.reshape(-1),
-        session_starts.reshape(-1),
-        query,
+        table,
+        own_half(query, core),
         swap_core(query),
-        grad,
+        own_half(grad, core),
         swap_core(grad),
     )
     bias, value0 = lax.optimization_barrier((bias, value0))

time: 108 us -> 106 us (0.981)
  local copies, waits for them, and re-layouts: 5.46 us -> 3.76 us
  starting transfers between devices: 62.9 us -> 61.8 us
    unnamed x19 -> x9, local copies, waits for them, and re-layouts: 5.33 us -> 0.79 us
    dynamic_slice x0 -> x3, local copies, waits for them, and re-layouts: none -> 2.83 us  [own_half(): return lax.dynamic_slice(block, (0, core * width), (ROWS, width))]
    all_to_all x1, waiting for transfers between devices: 9.99 us -> 12.5 us  [shards(): lax.all_to_all(partial.reshape(32, 32, HALF), ('zl', 'zh', 'y'), 0, 0, ti...]
    ppermute x12, starting transfers between devices: 13.6 us -> 12.1 us  [swap_core(): return lax.ppermute(block, 'c', [(0, 1), (1, 0)])]
    ppermute x12, waiting for transfers between devices: 2.88 us -> 1.76 us  [swap_core(): return lax.ppermute(block, 'c', [(0, 1), (1, 0)])]
  transfers between devices with their start and end apart: 24 -> 24, of which waited for: 7 -> 6; matrix products, arithmetic and copies ran while one was open for 1% -> 4% of each run, Pallas kernels for 15% -> 15%
where the time goes in v8:
time: 106 us
  starting transfers between devices  61.8 us (58%)
  waiting for transfers between devices  20.9 us (20%)
  Pallas kernels  17 us (16%)
  local copies, waits for them, and re-layouts  3.76 us (4%)
  other arithmetic  1.36 us (1%)
    ppermute x7, starting transfers between devices, shift_chips(): return lax.ppermute(block, CHIP, route)  25.4 us
    all_to_all x1, starting transfers between devices, shards(): lax.all_to_all(partial.reshape(32, 32, HALF), ('zl', 'zh', 'y'), 0, 0, ti...  16.9 us
    all_to_all x1, waiting for transfers between devices, shards(): lax.all_to_all(partial.reshape(32, 32, HALF), ('zl', 'zh', 'y'), 0, 0, ti...  12.5 us
    ppermute x12, starting transfers between devices, swap_core(): return lax.ppermute(block, 'c', [(0, 1), (1, 0)])  12.1 us
    ppermute x3, waiting for transfers between devices, shift_x(): return lax.ppermute(block, 'x', [(i, (i + distance) % 4) for i in range(4)])  6.67 us
    all_to_all x1, starting transfers between devices, shards(): gathered = lax.all_to_all(sent, 'x', 0, 0, tiled=True)  5.84 us
    pallas_call x1, Pallas kernels, backward_call(): pl.pallas_call(backward_kernel, grid_spec=pltpu.PrefetchScalarGridSpec(nu...  3.74 us
    pallas_call x1, Pallas kernels, forward_call(): pl.pallas_call(forward_kernel, grid=(GROUPS,), in_specs=[pl.BlockSpec((2,...  3.26 us
  transfers between devices with their start and end apart: 24, of which 6 were waited for; matrix products, arithmetic and copies ran while one was open for 4% of the time, Pallas kernels for 15%

profile of v8, /device:TPU:7, one launch (start us, length us, event | category | flops | bytes accessed | tf_op | source)
XLA Modules:
  0.0 105.8 jit_solution(12331834774095420171)
XLA Ops:
  5.2 3.2 %collective-permute-start.5 = (bf16[256,256]{1,0:T(8,128)(2,1)S(1)}, bf16[256,256]{1,0:T(8,128)(2,1)S(1)}, u32[]{:S(2)}, u32[]{:S(2)}) collective-permute-start(bf16[256,256]{1,0:T(8,128)(2,1)S(1)} %pick_keys.1.keys.k0), channel_id=1, source_target_pairs={{0,2},{2,4},{4,6},{6,8},{8,10},{10,12},{12,14},{14,16},{16,18},{18... | collective-permute-start | bytes 393224 | tf_op jit(solution)/shard_map/ppermute | solution.py:396
  8.4 1.0 constant_dynamic-slice_fusion.1.q_own
  10.0 4.5 %collective-permute-start.4 = (bf16[128,512]{1,0:T(8,128)(2,1)S(1)}, bf16[128,512]{1,0:T(8,128)(2,1)S(1)}, u32[]{:S(2)}, u32[]{:S(2)}) collective-permute-start(bf16[128,512]{1,0:T(8,128)(2,1)S(1)} %get-tuple-element.66), channel_id=1, source_target_pairs={{0,4},{2,6},{4,8},{6,10},{8,12},{10,14},{12,16},{14,18},{16,20},{1... | collective-permute-start | bytes 393224 | tf_op jit(solution)/shard_map/ppermute | solution.py:396
  14.5 1.0 constant_dynamic-slice_fusion.g_own
  16.3 7.8 %collective-permute-start.7 = (bf16[256,256]{1,0:T(8,128)(2,1)S(1)}, bf16[256,256]{1,0:T(8,128)(2,1)S(1)}, u32[]{:S(2)}, u32[]{:S(2)}) collective-permute-start(bf16[256,256]{1,0:T(8,128)(2,1)S(1)} %get-tuple-element.70.v0), channel_id=1, source_target_pairs={{0,2},{2,4},{4,6},{6,8},{8,10},{10,12},{12,14},{14,16},{16,18},{18... | collective-permute-start | bytes 393224 | tf_op jit(solution)/shard_map/ppermute | solution.py:396
  24.1 3.3 %forward_and_value_gradient.1 = (bf16[2,2,512,512]{3,2,1,0:T(8,128)(2,1)S(1)}, f32[256,256]{1,0:T(8,128)S(1)}, bf16[256,256]{1,0:T(8,128)(2,1)S(1)}, f32[128,256]{1,0:T(8,128)S(1)}) custom-call(f32[2,512,128]{2,1,0:T(8,128)S(1)} %get-tuple-element.63.bias, bf16[256,1024]{1,0:T(8,128)(2,1)S(1)} %get-tuple-element.64.q_ref, ...), custom_call_target="tpu_custom_call" | custom-call | flops 536870912 | bytes 6291456 | tf_op jit(solution)/shard_map/forward_and_value_gradient/pallas_call | solution.py:223
  27.4 2.1 %collective-permute-start.6 = (bf16[256,256]{1,0:T(8,128)(2,1)S(1)}, bf16[256,256]{1,0:T(8,128)(2,1)S(1)}, u32[]{:S(2)}, u32[]{:S(2)}) collective-permute-start(bf16[256,256]{1,0:T(8,128)(2,1)S(1)} %get-tuple-element.68), channel_id=1, source_target_pairs={{2,0},{4,2},{6,4},{8,6},{10,8},{12,10},{14,12},{16,14},{18,16},{20... | collective-permute-start | bytes 393224 | tf_op jit(solution)/shard_map/ppermute | solution.py:396
  29.4 1.9 %collective-permute-start.8 = (f32[128,256]{1,0:T(8,128)S(1)}, f32[128,256]{1,0:T(8,128)S(1)}, u32[]{:S(2)}, u32[]{:S(2)}) collective-permute-start(f32[128,256]{1,0:T(8,128)S(1)} %get-tuple-element.74), channel_id=1, source_target_pairs={{4,0},{6,2},{8,4},{10,6},{12,8},{14,10},{16,12},{18,14},{20,16},{2... | collective-permute-start | bytes 393224 | tf_op jit(solution)/shard_map/ppermute | solution.py:396
  31.4 3.7 %query_and_key_gradient.1 = (bf16[128,1024]{1,0:T(8,128)(2,1)S(1)}, bf16[128,1024]{1,0:T(8,128)(2,1)S(1)}, f32[256,256]{1,0:T(8,128)S(1)}, bf16[256,256]{1,0:T(8,128)(2,1)S(1)}, bf16[128,256]{1,0:T(8,128)(2,1)S(1)}) custom-call(s32[3]{0:T(128)S(1)} %pad_add_fusion.1.ids, bf16[2,2,512,512]{3,2,1,0:T(8,128)(2,1)S(1)} %get-tuple-element.69.prob_ref, ...), custom_call_target="tpu_custom_call" | custom-call | flops 805306368 | bytes 6291456 | tf_op jit(solution)/shard_map/query_and_key_gradient/pallas_call | solution.py:238
  36.2 1.4 %collective-permute-start.11 = (bf16[128,1024]{1,0:T(8,128)(2,1)S(1)}, bf16[128,1024]{1,0:T(8,128)(2,1)S(1)}, u32[]{:S(2)}, u32[]{:S(2)}) collective-permute-start(bf16[128,1024]{1,0:T(8,128)(2,1)S(1)} %get-tuple-element.80), channel_id=1, source_target_pairs={{0,24},{8,0},{16,8},{24,16},{1,25},{9,1},{17,9},{25,17},{2,26},{10... | collective-permute-start | bytes 786440 | tf_op jit(solution)/shard_map/ppermute | solution.py:400
  37.5 1.4 %value_gradient_total.1 = (bf16[128,256]{1,0:T(8,128)(2,1)S(1)}, bf16[128,256]{1,0:T(8,128)(2,1)S(1)}, bf16[4,256,256]{2,1,0:T(8,128)(2,1)}) custom-call(s32[3]{0:T(128)S(1)} %pad_add_fusion.1.ids, f32[256,256]{1,0:T(8,128)S(1)} %get-tuple-element.67.own, bf16[256,256]{1,0:T(8,128)(2,1)S(1)} %collective-permute-done.6.r1, ...), custom_call_target="tpu_custom_call" | custom-call | bytes 1048576 | tf_op jit(solution)/shard_map/value_gradient_total/pallas_call | solution.py:298
  38.9 5.8 %all-to-all-start = ((bf16[4,256,256]{2,1,0:T(8,128)(2,1)}), bf16[4,256,256]{2,1,0:T(8,128)(2,1)S(1)}, u32[]{:S(2)}, u32[]{:S(2)}) async-start(bf16[4,256,256]{2,1,0:T(8,128)(2,1)} %get-tuple-element.75), calls=%async_computation | async-start | bytes 1048576 | tf_op jit(solution)/shard_map/all_to_all | solution.py:452
  44.8 2.1 %collective-permute-start.12 = (bf16[128,1024]{1,0:T(8,128)(2,1)S(1)}, bf16[128,1024]{1,0:T(8,128)(2,1)S(1)}, u32[]{:S(2)}, u32[]{:S(2)}) collective-permute-start(bf16[128,1024]{1,0:T(8,128)(2,1)S(1)} %get-tuple-element.77.a0), channel_id=1, source_target_pairs={{0,1},{1,0},{2,3},{3,2},{4,5},{5,4},{6,7},{7,6},{8,9},{9,8},{10,11... | collective-permute-start | bytes 786440 | tf_op jit(solution)/shard_map/ppermute | solution.py:404
  47.0 1.7 %collective-permute-done.10.a2 = bf16[128,1024]{1,0:T(8,128)(2,1)S(1)} collective-permute-done((bf16[128,1024]{1,0:T(8,128)(2,1)S(1)}, bf16[128,1024]{1,0:T(8,128)(2,1)S(1)}, u32[]{:S(2)}, u32[]{:S(2)}) %collective-permute-start.10) | collective-permute-done | bytes 262176 | tf_op jit(solution)/shard_map/ppermute | solution.py:400
  48.7 3.7 %collective-permute-start.14 = (bf16[128,1024]{1,0:T(8,128)(2,1)S(1)}, bf16[128,1024]{1,0:T(8,128)(2,1)S(1)}, u32[]{:S(2)}, u32[]{:S(2)}) collective-permute-start(bf16[128,1024]{1,0:T(8,128)(2,1)S(1)} %collective-permute-done.10.a2), channel_id=1, source_target_pairs={{0,1},{1,0},{2,3},{3,2},{4,5},{5,4},{6,7},{7,6},{8,9},{9,8},{10,11... | collective-permute-start | bytes 786440 | tf_op jit(solution)/shard_map/ppermute | solution.py:404
  52.4 4.9 %collective-permute-done.11.a3 = bf16[128,1024]{1,0:T(8,128)(2,1)S(1)} collective-permute-done((bf16[128,1024]{1,0:T(8,128)(2,1)S(1)}, bf16[128,1024]{1,0:T(8,128)(2,1)S(1)}, u32[]{:S(2)}, u32[]{:S(2)}) %collective-permute-start.11) | collective-permute-done | bytes 262176 | tf_op jit(solution)/shard_map/ppermute | solution.py:400
  58.1 1.9 %collective-permute-start.16 = (bf16[256,256]{1,0:T(8,128)(2,1)S(1)}, bf16[256,256]{1,0:T(8,128)(2,1)S(1)}, u32[]{:S(2)}, u32[]{:S(2)}) collective-permute-start(bf16[256,256]{1,0:T(8,128)(2,1)S(1)} %get-tuple-element.81), channel_id=1, source_target_pairs={{2,0},{4,2},{6,4},{8,6},{10,8},{12,10},{14,12},{16,14},{18,16},{20... | collective-permute-start | bytes 393224 | tf_op jit(solution)/shard_map/ppermute | solution.py:396
  60.0 4.1 %collective-permute-start.17 = (bf16[128,256]{1,0:T(8,128)(2,1)}, bf16[128,256]{1,0:T(8,128)(2,1)S(1)}, u32[]{:S(2)}, u32[]{:S(2)}) collective-permute-start(bf16[128,256]{1,0:T(8,128)(2,1)} %copy-done.2), channel_id=1, source_target_pairs={{4,0},{6,2},{8,4},{10,6},{12,8},{14,10},{16,12},{18,14},{20,16},{2... | collective-permute-start | bytes 196616 | tf_op jit(solution)/shard_map/ppermute | solution.py:396
  64.1 3.3 %weight_gradient.1 = bf16[1024,256]{1,0:T(8,128)(2,1)} custom-call(s32[3]{0:T(128)S(1)} %pad_add_fusion.1.ids, bf16[4,256,256]{2,1,0:T(8,128)(2,1)S(1)} %all-to-all-done.grads, bf16[128,1024]{1,0:T(8,128)(2,1)S(1)} %get-tuple-element.77.a0, bf16[128,1024]{1,0:T(8,128)(2,1)S(1)} %collective-permute-done.9.a1, ...), custom_call_target="tpu_custom_call" | custom-call | flops 536870912 | bytes 3145728 | tf_op jit(solution)/shard_map/weight_gradient/pallas_call | solution.py:352
  67.4 16.9 %all-to-all-start.1 = ((bf16[32,32,256]{2,1,0:T(8,128)(2,1)}), bf16[32,32,256]{2,1,0:T(8,128)(2,1)S(1)}, u32[]{:S(2)}, u32[]{:S(2)}) async-start(bf16[32,32,256]{2,1,0:T(8,128)(2,1)} %bitcast.11), calls=%async_computation.1 | async-start | bytes 1048576 | tf_op jit(solution)/shard_map/all_to_all | solution.py:455
  84.3 1.0 collective-permute-start.18
  87.5 1.5 %join_outputs.1 = (bf16[128,2048]{1,0:T(8,128)(2,1)}, bf16[128,512]{1,0:T(8,128)(2,1)}, bf16[128,512]{1,0:T(8,128)(2,1)}) custom-call(s32[3]{0:T(128)S(1)} %pad_add_fusion.1.ids, bf16[128,1024]{1,0:T(8,128)(2,1)S(1)} %get-tuple-element.84.refs_0_, bf16[128,256]{1,0:T(8,128)(2,1)S(1)} %get-tuple-element.88.refs_1_, ...), custom_call_target="tpu_custom_call" | custom-call | bytes 524288 | tf_op jit(solution)/shard_map/join_outputs/pallas_call | solution.py:324
  88.9 12.5 %all-to-all-done.1.in_ref = bf16[32,32,256]{2,1,0:T(8,128)(2,1)S(1)} async-done(((bf16[32,32,256]{2,1,0:T(8,128)(2,1)}), bf16[32,32,256]{2,1,0:T(8,128)(2,1)S(1)}, u32[]{:S(2)}, u32[]{:S(2)}) %all-to-all-start.1) | async-done | bytes 524320 | tf_op jit(solution)/shard_map/all_to_all | solution.py:455
  102.0 2.3 %collective-permute-start.21 = (f32[16,256]{1,0:T(8,128)S(1)}, f32[16,256]{1,0:T(8,128)S(1)}, u32[]{:S(2)}, u32[]{:S(2)}) collective-permute-start(f32[16,256]{1,0:T(8,128)S(1)} %get-tuple-element.99), channel_id=1, source_target_pairs={{0,1},{1,0},{2,3},{3,2},{4,5},{5,4},{6,7},{7,6},{8,9},{9,8},{10,11... | collective-permute-start | bytes 49160 | tf_op jit(solution)/shard_map/ppermute | solution.py:404
  (52 shorter events, 11.9 us)
Async XLA Ops:
  0.6 3.3 %collective-permute-start = (bf16[128,512]{1,0:T(8,128)(2,1)}, bf16[128,512]{1,0:T(8,128)(2,1)S(1)}, u32[]{:S(2)}, u32[]{:S(2)}) collective-permute-start(bf16[128,512]{1,0:T(8,128)(2,1)} %bitcast.22), channel_id=1, source_target_pairs={{0,1},{1,0},{2,3},{3,2},{4,5},{5,4},{6,7},{7,6},{8,9},{9,8},{10,11... | collective-permute-start | bytes 393224 | tf_op jit(solution)/shard_map/ppermute | solution.py:404
  4.5 11.0 %collective-permute-start.1 = (bf16[128,2048]{1,0:T(8,128)(2,1)}, bf16[128,2048]{1,0:T(8,128)(2,1)S(1)}, u32[]{:S(2)}, u32[]{:S(2)}) collective-permute-start(bf16[128,2048]{1,0:T(8,128)(2,1)} %bitcast.18), channel_id=1, source_target_pairs={{0,1},{1,0},{2,3},{3,2},{4,5},{5,4},{6,7},{7,6},{8,9},{9,8},{10,11... | collective-permute-start | bytes 1572872 | tf_op jit(solution)/shard_map/ppermute | solution.py:404
  4.6 10.9 %collective-permute-start.2 = (bf16[128,2048]{1,0:T(8,128)(2,1)}, bf16[128,2048]{1,0:T(8,128)(2,1)S(1)}, u32[]{:S(2)}, u32[]{:S(2)}) collective-permute-start(bf16[128,2048]{1,0:T(8,128)(2,1)} %bitcast.20), channel_id=1, source_target_pairs={{0,1},{1,0},{2,3},{3,2},{4,5},{5,4},{6,7},{7,6},{8,9},{9,8},{10,11... | collective-permute-start | bytes 1572872 | tf_op jit(solution)/shard_map/ppermute | solution.py:404
  5.1 4.3 %collective-permute-start.3 = (bf16[128,512]{1,0:T(8,128)(2,1)}, bf16[128,512]{1,0:T(8,128)(2,1)S(1)}, u32[]{:S(2)}, u32[]{:S(2)}) collective-permute-start(bf16[128,512]{1,0:T(8,128)(2,1)} %bitcast.23), channel_id=1, source_target_pairs={{0,1},{1,0},{2,3},{3,2},{4,5},{5,4},{6,7},{7,6},{8,9},{9,8},{10,11... | collective-permute-start | bytes 393224 | tf_op jit(solution)/shard_map/ppermute | solution.py:404
  5.2 18.9 %collective-permute-start.5 = (bf16[256,256]{1,0:T(8,128)(2,1)S(1)}, bf16[256,256]{1,0:T(8,128)(2,1)S(1)}, u32[]{:S(2)}, u32[]{:S(2)}) collective-permute-start(bf16[256,256]{1,0:T(8,128)(2,1)S(1)} %pick_keys.1.keys.k0), channel_id=1, source_target_pairs={{0,2},{2,4},{4,6},{6,8},{8,10},{10,12},{12,14},{14,16},{16,18},{18... | collective-permute-start | bytes 393224 | tf_op jit(solution)/shard_map/ppermute | solution.py:396
  10.0 14.1 %collective-permute-start.4 = (bf16[128,512]{1,0:T(8,128)(2,1)S(1)}, bf16[128,512]{1,0:T(8,128)(2,1)S(1)}, u32[]{:S(2)}, u32[]{:S(2)}) collective-permute-start(bf16[128,512]{1,0:T(8,128)(2,1)S(1)} %get-tuple-element.66), channel_id=1, source_target_pairs={{0,4},{2,6},{4,8},{6,10},{8,12},{10,14},{12,16},{14,18},{16,20},{1... | collective-permute-start | bytes 393224 | tf_op jit(solution)/shard_map/ppermute | solution.py:396
  16.3 15.1 %collective-permute-start.7 = (bf16[256,256]{1,0:T(8,128)(2,1)S(1)}, bf16[256,256]{1,0:T(8,128)(2,1)S(1)}, u32[]{:S(2)}, u32[]{:S(2)}) collective-permute-start(bf16[256,256]{1,0:T(8,128)(2,1)S(1)} %get-tuple-element.70.v0), channel_id=1, source_target_pairs={{0,2},{2,4},{4,6},{6,8},{8,10},{10,12},{12,14},{14,16},{16,18},{18... | collective-permute-start | bytes 393224 | tf_op jit(solution)/shard_map/ppermute | solution.py:396
  27.4 10.2 %collective-permute-start.6 = (bf16[256,256]{1,0:T(8,128)(2,1)S(1)}, bf16[256,256]{1,0:T(8,128)(2,1)S(1)}, u32[]{:S(2)}, u32[]{:S(2)}) collective-permute-start(bf16[256,256]{1,0:T(8,128)(2,1)S(1)} %get-tuple-element.68), channel_id=1, source_target_pairs={{2,0},{4,2},{6,4},{8,6},{10,8},{12,10},{14,12},{16,14},{18,16},{20... | collective-permute-start | bytes 393224 | tf_op jit(solution)/shard_map/ppermute | solution.py:396
  29.4 8.1 %collective-permute-start.8 = (f32[128,256]{1,0:T(8,128)S(1)}, f32[128,256]{1,0:T(8,128)S(1)}, u32[]{:S(2)}, u32[]{:S(2)}) collective-permute-start(f32[128,256]{1,0:T(8,128)S(1)} %get-tuple-element.74), channel_id=1, source_target_pairs={{4,0},{6,2},{8,4},{10,6},{12,8},{14,10},{16,12},{18,14},{20,16},{2... | collective-permute-start | bytes 393224 | tf_op jit(solution)/shard_map/ppermute | solution.py:396
  36.0 10.9 %collective-permute-start.9 = (bf16[128,1024]{1,0:T(8,128)(2,1)S(1)}, bf16[128,1024]{1,0:T(8,128)(2,1)S(1)}, u32[]{:S(2)}, u32[]{:S(2)}) collective-permute-start(bf16[128,1024]{1,0:T(8,128)(2,1)S(1)} %get-tuple-element.78), channel_id=1, source_target_pairs={{0,8},{8,16},{16,24},{24,0},{1,9},{9,17},{17,25},{25,1},{2,10},{10... | collective-permute-start | bytes 786440 | tf_op jit(solution)/shard_map/ppermute | solution.py:400
  36.1 12.7 %collective-permute-start.10 = (bf16[128,1024]{1,0:T(8,128)(2,1)S(1)}, bf16[128,1024]{1,0:T(8,128)(2,1)S(1)}, u32[]{:S(2)}, u32[]{:S(2)}) collective-permute-start(bf16[128,1024]{1,0:T(8,128)(2,1)S(1)} %get-tuple-element.79), channel_id=1, source_target_pairs={{0,16},{8,24},{16,0},{24,8},{1,17},{9,25},{17,1},{25,9},{2,18},{10... | collective-permute-start | bytes 786440 | tf_op jit(solution)/shard_map/ppermute | solution.py:400
  36.2 21.2 %collective-permute-start.11 = (bf16[128,1024]{1,0:T(8,128)(2,1)S(1)}, bf16[128,1024]{1,0:T(8,128)(2,1)S(1)}, u32[]{:S(2)}, u32[]{:S(2)}) collective-permute-start(bf16[128,1024]{1,0:T(8,128)(2,1)S(1)} %get-tuple-element.80), channel_id=1, source_target_pairs={{0,24},{8,0},{16,8},{24,16},{1,25},{9,1},{17,9},{25,17},{2,26},{10... | collective-permute-start | bytes 786440 | tf_op jit(solution)/shard_map/ppermute | solution.py:400
  38.9 25.2 %all-to-all-start = ((bf16[4,256,256]{2,1,0:T(8,128)(2,1)}), bf16[4,256,256]{2,1,0:T(8,128)(2,1)S(1)}, u32[]{:S(2)}, u32[]{:S(2)}) async-start(bf16[4,256,256]{2,1,0:T(8,128)(2,1)} %get-tuple-element.75), calls=%async_computation | async-start | bytes 1048576 | tf_op jit(solution)/shard_map/all_to_all | solution.py:452
  44.8 15.3 %collective-permute-start.12 = (bf16[128,1024]{1,0:T(8,128)(2,1)S(1)}, bf16[128,1024]{1,0:T(8,128)(2,1)S(1)}, u32[]{:S(2)}, u32[]{:S(2)}) collective-permute-start(bf16[128,1024]{1,0:T(8,128)(2,1)S(1)} %get-tuple-element.77.a0), channel_id=1, source_target_pairs={{0,1},{1,0},{2,3},{3,2},{4,5},{5,4},{6,7},{7,6},{8,9},{9,8},{10,11... | collective-permute-start | bytes 786440 | tf_op jit(solution)/shard_map/ppermute | solution.py:404
  46.9 17.2 %collective-permute-start.13 = (bf16[128,1024]{1,0:T(8,128)(2,1)S(1)}, bf16[128,1024]{1,0:T(8,128)(2,1)S(1)}, u32[]{:S(2)}, u32[]{:S(2)}) collective-permute-start(bf16[128,1024]{1,0:T(8,128)(2,1)S(1)} %collective-permute-done.9.a1), channel_id=1, source_target_pairs={{0,1},{1,0},{2,3},{3,2},{4,5},{5,4},{6,7},{7,6},{8,9},{9,8},{10,11... | collective-permute-start | bytes 786440 | tf_op jit(solution)/shard_map/ppermute | solution.py:404
  48.7 15.4 %collective-permute-start.14 = (bf16[128,1024]{1,0:T(8,128)(2,1)S(1)}, bf16[128,1024]{1,0:T(8,128)(2,1)S(1)}, u32[]{:S(2)}, u32[]{:S(2)}) collective-permute-start(bf16[128,1024]{1,0:T(8,128)(2,1)S(1)} %collective-permute-done.10.a2), channel_id=1, source_target_pairs={{0,1},{1,0},{2,3},{3,2},{4,5},{5,4},{6,7},{7,6},{8,9},{9,8},{10,11... | collective-permute-start | bytes 786440 | tf_op jit(solution)/shard_map/ppermute | solution.py:404
  57.3 6.8 %collective-permute-start.15 = (bf16[128,1024]{1,0:T(8,128)(2,1)S(1)}, bf16[128,1024]{1,0:T(8,128)(2,1)S(1)}, u32[]{:S(2)}, u32[]{:S(2)}) collective-permute-start(bf16[128,1024]{1,0:T(8,128)(2,1)S(1)} %collective-permute-done.11.a3), channel_id=1, source_target_pairs={{0,1},{1,0},{2,3},{3,2},{4,5},{5,4},{6,7},{7,6},{8,9},{9,8},{10,11... | collective-permute-start | bytes 786440 | tf_op jit(solution)/shard_map/ppermute | solution.py:404
  58.1 9.3 %collective-permute-start.16 = (bf16[256,256]{1,0:T(8,128)(2,1)S(1)}, bf16[256,256]{1,0:T(8,128)(2,1)S(1)}, u32[]{:S(2)}, u32[]{:S(2)}) collective-permute-start(bf16[256,256]{1,0:T(8,128)(2,1)S(1)} %get-tuple-element.81), channel_id=1, source_target_pairs={{2,0},{4,2},{6,4},{8,6},{10,8},{12,10},{14,12},{16,14},{18,16},{20... | collective-permute-start | bytes 393224 | tf_op jit(solution)/shard_map/ppermute | solution.py:396
  60.0 7.4 %collective-permute-start.17 = (bf16[128,256]{1,0:T(8,128)(2,1)}, bf16[128,256]{1,0:T(8,128)(2,1)S(1)}, u32[]{:S(2)}, u32[]{:S(2)}) collective-permute-start(bf16[128,256]{1,0:T(8,128)(2,1)} %copy-done.2), channel_id=1, source_target_pairs={{4,0},{6,2},{8,4},{10,6},{12,8},{14,10},{16,12},{18,14},{20,16},{2... | collective-permute-start | bytes 196616 | tf_op jit(solution)/shard_map/ppermute | solution.py:396
  67.4 34.0 %all-to-all-start.1 = ((bf16[32,32,256]{2,1,0:T(8,128)(2,1)}), bf16[32,32,256]{2,1,0:T(8,128)(2,1)S(1)}, u32[]{:S(2)}, u32[]{:S(2)}) async-start(bf16[32,32,256]{2,1,0:T(8,128)(2,1)} %bitcast.11), calls=%async_computation.1 | async-start | bytes 1048576 | tf_op jit(solution)/shard_map/all_to_all | solution.py:455
  84.3 2.5 %collective-permute-start.18 = (bf16[128,1024]{1,0:T(8,128)(2,1)}, bf16[128,1024]{1,0:T(8,128)(2,1)S(1)}, u32[]{:S(2)}, u32[]{:S(2)}) collective-permute-start(bf16[128,1024]{1,0:T(8,128)(2,1)} %copy-done.1), channel_id=1, source_target_pairs={{0,1},{1,0},{2,3},{3,2},{4,5},{5,4},{6,7},{7,6},{8,9},{9,8},{10,11... | collective-permute-start | bytes 786440 | tf_op jit(solution)/shard_map/ppermute | solution.py:404
  85.4 1.5 %collective-permute-start.20 = (bf16[128,256]{1,0:T(8,128)(2,1)}, bf16[128,256]{1,0:T(8,128)(2,1)S(1)}, u32[]{:S(2)}, u32[]{:S(2)}) collective-permute-start(bf16[128,256]{1,0:T(8,128)(2,1)} %copy-done.3), channel_id=1, source_target_pairs={{0,1},{1,0},{2,3},{3,2},{4,5},{5,4},{6,7},{7,6},{8,9},{9,8},{10,11... | collective-permute-start | bytes 196616 | tf_op jit(solution)/shard_map/ppermute | solution.py:404
  86.1 1.4 %collective-permute-start.19 = (bf16[128,256]{1,0:T(8,128)(2,1)S(1)}, bf16[128,256]{1,0:T(8,128)(2,1)S(1)}, u32[]{:S(2)}, u32[]{:S(2)}) collective-permute-start(bf16[128,256]{1,0:T(8,128)(2,1)S(1)} %get-tuple-element.91), channel_id=1, source_target_pairs={{0,1},{1,0},{2,3},{3,2},{4,5},{5,4},{6,7},{7,6},{8,9},{9,8},{10,11... | collective-permute-start | bytes 196616 | tf_op jit(solution)/shard_map/ppermute | solution.py:404
  102.0 3.1 %collective-permute-start.21 = (f32[16,256]{1,0:T(8,128)S(1)}, f32[16,256]{1,0:T(8,128)S(1)}, u32[]{:S(2)}, u32[]{:S(2)}) collective-permute-start(f32[16,256]{1,0:T(8,128)S(1)} %get-tuple-element.99), channel_id=1, source_target_pairs={{0,1},{1,0},{2,3},{3,2},{4,5},{5,4},{6,7},{7,6},{8,9},{9,8},{10,11... | collective-permute-start | bytes 49160 | tf_op jit(solution)/shard_map/ppermute | solution.py:404
  (4 other events, 22.0 us)

commit v9 on v8

--- a/solution.py
+++ b/solution.py
@@ -227,7 +227,7 @@
         + [wide(2 * ROWS)] * 2
         + WINDOW,
         out_specs=[PROB_SPEC] + TERMS,
-        out_shape=[shape(GROUPS, 2, KEYS, WIDE)] + term_shapes(F32),
+        out_shape=[shape(GROUPS, 2, KEYS, WIDE)] + term_shapes(BF16),
         compiler_params=LARGE,
         cost_estimate=cost(4 * 16 * ROWS * KEYS * HEAD, 6),
         name="forward_and_value_gradient",
@@ -436,15 +436,15 @@
     values = [far2, shift_chips(value0, 1), value0]
 
     prob, value_own, value_t1, value_t2 = forward_call(bias, queries, grads, keys)
+    value_own, inputs = lax.optimization_barrier((value_own, inputs))
+    packed = pack_call(ids, inputs)
+    own = [packed[0]] + [shift_x(packed[d], d) for d in range(1, 4)]
+    other = [swap_core(block) for block in own]
     value_r2 = shift_chips(value_t2, -2)
     value_r1 = shift_chips(value_t1, -1)
     query_keep, query_send, key_own, key_t1, key_t2 = backward_call(
         ids, prob, queries, grads, keys, values
     )
-    inputs, query_send = lax.optimization_barrier((inputs, query_send))
-    packed = pack_call(ids, inputs)
-    own = [packed[0]] + [shift_x(packed[d], d) for d in range(1, 4)]
-    other = [swap_core(block) for block in own]
     value_r1, query_send = lax.optimization_barrier((value_r1, query_send))
     value_keep, value_send, sent = total_call(ids, value_own, value_r1, value_r2, True)
     key_r2 = shift_chips(key_t2, -2)

time: 106 us -> 105 us (level)
  waiting for transfers between devices: 20.9 us -> 15.9 us
  starting transfers between devices: 61.8 us -> 64.2 us
  local copies, waits for them, and re-layouts: 3.76 us -> 5.08 us
    ppermute x7, starting transfers between devices: 25.4 us -> 33.5 us  [shift_chips(): return lax.ppermute(block, CHIP, route)]
    ppermute x3, waiting for transfers between devices: 6.67 us -> 0.01 us  [shift_x(): return lax.ppermute(block, 'x', [(i, (i + distance) % 4) for i in range(4)])]
    ppermute x12, starting transfers between devices: 12.1 us -> 8.82 us  [swap_core(): return lax.ppermute(block, 'c', [(0, 1), (1, 0)])]
    ppermute x7, waiting for transfers between devices: 0.02 us -> 1.52 us  [shift_chips(): return lax.ppermute(block, CHIP, route)]
    all_to_all x1, starting transfers between devices: 5.84 us -> 4.45 us  [shards(): gathered = lax.all_to_all(sent, 'x', 0, 0, tiled=True)]
    unnamed x9, local copies, waits for them, and re-layouts: 0.79 us -> 2.11 us
where the time goes in v9:
time: 105 us; the launch traced here: 104 us
  starting transfers between devices  64.2 us (61%)
  Pallas kernels  17 us (16%)
  waiting for transfers between devices  15.9 us (15%)
  local copies, waits for them, and re-layouts  5.08 us (5%)
  other arithmetic  1.36 us (1%)
    ppermute x7, starting transfers between devices, shift_chips(): return lax.ppermute(block, CHIP, route)  33.5 us
    all_to_all x1, starting transfers between devices, shards(): lax.all_to_all(partial.reshape(32, 32, HALF), ('zl', 'zh', 'y'), 0, 0, ti...  15.9 us
    all_to_all x1, waiting for transfers between devices, shards(): lax.all_to_all(partial.reshape(32, 32, HALF), ('zl', 'zh', 'y'), 0, 0, ti...  12.6 us
    ppermute x12, starting transfers between devices, swap_core(): return lax.ppermute(block, 'c', [(0, 1), (1, 0)])  8.82 us
    all_to_all x1, starting transfers between devices, shards(): gathered = lax.all_to_all(sent, 'x', 0, 0, tiled=True)  4.45 us
    pallas_call x1, Pallas kernels, backward_call(): pl.pallas_call(backward_kernel, grid_spec=pltpu.PrefetchScalarGridSpec(nu...  3.75 us
    pallas_call x1, Pallas kernels, weight_call(): pl.pallas_call(weight_kernel, grid_spec=pltpu.PrefetchScalarGridSpec(num_...  3.25 us
    pallas_call x1, Pallas kernels, forward_call(): pl.pallas_call(forward_kernel, grid=(GROUPS,), in_specs=[pl.BlockSpec((2,...  3.25 us
  transfers between devices with their start and end apart: 24, of which 6 were waited for; matrix products, arithmetic and copies ran while one was open for 4% of the time, Pallas kernels for 15%

profile of v9, /device:TPU:7, one launch (start us, length us, event | category | flops | bytes accessed | tf_op | source)
XLA Modules:
  0.0 104.5 jit_solution(16262813364576507476)
XLA Ops:
  3.1 0.9 dynamic-slice_bitcast_fusion
  5.2 3.2 %collective-permute-start.5 = (bf16[256,256]{1,0:T(8,128)(2,1)S(1)}, bf16[256,256]{1,0:T(8,128)(2,1)S(1)}, u32[]{:S(2)}, u32[]{:S(2)}) collective-permute-start(bf16[256,256]{1,0:T(8,128)(2,1)S(1)} %pick_keys.1.keys.k0), channel_id=1, source_target_pairs={{0,2},{2,4},{4,6},{6,8},{8,10},{10,12},{12,14},{14,16},{16,18},{18... | collective-permute-start | bytes 393224 | tf_op jit(solution)/shard_map/ppermute | solution.py:396
  8.4 1.0 constant_dynamic-slice_fusion.1.q_own
  10.0 4.7 %collective-permute-start.4 = (bf16[128,512]{1,0:T(8,128)(2,1)S(1)}, bf16[128,512]{1,0:T(8,128)(2,1)S(1)}, u32[]{:S(2)}, u32[]{:S(2)}) collective-permute-start(bf16[128,512]{1,0:T(8,128)(2,1)S(1)} %get-tuple-element.66), channel_id=1, source_target_pairs={{0,4},{2,6},{4,8},{6,10},{8,12},{10,14},{12,16},{14,18},{16,20},{1... | collective-permute-start | bytes 393224 | tf_op jit(solution)/shard_map/ppermute | solution.py:396
  14.7 1.0 constant_dynamic-slice_fusion.g_own
  16.4 7.8 %collective-permute-start.7 = (bf16[256,256]{1,0:T(8,128)(2,1)S(1)}, bf16[256,256]{1,0:T(8,128)(2,1)S(1)}, u32[]{:S(2)}, u32[]{:S(2)}) collective-permute-start(bf16[256,256]{1,0:T(8,128)(2,1)S(1)} %get-tuple-element.71.v0), channel_id=1, source_target_pairs={{0,2},{2,4},{4,6},{6,8},{8,10},{10,12},{12,14},{14,16},{16,18},{18... | collective-permute-start | bytes 393224 | tf_op jit(solution)/shard_map/ppermute | solution.py:396
  24.2 3.2 %forward_and_value_gradient.1 = (bf16[2,2,512,512]{3,2,1,0:T(8,128)(2,1)S(1)}, f32[256,256]{1,0:T(8,128)S(1)}, bf16[256,256]{1,0:T(8,128)(2,1)S(1)}, bf16[128,256]{1,0:T(8,128)(2,1)S(1)}) custom-call(f32[2,512,128]{2,1,0:T(8,128)S(1)} %get-tuple-element.63.bias, bf16[256,1024]{1,0:T(8,128)(2,1)S(1)} %get-tuple-element.64.q_ref, ...), custom_call_target="tpu_custom_call" | custom-call | flops 536870912 | bytes 6291456 | tf_op jit(solution)/shard_map/forward_and_value_gradient/pallas_call | solution.py:223
  27.5 1.9 %collective-permute-start.6 = (bf16[256,256]{1,0:T(8,128)(2,1)S(1)}, bf16[256,256]{1,0:T(8,128)(2,1)S(1)}, u32[]{:S(2)}, u32[]{:S(2)}) collective-permute-start(bf16[256,256]{1,0:T(8,128)(2,1)S(1)} %get-tuple-element.69), channel_id=1, source_target_pairs={{2,0},{4,2},{6,4},{8,6},{10,8},{12,10},{14,12},{16,14},{18,16},{20... | collective-permute-start | bytes 393224 | tf_op jit(solution)/shard_map/ppermute | solution.py:396
  30.4 1.4 %collective-permute-start.11 = (bf16[128,1024]{1,0:T(8,128)(2,1)S(1)}, bf16[128,1024]{1,0:T(8,128)(2,1)S(1)}, u32[]{:S(2)}, u32[]{:S(2)}) collective-permute-start(bf16[128,1024]{1,0:T(8,128)(2,1)S(1)} %get-tuple-element.80), channel_id=1, source_target_pairs={{0,24},{8,0},{16,8},{24,16},{1,25},{9,1},{17,9},{25,17},{2,26},{10... | collective-permute-start | bytes 786440 | tf_op jit(solution)/shard_map/ppermute | solution.py:400
  31.8 5.8 %collective-permute-start.8 = (bf16[128,256]{1,0:T(8,128)(2,1)S(1)}, bf16[128,256]{1,0:T(8,128)(2,1)S(1)}, u32[]{:S(2)}, u32[]{:S(2)}) collective-permute-start(bf16[128,256]{1,0:T(8,128)(2,1)S(1)} %get-tuple-element.74), channel_id=1, source_target_pairs={{4,0},{6,2},{8,4},{10,6},{12,8},{14,10},{16,12},{18,14},{20,16},{2... | collective-permute-start | bytes 196616 | tf_op jit(solution)/shard_map/ppermute | solution.py:396
  37.6 3.7 %query_and_key_gradient.1 = (bf16[128,1024]{1,0:T(8,128)(2,1)S(1)}, bf16[128,1024]{1,0:T(8,128)(2,1)S(1)}, f32[256,256]{1,0:T(8,128)S(1)}, bf16[256,256]{1,0:T(8,128)(2,1)S(1)}, bf16[128,256]{1,0:T(8,128)(2,1)S(1)}) custom-call(s32[3]{0:T(128)S(1)} %pad_add_fusion.1.ids, bf16[2,2,512,512]{3,2,1,0:T(8,128)(2,1)S(1)} %get-tuple-element.70.prob_ref, ...), custom_call_target="tpu_custom_call" | custom-call | flops 805306368 | bytes 6291456 | tf_op jit(solution)/shard_map/query_and_key_gradient/pallas_call | solution.py:238
  42.7 1.2 %collective-permute-done.8.r2 = bf16[128,256]{1,0:T(8,128)(2,1)S(1)} collective-permute-done((bf16[128,256]{1,0:T(8,128)(2,1)S(1)}, bf16[128,256]{1,0:T(8,128)(2,1)S(1)}, u32[]{:S(2)}, u32[]{:S(2)}) %collective-permute-start.8) | collective-permute-done | bytes 65568 | tf_op jit(solution)/shard_map/ppermute | solution.py:396
  43.9 1.4 %value_gradient_total.1 = (bf16[128,256]{1,0:T(8,128)(2,1)S(1)}, bf16[128,256]{1,0:T(8,128)(2,1)S(1)}, bf16[4,256,256]{2,1,0:T(8,128)(2,1)}) custom-call(s32[3]{0:T(128)S(1)} %pad_add_fusion.1.ids, f32[256,256]{1,0:T(8,128)S(1)} %get-tuple-element.68.own, bf16[256,256]{1,0:T(8,128)(2,1)S(1)} %collective-permute-done.6.r1, ...), custom_call_target="tpu_custom_call" | custom-call | bytes 1048576 | tf_op jit(solution)/shard_map/value_gradient_total/pallas_call | solution.py:298
  45.3 4.4 %all-to-all-start = ((bf16[4,256,256]{2,1,0:T(8,128)(2,1)}), bf16[4,256,256]{2,1,0:T(8,128)(2,1)S(1)}, u32[]{:S(2)}, u32[]{:S(2)}) async-start(bf16[4,256,256]{2,1,0:T(8,128)(2,1)} %get-tuple-element.75), calls=%async_computation | async-start | bytes 1048576 | tf_op jit(solution)/shard_map/all_to_all | solution.py:452
  49.8 2.9 %collective-permute-start.12 = (bf16[128,1024]{1,0:T(8,128)(2,1)S(1)}, bf16[128,1024]{1,0:T(8,128)(2,1)S(1)}, u32[]{:S(2)}, u32[]{:S(2)}) collective-permute-start(bf16[128,1024]{1,0:T(8,128)(2,1)S(1)} %get-tuple-element.77.a0), channel_id=1, source_target_pairs={{0,1},{1,0},{2,3},{3,2},{4,5},{5,4},{6,7},{7,6},{8,9},{9,8},{10,11... | collective-permute-start | bytes 786440 | tf_op jit(solution)/shard_map/ppermute | solution.py:404
  53.3 7.1 %collective-permute-start.16 = (bf16[256,256]{1,0:T(8,128)(2,1)S(1)}, bf16[256,256]{1,0:T(8,128)(2,1)S(1)}, u32[]{:S(2)}, u32[]{:S(2)}) collective-permute-start(bf16[256,256]{1,0:T(8,128)(2,1)S(1)} %get-tuple-element.81), channel_id=1, source_target_pairs={{2,0},{4,2},{6,4},{8,6},{10,8},{12,10},{14,12},{16,14},{18,16},{20... | collective-permute-start | bytes 393224 | tf_op jit(solution)/shard_map/ppermute | solution.py:396
  60.4 3.1 %collective-permute-start.17 = (bf16[128,256]{1,0:T(8,128)(2,1)}, bf16[128,256]{1,0:T(8,128)(2,1)S(1)}, u32[]{:S(2)}, u32[]{:S(2)}) collective-permute-start(bf16[128,256]{1,0:T(8,128)(2,1)} %copy-done.3), channel_id=1, source_target_pairs={{4,0},{6,2},{8,4},{10,6},{12,8},{14,10},{16,12},{18,14},{20,16},{2... | collective-permute-start | bytes 196616 | tf_op jit(solution)/shard_map/ppermute | solution.py:396
  63.5 3.3 %weight_gradient.1 = bf16[1024,256]{1,0:T(8,128)(2,1)} custom-call(s32[3]{0:T(128)S(1)} %pad_add_fusion.1.ids, bf16[4,256,256]{2,1,0:T(8,128)(2,1)S(1)} %all-to-all-done.grads, bf16[128,1024]{1,0:T(8,128)(2,1)S(1)} %get-tuple-element.77.a0, bf16[128,1024]{1,0:T(8,128)(2,1)S(1)} %collective-permute-done.9.a1, ...), custom_call_target="tpu_custom_call" | custom-call | flops 536870912 | bytes 3145728 | tf_op jit(solution)/shard_map/weight_gradient/pallas_call | solution.py:352
  67.1 15.9 %all-to-all-start.1 = ((bf16[32,32,256]{2,1,0:T(8,128)(2,1)}), bf16[32,32,256]{2,1,0:T(8,128)(2,1)S(1)}, u32[]{:S(2)}, u32[]{:S(2)}) async-start(bf16[32,32,256]{2,1,0:T(8,128)(2,1)} %bitcast.11), calls=%async_computation.1 | async-start | bytes 1048576 | tf_op jit(solution)/shard_map/all_to_all | solution.py:455
  83.0 0.8 collective-permute-start.18
  85.9 1.5 %join_outputs.1 = (bf16[128,2048]{1,0:T(8,128)(2,1)}, bf16[128,512]{1,0:T(8,128)(2,1)}, bf16[128,512]{1,0:T(8,128)(2,1)}) custom-call(s32[3]{0:T(128)S(1)} %pad_add_fusion.1.ids, bf16[128,1024]{1,0:T(8,128)(2,1)S(1)} %get-tuple-element.84.refs_0_, bf16[128,256]{1,0:T(8,128)(2,1)S(1)} %get-tuple-element.88.refs_1_, ...), custom_call_target="tpu_custom_call" | custom-call | bytes 524288 | tf_op jit(solution)/shard_map/join_outputs/pallas_call | solution.py:324
  87.4 12.6 %all-to-all-done.1.in_ref = bf16[32,32,256]{2,1,0:T(8,128)(2,1)S(1)} async-done(((bf16[32,32,256]{2,1,0:T(8,128)(2,1)}), bf16[32,32,256]{2,1,0:T(8,128)(2,1)S(1)}, u32[]{:S(2)}, u32[]{:S(2)}) %all-to-all-start.1) | async-done | bytes 524320 | tf_op jit(solution)/shard_map/all_to_all | solution.py:455
  100.6 2.4 %collective-permute-start.21 = (f32[16,256]{1,0:T(8,128)S(1)}, f32[16,256]{1,0:T(8,128)S(1)}, u32[]{:S(2)}, u32[]{:S(2)}) collective-permute-start(f32[16,256]{1,0:T(8,128)S(1)} %get-tuple-element.99), channel_id=1, source_target_pairs={{0,1},{1,0},{2,3},{3,2},{4,5},{5,4},{6,7},{7,6},{8,9},{9,8},{10,11... | collective-permute-start | bytes 49160 | tf_op jit(solution)/shard_map/ppermute | solution.py:404
  103.0 0.8 collective-permute-done.21
  (52 shorter events, 11.6 us)
Async XLA Ops:
  0.6 3.3 %collective-permute-start = (bf16[128,512]{1,0:T(8,128)(2,1)}, bf16[128,512]{1,0:T(8,128)(2,1)S(1)}, u32[]{:S(2)}, u32[]{:S(2)}) collective-permute-start(bf16[128,512]{1,0:T(8,128)(2,1)} %bitcast.22), channel_id=1, source_target_pairs={{0,1},{1,0},{2,3},{3,2},{4,5},{5,4},{6,7},{7,6},{8,9},{9,8},{10,11... | collective-permute-start | bytes 393224 | tf_op jit(solution)/shard_map/ppermute | solution.py:404
  4.5 11.1 %collective-permute-start.1 = (bf16[128,2048]{1,0:T(8,128)(2,1)}, bf16[128,2048]{1,0:T(8,128)(2,1)S(1)}, u32[]{:S(2)}, u32[]{:S(2)}) collective-permute-start(bf16[128,2048]{1,0:T(8,128)(2,1)} %bitcast.18), channel_id=1, source_target_pairs={{0,1},{1,0},{2,3},{3,2},{4,5},{5,4},{6,7},{7,6},{8,9},{9,8},{10,11... | collective-permute-start | bytes 1572872 | tf_op jit(solution)/shard_map/ppermute | solution.py:404
  4.6 11.0 %collective-permute-start.2 = (bf16[128,2048]{1,0:T(8,128)(2,1)}, bf16[128,2048]{1,0:T(8,128)(2,1)S(1)}, u32[]{:S(2)}, u32[]{:S(2)}) collective-permute-start(bf16[128,2048]{1,0:T(8,128)(2,1)} %bitcast.20), channel_id=1, source_target_pairs={{0,1},{1,0},{2,3},{3,2},{4,5},{5,4},{6,7},{7,6},{8,9},{9,8},{10,11... | collective-permute-start | bytes 1572872 | tf_op jit(solution)/shard_map/ppermute | solution.py:404
  5.1 4.3 %collective-permute-start.3 = (bf16[128,512]{1,0:T(8,128)(2,1)}, bf16[128,512]{1,0:T(8,128)(2,1)S(1)}, u32[]{:S(2)}, u32[]{:S(2)}) collective-permute-start(bf16[128,512]{1,0:T(8,128)(2,1)} %bitcast.23), channel_id=1, source_target_pairs={{0,1},{1,0},{2,3},{3,2},{4,5},{5,4},{6,7},{7,6},{8,9},{9,8},{10,11... | collective-permute-start | bytes 393224 | tf_op jit(solution)/shard_map/ppermute | solution.py:404
  5.2 19.0 %collective-permute-start.5 = (bf16[256,256]{1,0:T(8,128)(2,1)S(1)}, bf16[256,256]{1,0:T(8,128)(2,1)S(1)}, u32[]{:S(2)}, u32[]{:S(2)}) collective-permute-start(bf16[256,256]{1,0:T(8,128)(2,1)S(1)} %pick_keys.1.keys.k0), channel_id=1, source_target_pairs={{0,2},{2,4},{4,6},{6,8},{8,10},{10,12},{12,14},{14,16},{16,18},{18... | collective-permute-start | bytes 393224 | tf_op jit(solution)/shard_map/ppermute | solution.py:396
  10.0 14.2 %collective-permute-start.4 = (bf16[128,512]{1,0:T(8,128)(2,1)S(1)}, bf16[128,512]{1,0:T(8,128)(2,1)S(1)}, u32[]{:S(2)}, u32[]{:S(2)}) collective-permute-start(bf16[128,512]{1,0:T(8,128)(2,1)S(1)} %get-tuple-element.66), channel_id=1, source_target_pairs={{0,4},{2,6},{4,8},{6,10},{8,12},{10,14},{12,16},{14,18},{16,20},{1... | collective-permute-start | bytes 393224 | tf_op jit(solution)/shard_map/ppermute | solution.py:396
  16.4 15.4 %collective-permute-start.7 = (bf16[256,256]{1,0:T(8,128)(2,1)S(1)}, bf16[256,256]{1,0:T(8,128)(2,1)S(1)}, u32[]{:S(2)}, u32[]{:S(2)}) collective-permute-start(bf16[256,256]{1,0:T(8,128)(2,1)S(1)} %get-tuple-element.71.v0), channel_id=1, source_target_pairs={{0,2},{2,4},{4,6},{6,8},{8,10},{10,12},{12,14},{14,16},{16,18},{18... | collective-permute-start | bytes 393224 | tf_op jit(solution)/shard_map/ppermute | solution.py:396
  27.5 14.6 %collective-permute-start.6 = (bf16[256,256]{1,0:T(8,128)(2,1)S(1)}, bf16[256,256]{1,0:T(8,128)(2,1)S(1)}, u32[]{:S(2)}, u32[]{:S(2)}) collective-permute-start(bf16[256,256]{1,0:T(8,128)(2,1)S(1)} %get-tuple-element.69), channel_id=1, source_target_pairs={{2,0},{4,2},{6,4},{8,6},{10,8},{12,10},{14,12},{16,14},{18,16},{20... | collective-permute-start | bytes 393224 | tf_op jit(solution)/shard_map/ppermute | solution.py:396
  30.3 22.4 %collective-permute-start.9 = (bf16[128,1024]{1,0:T(8,128)(2,1)S(1)}, bf16[128,1024]{1,0:T(8,128)(2,1)S(1)}, u32[]{:S(2)}, u32[]{:S(2)}) collective-permute-start(bf16[128,1024]{1,0:T(8,128)(2,1)S(1)} %get-tuple-element.78), channel_id=1, source_target_pairs={{0,8},{8,16},{16,24},{24,0},{1,9},{9,17},{17,25},{25,1},{2,10},{10... | collective-permute-start | bytes 786440 | tf_op jit(solution)/shard_map/ppermute | solution.py:400
  30.3 22.4 %collective-permute-start.10 = (bf16[128,1024]{1,0:T(8,128)(2,1)S(1)}, bf16[128,1024]{1,0:T(8,128)(2,1)S(1)}, u32[]{:S(2)}, u32[]{:S(2)}) collective-permute-start(bf16[128,1024]{1,0:T(8,128)(2,1)S(1)} %get-tuple-element.79), channel_id=1, source_target_pairs={{0,16},{8,24},{16,0},{24,8},{1,17},{9,25},{17,1},{25,9},{2,18},{10... | collective-permute-start | bytes 786440 | tf_op jit(solution)/shard_map/ppermute | solution.py:400
  30.4 22.8 %collective-permute-start.11 = (bf16[128,1024]{1,0:T(8,128)(2,1)S(1)}, bf16[128,1024]{1,0:T(8,128)(2,1)S(1)}, u32[]{:S(2)}, u32[]{:S(2)}) collective-permute-start(bf16[128,1024]{1,0:T(8,128)(2,1)S(1)} %get-tuple-element.80), channel_id=1, source_target_pairs={{0,24},{8,0},{16,8},{24,16},{1,25},{9,1},{17,9},{25,17},{2,26},{10... | collective-permute-start | bytes 786440 | tf_op jit(solution)/shard_map/ppermute | solution.py:400
  31.8 12.1 %collective-permute-start.8 = (bf16[128,256]{1,0:T(8,128)(2,1)S(1)}, bf16[128,256]{1,0:T(8,128)(2,1)S(1)}, u32[]{:S(2)}, u32[]{:S(2)}) collective-permute-start(bf16[128,256]{1,0:T(8,128)(2,1)S(1)} %get-tuple-element.74), channel_id=1, source_target_pairs={{4,0},{6,2},{8,4},{10,6},{12,8},{14,10},{16,12},{18,14},{20,16},{2... | collective-permute-start | bytes 196616 | tf_op jit(solution)/shard_map/ppermute | solution.py:396
  45.3 18.2 %all-to-all-start = ((bf16[4,256,256]{2,1,0:T(8,128)(2,1)}), bf16[4,256,256]{2,1,0:T(8,128)(2,1)S(1)}, u32[]{:S(2)}, u32[]{:S(2)}) async-start(bf16[4,256,256]{2,1,0:T(8,128)(2,1)} %get-tuple-element.75), calls=%async_computation | async-start | bytes 1048576 | tf_op jit(solution)/shard_map/all_to_all | solution.py:452
  49.8 10.6 %collective-permute-start.12 = (bf16[128,1024]{1,0:T(8,128)(2,1)S(1)}, bf16[128,1024]{1,0:T(8,128)(2,1)S(1)}, u32[]{:S(2)}, u32[]{:S(2)}) collective-permute-start(bf16[128,1024]{1,0:T(8,128)(2,1)S(1)} %get-tuple-element.77.a0), channel_id=1, source_target_pairs={{0,1},{1,0},{2,3},{3,2},{4,5},{5,4},{6,7},{7,6},{8,9},{9,8},{10,11... | collective-permute-start | bytes 786440 | tf_op jit(solution)/shard_map/ppermute | solution.py:404
  52.7 10.8 %collective-permute-start.13 = (bf16[128,1024]{1,0:T(8,128)(2,1)S(1)}, bf16[128,1024]{1,0:T(8,128)(2,1)S(1)}, u32[]{:S(2)}, u32[]{:S(2)}) collective-permute-start(bf16[128,1024]{1,0:T(8,128)(2,1)S(1)} %collective-permute-done.9.a1), channel_id=1, source_target_pairs={{0,1},{1,0},{2,3},{3,2},{4,5},{5,4},{6,7},{7,6},{8,9},{9,8},{10,11... | collective-permute-start | bytes 786440 | tf_op jit(solution)/shard_map/ppermute | solution.py:404
  52.7 10.8 %collective-permute-start.14 = (bf16[128,1024]{1,0:T(8,128)(2,1)S(1)}, bf16[128,1024]{1,0:T(8,128)(2,1)S(1)}, u32[]{:S(2)}, u32[]{:S(2)}) collective-permute-start(bf16[128,1024]{1,0:T(8,128)(2,1)S(1)} %collective-permute-done.10.a2), channel_id=1, source_target_pairs={{0,1},{1,0},{2,3},{3,2},{4,5},{5,4},{6,7},{7,6},{8,9},{9,8},{10,11... | collective-permute-start | bytes 786440 | tf_op jit(solution)/shard_map/ppermute | solution.py:404
  53.2 10.3 %collective-permute-start.15 = (bf16[128,1024]{1,0:T(8,128)(2,1)S(1)}, bf16[128,1024]{1,0:T(8,128)(2,1)S(1)}, u32[]{:S(2)}, u32[]{:S(2)}) collective-permute-start(bf16[128,1024]{1,0:T(8,128)(2,1)S(1)} %collective-permute-done.11.a3), channel_id=1, source_target_pairs={{0,1},{1,0},{2,3},{3,2},{4,5},{5,4},{6,7},{7,6},{8,9},{9,8},{10,11... | collective-permute-start | bytes 786440 | tf_op jit(solution)/shard_map/ppermute | solution.py:404
  53.3 13.8 %collective-permute-start.16 = (bf16[256,256]{1,0:T(8,128)(2,1)S(1)}, bf16[256,256]{1,0:T(8,128)(2,1)S(1)}, u32[]{:S(2)}, u32[]{:S(2)}) collective-permute-start(bf16[256,256]{1,0:T(8,128)(2,1)S(1)} %get-tuple-element.81), channel_id=1, source_target_pairs={{2,0},{4,2},{6,4},{8,6},{10,8},{12,10},{14,12},{16,14},{18,16},{20... | collective-permute-start | bytes 393224 | tf_op jit(solution)/shard_map/ppermute | solution.py:396
  60.4 6.7 %collective-permute-start.17 = (bf16[128,256]{1,0:T(8,128)(2,1)}, bf16[128,256]{1,0:T(8,128)(2,1)S(1)}, u32[]{:S(2)}, u32[]{:S(2)}) collective-permute-start(bf16[128,256]{1,0:T(8,128)(2,1)} %copy-done.3), channel_id=1, source_target_pairs={{4,0},{6,2},{8,4},{10,6},{12,8},{14,10},{16,12},{18,14},{20,16},{2... | collective-permute-start | bytes 196616 | tf_op jit(solution)/shard_map/ppermute | solution.py:396
  67.1 32.9 %all-to-all-start.1 = ((bf16[32,32,256]{2,1,0:T(8,128)(2,1)}), bf16[32,32,256]{2,1,0:T(8,128)(2,1)S(1)}, u32[]{:S(2)}, u32[]{:S(2)}) async-start(bf16[32,32,256]{2,1,0:T(8,128)(2,1)} %bitcast.11), calls=%async_computation.1 | async-start | bytes 1048576 | tf_op jit(solution)/shard_map/all_to_all | solution.py:455
  83.0 2.3 %collective-permute-start.18 = (bf16[128,1024]{1,0:T(8,128)(2,1)}, bf16[128,1024]{1,0:T(8,128)(2,1)S(1)}, u32[]{:S(2)}, u32[]{:S(2)}) collective-permute-start(bf16[128,1024]{1,0:T(8,128)(2,1)} %copy-done.1), channel_id=1, source_target_pairs={{0,1},{1,0},{2,3},{3,2},{4,5},{5,4},{6,7},{7,6},{8,9},{9,8},{10,11... | collective-permute-start | bytes 786440 | tf_op jit(solution)/shard_map/ppermute | solution.py:404
  83.8 1.5 %collective-permute-start.20 = (bf16[128,256]{1,0:T(8,128)(2,1)}, bf16[128,256]{1,0:T(8,128)(2,1)S(1)}, u32[]{:S(2)}, u32[]{:S(2)}) collective-permute-start(bf16[128,256]{1,0:T(8,128)(2,1)} %copy-done.2), channel_id=1, source_target_pairs={{0,1},{1,0},{2,3},{3,2},{4,5},{5,4},{6,7},{7,6},{8,9},{9,8},{10,11... | collective-permute-start | bytes 196616 | tf_op jit(solution)/shard_map/ppermute | solution.py:404
  84.5 1.4 %collective-permute-start.19 = (bf16[128,256]{1,0:T(8,128)(2,1)S(1)}, bf16[128,256]{1,0:T(8,128)(2,1)S(1)}, u32[]{:S(2)}, u32[]{:S(2)}) collective-permute-start(bf16[128,256]{1,0:T(8,128)(2,1)S(1)} %get-tuple-element.91), channel_id=1, source_target_pairs={{0,1},{1,0},{2,3},{3,2},{4,5},{5,4},{6,7},{7,6},{8,9},{9,8},{10,11... | collective-permute-start | bytes 196616 | tf_op jit(solution)/shard_map/ppermute | solution.py:404
  100.6 3.2 %collective-permute-start.21 = (f32[16,256]{1,0:T(8,128)S(1)}, f32[16,256]{1,0:T(8,128)S(1)}, u32[]{:S(2)}, u32[]{:S(2)}) collective-permute-start(f32[16,256]{1,0:T(8,128)S(1)} %get-tuple-element.99), channel_id=1, source_target_pairs={{0,1},{1,0},{2,3},{3,2},{4,5},{5,4},{6,7},{7,6},{8,9},{9,8},{10,11... | collective-permute-start | bytes 49160 | tf_op jit(solution)/shard_map/ppermute | solution.py:404
  (4 other events, 35.8 us)

commit v10 on v9

--- a/solution.py
+++ b/solution.py
@@ -28,6 +28,7 @@
 N_SHARD = 64
 NSTART = 64
 MIB = 1024 * 1024
+EXTRA = 96
 PARAMS = pltpu.CompilerParams(vmem_limit_bytes=8 * MIB)
 LARGE = pltpu.CompilerParams(vmem_limit_bytes=24 * MIB)
 WHOLE = pl.BlockSpec(memory_space=pltpu.VMEM)
@@ -193,12 +194,11 @@
         terms.append(nn(grad_score, stack_heads(q_ref[rows, :])) * SCALE)
         query_grad = tn(grad_score, keys[window]) * SCALE
         for h in range(PER_GROUP):
-            gq_ref[s, :, h * HEAD : (h + 1) * HEAD] = query_grad[h * ROWS : (h + 1) * ROWS].astype(
-                BF16
-            )
+            gq_ref[s, :, h * HEAD : (h + 1) * HEAD] = query_grad[h * ROWS : (h + 1) * ROWS]
     spread(own_ref, far1, far2, *terms)
-    keep_ref[...] = gq_ref[core]
-    send_ref[...] = gq_ref[1 - core]
+    keep_ref[...] = gq_ref[core].astype(BF16)
+    send_ref[:ROWS] = gq_ref[1 - core]
+    send_ref[ROWS:] = gq_ref[core, :EXTRA]
 
 
 def narrow(rows, shift=0):
@@ -241,10 +241,14 @@
             num_scalar_prefetch=1,
             grid=(GROUPS,),
             in_specs=[PROB_SPEC] + [wide(2 * ROWS)] * 2 + WINDOW + VALUE_WINDOW,
-            out_specs=[wide(ROWS)] * 2 + TERMS,
-            scratch_shapes=[pltpu.VMEM((2, ROWS, WIDE), BF16)],
-        ),
-        out_shape=[shape(ROWS, GROUPS * WIDE)] * 2 + term_shapes(BF16),
+            out_specs=[wide(ROWS), wide(ROWS + EXTRA)] + TERMS,
+            scratch_shapes=[pltpu.VMEM((2, ROWS, WIDE), F32)],
+        ),
+        out_shape=[
+            shape(ROWS, GROUPS * WIDE),
+            shape(ROWS + EXTRA, GROUPS * WIDE, dtype=F32),
+        ]
+        + term_shapes(F32),
         compiler_params=LARGE,
         cost_estimate=cost(6 * 16 * ROWS * KEYS * HEAD, 6),
         name="query_and_key_gradient",
@@ -311,29 +315,30 @@
     )(ids, own, r1, r2)
 
 
-def join_kernel(ids, *refs):
+def join_kernel(ids, query, query_other, key, key_other, value, value_other, gq, gk, gv):
     core = ids[2]
-    count = len(refs) // 3
-    for keep, other, out in zip(refs[:count], refs[count : 2 * count], refs[2 * count :]):
-        width = keep.shape[1]
-        out[:, pl.ds(pl.multiple_of(core * width, HEAD), width)] = keep[...]
-        out[:, pl.ds(pl.multiple_of((1 - core) * width, HEAD), width)] = other[...]
-
-
-def join_call(ids, keep, other, name):
+    parts = (
+        (gq, query[...], query_other[:ROWS]),
+        (gk, key[...], key_other[...]),
+        (gv, value[...], value_other[...]),
+    )
+    for out, own, other in parts:
+        width = own.shape[1]
+        out[:, pl.ds(pl.multiple_of(core * width, HEAD), width)] = own.astype(BF16)
+        out[:, pl.ds(pl.multiple_of((1 - core) * width, HEAD), width)] = other.astype(BF16)
+
+
+def join_call(ids, *blocks):
     return pl.pallas_call(
         join_kernel,
         grid_spec=pltpu.PrefetchScalarGridSpec(
-            num_scalar_prefetch=1,
-            grid=(1,),
-            in_specs=[WHOLE] * (2 * len(keep)),
-            out_specs=[WHOLE] * len(keep),
-        ),
-        out_shape=[shape(a.shape[0], 2 * a.shape[1], dtype=a.dtype) for a in keep],
-        compiler_params=PARAMS,
-        cost_estimate=cost(0, 0.5),
-        name=name,
-    )(ids, *keep, *other)
+            num_scalar_prefetch=1, grid=(1,), in_specs=[WHOLE] * 6, out_specs=[WHOLE] * 3
+        ),
+        out_shape=[shape(ROWS, 2 * a.shape[1]) for a in blocks[::2]],
+        compiler_params=PARAMS,
+        cost_estimate=cost(0, 2),
+        name="join_outputs",
+    )(ids, *blocks)
 
 
 def weight_kernel(ids, grads, a0, a1, a2, a3, b0, b1, b2, b3, out_ref):
@@ -451,15 +456,18 @@
     key_r1 = shift_chips(key_t1, -1)
     gathered = lax.all_to_all(sent, "x", 0, 0, tiled=True)
     partial = weight_call(ids, gathered, own, other)
-    partial, key_r1, key_r2 = lax.optimization_barrier((partial, key_r1, key_r2))
     partial = lax.all_to_all(partial.reshape(32, 32, HALF), ("zl", "zh", "y"), 0, 0, tiled=True)
 
     key_keep, key_send = total_call(ids, key_own, key_r1, key_r2, False)
+    key_keep, query_send = lax.optimization_barrier((key_keep, query_send))
     grad_query, grad_key, grad_value = join_call(
         ids,
-        [query_keep, key_keep, value_keep],
-        [swap_core(query_send), swap_core(key_send), swap_core(value_send)],
-        "join_outputs",
+        query_keep,
+        swap_core(query_send),
+        key_keep,
+        swap_core(key_send),
+        value_keep,
+        swap_core(value_send),
     )
     partial, grad_query = lax.optimization_barrier((partial, grad_query))
     row_keep, row_send = final_call(ids, partial)

time: 105 us -> 101 us (0.962)
  starting transfers between devices: 64.2 us -> 62.1 us
  waiting for transfers between devices: 15.9 us -> 14.5 us
    all_to_all x1, starting transfers between devices: 15.9 us -> 12.3 us  [shards(): lax.all_to_all(partial.reshape(32, 32, HALF), ('zl', 'zh', 'y'), 0, 0, ti...]
    all_to_all x1, waiting for transfers between devices: 12.6 us -> 10.1 us  [shards(): lax.all_to_all(partial.reshape(32, 32, HALF), ('zl', 'zh', 'y'), 0, 0, ti...]
    ppermute x12, starting transfers between devices: 8.82 us -> 10 us  [swap_core(): return lax.ppermute(block, 'c', [(0, 1), (1, 0)])]
    ppermute x12, waiting for transfers between devices: 1.76 us -> 2.85 us  [swap_core(): return lax.ppermute(block, 'c', [(0, 1), (1, 0)])]
    unnamed x9 -> x11, local copies, waits for them, and re-layouts: 2.11 us -> 1.71 us
  transfers between devices with their start and end apart: 24 -> 24, of which waited for: 6 -> 4; matrix products, arithmetic and copies ran while one was open for 4% -> 4% of each run, Pallas kernels for 15% -> 16%
where the time goes in v10:
time: 101 us
  starting transfers between devices  62.1 us (61%)
  Pallas kernels  17.1 us (17%)
  waiting for transfers between devices  14.5 us (14%)
  local copies, waits for them, and re-layouts  4.68 us (5%)
  other arithmetic  1.36 us (1%)
    ppermute x7, starting transfers between devices, shift_chips(): return lax.ppermute(block, CHIP, route)  33.9 us
    all_to_all x1, starting transfers between devices, shards(): lax.all_to_all(partial.reshape(32, 32, HALF), ('zl', 'zh', 'y'), 0, 0, ti...  12.3 us
    all_to_all x1, waiting for transfers between devices, shards(): lax.all_to_all(partial.reshape(32, 32, HALF), ('zl', 'zh', 'y'), 0, 0, ti...  10.1 us
    ppermute x12, starting transfers between devices, swap_core(): return lax.ppermute(block, 'c', [(0, 1), (1, 0)])  10 us
    all_to_all x1, starting transfers between devices, shards(): gathered = lax.all_to_all(sent, 'x', 0, 0, tiled=True)  4.33 us
    pallas_call x1, Pallas kernels, backward_call(): pl.pallas_call(backward_kernel, grid_spec=pltpu.PrefetchScalarGridSpec(nu...  3.82 us
    pallas_call x1, Pallas kernels, forward_call(): pl.pallas_call(forward_kernel, grid=(GROUPS,), in_specs=[pl.BlockSpec((2,...  3.25 us
    pallas_call x1, Pallas kernels, weight_call(): pl.pallas_call(weight_kernel, grid_spec=pltpu.PrefetchScalarGridSpec(num_...  3.23 us
  transfers between devices with their start and end apart: 24, of which 4 were waited for; matrix products, arithmetic and copies ran while one was open for 4% of the time, Pallas kernels for 16%

profile of v10, /device:TPU:7, one launch (start us, length us, event | category | flops | bytes accessed | tf_op | source)
XLA Modules:
  0.0 100.6 jit_solution(3249381184050034112)
XLA Ops:
  5.2 3.2 %collective-permute-start.5 = (bf16[256,256]{1,0:T(8,128)(2,1)S(1)}, bf16[256,256]{1,0:T(8,128)(2,1)S(1)}, u32[]{:S(2)}, u32[]{:S(2)}) collective-permute-start(bf16[256,256]{1,0:T(8,128)(2,1)S(1)} %pick_keys.1.keys.k0), channel_id=1, source_target_pairs={{0,2},{2,4},{4,6},{6,8},{8,10},{10,12},{12,14},{14,16},{16,18},{18... | collective-permute-start | bytes 393224 | tf_op jit(solution)/shard_map/ppermute | solution.py:401
  8.4 1.0 constant_dynamic-slice_fusion.1.q_own
  10.0 4.7 %collective-permute-start.4 = (bf16[128,512]{1,0:T(8,128)(2,1)S(1)}, bf16[128,512]{1,0:T(8,128)(2,1)S(1)}, u32[]{:S(2)}, u32[]{:S(2)}) collective-permute-start(bf16[128,512]{1,0:T(8,128)(2,1)S(1)} %get-tuple-element.65), channel_id=1, source_target_pairs={{0,4},{2,6},{4,8},{6,10},{8,12},{10,14},{12,16},{14,18},{16,20},{1... | collective-permute-start | bytes 393224 | tf_op jit(solution)/shard_map/ppermute | solution.py:401
  14.7 1.0 constant_dynamic-slice_fusion.g_own
  16.4 7.8 %collective-permute-start.7 = (bf16[256,256]{1,0:T(8,128)(2,1)S(1)}, bf16[256,256]{1,0:T(8,128)(2,1)S(1)}, u32[]{:S(2)}, u32[]{:S(2)}) collective-permute-start(bf16[256,256]{1,0:T(8,128)(2,1)S(1)} %get-tuple-element.70.v0), channel_id=1, source_target_pairs={{0,2},{2,4},{4,6},{6,8},{8,10},{10,12},{12,14},{14,16},{16,18},{18... | collective-permute-start | bytes 393224 | tf_op jit(solution)/shard_map/ppermute | solution.py:401
  24.2 3.2 %forward_and_value_gradient.1 = (bf16[2,2,512,512]{3,2,1,0:T(8,128)(2,1)S(1)}, f32[256,256]{1,0:T(8,128)S(1)}, bf16[256,256]{1,0:T(8,128)(2,1)S(1)}, bf16[128,256]{1,0:T(8,128)(2,1)S(1)}) custom-call(f32[2,512,128]{2,1,0:T(8,128)S(1)} %get-tuple-element.62.bias, bf16[256,1024]{1,0:T(8,128)(2,1)S(1)} %get-tuple-element.63.q_ref, ...), custom_call_target="tpu_custom_call" | custom-call | flops 536870912 | bytes 6291456 | tf_op jit(solution)/shard_map/forward_and_value_gradient/pallas_call | solution.py:223
  27.5 1.9 %collective-permute-start.6 = (bf16[256,256]{1,0:T(8,128)(2,1)S(1)}, bf16[256,256]{1,0:T(8,128)(2,1)S(1)}, u32[]{:S(2)}, u32[]{:S(2)}) collective-permute-start(bf16[256,256]{1,0:T(8,128)(2,1)S(1)} %get-tuple-element.68), channel_id=1, source_target_pairs={{2,0},{4,2},{6,4},{8,6},{10,8},{12,10},{14,12},{16,14},{18,16},{20... | collective-permute-start | bytes 393224 | tf_op jit(solution)/shard_map/ppermute | solution.py:401
  30.4 1.4 %collective-permute-start.11 = (bf16[128,1024]{1,0:T(8,128)(2,1)S(1)}, bf16[128,1024]{1,0:T(8,128)(2,1)S(1)}, u32[]{:S(2)}, u32[]{:S(2)}) collective-permute-start(bf16[128,1024]{1,0:T(8,128)(2,1)S(1)} %get-tuple-element.79), channel_id=1, source_target_pairs={{0,24},{8,0},{16,8},{24,16},{1,25},{9,1},{17,9},{25,17},{2,26},{10... | collective-permute-start | bytes 786440 | tf_op jit(solution)/shard_map/ppermute | solution.py:405
  31.8 5.8 %collective-permute-start.8 = (bf16[128,256]{1,0:T(8,128)(2,1)S(1)}, bf16[128,256]{1,0:T(8,128)(2,1)S(1)}, u32[]{:S(2)}, u32[]{:S(2)}) collective-permute-start(bf16[128,256]{1,0:T(8,128)(2,1)S(1)} %get-tuple-element.73), channel_id=1, source_target_pairs={{4,0},{6,2},{8,4},{10,6},{12,8},{14,10},{16,12},{18,14},{20,16},{2... | collective-permute-start | bytes 196616 | tf_op jit(solution)/shard_map/ppermute | solution.py:401
  37.6 3.8 %query_and_key_gradient.1 = (bf16[128,1024]{1,0:T(8,128)(2,1)S(1)}, f32[224,1024]{1,0:T(8,128)S(1)}, f32[256,256]{1,0:T(8,128)S(1)}, bf16[256,256]{1,0:T(8,128)(2,1)S(1)}, f32[128,256]{1,0:T(8,128)S(1)}) custom-call(s32[3]{0:T(128)S(1)} %pad_add_fusion.1.ids, bf16[2,2,512,512]{3,2,1,0:T(8,128)(2,1)S(1)} %get-tuple-element.69.prob_ref, ...), custom_call_target="tpu_custom_call" | custom-call | flops 805306368 | bytes 6291456 | tf_op jit(solution)/shard_map/query_and_key_gradient/pallas_call | solution.py:238
  41.5 0.9 copy-done.1
  42.4 1.5 %collective-permute-done.8.r2 = bf16[128,256]{1,0:T(8,128)(2,1)S(1)} collective-permute-done((bf16[128,256]{1,0:T(8,128)(2,1)S(1)}, bf16[128,256]{1,0:T(8,128)(2,1)S(1)}, u32[]{:S(2)}, u32[]{:S(2)}) %collective-permute-start.8) | collective-permute-done | bytes 65568 | tf_op jit(solution)/shard_map/ppermute | solution.py:401
  43.9 1.4 %value_gradient_total.1 = (bf16[128,256]{1,0:T(8,128)(2,1)S(1)}, bf16[128,256]{1,0:T(8,128)(2,1)S(1)}, bf16[4,256,256]{2,1,0:T(8,128)(2,1)}) custom-call(s32[3]{0:T(128)S(1)} %pad_add_fusion.1.ids, f32[256,256]{1,0:T(8,128)S(1)} %get-tuple-element.67.own, bf16[256,256]{1,0:T(8,128)(2,1)S(1)} %collective-permute-done.6.r1, ...), custom_call_target="tpu_custom_call" | custom-call | bytes 1048576 | tf_op jit(solution)/shard_map/value_gradient_total/pallas_call | solution.py:302
  45.3 4.3 %all-to-all-start = ((bf16[4,256,256]{2,1,0:T(8,128)(2,1)}), bf16[4,256,256]{2,1,0:T(8,128)(2,1)S(1)}, u32[]{:S(2)}, u32[]{:S(2)}) async-start(bf16[4,256,256]{2,1,0:T(8,128)(2,1)} %get-tuple-element.74), calls=%async_computation | async-start | bytes 1048576 | tf_op jit(solution)/shard_map/all_to_all | solution.py:457
  49.6 2.7 %collective-permute-start.12 = (bf16[128,1024]{1,0:T(8,128)(2,1)S(1)}, bf16[128,1024]{1,0:T(8,128)(2,1)S(1)}, u32[]{:S(2)}, u32[]{:S(2)}) collective-permute-start(bf16[128,1024]{1,0:T(8,128)(2,1)S(1)} %get-tuple-element.76.a0), channel_id=1, source_target_pairs={{0,1},{1,0},{2,3},{3,2},{4,5},{5,4},{6,7},{7,6},{8,9},{9,8},{10,11... | collective-permute-start | bytes 786440 | tf_op jit(solution)/shard_map/ppermute | solution.py:409
  53.0 7.4 %collective-permute-start.16 = (bf16[256,256]{1,0:T(8,128)(2,1)}, bf16[256,256]{1,0:T(8,128)(2,1)S(1)}, u32[]{:S(2)}, u32[]{:S(2)}) collective-permute-start(bf16[256,256]{1,0:T(8,128)(2,1)} %copy-done.3), channel_id=1, source_target_pairs={{2,0},{4,2},{6,4},{8,6},{10,8},{12,10},{14,12},{16,14},{18,16},{20... | collective-permute-start | bytes 393224 | tf_op jit(solution)/shard_map/ppermute | solution.py:401
  60.4 3.1 %collective-permute-start.17 = (f32[128,256]{1,0:T(8,128)}, f32[128,256]{1,0:T(8,128)S(1)}, u32[]{:S(2)}, u32[]{:S(2)}) collective-permute-start(f32[128,256]{1,0:T(8,128)} %copy-done.2), channel_id=1, source_target_pairs={{4,0},{6,2},{8,4},{10,6},{12,8},{14,10},{16,12},{18,14},{20,16},{2... | collective-permute-start | bytes 393224 | tf_op jit(solution)/shard_map/ppermute | solution.py:401
  63.6 3.2 %weight_gradient.1 = bf16[1024,256]{1,0:T(8,128)(2,1)} custom-call(s32[3]{0:T(128)S(1)} %pad_add_fusion.1.ids, bf16[4,256,256]{2,1,0:T(8,128)(2,1)S(1)} %all-to-all-done.grads, bf16[128,1024]{1,0:T(8,128)(2,1)S(1)} %get-tuple-element.76.a0, bf16[128,1024]{1,0:T(8,128)(2,1)S(1)} %collective-permute-done.9.a1, ...), custom_call_target="tpu_custom_call" | custom-call | flops 536870912 | bytes 3145728 | tf_op jit(solution)/shard_map/weight_gradient/pallas_call | solution.py:357
  66.8 12.3 %all-to-all-start.1 = ((bf16[32,32,256]{2,1,0:T(8,128)(2,1)}), bf16[32,32,256]{2,1,0:T(8,128)(2,1)S(1)}, u32[]{:S(2)}, u32[]{:S(2)}) async-start(bf16[32,32,256]{2,1,0:T(8,128)(2,1)} %bitcast.11), calls=%async_computation.1 | async-start | bytes 1048576 | tf_op jit(solution)/shard_map/all_to_all | solution.py:459
  79.8 1.3 %collective-permute-start.18 = (f32[224,1024]{1,0:T(8,128)}, f32[224,1024]{1,0:T(8,128)S(1)}, u32[]{:S(2)}, u32[]{:S(2)}) collective-permute-start(f32[224,1024]{1,0:T(8,128)} %copy-done.1), channel_id=1, source_target_pairs={{0,1},{1,0},{2,3},{3,2},{4,5},{5,4},{6,7},{7,6},{8,9},{9,8},{10,11... | collective-permute-start | bytes 2752520 | tf_op jit(solution)/shard_map/ppermute | solution.py:409
  81.6 2.0 %collective-permute-done.20.value_other = bf16[128,256]{1,0:T(8,128)(2,1)S(1)} collective-permute-done((bf16[128,256]{1,0:T(8,128)(2,1)}, bf16[128,256]{1,0:T(8,128)(2,1)S(1)}, u32[]{:S(2)}, u32[]{:S(2)}) %collective-permute-start.20) | collective-permute-done | bytes 65568 | tf_op jit(solution)/shard_map/ppermute | solution.py:409
  83.6 1.5 %join_outputs.1 = (bf16[128,2048]{1,0:T(8,128)(2,1)}, bf16[128,512]{1,0:T(8,128)(2,1)}, bf16[128,512]{1,0:T(8,128)(2,1)}) custom-call(s32[3]{0:T(128)S(1)} %pad_add_fusion.1.ids, bf16[128,1024]{1,0:T(8,128)(2,1)S(1)} %get-tuple-element.80.query, f32[224,1024]{1,0:T(8,128)S(1)} %collective-permute-done.18.query_other, ...), custom_call_target="tpu_custom_call" | custom-call | bytes 2097152 | tf_op jit(solution)/shard_map/join_outputs/pallas_call | solution.py:332
  85.1 10.1 %all-to-all-done.1.in_ref = bf16[32,32,256]{2,1,0:T(8,128)(2,1)S(1)} async-done(((bf16[32,32,256]{2,1,0:T(8,128)(2,1)}), bf16[32,32,256]{2,1,0:T(8,128)(2,1)S(1)}, u32[]{:S(2)}, u32[]{:S(2)}) %all-to-all-start.1) | async-done | bytes 524320 | tf_op jit(solution)/shard_map/all_to_all | solution.py:459
  95.8 3.4 %collective-permute-start.21 = (f32[16,256]{1,0:T(8,128)S(1)}, f32[16,256]{1,0:T(8,128)S(1)}, u32[]{:S(2)}, u32[]{:S(2)}) collective-permute-start(f32[16,256]{1,0:T(8,128)S(1)} %get-tuple-element.97), channel_id=1, source_target_pairs={{0,1},{1,0},{2,3},{3,2},{4,5},{5,4},{6,7},{7,6},{8,9},{9,8},{10,11... | collective-permute-start | bytes 49160 | tf_op jit(solution)/shard_map/ppermute | solution.py:409
  (54 shorter events, 10.7 us)
Async XLA Ops:
  0.6 3.3 %collective-permute-start = (bf16[128,512]{1,0:T(8,128)(2,1)}, bf16[128,512]{1,0:T(8,128)(2,1)S(1)}, u32[]{:S(2)}, u32[]{:S(2)}) collective-permute-start(bf16[128,512]{1,0:T(8,128)(2,1)} %bitcast.22), channel_id=1, source_target_pairs={{0,1},{1,0},{2,3},{3,2},{4,5},{5,4},{6,7},{7,6},{8,9},{9,8},{10,11... | collective-permute-start | bytes 393224 | tf_op jit(solution)/shard_map/ppermute | solution.py:409
  4.5 11.1 %collective-permute-start.1 = (bf16[128,2048]{1,0:T(8,128)(2,1)}, bf16[128,2048]{1,0:T(8,128)(2,1)S(1)}, u32[]{:S(2)}, u32[]{:S(2)}) collective-permute-start(bf16[128,2048]{1,0:T(8,128)(2,1)} %bitcast.18), channel_id=1, source_target_pairs={{0,1},{1,0},{2,3},{3,2},{4,5},{5,4},{6,7},{7,6},{8,9},{9,8},{10,11... | collective-permute-start | bytes 1572872 | tf_op jit(solution)/shard_map/ppermute | solution.py:409
  4.6 11.0 %collective-permute-start.2 = (bf16[128,2048]{1,0:T(8,128)(2,1)}, bf16[128,2048]{1,0:T(8,128)(2,1)S(1)}, u32[]{:S(2)}, u32[]{:S(2)}) collective-permute-start(bf16[128,2048]{1,0:T(8,128)(2,1)} %bitcast.20), channel_id=1, source_target_pairs={{0,1},{1,0},{2,3},{3,2},{4,5},{5,4},{6,7},{7,6},{8,9},{9,8},{10,11... | collective-permute-start | bytes 1572872 | tf_op jit(solution)/shard_map/ppermute | solution.py:409
  5.1 4.3 %collective-permute-start.3 = (bf16[128,512]{1,0:T(8,128)(2,1)}, bf16[128,512]{1,0:T(8,128)(2,1)S(1)}, u32[]{:S(2)}, u32[]{:S(2)}) collective-permute-start(bf16[128,512]{1,0:T(8,128)(2,1)} %bitcast.23), channel_id=1, source_target_pairs={{0,1},{1,0},{2,3},{3,2},{4,5},{5,4},{6,7},{7,6},{8,9},{9,8},{10,11... | collective-permute-start | bytes 393224 | tf_op jit(solution)/shard_map/ppermute | solution.py:409
  5.2 19.0 %collective-permute-start.5 = (bf16[256,256]{1,0:T(8,128)(2,1)S(1)}, bf16[256,256]{1,0:T(8,128)(2,1)S(1)}, u32[]{:S(2)}, u32[]{:S(2)}) collective-permute-start(bf16[256,256]{1,0:T(8,128)(2,1)S(1)} %pick_keys.1.keys.k0), channel_id=1, source_target_pairs={{0,2},{2,4},{4,6},{6,8},{8,10},{10,12},{12,14},{14,16},{16,18},{18... | collective-permute-start | bytes 393224 | tf_op jit(solution)/shard_map/ppermute | solution.py:401
  10.0 14.2 %collective-permute-start.4 = (bf16[128,512]{1,0:T(8,128)(2,1)S(1)}, bf16[128,512]{1,0:T(8,128)(2,1)S(1)}, u32[]{:S(2)}, u32[]{:S(2)}) collective-permute-start(bf16[128,512]{1,0:T(8,128)(2,1)S(1)} %get-tuple-element.65), channel_id=1, source_target_pairs={{0,4},{2,6},{4,8},{6,10},{8,12},{10,14},{12,16},{14,18},{16,20},{1... | collective-permute-start | bytes 393224 | tf_op jit(solution)/shard_map/ppermute | solution.py:401
  16.4 15.4 %collective-permute-start.7 = (bf16[256,256]{1,0:T(8,128)(2,1)S(1)}, bf16[256,256]{1,0:T(8,128)(2,1)S(1)}, u32[]{:S(2)}, u32[]{:S(2)}) collective-permute-start(bf16[256,256]{1,0:T(8,128)(2,1)S(1)} %get-tuple-element.70.v0), channel_id=1, source_target_pairs={{0,2},{2,4},{4,6},{6,8},{8,10},{10,12},{12,14},{14,16},{16,18},{18... | collective-permute-start | bytes 393224 | tf_op jit(solution)/shard_map/ppermute | solution.py:401
  27.5 14.9 %collective-permute-start.6 = (bf16[256,256]{1,0:T(8,128)(2,1)S(1)}, bf16[256,256]{1,0:T(8,128)(2,1)S(1)}, u32[]{:S(2)}, u32[]{:S(2)}) collective-permute-start(bf16[256,256]{1,0:T(8,128)(2,1)S(1)} %get-tuple-element.68), channel_id=1, source_target_pairs={{2,0},{4,2},{6,4},{8,6},{10,8},{12,10},{14,12},{16,14},{18,16},{20... | collective-permute-start | bytes 393224 | tf_op jit(solution)/shard_map/ppermute | solution.py:401
  30.3 22.1 %collective-permute-start.9 = (bf16[128,1024]{1,0:T(8,128)(2,1)S(1)}, bf16[128,1024]{1,0:T(8,128)(2,1)S(1)}, u32[]{:S(2)}, u32[]{:S(2)}) collective-permute-start(bf16[128,1024]{1,0:T(8,128)(2,1)S(1)} %get-tuple-element.77), channel_id=1, source_target_pairs={{0,8},{8,16},{16,24},{24,0},{1,9},{9,17},{17,25},{25,1},{2,10},{10... | collective-permute-start | bytes 786440 | tf_op jit(solution)/shard_map/ppermute | solution.py:405
  30.3 22.1 %collective-permute-start.10 = (bf16[128,1024]{1,0:T(8,128)(2,1)S(1)}, bf16[128,1024]{1,0:T(8,128)(2,1)S(1)}, u32[]{:S(2)}, u32[]{:S(2)}) collective-permute-start(bf16[128,1024]{1,0:T(8,128)(2,1)S(1)} %get-tuple-element.78), channel_id=1, source_target_pairs={{0,16},{8,24},{16,0},{24,8},{1,17},{9,25},{17,1},{25,9},{2,18},{10... | collective-permute-start | bytes 786440 | tf_op jit(solution)/shard_map/ppermute | solution.py:405
  30.4 22.4 %collective-permute-start.11 = (bf16[128,1024]{1,0:T(8,128)(2,1)S(1)}, bf16[128,1024]{1,0:T(8,128)(2,1)S(1)}, u32[]{:S(2)}, u32[]{:S(2)}) collective-permute-start(bf16[128,1024]{1,0:T(8,128)(2,1)S(1)} %get-tuple-element.79), channel_id=1, source_target_pairs={{0,24},{8,0},{16,8},{24,16},{1,25},{9,1},{17,9},{25,17},{2,26},{10... | collective-permute-start | bytes 786440 | tf_op jit(solution)/shard_map/ppermute | solution.py:405
  31.8 12.1 %collective-permute-start.8 = (bf16[128,256]{1,0:T(8,128)(2,1)S(1)}, bf16[128,256]{1,0:T(8,128)(2,1)S(1)}, u32[]{:S(2)}, u32[]{:S(2)}) collective-permute-start(bf16[128,256]{1,0:T(8,128)(2,1)S(1)} %get-tuple-element.73), channel_id=1, source_target_pairs={{4,0},{6,2},{8,4},{10,6},{12,8},{14,10},{16,12},{18,14},{20,16},{2... | collective-permute-start | bytes 196616 | tf_op jit(solution)/shard_map/ppermute | solution.py:401
  45.3 18.2 %all-to-all-start = ((bf16[4,256,256]{2,1,0:T(8,128)(2,1)}), bf16[4,256,256]{2,1,0:T(8,128)(2,1)S(1)}, u32[]{:S(2)}, u32[]{:S(2)}) async-start(bf16[4,256,256]{2,1,0:T(8,128)(2,1)} %get-tuple-element.74), calls=%async_computation | async-start | bytes 1048576 | tf_op jit(solution)/shard_map/all_to_all | solution.py:457
  49.6 10.7 %collective-permute-start.12 = (bf16[128,1024]{1,0:T(8,128)(2,1)S(1)}, bf16[128,1024]{1,0:T(8,128)(2,1)S(1)}, u32[]{:S(2)}, u32[]{:S(2)}) collective-permute-start(bf16[128,1024]{1,0:T(8,128)(2,1)S(1)} %get-tuple-element.76.a0), channel_id=1, source_target_pairs={{0,1},{1,0},{2,3},{3,2},{4,5},{5,4},{6,7},{7,6},{8,9},{9,8},{10,11... | collective-permute-start | bytes 786440 | tf_op jit(solution)/shard_map/ppermute | solution.py:409
  52.4 11.2 %collective-permute-start.13 = (bf16[128,1024]{1,0:T(8,128)(2,1)S(1)}, bf16[128,1024]{1,0:T(8,128)(2,1)S(1)}, u32[]{:S(2)}, u32[]{:S(2)}) collective-permute-start(bf16[128,1024]{1,0:T(8,128)(2,1)S(1)} %collective-permute-done.9.a1), channel_id=1, source_target_pairs={{0,1},{1,0},{2,3},{3,2},{4,5},{5,4},{6,7},{7,6},{8,9},{9,8},{10,11... | collective-permute-start | bytes 786440 | tf_op jit(solution)/shard_map/ppermute | solution.py:409
  52.5 11.1 %collective-permute-start.14 = (bf16[128,1024]{1,0:T(8,128)(2,1)S(1)}, bf16[128,1024]{1,0:T(8,128)(2,1)S(1)}, u32[]{:S(2)}, u32[]{:S(2)}) collective-permute-start(bf16[128,1024]{1,0:T(8,128)(2,1)S(1)} %collective-permute-done.10.a2), channel_id=1, source_target_pairs={{0,1},{1,0},{2,3},{3,2},{4,5},{5,4},{6,7},{7,6},{8,9},{9,8},{10,11... | collective-permute-start | bytes 786440 | tf_op jit(solution)/shard_map/ppermute | solution.py:409
  52.9 10.7 %collective-permute-start.15 = (bf16[128,1024]{1,0:T(8,128)(2,1)S(1)}, bf16[128,1024]{1,0:T(8,128)(2,1)S(1)}, u32[]{:S(2)}, u32[]{:S(2)}) collective-permute-start(bf16[128,1024]{1,0:T(8,128)(2,1)S(1)} %collective-permute-done.11.a3), channel_id=1, source_target_pairs={{0,1},{1,0},{2,3},{3,2},{4,5},{5,4},{6,7},{7,6},{8,9},{9,8},{10,11... | collective-permute-start | bytes 786440 | tf_op jit(solution)/shard_map/ppermute | solution.py:409
  53.0 26.2 %collective-permute-start.16 = (bf16[256,256]{1,0:T(8,128)(2,1)}, bf16[256,256]{1,0:T(8,128)(2,1)S(1)}, u32[]{:S(2)}, u32[]{:S(2)}) collective-permute-start(bf16[256,256]{1,0:T(8,128)(2,1)} %copy-done.3), channel_id=1, source_target_pairs={{2,0},{4,2},{6,4},{8,6},{10,8},{12,10},{14,12},{16,14},{18,16},{20... | collective-permute-start | bytes 393224 | tf_op jit(solution)/shard_map/ppermute | solution.py:401
  60.4 18.8 %collective-permute-start.17 = (f32[128,256]{1,0:T(8,128)}, f32[128,256]{1,0:T(8,128)S(1)}, u32[]{:S(2)}, u32[]{:S(2)}) collective-permute-start(f32[128,256]{1,0:T(8,128)} %copy-done.2), channel_id=1, source_target_pairs={{4,0},{6,2},{8,4},{10,6},{12,8},{14,10},{16,12},{18,14},{20,16},{2... | collective-permute-start | bytes 393224 | tf_op jit(solution)/shard_map/ppermute | solution.py:401
  66.8 28.4 %all-to-all-start.1 = ((bf16[32,32,256]{2,1,0:T(8,128)(2,1)}), bf16[32,32,256]{2,1,0:T(8,128)(2,1)S(1)}, u32[]{:S(2)}, u32[]{:S(2)}) async-start(bf16[32,32,256]{2,1,0:T(8,128)(2,1)} %bitcast.11), calls=%async_computation.1 | async-start | bytes 1048576 | tf_op jit(solution)/shard_map/all_to_all | solution.py:459
  79.8 3.8 %collective-permute-start.18 = (f32[224,1024]{1,0:T(8,128)}, f32[224,1024]{1,0:T(8,128)S(1)}, u32[]{:S(2)}, u32[]{:S(2)}) collective-permute-start(f32[224,1024]{1,0:T(8,128)} %copy-done.1), channel_id=1, source_target_pairs={{0,1},{1,0},{2,3},{3,2},{4,5},{5,4},{6,7},{7,6},{8,9},{9,8},{10,11... | collective-permute-start | bytes 2752520 | tf_op jit(solution)/shard_map/ppermute | solution.py:409
  81.1 2.5 %collective-permute-start.20 = (bf16[128,256]{1,0:T(8,128)(2,1)}, bf16[128,256]{1,0:T(8,128)(2,1)S(1)}, u32[]{:S(2)}, u32[]{:S(2)}) collective-permute-start(bf16[128,256]{1,0:T(8,128)(2,1)} %copy-done.4), channel_id=1, source_target_pairs={{0,1},{1,0},{2,3},{3,2},{4,5},{5,4},{6,7},{7,6},{8,9},{9,8},{10,11... | collective-permute-start | bytes 196616 | tf_op jit(solution)/shard_map/ppermute | solution.py:409
  81.2 2.4 %collective-permute-start.19 = (bf16[128,256]{1,0:T(8,128)(2,1)S(1)}, bf16[128,256]{1,0:T(8,128)(2,1)S(1)}, u32[]{:S(2)}, u32[]{:S(2)}) collective-permute-start(bf16[128,256]{1,0:T(8,128)(2,1)S(1)} %get-tuple-element.88), channel_id=1, source_target_pairs={{0,1},{1,0},{2,3},{3,2},{4,5},{5,4},{6,7},{7,6},{8,9},{9,8},{10,11... | collective-permute-start | bytes 196616 | tf_op jit(solution)/shard_map/ppermute | solution.py:409
  95.8 4.2 %collective-permute-start.21 = (f32[16,256]{1,0:T(8,128)S(1)}, f32[16,256]{1,0:T(8,128)S(1)}, u32[]{:S(2)}, u32[]{:S(2)}) collective-permute-start(f32[16,256]{1,0:T(8,128)S(1)} %get-tuple-element.97), channel_id=1, source_target_pairs={{0,1},{1,0},{2,3},{3,2},{4,5},{5,4},{6,7},{7,6},{8,9},{9,8},{10,11... | collective-permute-start | bytes 49160 | tf_op jit(solution)/shard_map/ppermute | solution.py:409
  (5 other events, 61.9 us)

commit v11 on v10

--- a/solution.py
+++ b/solution.py
@@ -227,7 +227,7 @@
         + [wide(2 * ROWS)] * 2
         + WINDOW,
         out_specs=[PROB_SPEC] + TERMS,
-        out_shape=[shape(GROUPS, 2, KEYS, WIDE)] + term_shapes(BF16),
+        out_shape=[shape(GROUPS, 2, KEYS, WIDE)] + term_shapes(F32),
         compiler_params=LARGE,
         cost_estimate=cost(4 * 16 * ROWS * KEYS * HEAD, 6),
         name="forward_and_value_gradient",

time: 101 us -> 104 us (1.030)
  the two profiles are of different devices: /device:TPU:7 before, /device:TPU:1 now
where the time goes in v11:
time: 104 us; the launch traced here: 103 us
  starting transfers between devices  59.7 us (57%)
  waiting for transfers between devices  19.4 us (19%)
  Pallas kernels  17.1 us (16%)
  local copies, waits for them, and re-layouts  4.68 us (4%)
  other arithmetic  1.36 us (1%)
    all_to_all x1, starting transfers between devices, shards(): lax.all_to_all(partial.reshape(32, 32, HALF), ('zl', 'zh', 'y'), 0, 0, ti...  19.1 us
    ppermute x7, starting transfers between devices, shift_chips(): return lax.ppermute(block, CHIP, route)  13.5 us
    ppermute x12, starting transfers between devices, swap_core(): return lax.ppermute(block, 'c', [(0, 1), (1, 0)])  13.1 us
    ppermute x3, starting transfers between devices, shift_x(): return lax.ppermute(block, 'x', [(i, (i + distance) % 4) for i in range(4)])  10.6 us
    all_to_all x1, waiting for transfers between devices, shards(): lax.all_to_all(partial.reshape(32, 32, HALF), ('zl', 'zh', 'y'), 0, 0, ti...  10.1 us
    ppermute x3, waiting for transfers between devices, shift_x(): return lax.ppermute(block, 'x', [(i, (i + distance) % 4) for i in range(4)])  6.41 us
    pallas_call x1, Pallas kernels, backward_call(): pl.pallas_call(backward_kernel, grid_spec=pltpu.PrefetchScalarGridSpec(nu...  3.81 us
    all_to_all x1, starting transfers between devices, shards(): gathered = lax.all_to_all(sent, 'x', 0, 0, tiled=True)  3.47 us
  transfers between devices with their start and end apart: 24, of which 4 were waited for; matrix products, arithmetic and copies ran while one was open for 4% of the time, Pallas kernels for 15%

profile of v11, /device:TPU:1, one launch (start us, length us, event | category | flops | bytes accessed | tf_op | source)
XLA Modules:
  0.0 103.2 jit_solution(7597921033363184853)
XLA Ops:
  0.6 3.3 %collective-permute-start = (bf16[128,512]{1,0:T(8,128)(2,1)}, bf16[128,512]{1,0:T(8,128)(2,1)S(1)}, u32[]{:S(2)}, u32[]{:S(2)}) collective-permute-start(bf16[128,512]{1,0:T(8,128)(2,1)} %bitcast.22), channel_id=1, source_target_pairs={{0,1},{1,0},{2,3},{3,2},{4,5},{5,4},{6,7},{7,6},{8,9},{9,8},{10,11... | collective-permute-start | bytes 393224 | tf_op jit(solution)/shard_map/ppermute | solution.py:409
  7.8 1.5 %collective-permute-start.5 = (bf16[256,256]{1,0:T(8,128)(2,1)S(1)}, bf16[256,256]{1,0:T(8,128)(2,1)S(1)}, u32[]{:S(2)}, u32[]{:S(2)}) collective-permute-start(bf16[256,256]{1,0:T(8,128)(2,1)S(1)} %pick_keys.1.keys.k0), channel_id=1, source_target_pairs={{0,2},{2,4},{4,6},{6,8},{8,10},{10,12},{12,14},{14,16},{16,18},{18... | collective-permute-start | bytes 393224 | tf_op jit(solution)/shard_map/ppermute | solution.py:401
  10.8 4.7 %collective-permute-start.4 = (bf16[128,512]{1,0:T(8,128)(2,1)S(1)}, bf16[128,512]{1,0:T(8,128)(2,1)S(1)}, u32[]{:S(2)}, u32[]{:S(2)}) collective-permute-start(bf16[128,512]{1,0:T(8,128)(2,1)S(1)} %get-tuple-element.65), channel_id=1, source_target_pairs={{0,4},{2,6},{4,8},{6,10},{8,12},{10,14},{12,16},{14,18},{16,20},{1... | collective-permute-start | bytes 393224 | tf_op jit(solution)/shard_map/ppermute | solution.py:401
  17.2 2.2 %collective-permute-start.7 = (bf16[256,256]{1,0:T(8,128)(2,1)S(1)}, bf16[256,256]{1,0:T(8,128)(2,1)S(1)}, u32[]{:S(2)}, u32[]{:S(2)}) collective-permute-start(bf16[256,256]{1,0:T(8,128)(2,1)S(1)} %get-tuple-element.70.v0), channel_id=1, source_target_pairs={{0,2},{2,4},{4,6},{6,8},{8,10},{10,12},{12,14},{14,16},{16,18},{18... | collective-permute-start | bytes 393224 | tf_op jit(solution)/shard_map/ppermute | solution.py:401
  19.4 3.3 %forward_and_value_gradient.1 = (bf16[2,2,512,512]{3,2,1,0:T(8,128)(2,1)S(1)}, f32[256,256]{1,0:T(8,128)S(1)}, bf16[256,256]{1,0:T(8,128)(2,1)S(1)}, f32[128,256]{1,0:T(8,128)S(1)}) custom-call(f32[2,512,128]{2,1,0:T(8,128)S(1)} %get-tuple-element.62.bias, bf16[256,1024]{1,0:T(8,128)(2,1)S(1)} %get-tuple-element.63.q_ref, ...), custom_call_target="tpu_custom_call" | custom-call | flops 536870912 | bytes 6291456 | tf_op jit(solution)/shard_map/forward_and_value_gradient/pallas_call | solution.py:223
  22.7 1.3 %collective-permute-start.6 = (bf16[256,256]{1,0:T(8,128)(2,1)S(1)}, bf16[256,256]{1,0:T(8,128)(2,1)S(1)}, u32[]{:S(2)}, u32[]{:S(2)}) collective-permute-start(bf16[256,256]{1,0:T(8,128)(2,1)S(1)} %get-tuple-element.68), channel_id=1, source_target_pairs={{2,0},{4,2},{6,4},{8,6},{10,8},{12,10},{14,12},{16,14},{18,16},{20... | collective-permute-start | bytes 393224 | tf_op jit(solution)/shard_map/ppermute | solution.py:401
  24.0 1.3 %collective-permute-start.8 = (f32[128,256]{1,0:T(8,128)S(1)}, f32[128,256]{1,0:T(8,128)S(1)}, u32[]{:S(2)}, u32[]{:S(2)}) collective-permute-start(f32[128,256]{1,0:T(8,128)S(1)} %get-tuple-element.73), channel_id=1, source_target_pairs={{4,0},{6,2},{8,4},{10,6},{12,8},{14,10},{16,12},{18,14},{20,16},{2... | collective-permute-start | bytes 393224 | tf_op jit(solution)/shard_map/ppermute | solution.py:401
  26.2 5.8 %collective-permute-start.9 = (bf16[128,1024]{1,0:T(8,128)(2,1)S(1)}, bf16[128,1024]{1,0:T(8,128)(2,1)S(1)}, u32[]{:S(2)}, u32[]{:S(2)}) collective-permute-start(bf16[128,1024]{1,0:T(8,128)(2,1)S(1)} %get-tuple-element.77), channel_id=1, source_target_pairs={{0,8},{8,16},{16,24},{24,0},{1,9},{9,17},{17,25},{25,1},{2,10},{10... | collective-permute-start | bytes 786440 | tf_op jit(solution)/shard_map/ppermute | solution.py:405
  32.0 4.8 %collective-permute-start.10 = (bf16[128,1024]{1,0:T(8,128)(2,1)S(1)}, bf16[128,1024]{1,0:T(8,128)(2,1)S(1)}, u32[]{:S(2)}, u32[]{:S(2)}) collective-permute-start(bf16[128,1024]{1,0:T(8,128)(2,1)S(1)} %get-tuple-element.78), channel_id=1, source_target_pairs={{0,16},{8,24},{16,0},{24,8},{1,17},{9,25},{17,1},{25,9},{2,18},{10... | collective-permute-start | bytes 786440 | tf_op jit(solution)/shard_map/ppermute | solution.py:405
  36.8 3.8 %query_and_key_gradient.1 = (bf16[128,1024]{1,0:T(8,128)(2,1)S(1)}, f32[224,1024]{1,0:T(8,128)S(1)}, f32[256,256]{1,0:T(8,128)S(1)}, bf16[256,256]{1,0:T(8,128)(2,1)S(1)}, f32[128,256]{1,0:T(8,128)S(1)}) custom-call(s32[3]{0:T(128)S(1)} %pad_add_fusion.1.ids, bf16[2,2,512,512]{3,2,1,0:T(8,128)(2,1)S(1)} %get-tuple-element.69.prob_ref, ...), custom_call_target="tpu_custom_call" | custom-call | flops 805306368 | bytes 6291456 | tf_op jit(solution)/shard_map/query_and_key_gradient/pallas_call | solution.py:238
  41.5 1.4 %value_gradient_total.1 = (bf16[128,256]{1,0:T(8,128)(2,1)S(1)}, bf16[128,256]{1,0:T(8,128)(2,1)S(1)}, bf16[4,256,256]{2,1,0:T(8,128)(2,1)}) custom-call(s32[3]{0:T(128)S(1)} %pad_add_fusion.1.ids, f32[256,256]{1,0:T(8,128)S(1)} %get-tuple-element.67.own, bf16[256,256]{1,0:T(8,128)(2,1)S(1)} %collective-permute-done.6.r1, ...), custom_call_target="tpu_custom_call" | custom-call | bytes 1048576 | tf_op jit(solution)/shard_map/value_gradient_total/pallas_call | solution.py:302
  42.9 3.5 %all-to-all-start = ((bf16[4,256,256]{2,1,0:T(8,128)(2,1)}), bf16[4,256,256]{2,1,0:T(8,128)(2,1)S(1)}, u32[]{:S(2)}, u32[]{:S(2)}) async-start(bf16[4,256,256]{2,1,0:T(8,128)(2,1)} %get-tuple-element.74), calls=%async_computation | async-start | bytes 1048576 | tf_op jit(solution)/shard_map/all_to_all | solution.py:457
  46.4 1.9 %collective-permute-start.12 = (bf16[128,1024]{1,0:T(8,128)(2,1)S(1)}, bf16[128,1024]{1,0:T(8,128)(2,1)S(1)}, u32[]{:S(2)}, u32[]{:S(2)}) collective-permute-start(bf16[128,1024]{1,0:T(8,128)(2,1)S(1)} %get-tuple-element.76.a0), channel_id=1, source_target_pairs={{0,1},{1,0},{2,3},{3,2},{4,5},{5,4},{6,7},{7,6},{8,9},{9,8},{10,11... | collective-permute-start | bytes 786440 | tf_op jit(solution)/shard_map/ppermute | solution.py:409
  48.4 1.2 %collective-permute-start.14 = (bf16[128,1024]{1,0:T(8,128)(2,1)S(1)}, bf16[128,1024]{1,0:T(8,128)(2,1)S(1)}, u32[]{:S(2)}, u32[]{:S(2)}) collective-permute-start(bf16[128,1024]{1,0:T(8,128)(2,1)S(1)} %collective-permute-done.10.a2), channel_id=1, source_target_pairs={{0,1},{1,0},{2,3},{3,2},{4,5},{5,4},{6,7},{7,6},{8,9},{9,8},{10,11... | collective-permute-start | bytes 786440 | tf_op jit(solution)/shard_map/ppermute | solution.py:409
  49.6 6.4 %collective-permute-done.11.a3 = bf16[128,1024]{1,0:T(8,128)(2,1)S(1)} collective-permute-done((bf16[128,1024]{1,0:T(8,128)(2,1)S(1)}, bf16[128,1024]{1,0:T(8,128)(2,1)S(1)}, u32[]{:S(2)}, u32[]{:S(2)}) %collective-permute-start.11) | collective-permute-done | bytes 262176 | tf_op jit(solution)/shard_map/ppermute | solution.py:405
  56.6 1.3 %collective-permute-start.16 = (bf16[256,256]{1,0:T(8,128)(2,1)}, bf16[256,256]{1,0:T(8,128)(2,1)S(1)}, u32[]{:S(2)}, u32[]{:S(2)}) collective-permute-start(bf16[256,256]{1,0:T(8,128)(2,1)} %copy-done.3), channel_id=1, source_target_pairs={{2,0},{4,2},{6,4},{8,6},{10,8},{12,10},{14,12},{16,14},{18,16},{20... | collective-permute-start | bytes 393224 | tf_op jit(solution)/shard_map/ppermute | solution.py:401
  57.9 1.3 %collective-permute-start.17 = (f32[128,256]{1,0:T(8,128)}, f32[128,256]{1,0:T(8,128)S(1)}, u32[]{:S(2)}, u32[]{:S(2)}) collective-permute-start(f32[128,256]{1,0:T(8,128)} %copy-done.2), channel_id=1, source_target_pairs={{4,0},{6,2},{8,4},{10,6},{12,8},{14,10},{16,12},{18,14},{20,16},{2... | collective-permute-start | bytes 393224 | tf_op jit(solution)/shard_map/ppermute | solution.py:401
  59.3 3.2 %weight_gradient.1 = bf16[1024,256]{1,0:T(8,128)(2,1)} custom-call(s32[3]{0:T(128)S(1)} %pad_add_fusion.1.ids, bf16[4,256,256]{2,1,0:T(8,128)(2,1)S(1)} %all-to-all-done.grads, bf16[128,1024]{1,0:T(8,128)(2,1)S(1)} %get-tuple-element.76.a0, bf16[128,1024]{1,0:T(8,128)(2,1)S(1)} %collective-permute-done.9.a1, ...), custom_call_target="tpu_custom_call" | custom-call | flops 536870912 | bytes 3145728 | tf_op jit(solution)/shard_map/weight_gradient/pallas_call | solution.py:357
  62.5 19.1 %all-to-all-start.1 = ((bf16[32,32,256]{2,1,0:T(8,128)(2,1)}), bf16[32,32,256]{2,1,0:T(8,128)(2,1)S(1)}, u32[]{:S(2)}, u32[]{:S(2)}) async-start(bf16[32,32,256]{2,1,0:T(8,128)(2,1)} %bitcast.11), calls=%async_computation.1 | async-start | bytes 1048576 | tf_op jit(solution)/shard_map/all_to_all | solution.py:459
  82.3 1.3 %collective-permute-start.18 = (f32[224,1024]{1,0:T(8,128)}, f32[224,1024]{1,0:T(8,128)S(1)}, u32[]{:S(2)}, u32[]{:S(2)}) collective-permute-start(f32[224,1024]{1,0:T(8,128)} %copy-done.1), channel_id=1, source_target_pairs={{0,1},{1,0},{2,3},{3,2},{4,5},{5,4},{6,7},{7,6},{8,9},{9,8},{10,11... | collective-permute-start | bytes 2752520 | tf_op jit(solution)/shard_map/ppermute | solution.py:409
  84.1 2.0 %collective-permute-done.20.value_other = bf16[128,256]{1,0:T(8,128)(2,1)S(1)} collective-permute-done((bf16[128,256]{1,0:T(8,128)(2,1)}, bf16[128,256]{1,0:T(8,128)(2,1)S(1)}, u32[]{:S(2)}, u32[]{:S(2)}) %collective-permute-start.20) | collective-permute-done | bytes 65568 | tf_op jit(solution)/shard_map/ppermute | solution.py:409
  86.1 1.5 %join_outputs.1 = (bf16[128,2048]{1,0:T(8,128)(2,1)}, bf16[128,512]{1,0:T(8,128)(2,1)}, bf16[128,512]{1,0:T(8,128)(2,1)}) custom-call(s32[3]{0:T(128)S(1)} %pad_add_fusion.1.ids, bf16[128,1024]{1,0:T(8,128)(2,1)S(1)} %get-tuple-element.80.query, f32[224,1024]{1,0:T(8,128)S(1)} %collective-permute-done.18.query_other, ...), custom_call_target="tpu_custom_call" | custom-call | bytes 2097152 | tf_op jit(solution)/shard_map/join_outputs/pallas_call | solution.py:332
  87.6 10.1 %all-to-all-done.1.in_ref = bf16[32,32,256]{2,1,0:T(8,128)(2,1)S(1)} async-done(((bf16[32,32,256]{2,1,0:T(8,128)(2,1)}), bf16[32,32,256]{2,1,0:T(8,128)(2,1)S(1)}, u32[]{:S(2)}, u32[]{:S(2)}) %all-to-all-start.1) | async-done | bytes 524320 | tf_op jit(solution)/shard_map/all_to_all | solution.py:459
  98.3 3.4 %collective-permute-start.21 = (f32[16,256]{1,0:T(8,128)S(1)}, f32[16,256]{1,0:T(8,128)S(1)}, u32[]{:S(2)}, u32[]{:S(2)}) collective-permute-start(f32[16,256]{1,0:T(8,128)S(1)} %get-tuple-element.97), channel_id=1, source_target_pairs={{0,1},{1,0},{2,3},{3,2},{4,5},{5,4},{6,7},{7,6},{8,9},{9,8},{10,11... | collective-permute-start | bytes 49160 | tf_op jit(solution)/shard_map/ppermute | solution.py:409
  (54 shorter events, 12.7 us)
Async XLA Ops:
  0.6 5.9 %collective-permute-start = (bf16[128,512]{1,0:T(8,128)(2,1)}, bf16[128,512]{1,0:T(8,128)(2,1)S(1)}, u32[]{:S(2)}, u32[]{:S(2)}) collective-permute-start(bf16[128,512]{1,0:T(8,128)(2,1)} %bitcast.22), channel_id=1, source_target_pairs={{0,1},{1,0},{2,3},{3,2},{4,5},{5,4},{6,7},{7,6},{8,9},{9,8},{10,11... | collective-permute-start | bytes 393224 | tf_op jit(solution)/shard_map/ppermute | solution.py:409
  7.1 9.4 %collective-permute-start.1 = (bf16[128,2048]{1,0:T(8,128)(2,1)}, bf16[128,2048]{1,0:T(8,128)(2,1)S(1)}, u32[]{:S(2)}, u32[]{:S(2)}) collective-permute-start(bf16[128,2048]{1,0:T(8,128)(2,1)} %bitcast.18), channel_id=1, source_target_pairs={{0,1},{1,0},{2,3},{3,2},{4,5},{5,4},{6,7},{7,6},{8,9},{9,8},{10,11... | collective-permute-start | bytes 1572872 | tf_op jit(solution)/shard_map/ppermute | solution.py:409
  7.2 9.3 %collective-permute-start.2 = (bf16[128,2048]{1,0:T(8,128)(2,1)}, bf16[128,2048]{1,0:T(8,128)(2,1)S(1)}, u32[]{:S(2)}, u32[]{:S(2)}) collective-permute-start(bf16[128,2048]{1,0:T(8,128)(2,1)} %bitcast.20), channel_id=1, source_target_pairs={{0,1},{1,0},{2,3},{3,2},{4,5},{5,4},{6,7},{7,6},{8,9},{9,8},{10,11... | collective-permute-start | bytes 1572872 | tf_op jit(solution)/shard_map/ppermute | solution.py:409
  7.7 2.6 %collective-permute-start.3 = (bf16[128,512]{1,0:T(8,128)(2,1)}, bf16[128,512]{1,0:T(8,128)(2,1)S(1)}, u32[]{:S(2)}, u32[]{:S(2)}) collective-permute-start(bf16[128,512]{1,0:T(8,128)(2,1)} %bitcast.23), channel_id=1, source_target_pairs={{0,1},{1,0},{2,3},{3,2},{4,5},{5,4},{6,7},{7,6},{8,9},{9,8},{10,11... | collective-permute-start | bytes 393224 | tf_op jit(solution)/shard_map/ppermute | solution.py:409
  7.8 11.7 %collective-permute-start.5 = (bf16[256,256]{1,0:T(8,128)(2,1)S(1)}, bf16[256,256]{1,0:T(8,128)(2,1)S(1)}, u32[]{:S(2)}, u32[]{:S(2)}) collective-permute-start(bf16[256,256]{1,0:T(8,128)(2,1)S(1)} %pick_keys.1.keys.k0), channel_id=1, source_target_pairs={{0,2},{2,4},{4,6},{6,8},{8,10},{10,12},{12,14},{14,16},{16,18},{18... | collective-permute-start | bytes 393224 | tf_op jit(solution)/shard_map/ppermute | solution.py:401
  10.8 8.6 %collective-permute-start.4 = (bf16[128,512]{1,0:T(8,128)(2,1)S(1)}, bf16[128,512]{1,0:T(8,128)(2,1)S(1)}, u32[]{:S(2)}, u32[]{:S(2)}) collective-permute-start(bf16[128,512]{1,0:T(8,128)(2,1)S(1)} %get-tuple-element.65), channel_id=1, source_target_pairs={{0,4},{2,6},{4,8},{6,10},{8,12},{10,14},{12,16},{14,18},{16,20},{1... | collective-permute-start | bytes 393224 | tf_op jit(solution)/shard_map/ppermute | solution.py:401
  17.2 19.5 %collective-permute-start.7 = (bf16[256,256]{1,0:T(8,128)(2,1)S(1)}, bf16[256,256]{1,0:T(8,128)(2,1)S(1)}, u32[]{:S(2)}, u32[]{:S(2)}) collective-permute-start(bf16[256,256]{1,0:T(8,128)(2,1)S(1)} %get-tuple-element.70.v0), channel_id=1, source_target_pairs={{0,2},{2,4},{4,6},{6,8},{8,10},{10,12},{12,14},{14,16},{16,18},{18... | collective-permute-start | bytes 393224 | tf_op jit(solution)/shard_map/ppermute | solution.py:401
  22.7 18.8 %collective-permute-start.6 = (bf16[256,256]{1,0:T(8,128)(2,1)S(1)}, bf16[256,256]{1,0:T(8,128)(2,1)S(1)}, u32[]{:S(2)}, u32[]{:S(2)}) collective-permute-start(bf16[256,256]{1,0:T(8,128)(2,1)S(1)} %get-tuple-element.68), channel_id=1, source_target_pairs={{2,0},{4,2},{6,4},{8,6},{10,8},{12,10},{14,12},{16,14},{18,16},{20... | collective-permute-start | bytes 393224 | tf_op jit(solution)/shard_map/ppermute | solution.py:401
  24.0 17.5 %collective-permute-start.8 = (f32[128,256]{1,0:T(8,128)S(1)}, f32[128,256]{1,0:T(8,128)S(1)}, u32[]{:S(2)}, u32[]{:S(2)}) collective-permute-start(f32[128,256]{1,0:T(8,128)S(1)} %get-tuple-element.73), channel_id=1, source_target_pairs={{4,0},{6,2},{8,4},{10,6},{12,8},{14,10},{16,12},{18,14},{20,16},{2... | collective-permute-start | bytes 393224 | tf_op jit(solution)/shard_map/ppermute | solution.py:401
  26.2 22.2 %collective-permute-start.9 = (bf16[128,1024]{1,0:T(8,128)(2,1)S(1)}, bf16[128,1024]{1,0:T(8,128)(2,1)S(1)}, u32[]{:S(2)}, u32[]{:S(2)}) collective-permute-start(bf16[128,1024]{1,0:T(8,128)(2,1)S(1)} %get-tuple-element.77), channel_id=1, source_target_pairs={{0,8},{8,16},{16,24},{24,0},{1,9},{9,17},{17,25},{25,1},{2,10},{10... | collective-permute-start | bytes 786440 | tf_op jit(solution)/shard_map/ppermute | solution.py:405
  32.0 16.4 %collective-permute-start.10 = (bf16[128,1024]{1,0:T(8,128)(2,1)S(1)}, bf16[128,1024]{1,0:T(8,128)(2,1)S(1)}, u32[]{:S(2)}, u32[]{:S(2)}) collective-permute-start(bf16[128,1024]{1,0:T(8,128)(2,1)S(1)} %get-tuple-element.78), channel_id=1, source_target_pairs={{0,16},{8,24},{16,0},{24,8},{1,17},{9,25},{17,1},{25,9},{2,18},{10... | collective-permute-start | bytes 786440 | tf_op jit(solution)/shard_map/ppermute | solution.py:405
  36.8 19.3 %collective-permute-start.11 = (bf16[128,1024]{1,0:T(8,128)(2,1)S(1)}, bf16[128,1024]{1,0:T(8,128)(2,1)S(1)}, u32[]{:S(2)}, u32[]{:S(2)}) collective-permute-start(bf16[128,1024]{1,0:T(8,128)(2,1)S(1)} %get-tuple-element.79), channel_id=1, source_target_pairs={{0,24},{8,0},{16,8},{24,16},{1,25},{9,1},{17,9},{25,17},{2,26},{10... | collective-permute-start | bytes 786440 | tf_op jit(solution)/shard_map/ppermute | solution.py:405
  42.9 16.3 %all-to-all-start = ((bf16[4,256,256]{2,1,0:T(8,128)(2,1)}), bf16[4,256,256]{2,1,0:T(8,128)(2,1)S(1)}, u32[]{:S(2)}, u32[]{:S(2)}) async-start(bf16[4,256,256]{2,1,0:T(8,128)(2,1)} %get-tuple-element.74), calls=%async_computation | async-start | bytes 1048576 | tf_op jit(solution)/shard_map/all_to_all | solution.py:457
  46.4 11.5 %collective-permute-start.12 = (bf16[128,1024]{1,0:T(8,128)(2,1)S(1)}, bf16[128,1024]{1,0:T(8,128)(2,1)S(1)}, u32[]{:S(2)}, u32[]{:S(2)}) collective-permute-start(bf16[128,1024]{1,0:T(8,128)(2,1)S(1)} %get-tuple-element.76.a0), channel_id=1, source_target_pairs={{0,1},{1,0},{2,3},{3,2},{4,5},{5,4},{6,7},{7,6},{8,9},{9,8},{10,11... | collective-permute-start | bytes 786440 | tf_op jit(solution)/shard_map/ppermute | solution.py:409
  48.3 10.9 %collective-permute-start.13 = (bf16[128,1024]{1,0:T(8,128)(2,1)S(1)}, bf16[128,1024]{1,0:T(8,128)(2,1)S(1)}, u32[]{:S(2)}, u32[]{:S(2)}) collective-permute-start(bf16[128,1024]{1,0:T(8,128)(2,1)S(1)} %collective-permute-done.9.a1), channel_id=1, source_target_pairs={{0,1},{1,0},{2,3},{3,2},{4,5},{5,4},{6,7},{7,6},{8,9},{9,8},{10,11... | collective-permute-start | bytes 786440 | tf_op jit(solution)/shard_map/ppermute | solution.py:409
  48.4 10.8 %collective-permute-start.14 = (bf16[128,1024]{1,0:T(8,128)(2,1)S(1)}, bf16[128,1024]{1,0:T(8,128)(2,1)S(1)}, u32[]{:S(2)}, u32[]{:S(2)}) collective-permute-start(bf16[128,1024]{1,0:T(8,128)(2,1)S(1)} %collective-permute-done.10.a2), channel_id=1, source_target_pairs={{0,1},{1,0},{2,3},{3,2},{4,5},{5,4},{6,7},{7,6},{8,9},{9,8},{10,11... | collective-permute-start | bytes 786440 | tf_op jit(solution)/shard_map/ppermute | solution.py:409
  56.0 3.2 %collective-permute-start.15 = (bf16[128,1024]{1,0:T(8,128)(2,1)S(1)}, bf16[128,1024]{1,0:T(8,128)(2,1)S(1)}, u32[]{:S(2)}, u32[]{:S(2)}) collective-permute-start(bf16[128,1024]{1,0:T(8,128)(2,1)S(1)} %collective-permute-done.11.a3), channel_id=1, source_target_pairs={{0,1},{1,0},{2,3},{3,2},{4,5},{5,4},{6,7},{7,6},{8,9},{9,8},{10,11... | collective-permute-start | bytes 786440 | tf_op jit(solution)/shard_map/ppermute | solution.py:409
  56.6 25.0 %collective-permute-start.16 = (bf16[256,256]{1,0:T(8,128)(2,1)}, bf16[256,256]{1,0:T(8,128)(2,1)S(1)}, u32[]{:S(2)}, u32[]{:S(2)}) collective-permute-start(bf16[256,256]{1,0:T(8,128)(2,1)} %copy-done.3), channel_id=1, source_target_pairs={{2,0},{4,2},{6,4},{8,6},{10,8},{12,10},{14,12},{16,14},{18,16},{20... | collective-permute-start | bytes 393224 | tf_op jit(solution)/shard_map/ppermute | solution.py:401
  57.9 23.8 %collective-permute-start.17 = (f32[128,256]{1,0:T(8,128)}, f32[128,256]{1,0:T(8,128)S(1)}, u32[]{:S(2)}, u32[]{:S(2)}) collective-permute-start(f32[128,256]{1,0:T(8,128)} %copy-done.2), channel_id=1, source_target_pairs={{4,0},{6,2},{8,4},{10,6},{12,8},{14,10},{16,12},{18,14},{20,16},{2... | collective-permute-start | bytes 393224 | tf_op jit(solution)/shard_map/ppermute | solution.py:401
  62.5 35.2 %all-to-all-start.1 = ((bf16[32,32,256]{2,1,0:T(8,128)(2,1)}), bf16[32,32,256]{2,1,0:T(8,128)(2,1)S(1)}, u32[]{:S(2)}, u32[]{:S(2)}) async-start(bf16[32,32,256]{2,1,0:T(8,128)(2,1)} %bitcast.11), calls=%async_computation.1 | async-start | bytes 1048576 | tf_op jit(solution)/shard_map/all_to_all | solution.py:459
  82.3 3.8 %collective-permute-start.18 = (f32[224,1024]{1,0:T(8,128)}, f32[224,1024]{1,0:T(8,128)S(1)}, u32[]{:S(2)}, u32[]{:S(2)}) collective-permute-start(f32[224,1024]{1,0:T(8,128)} %copy-done.1), channel_id=1, source_target_pairs={{0,1},{1,0},{2,3},{3,2},{4,5},{5,4},{6,7},{7,6},{8,9},{9,8},{10,11... | collective-permute-start | bytes 2752520 | tf_op jit(solution)/shard_map/ppermute | solution.py:409
  83.6 2.5 %collective-permute-start.20 = (bf16[128,256]{1,0:T(8,128)(2,1)}, bf16[128,256]{1,0:T(8,128)(2,1)S(1)}, u32[]{:S(2)}, u32[]{:S(2)}) collective-permute-start(bf16[128,256]{1,0:T(8,128)(2,1)} %copy-done.4), channel_id=1, source_target_pairs={{0,1},{1,0},{2,3},{3,2},{4,5},{5,4},{6,7},{7,6},{8,9},{9,8},{10,11... | collective-permute-start | bytes 196616 | tf_op jit(solution)/shard_map/ppermute | solution.py:409
  83.7 2.4 %collective-permute-start.19 = (bf16[128,256]{1,0:T(8,128)(2,1)S(1)}, bf16[128,256]{1,0:T(8,128)(2,1)S(1)}, u32[]{:S(2)}, u32[]{:S(2)}) collective-permute-start(bf16[128,256]{1,0:T(8,128)(2,1)S(1)} %get-tuple-element.88), channel_id=1, source_target_pairs={{0,1},{1,0},{2,3},{3,2},{4,5},{5,4},{6,7},{7,6},{8,9},{9,8},{10,11... | collective-permute-start | bytes 196616 | tf_op jit(solution)/shard_map/ppermute | solution.py:409
  98.3 4.2 %collective-permute-start.21 = (f32[16,256]{1,0:T(8,128)S(1)}, f32[16,256]{1,0:T(8,128)S(1)}, u32[]{:S(2)}, u32[]{:S(2)}) collective-permute-start(f32[16,256]{1,0:T(8,128)S(1)} %get-tuple-element.97), channel_id=1, source_target_pairs={{0,1},{1,0},{2,3},{3,2},{4,5},{5,4},{6,7},{7,6},{8,9},{9,8},{10,11... | collective-permute-start | bytes 49160 | tf_op jit(solution)/shard_map/ppermute | solution.py:409
  (5 other events, 43.2 us)

commit v12 on v10

--- a/solution.py
+++ b/solution.py
@@ -255,6 +255,20 @@
     )(ids, prob, queries, grads, *keys, *values)
 
 
+def widen_kernel(in_ref, out_ref):
+    out_ref[...] = in_ref[...].astype(F32)
+
+
+def widen_call(block):
+    return pl.pallas_call(
+        widen_kernel,
+        out_shape=shape(*block.shape, dtype=F32),
+        compiler_params=PARAMS,
+        cost_estimate=cost(0, 0.25),
+        name="widen",
+    )(block)
+
+
 def pack_kernel(ids, in_ref, o0, o1, o2, o3):
     for d, out_ref in enumerate((o0, o1, o2, o3)):
         x = (ids[1] + d) & 3
@@ -445,7 +459,7 @@
     packed = pack_call(ids, inputs)
     own = [packed[0]] + [shift_x(packed[d], d) for d in range(1, 4)]
     other = [swap_core(block) for block in own]
-    value_r2 = shift_chips(value_t2, -2)
+    value_r2 = widen_call(shift_chips(value_t2, -2))
     value_r1 = shift_chips(value_t1, -1)
     query_keep, query_send, key_own, key_t1, key_t2 = backward_call(
         ids, prob, queries, grads, keys, values

time: 101 us -> 102 us (level)
  the two profiles are of different devices: /device:TPU:7 before, /device:TPU:1 now
where the time goes in v12:
time: 102 us
  starting transfers between devices  60.2 us (59%)
  waiting for transfers between devices  17.5 us (17%)
  Pallas kernels  17.1 us (17%)
  local copies, waits for them, and re-layouts  4.77 us (5%)
  other arithmetic  1.36 us (1%)
    all_to_all x1, starting transfers between devices, shards(): lax.all_to_all(partial.reshape(32, 32, HALF), ('zl', 'zh', 'y'), 0, 0, ti...  19.7 us
    ppermute x12, starting transfers between devices, swap_core(): return lax.ppermute(block, 'c', [(0, 1), (1, 0)])  13.5 us
    ppermute x7, starting transfers between devices, shift_chips(): return lax.ppermute(block, CHIP, route)  12.4 us
    ppermute x3, starting transfers between devices, shift_x(): return lax.ppermute(block, 'x', [(i, (i + distance) % 4) for i in range(4)])  11.2 us
    all_to_all x1, waiting for transfers between devices, shards(): lax.all_to_all(partial.reshape(32, 32, HALF), ('zl', 'zh', 'y'), 0, 0, ti...  10.1 us
    ppermute x12, waiting for transfers between devices, swap_core(): return lax.ppermute(block, 'c', [(0, 1), (1, 0)])  3.83 us
    pallas_call x1, Pallas kernels, backward_call(): pl.pallas_call(backward_kernel, grid_spec=pltpu.PrefetchScalarGridSpec(nu...  3.82 us
    all_to_all x1, starting transfers between devices, shards(): gathered = lax.all_to_all(sent, 'x', 0, 0, tiled=True)  3.47 us
  transfers between devices with their start and end apart: 24, of which 6 were waited for; matrix products, arithmetic and copies ran while one was open for 4% of the time, Pallas kernels for 16%

profile of v12, /device:TPU:1, one launch (start us, length us, event | category | flops | bytes accessed | tf_op | source)
XLA Modules:
  0.0 101.9 jit_solution(6895454176628443418)
XLA Ops:
  0.6 3.3 %collective-permute-start = (bf16[128,512]{1,0:T(8,128)(2,1)}, bf16[128,512]{1,0:T(8,128)(2,1)S(1)}, u32[]{:S(2)}, u32[]{:S(2)}) collective-permute-start(bf16[128,512]{1,0:T(8,128)(2,1)} %bitcast.22), channel_id=1, source_target_pairs={{0,1},{1,0},{2,3},{3,2},{4,5},{5,4},{6,7},{7,6},{8,9},{9,8},{10,11... | collective-permute-start | bytes 393224 | tf_op jit(solution)/shard_map/ppermute | solution.py:423
  7.8 1.5 %collective-permute-start.5 = (bf16[256,256]{1,0:T(8,128)(2,1)S(1)}, bf16[256,256]{1,0:T(8,128)(2,1)S(1)}, u32[]{:S(2)}, u32[]{:S(2)}) collective-permute-start(bf16[256,256]{1,0:T(8,128)(2,1)S(1)} %pick_keys.1.keys.k0), channel_id=1, source_target_pairs={{0,2},{2,4},{4,6},{6,8},{8,10},{10,12},{12,14},{14,16},{16,18},{18... | collective-permute-start | bytes 393224 | tf_op jit(solution)/shard_map/ppermute | solution.py:415
  10.8 3.6 %collective-permute-start.4 = (bf16[128,512]{1,0:T(8,128)(2,1)S(1)}, bf16[128,512]{1,0:T(8,128)(2,1)S(1)}, u32[]{:S(2)}, u32[]{:S(2)}) collective-permute-start(bf16[128,512]{1,0:T(8,128)(2,1)S(1)} %get-tuple-element.65), channel_id=1, source_target_pairs={{0,4},{2,6},{4,8},{6,10},{8,12},{10,14},{12,16},{14,18},{16,20},{1... | collective-permute-start | bytes 393224 | tf_op jit(solution)/shard_map/ppermute | solution.py:415
  15.4 1.1 %constant_dynamic-slice_fusion.g_own = bf16[128,1024]{1,0:T(8,128)(2,1)S(1)} fusion(bf16[128,2048]{1,0:T(8,128)(2,1)} %bitcast.21, s32[]{:T(128)S(6)} %select_n.21), kind=kLoop, calls=%fused_computation.6 | loop fusion | bytes 524292 | tf_op jit(solution)/shard_map/dynamic_slice | solution.py:428
  17.2 2.2 %collective-permute-start.7 = (bf16[256,256]{1,0:T(8,128)(2,1)S(1)}, bf16[256,256]{1,0:T(8,128)(2,1)S(1)}, u32[]{:S(2)}, u32[]{:S(2)}) collective-permute-start(bf16[256,256]{1,0:T(8,128)(2,1)S(1)} %get-tuple-element.70.v0), channel_id=1, source_target_pairs={{0,2},{2,4},{4,6},{6,8},{8,10},{10,12},{12,14},{14,16},{16,18},{18... | collective-permute-start | bytes 393224 | tf_op jit(solution)/shard_map/ppermute | solution.py:415
  19.4 3.3 %forward_and_value_gradient.1 = (bf16[2,2,512,512]{3,2,1,0:T(8,128)(2,1)S(1)}, f32[256,256]{1,0:T(8,128)S(1)}, bf16[256,256]{1,0:T(8,128)(2,1)S(1)}, bf16[128,256]{1,0:T(8,128)(2,1)S(1)}) custom-call(f32[2,512,128]{2,1,0:T(8,128)S(1)} %get-tuple-element.62.bias, bf16[256,1024]{1,0:T(8,128)(2,1)S(1)} %get-tuple-element.63.q_ref, ...), custom_call_target="tpu_custom_call" | custom-call | flops 536870912 | bytes 6291456 | tf_op jit(solution)/shard_map/forward_and_value_gradient/pallas_call | solution.py:223
  22.7 1.3 %collective-permute-start.8 = (bf16[128,256]{1,0:T(8,128)(2,1)S(1)}, bf16[128,256]{1,0:T(8,128)(2,1)S(1)}, u32[]{:S(2)}, u32[]{:S(2)}) collective-permute-start(bf16[128,256]{1,0:T(8,128)(2,1)S(1)} %get-tuple-element.73), channel_id=1, source_target_pairs={{4,0},{6,2},{8,4},{10,6},{12,8},{14,10},{16,12},{18,14},{20,16},{2... | collective-permute-start | bytes 196616 | tf_op jit(solution)/shard_map/ppermute | solution.py:415
  24.0 1.3 %collective-permute-start.6 = (bf16[256,256]{1,0:T(8,128)(2,1)S(1)}, bf16[256,256]{1,0:T(8,128)(2,1)S(1)}, u32[]{:S(2)}, u32[]{:S(2)}) collective-permute-start(bf16[256,256]{1,0:T(8,128)(2,1)S(1)} %get-tuple-element.68), channel_id=1, source_target_pairs={{2,0},{4,2},{6,4},{8,6},{10,8},{12,10},{14,12},{16,14},{18,16},{20... | collective-permute-start | bytes 393224 | tf_op jit(solution)/shard_map/ppermute | solution.py:415
  26.1 5.8 %collective-permute-start.9 = (bf16[128,1024]{1,0:T(8,128)(2,1)S(1)}, bf16[128,1024]{1,0:T(8,128)(2,1)S(1)}, u32[]{:S(2)}, u32[]{:S(2)}) collective-permute-start(bf16[128,1024]{1,0:T(8,128)(2,1)S(1)} %get-tuple-element.77), channel_id=1, source_target_pairs={{0,8},{8,16},{16,24},{24,0},{1,9},{9,17},{17,25},{25,1},{2,10},{10... | collective-permute-start | bytes 786440 | tf_op jit(solution)/shard_map/ppermute | solution.py:419
  31.9 4.8 %collective-permute-start.10 = (bf16[128,1024]{1,0:T(8,128)(2,1)S(1)}, bf16[128,1024]{1,0:T(8,128)(2,1)S(1)}, u32[]{:S(2)}, u32[]{:S(2)}) collective-permute-start(bf16[128,1024]{1,0:T(8,128)(2,1)S(1)} %get-tuple-element.78), channel_id=1, source_target_pairs={{0,16},{8,24},{16,0},{24,8},{1,17},{9,25},{17,1},{25,9},{2,18},{10... | collective-permute-start | bytes 786440 | tf_op jit(solution)/shard_map/ppermute | solution.py:419
  37.3 3.8 %query_and_key_gradient.1 = (bf16[128,1024]{1,0:T(8,128)(2,1)S(1)}, f32[224,1024]{1,0:T(8,128)S(1)}, f32[256,256]{1,0:T(8,128)S(1)}, bf16[256,256]{1,0:T(8,128)(2,1)S(1)}, f32[128,256]{1,0:T(8,128)S(1)}) custom-call(s32[3]{0:T(128)S(1)} %pad_add_fusion.1.ids, bf16[2,2,512,512]{3,2,1,0:T(8,128)(2,1)S(1)} %get-tuple-element.69.prob_ref, ...), custom_call_target="tpu_custom_call" | custom-call | flops 805306368 | bytes 6291456 | tf_op jit(solution)/shard_map/query_and_key_gradient/pallas_call | solution.py:238
  42.1 1.4 %value_gradient_total.1 = (bf16[128,256]{1,0:T(8,128)(2,1)S(1)}, bf16[128,256]{1,0:T(8,128)(2,1)S(1)}, bf16[4,256,256]{2,1,0:T(8,128)(2,1)}) custom-call(s32[3]{0:T(128)S(1)} %pad_add_fusion.1.ids, f32[256,256]{1,0:T(8,128)S(1)} %get-tuple-element.67.own, bf16[256,256]{1,0:T(8,128)(2,1)S(1)} %collective-permute-done.6.r1, f32[128,256]{1,0:T(8,128)S(1)} %widen.1.r2), custom_call_target="tpu_custom_call" | custom-call | bytes 1048576 | tf_op jit(solution)/shard_map/value_gradient_total/pallas_call | solution.py:316
  43.5 3.5 %all-to-all-start = ((bf16[4,256,256]{2,1,0:T(8,128)(2,1)}), bf16[4,256,256]{2,1,0:T(8,128)(2,1)S(1)}, u32[]{:S(2)}, u32[]{:S(2)}) async-start(bf16[4,256,256]{2,1,0:T(8,128)(2,1)} %get-tuple-element.74), calls=%async_computation | async-start | bytes 1048576 | tf_op jit(solution)/shard_map/all_to_all | solution.py:471
  46.9 2.8 %collective-permute-start.12 = (bf16[128,1024]{1,0:T(8,128)(2,1)S(1)}, bf16[128,1024]{1,0:T(8,128)(2,1)S(1)}, u32[]{:S(2)}, u32[]{:S(2)}) collective-permute-start(bf16[128,1024]{1,0:T(8,128)(2,1)S(1)} %get-tuple-element.76.a0), channel_id=1, source_target_pairs={{0,1},{1,0},{2,3},{3,2},{4,5},{5,4},{6,7},{7,6},{8,9},{9,8},{10,11... | collective-permute-start | bytes 786440 | tf_op jit(solution)/shard_map/ppermute | solution.py:423
  50.2 2.7 %collective-permute-done.11.a3 = bf16[128,1024]{1,0:T(8,128)(2,1)S(1)} collective-permute-done((bf16[128,1024]{1,0:T(8,128)(2,1)S(1)}, bf16[128,1024]{1,0:T(8,128)(2,1)S(1)}, u32[]{:S(2)}, u32[]{:S(2)}) %collective-permute-start.11) | collective-permute-done | bytes 262176 | tf_op jit(solution)/shard_map/ppermute | solution.py:419
  53.9 1.3 %collective-permute-start.16 = (bf16[256,256]{1,0:T(8,128)(2,1)}, bf16[256,256]{1,0:T(8,128)(2,1)S(1)}, u32[]{:S(2)}, u32[]{:S(2)}) collective-permute-start(bf16[256,256]{1,0:T(8,128)(2,1)} %copy-done.3), channel_id=1, source_target_pairs={{2,0},{4,2},{6,4},{8,6},{10,8},{12,10},{14,12},{16,14},{18,16},{20... | collective-permute-start | bytes 393224 | tf_op jit(solution)/shard_map/ppermute | solution.py:415
  55.2 1.3 %collective-permute-start.17 = (f32[128,256]{1,0:T(8,128)}, f32[128,256]{1,0:T(8,128)S(1)}, u32[]{:S(2)}, u32[]{:S(2)}) collective-permute-start(f32[128,256]{1,0:T(8,128)} %copy-done.2), channel_id=1, source_target_pairs={{4,0},{6,2},{8,4},{10,6},{12,8},{14,10},{16,12},{18,14},{20,16},{2... | collective-permute-start | bytes 393224 | tf_op jit(solution)/shard_map/ppermute | solution.py:415
  57.4 3.2 %weight_gradient.1 = bf16[1024,256]{1,0:T(8,128)(2,1)} custom-call(s32[3]{0:T(128)S(1)} %pad_add_fusion.1.ids, bf16[4,256,256]{2,1,0:T(8,128)(2,1)S(1)} %all-to-all-done.grads, bf16[128,1024]{1,0:T(8,128)(2,1)S(1)} %get-tuple-element.76.a0, bf16[128,1024]{1,0:T(8,128)(2,1)S(1)} %collective-permute-done.9.a1, ...), custom_call_target="tpu_custom_call" | custom-call | flops 536870912 | bytes 3145728 | tf_op jit(solution)/shard_map/weight_gradient/pallas_call | solution.py:371
  60.7 19.7 %all-to-all-start.1 = ((bf16[32,32,256]{2,1,0:T(8,128)(2,1)}), bf16[32,32,256]{2,1,0:T(8,128)(2,1)S(1)}, u32[]{:S(2)}, u32[]{:S(2)}) async-start(bf16[32,32,256]{2,1,0:T(8,128)(2,1)} %bitcast.11), calls=%async_computation.1 | async-start | bytes 1048576 | tf_op jit(solution)/shard_map/all_to_all | solution.py:473
  81.0 1.3 %collective-permute-start.18 = (f32[224,1024]{1,0:T(8,128)}, f32[224,1024]{1,0:T(8,128)S(1)}, u32[]{:S(2)}, u32[]{:S(2)}) collective-permute-start(f32[224,1024]{1,0:T(8,128)} %copy-done.1), channel_id=1, source_target_pairs={{0,1},{1,0},{2,3},{3,2},{4,5},{5,4},{6,7},{7,6},{8,9},{9,8},{10,11... | collective-permute-start | bytes 2752520 | tf_op jit(solution)/shard_map/ppermute | solution.py:423
  82.8 2.0 %collective-permute-done.20.value_other = bf16[128,256]{1,0:T(8,128)(2,1)S(1)} collective-permute-done((bf16[128,256]{1,0:T(8,128)(2,1)}, bf16[128,256]{1,0:T(8,128)(2,1)S(1)}, u32[]{:S(2)}, u32[]{:S(2)}) %collective-permute-start.20) | collective-permute-done | bytes 65568 | tf_op jit(solution)/shard_map/ppermute | solution.py:423
  84.8 1.5 %join_outputs.1 = (bf16[128,2048]{1,0:T(8,128)(2,1)}, bf16[128,512]{1,0:T(8,128)(2,1)}, bf16[128,512]{1,0:T(8,128)(2,1)}) custom-call(s32[3]{0:T(128)S(1)} %pad_add_fusion.1.ids, bf16[128,1024]{1,0:T(8,128)(2,1)S(1)} %get-tuple-element.80.query, f32[224,1024]{1,0:T(8,128)S(1)} %collective-permute-done.18.query_other, ...), custom_call_target="tpu_custom_call" | custom-call | bytes 2097152 | tf_op jit(solution)/shard_map/join_outputs/pallas_call | solution.py:346
  86.3 10.1 %all-to-all-done.1.in_ref = bf16[32,32,256]{2,1,0:T(8,128)(2,1)S(1)} async-done(((bf16[32,32,256]{2,1,0:T(8,128)(2,1)}), bf16[32,32,256]{2,1,0:T(8,128)(2,1)S(1)}, u32[]{:S(2)}, u32[]{:S(2)}) %all-to-all-start.1) | async-done | bytes 524320 | tf_op jit(solution)/shard_map/all_to_all | solution.py:473
  97.0 3.4 %collective-permute-start.21 = (f32[16,256]{1,0:T(8,128)S(1)}, f32[16,256]{1,0:T(8,128)S(1)}, u32[]{:S(2)}, u32[]{:S(2)}) collective-permute-start(f32[16,256]{1,0:T(8,128)S(1)} %get-tuple-element.97), channel_id=1, source_target_pairs={{0,1},{1,0},{2,3},{3,2},{4,5},{5,4},{6,7},{7,6},{8,9},{9,8},{10,11... | collective-permute-start | bytes 49160 | tf_op jit(solution)/shard_map/ppermute | solution.py:423
  (55 shorter events, 15.0 us)
Async XLA Ops:
  0.6 5.9 %collective-permute-start = (bf16[128,512]{1,0:T(8,128)(2,1)}, bf16[128,512]{1,0:T(8,128)(2,1)S(1)}, u32[]{:S(2)}, u32[]{:S(2)}) collective-permute-start(bf16[128,512]{1,0:T(8,128)(2,1)} %bitcast.22), channel_id=1, source_target_pairs={{0,1},{1,0},{2,3},{3,2},{4,5},{5,4},{6,7},{7,6},{8,9},{9,8},{10,11... | collective-permute-start | bytes 393224 | tf_op jit(solution)/shard_map/ppermute | solution.py:423
  7.1 9.3 %collective-permute-start.1 = (bf16[128,2048]{1,0:T(8,128)(2,1)}, bf16[128,2048]{1,0:T(8,128)(2,1)S(1)}, u32[]{:S(2)}, u32[]{:S(2)}) collective-permute-start(bf16[128,2048]{1,0:T(8,128)(2,1)} %bitcast.18), channel_id=1, source_target_pairs={{0,1},{1,0},{2,3},{3,2},{4,5},{5,4},{6,7},{7,6},{8,9},{9,8},{10,11... | collective-permute-start | bytes 1572872 | tf_op jit(solution)/shard_map/ppermute | solution.py:423
  7.2 9.2 %collective-permute-start.2 = (bf16[128,2048]{1,0:T(8,128)(2,1)}, bf16[128,2048]{1,0:T(8,128)(2,1)S(1)}, u32[]{:S(2)}, u32[]{:S(2)}) collective-permute-start(bf16[128,2048]{1,0:T(8,128)(2,1)} %bitcast.20), channel_id=1, source_target_pairs={{0,1},{1,0},{2,3},{3,2},{4,5},{5,4},{6,7},{7,6},{8,9},{9,8},{10,11... | collective-permute-start | bytes 1572872 | tf_op jit(solution)/shard_map/ppermute | solution.py:423
  7.7 2.5 %collective-permute-start.3 = (bf16[128,512]{1,0:T(8,128)(2,1)}, bf16[128,512]{1,0:T(8,128)(2,1)S(1)}, u32[]{:S(2)}, u32[]{:S(2)}) collective-permute-start(bf16[128,512]{1,0:T(8,128)(2,1)} %bitcast.23), channel_id=1, source_target_pairs={{0,1},{1,0},{2,3},{3,2},{4,5},{5,4},{6,7},{7,6},{8,9},{9,8},{10,11... | collective-permute-start | bytes 393224 | tf_op jit(solution)/shard_map/ppermute | solution.py:423
  7.8 11.6 %collective-permute-start.5 = (bf16[256,256]{1,0:T(8,128)(2,1)S(1)}, bf16[256,256]{1,0:T(8,128)(2,1)S(1)}, u32[]{:S(2)}, u32[]{:S(2)}) collective-permute-start(bf16[256,256]{1,0:T(8,128)(2,1)S(1)} %pick_keys.1.keys.k0), channel_id=1, source_target_pairs={{0,2},{2,4},{4,6},{6,8},{8,10},{10,12},{12,14},{14,16},{16,18},{18... | collective-permute-start | bytes 393224 | tf_op jit(solution)/shard_map/ppermute | solution.py:415
  10.8 8.6 %collective-permute-start.4 = (bf16[128,512]{1,0:T(8,128)(2,1)S(1)}, bf16[128,512]{1,0:T(8,128)(2,1)S(1)}, u32[]{:S(2)}, u32[]{:S(2)}) collective-permute-start(bf16[128,512]{1,0:T(8,128)(2,1)S(1)} %get-tuple-element.65), channel_id=1, source_target_pairs={{0,4},{2,6},{4,8},{6,10},{8,12},{10,14},{12,16},{14,18},{16,20},{1... | collective-permute-start | bytes 393224 | tf_op jit(solution)/shard_map/ppermute | solution.py:415
  17.2 20.1 %collective-permute-start.7 = (bf16[256,256]{1,0:T(8,128)(2,1)S(1)}, bf16[256,256]{1,0:T(8,128)(2,1)S(1)}, u32[]{:S(2)}, u32[]{:S(2)}) collective-permute-start(bf16[256,256]{1,0:T(8,128)(2,1)S(1)} %get-tuple-element.70.v0), channel_id=1, source_target_pairs={{0,2},{2,4},{4,6},{6,8},{8,10},{10,12},{12,14},{14,16},{16,18},{18... | collective-permute-start | bytes 393224 | tf_op jit(solution)/shard_map/ppermute | solution.py:415
  22.7 14.0 %collective-permute-start.8 = (bf16[128,256]{1,0:T(8,128)(2,1)S(1)}, bf16[128,256]{1,0:T(8,128)(2,1)S(1)}, u32[]{:S(2)}, u32[]{:S(2)}) collective-permute-start(bf16[128,256]{1,0:T(8,128)(2,1)S(1)} %get-tuple-element.73), channel_id=1, source_target_pairs={{4,0},{6,2},{8,4},{10,6},{12,8},{14,10},{16,12},{18,14},{20,16},{2... | collective-permute-start | bytes 196616 | tf_op jit(solution)/shard_map/ppermute | solution.py:415
  24.0 18.1 %collective-permute-start.6 = (bf16[256,256]{1,0:T(8,128)(2,1)S(1)}, bf16[256,256]{1,0:T(8,128)(2,1)S(1)}, u32[]{:S(2)}, u32[]{:S(2)}) collective-permute-start(bf16[256,256]{1,0:T(8,128)(2,1)S(1)} %get-tuple-element.68), channel_id=1, source_target_pairs={{2,0},{4,2},{6,4},{8,6},{10,8},{12,10},{14,12},{16,14},{18,16},{20... | collective-permute-start | bytes 393224 | tf_op jit(solution)/shard_map/ppermute | solution.py:415
  26.1 23.6 %collective-permute-start.9 = (bf16[128,1024]{1,0:T(8,128)(2,1)S(1)}, bf16[128,1024]{1,0:T(8,128)(2,1)S(1)}, u32[]{:S(2)}, u32[]{:S(2)}) collective-permute-start(bf16[128,1024]{1,0:T(8,128)(2,1)S(1)} %get-tuple-element.77), channel_id=1, source_target_pairs={{0,8},{8,16},{16,24},{24,0},{1,9},{9,17},{17,25},{25,1},{2,10},{10... | collective-permute-start | bytes 786440 | tf_op jit(solution)/shard_map/ppermute | solution.py:419
  31.9 17.9 %collective-permute-start.10 = (bf16[128,1024]{1,0:T(8,128)(2,1)S(1)}, bf16[128,1024]{1,0:T(8,128)(2,1)S(1)}, u32[]{:S(2)}, u32[]{:S(2)}) collective-permute-start(bf16[128,1024]{1,0:T(8,128)(2,1)S(1)} %get-tuple-element.78), channel_id=1, source_target_pairs={{0,16},{8,24},{16,0},{24,8},{1,17},{9,25},{17,1},{25,9},{2,18},{10... | collective-permute-start | bytes 786440 | tf_op jit(solution)/shard_map/ppermute | solution.py:419
  36.7 16.2 %collective-permute-start.11 = (bf16[128,1024]{1,0:T(8,128)(2,1)S(1)}, bf16[128,1024]{1,0:T(8,128)(2,1)S(1)}, u32[]{:S(2)}, u32[]{:S(2)}) collective-permute-start(bf16[128,1024]{1,0:T(8,128)(2,1)S(1)} %get-tuple-element.79), channel_id=1, source_target_pairs={{0,24},{8,0},{16,8},{24,16},{1,25},{9,1},{17,9},{25,17},{2,26},{10... | collective-permute-start | bytes 786440 | tf_op jit(solution)/shard_map/ppermute | solution.py:419
  43.5 14.0 %all-to-all-start = ((bf16[4,256,256]{2,1,0:T(8,128)(2,1)}), bf16[4,256,256]{2,1,0:T(8,128)(2,1)S(1)}, u32[]{:S(2)}, u32[]{:S(2)}) async-start(bf16[4,256,256]{2,1,0:T(8,128)(2,1)} %get-tuple-element.74), calls=%async_computation | async-start | bytes 1048576 | tf_op jit(solution)/shard_map/all_to_all | solution.py:471
  46.9 8.3 %collective-permute-start.12 = (bf16[128,1024]{1,0:T(8,128)(2,1)S(1)}, bf16[128,1024]{1,0:T(8,128)(2,1)S(1)}, u32[]{:S(2)}, u32[]{:S(2)}) collective-permute-start(bf16[128,1024]{1,0:T(8,128)(2,1)S(1)} %get-tuple-element.76.a0), channel_id=1, source_target_pairs={{0,1},{1,0},{2,3},{3,2},{4,5},{5,4},{6,7},{7,6},{8,9},{9,8},{10,11... | collective-permute-start | bytes 786440 | tf_op jit(solution)/shard_map/ppermute | solution.py:423
  49.7 7.7 %collective-permute-start.13 = (bf16[128,1024]{1,0:T(8,128)(2,1)S(1)}, bf16[128,1024]{1,0:T(8,128)(2,1)S(1)}, u32[]{:S(2)}, u32[]{:S(2)}) collective-permute-start(bf16[128,1024]{1,0:T(8,128)(2,1)S(1)} %collective-permute-done.9.a1), channel_id=1, source_target_pairs={{0,1},{1,0},{2,3},{3,2},{4,5},{5,4},{6,7},{7,6},{8,9},{9,8},{10,11... | collective-permute-start | bytes 786440 | tf_op jit(solution)/shard_map/ppermute | solution.py:423
  49.8 7.6 %collective-permute-start.14 = (bf16[128,1024]{1,0:T(8,128)(2,1)S(1)}, bf16[128,1024]{1,0:T(8,128)(2,1)S(1)}, u32[]{:S(2)}, u32[]{:S(2)}) collective-permute-start(bf16[128,1024]{1,0:T(8,128)(2,1)S(1)} %collective-permute-done.10.a2), channel_id=1, source_target_pairs={{0,1},{1,0},{2,3},{3,2},{4,5},{5,4},{6,7},{7,6},{8,9},{9,8},{10,11... | collective-permute-start | bytes 786440 | tf_op jit(solution)/shard_map/ppermute | solution.py:423
  52.9 4.5 %collective-permute-start.15 = (bf16[128,1024]{1,0:T(8,128)(2,1)S(1)}, bf16[128,1024]{1,0:T(8,128)(2,1)S(1)}, u32[]{:S(2)}, u32[]{:S(2)}) collective-permute-start(bf16[128,1024]{1,0:T(8,128)(2,1)S(1)} %collective-permute-done.11.a3), channel_id=1, source_target_pairs={{0,1},{1,0},{2,3},{3,2},{4,5},{5,4},{6,7},{7,6},{8,9},{9,8},{10,11... | collective-permute-start | bytes 786440 | tf_op jit(solution)/shard_map/ppermute | solution.py:423
  53.9 26.4 %collective-permute-start.16 = (bf16[256,256]{1,0:T(8,128)(2,1)}, bf16[256,256]{1,0:T(8,128)(2,1)S(1)}, u32[]{:S(2)}, u32[]{:S(2)}) collective-permute-start(bf16[256,256]{1,0:T(8,128)(2,1)} %copy-done.3), channel_id=1, source_target_pairs={{2,0},{4,2},{6,4},{8,6},{10,8},{12,10},{14,12},{16,14},{18,16},{20... | collective-permute-start | bytes 393224 | tf_op jit(solution)/shard_map/ppermute | solution.py:415
  55.2 25.1 %collective-permute-start.17 = (f32[128,256]{1,0:T(8,128)}, f32[128,256]{1,0:T(8,128)S(1)}, u32[]{:S(2)}, u32[]{:S(2)}) collective-permute-start(f32[128,256]{1,0:T(8,128)} %copy-done.2), channel_id=1, source_target_pairs={{4,0},{6,2},{8,4},{10,6},{12,8},{14,10},{16,12},{18,14},{20,16},{2... | collective-permute-start | bytes 393224 | tf_op jit(solution)/shard_map/ppermute | solution.py:415
  60.7 35.7 %all-to-all-start.1 = ((bf16[32,32,256]{2,1,0:T(8,128)(2,1)}), bf16[32,32,256]{2,1,0:T(8,128)(2,1)S(1)}, u32[]{:S(2)}, u32[]{:S(2)}) async-start(bf16[32,32,256]{2,1,0:T(8,128)(2,1)} %bitcast.11), calls=%async_computation.1 | async-start | bytes 1048576 | tf_op jit(solution)/shard_map/all_to_all | solution.py:473
  81.0 3.8 %collective-permute-start.18 = (f32[224,1024]{1,0:T(8,128)}, f32[224,1024]{1,0:T(8,128)S(1)}, u32[]{:S(2)}, u32[]{:S(2)}) collective-permute-start(f32[224,1024]{1,0:T(8,128)} %copy-done.1), channel_id=1, source_target_pairs={{0,1},{1,0},{2,3},{3,2},{4,5},{5,4},{6,7},{7,6},{8,9},{9,8},{10,11... | collective-permute-start | bytes 2752520 | tf_op jit(solution)/shard_map/ppermute | solution.py:423
  82.3 2.5 %collective-permute-start.20 = (bf16[128,256]{1,0:T(8,128)(2,1)}, bf16[128,256]{1,0:T(8,128)(2,1)S(1)}, u32[]{:S(2)}, u32[]{:S(2)}) collective-permute-start(bf16[128,256]{1,0:T(8,128)(2,1)} %copy-done.4), channel_id=1, source_target_pairs={{0,1},{1,0},{2,3},{3,2},{4,5},{5,4},{6,7},{7,6},{8,9},{9,8},{10,11... | collective-permute-start | bytes 196616 | tf_op jit(solution)/shard_map/ppermute | solution.py:423
  82.4 2.4 %collective-permute-start.19 = (bf16[128,256]{1,0:T(8,128)(2,1)S(1)}, bf16[128,256]{1,0:T(8,128)(2,1)S(1)}, u32[]{:S(2)}, u32[]{:S(2)}) collective-permute-start(bf16[128,256]{1,0:T(8,128)(2,1)S(1)} %get-tuple-element.88), channel_id=1, source_target_pairs={{0,1},{1,0},{2,3},{3,2},{4,5},{5,4},{6,7},{7,6},{8,9},{9,8},{10,11... | collective-permute-start | bytes 196616 | tf_op jit(solution)/shard_map/ppermute | solution.py:423
  97.0 4.2 %collective-permute-start.21 = (f32[16,256]{1,0:T(8,128)S(1)}, f32[16,256]{1,0:T(8,128)S(1)}, u32[]{:S(2)}, u32[]{:S(2)}) collective-permute-start(f32[16,256]{1,0:T(8,128)S(1)} %get-tuple-element.97), channel_id=1, source_target_pairs={{0,1},{1,0},{2,3},{3,2},{4,5},{5,4},{6,7},{7,6},{8,9},{9,8},{10,11... | collective-permute-start | bytes 49160 | tf_op jit(solution)/shard_map/ppermute | solution.py:423
  (5 other events, 43.5 us)

commit v13 on v12

--- a/solution.py
+++ b/solution.py
@@ -248,7 +248,7 @@
             shape(ROWS, GROUPS * WIDE),
             shape(ROWS + EXTRA, GROUPS * WIDE, dtype=F32),
         ]
-        + term_shapes(F32),
+        + term_shapes(BF16),
         compiler_params=LARGE,
         cost_estimate=cost(6 * 16 * ROWS * KEYS * HEAD, 6),
         name="query_and_key_gradient",
@@ -459,14 +459,14 @@
     packed = pack_call(ids, inputs)
     own = [packed[0]] + [shift_x(packed[d], d) for d in range(1, 4)]
     other = [swap_core(block) for block in own]
-    value_r2 = widen_call(shift_chips(value_t2, -2))
+    value_r2 = shift_chips(value_t2, -2)
     value_r1 = shift_chips(value_t1, -1)
     query_keep, query_send, key_own, key_t1, key_t2 = backward_call(
         ids, prob, queries, grads, keys, values
     )
     value_r1, query_send = lax.optimization_barrier((value_r1, query_send))
     value_keep, value_send, sent = total_call(ids, value_own, value_r1, value_r2, True)
-    key_r2 = shift_chips(key_t2, -2)
+    key_r2 = widen_call(shift_chips(key_t2, -2))
     key_r1 = shift_chips(key_t1, -1)
     gathered = lax.all_to_all(sent, "x", 0, 0, tiled=True)
     partial = weight_call(ids, gathered, own, other)

time: 102 us -> 103 us (level)
  the two profiles are of different devices: /device:TPU:1 before, /device:TPU:63 now
where the time goes in v13:
time: 103 us; the launch traced here: 102 us
  starting transfers between devices  53.7 us (52%)
  waiting for transfers between devices  24.3 us (24%)
  Pallas kernels  17.1 us (17%)
  local copies, waits for them, and re-layouts  4.68 us (5%)
  other arithmetic  1.36 us (1%)
    ppermute x7, starting transfers between devices, shift_chips(): return lax.ppermute(block, CHIP, route)  24.7 us
    ppermute x7, waiting for transfers between devices, shift_chips(): return lax.ppermute(block, CHIP, route)  21.4 us
    all_to_all x1, starting transfers between devices, shards(): lax.all_to_all(partial.reshape(32, 32, HALF), ('zl', 'zh', 'y'), 0, 0, ti...  12.1 us
    ppermute x12, starting transfers between devices, swap_core(): return lax.ppermute(block, 'c', [(0, 1), (1, 0)])  11.5 us
    all_to_all x1, starting transfers between devices, shards(): gathered = lax.all_to_all(sent, 'x', 0, 0, tiled=True)  3.94 us
    pallas_call x1, Pallas kernels, backward_call(): pl.pallas_call(backward_kernel, grid_spec=pltpu.PrefetchScalarGridSpec(nu...  3.82 us
    pallas_call x1, Pallas kernels, weight_call(): pl.pallas_call(weight_kernel, grid_spec=pltpu.PrefetchScalarGridSpec(num_...  3.25 us
    pallas_call x1, Pallas kernels, forward_call(): pl.pallas_call(forward_kernel, grid=(GROUPS,), in_specs=[pl.BlockSpec((2,...  3.25 us
  transfers between devices with their start and end apart: 24, of which 5 were waited for; matrix products, arithmetic and copies ran while one was open for 4% of the time, Pallas kernels for 16%

profile of v13, /device:TPU:63, one launch (start us, length us, event | category | flops | bytes accessed | tf_op | source)
XLA Modules:
  0.0 102.1 jit_solution(12044256623573971377)
XLA Ops:
  5.2 7.5 %collective-permute-start.5 = (bf16[256,256]{1,0:T(8,128)(2,1)S(1)}, bf16[256,256]{1,0:T(8,128)(2,1)S(1)}, u32[]{:S(2)}, u32[]{:S(2)}) collective-permute-start(bf16[256,256]{1,0:T(8,128)(2,1)S(1)} %pick_keys.1.keys.k0), channel_id=1, source_target_pairs={{0,2},{2,4},{4,6},{6,8},{8,10},{10,12},{12,14},{14,16},{16,18},{18... | collective-permute-start | bytes 393224 | tf_op jit(solution)/shard_map/ppermute | solution.py:415
  12.7 1.0 constant_dynamic-slice_fusion.1.q_own
  14.3 4.3 %collective-permute-start.4 = (bf16[128,512]{1,0:T(8,128)(2,1)S(1)}, bf16[128,512]{1,0:T(8,128)(2,1)S(1)}, u32[]{:S(2)}, u32[]{:S(2)}) collective-permute-start(bf16[128,512]{1,0:T(8,128)(2,1)S(1)} %get-tuple-element.65), channel_id=1, source_target_pairs={{0,4},{2,6},{4,8},{6,10},{8,12},{10,14},{12,16},{14,18},{16,20},{1... | collective-permute-start | bytes 393224 | tf_op jit(solution)/shard_map/ppermute | solution.py:415
  18.6 1.0 constant_dynamic-slice_fusion.g_own
  20.4 3.5 %collective-permute-start.7 = (bf16[256,256]{1,0:T(8,128)(2,1)S(1)}, bf16[256,256]{1,0:T(8,128)(2,1)S(1)}, u32[]{:S(2)}, u32[]{:S(2)}) collective-permute-start(bf16[256,256]{1,0:T(8,128)(2,1)S(1)} %get-tuple-element.70.v0), channel_id=1, source_target_pairs={{0,2},{2,4},{4,6},{6,8},{8,10},{10,12},{12,14},{14,16},{16,18},{18... | collective-permute-start | bytes 393224 | tf_op jit(solution)/shard_map/ppermute | solution.py:415
  23.9 3.2 %forward_and_value_gradient.1 = (bf16[2,2,512,512]{3,2,1,0:T(8,128)(2,1)S(1)}, f32[256,256]{1,0:T(8,128)S(1)}, bf16[256,256]{1,0:T(8,128)(2,1)S(1)}, bf16[128,256]{1,0:T(8,128)(2,1)S(1)}) custom-call(f32[2,512,128]{2,1,0:T(8,128)S(1)} %get-tuple-element.62.bias, bf16[256,1024]{1,0:T(8,128)(2,1)S(1)} %get-tuple-element.63.q_ref, ...), custom_call_target="tpu_custom_call" | custom-call | flops 536870912 | bytes 6291456 | tf_op jit(solution)/shard_map/forward_and_value_gradient/pallas_call | solution.py:223
  27.2 1.9 %collective-permute-start.6 = (bf16[256,256]{1,0:T(8,128)(2,1)S(1)}, bf16[256,256]{1,0:T(8,128)(2,1)S(1)}, u32[]{:S(2)}, u32[]{:S(2)}) collective-permute-start(bf16[256,256]{1,0:T(8,128)(2,1)S(1)} %get-tuple-element.68), channel_id=1, source_target_pairs={{2,0},{4,2},{6,4},{8,6},{10,8},{12,10},{14,12},{16,14},{18,16},{20... | collective-permute-start | bytes 393224 | tf_op jit(solution)/shard_map/ppermute | solution.py:415
  30.1 1.4 %collective-permute-start.11 = (bf16[128,1024]{1,0:T(8,128)(2,1)S(1)}, bf16[128,1024]{1,0:T(8,128)(2,1)S(1)}, u32[]{:S(2)}, u32[]{:S(2)}) collective-permute-start(bf16[128,1024]{1,0:T(8,128)(2,1)S(1)} %get-tuple-element.79), channel_id=1, source_target_pairs={{0,24},{8,0},{16,8},{24,16},{1,25},{9,1},{17,9},{25,17},{2,26},{10... | collective-permute-start | bytes 786440 | tf_op jit(solution)/shard_map/ppermute | solution.py:419
  31.5 2.4 %collective-permute-start.8 = (bf16[128,256]{1,0:T(8,128)(2,1)S(1)}, bf16[128,256]{1,0:T(8,128)(2,1)S(1)}, u32[]{:S(2)}, u32[]{:S(2)}) collective-permute-start(bf16[128,256]{1,0:T(8,128)(2,1)S(1)} %get-tuple-element.73), channel_id=1, source_target_pairs={{4,0},{6,2},{8,4},{10,6},{12,8},{14,10},{16,12},{18,14},{20,16},{2... | collective-permute-start | bytes 196616 | tf_op jit(solution)/shard_map/ppermute | solution.py:415
  33.9 3.8 %query_and_key_gradient.1 = (bf16[128,1024]{1,0:T(8,128)(2,1)S(1)}, f32[224,1024]{1,0:T(8,128)S(1)}, f32[256,256]{1,0:T(8,128)S(1)}, bf16[256,256]{1,0:T(8,128)(2,1)S(1)}, bf16[128,256]{1,0:T(8,128)(2,1)S(1)}) custom-call(s32[3]{0:T(128)S(1)} %pad_add_fusion.1.ids, bf16[2,2,512,512]{3,2,1,0:T(8,128)(2,1)S(1)} %get-tuple-element.69.prob_ref, ...), custom_call_target="tpu_custom_call" | custom-call | flops 805306368 | bytes 6291456 | tf_op jit(solution)/shard_map/query_and_key_gradient/pallas_call | solution.py:238
  37.8 0.9 copy-done.1
  38.7 5.8 %collective-permute-done.6.r1 = bf16[256,256]{1,0:T(8,128)(2,1)S(1)} collective-permute-done((bf16[256,256]{1,0:T(8,128)(2,1)S(1)}, bf16[256,256]{1,0:T(8,128)(2,1)S(1)}, u32[]{:S(2)}, u32[]{:S(2)}) %collective-permute-start.6) | collective-permute-done | bytes 131104 | tf_op jit(solution)/shard_map/ppermute | solution.py:415
  44.5 2.3 %collective-permute-done.8.r2 = bf16[128,256]{1,0:T(8,128)(2,1)S(1)} collective-permute-done((bf16[128,256]{1,0:T(8,128)(2,1)S(1)}, bf16[128,256]{1,0:T(8,128)(2,1)S(1)}, u32[]{:S(2)}, u32[]{:S(2)}) %collective-permute-start.8) | collective-permute-done | bytes 65568 | tf_op jit(solution)/shard_map/ppermute | solution.py:415
  46.8 1.4 %value_gradient_total.1 = (bf16[128,256]{1,0:T(8,128)(2,1)S(1)}, bf16[128,256]{1,0:T(8,128)(2,1)S(1)}, bf16[4,256,256]{2,1,0:T(8,128)(2,1)}) custom-call(s32[3]{0:T(128)S(1)} %pad_add_fusion.1.ids, f32[256,256]{1,0:T(8,128)S(1)} %get-tuple-element.67.own, bf16[256,256]{1,0:T(8,128)(2,1)S(1)} %collective-permute-done.6.r1, ...), custom_call_target="tpu_custom_call" | custom-call | bytes 1048576 | tf_op jit(solution)/shard_map/value_gradient_total/pallas_call | solution.py:316
  48.2 3.9 %all-to-all-start = ((bf16[4,256,256]{2,1,0:T(8,128)(2,1)}), bf16[4,256,256]{2,1,0:T(8,128)(2,1)S(1)}, u32[]{:S(2)}, u32[]{:S(2)}) async-start(bf16[4,256,256]{2,1,0:T(8,128)(2,1)} %get-tuple-element.74), calls=%async_computation | async-start | bytes 1048576 | tf_op jit(solution)/shard_map/all_to_all | solution.py:471
  52.1 3.7 %collective-permute-start.12 = (bf16[128,1024]{1,0:T(8,128)(2,1)S(1)}, bf16[128,1024]{1,0:T(8,128)(2,1)S(1)}, u32[]{:S(2)}, u32[]{:S(2)}) collective-permute-start(bf16[128,1024]{1,0:T(8,128)(2,1)S(1)} %get-tuple-element.76.a0), channel_id=1, source_target_pairs={{0,1},{1,0},{2,3},{3,2},{4,5},{5,4},{6,7},{7,6},{8,9},{9,8},{10,11... | collective-permute-start | bytes 786440 | tf_op jit(solution)/shard_map/ppermute | solution.py:423
  56.4 1.9 %collective-permute-start.16 = (bf16[256,256]{1,0:T(8,128)(2,1)S(1)}, bf16[256,256]{1,0:T(8,128)(2,1)S(1)}, u32[]{:S(2)}, u32[]{:S(2)}) collective-permute-start(bf16[256,256]{1,0:T(8,128)(2,1)S(1)} %get-tuple-element.82), channel_id=1, source_target_pairs={{2,0},{4,2},{6,4},{8,6},{10,8},{12,10},{14,12},{16,14},{18,16},{20... | collective-permute-start | bytes 393224 | tf_op jit(solution)/shard_map/ppermute | solution.py:415
  58.4 3.3 %weight_gradient.1 = bf16[1024,256]{1,0:T(8,128)(2,1)} custom-call(s32[3]{0:T(128)S(1)} %pad_add_fusion.1.ids, bf16[4,256,256]{2,1,0:T(8,128)(2,1)S(1)} %all-to-all-done.grads, bf16[128,1024]{1,0:T(8,128)(2,1)S(1)} %get-tuple-element.76.a0, bf16[128,1024]{1,0:T(8,128)(2,1)S(1)} %collective-permute-done.9.a1, ...), custom_call_target="tpu_custom_call" | custom-call | flops 536870912 | bytes 3145728 | tf_op jit(solution)/shard_map/weight_gradient/pallas_call | solution.py:371
  61.7 12.1 %all-to-all-start.1 = ((bf16[32,32,256]{2,1,0:T(8,128)(2,1)}), bf16[32,32,256]{2,1,0:T(8,128)(2,1)S(1)}, u32[]{:S(2)}, u32[]{:S(2)}) async-start(bf16[32,32,256]{2,1,0:T(8,128)(2,1)} %bitcast.11), calls=%async_computation.1 | async-start | bytes 1048576 | tf_op jit(solution)/shard_map/all_to_all | solution.py:473
  73.8 3.1 %collective-permute-start.17 = (bf16[128,256]{1,0:T(8,128)(2,1)}, bf16[128,256]{1,0:T(8,128)(2,1)S(1)}, u32[]{:S(2)}, u32[]{:S(2)}) collective-permute-start(bf16[128,256]{1,0:T(8,128)(2,1)} %copy-done.3), channel_id=1, source_target_pairs={{4,0},{6,2},{8,4},{10,6},{12,8},{14,10},{16,12},{18,14},{20,16},{2... | collective-permute-start | bytes 196616 | tf_op jit(solution)/shard_map/ppermute | solution.py:415
  76.9 13.3 %collective-permute-done.17.in_ref = bf16[128,256]{1,0:T(8,128)(2,1)S(1)} collective-permute-done((bf16[128,256]{1,0:T(8,128)(2,1)}, bf16[128,256]{1,0:T(8,128)(2,1)S(1)}, u32[]{:S(2)}, u32[]{:S(2)}) %collective-permute-start.17) | collective-permute-done | bytes 65568 | tf_op jit(solution)/shard_map/ppermute | solution.py:415
  90.8 4.8 %collective-permute-start.18 = (f32[224,1024]{1,0:T(8,128)}, f32[224,1024]{1,0:T(8,128)S(1)}, u32[]{:S(2)}, u32[]{:S(2)}) collective-permute-start(f32[224,1024]{1,0:T(8,128)} %copy-done.1), channel_id=1, source_target_pairs={{0,1},{1,0},{2,3},{3,2},{4,5},{5,4},{6,7},{7,6},{8,9},{9,8},{10,11... | collective-permute-start | bytes 2752520 | tf_op jit(solution)/shard_map/ppermute | solution.py:423
  96.1 2.0 %collective-permute-done.20.value_other = bf16[128,256]{1,0:T(8,128)(2,1)S(1)} collective-permute-done((bf16[128,256]{1,0:T(8,128)(2,1)}, bf16[128,256]{1,0:T(8,128)(2,1)S(1)}, u32[]{:S(2)}, u32[]{:S(2)}) %collective-permute-start.20) | collective-permute-done | bytes 65568 | tf_op jit(solution)/shard_map/ppermute | solution.py:423
  98.0 1.5 %join_outputs.1 = (bf16[128,2048]{1,0:T(8,128)(2,1)}, bf16[128,512]{1,0:T(8,128)(2,1)}, bf16[128,512]{1,0:T(8,128)(2,1)}) custom-call(s32[3]{0:T(128)S(1)} %pad_add_fusion.1.ids, bf16[128,1024]{1,0:T(8,128)(2,1)S(1)} %get-tuple-element.80.query, f32[224,1024]{1,0:T(8,128)S(1)} %collective-permute-done.18.query_other, ...), custom_call_target="tpu_custom_call" | custom-call | bytes 2097152 | tf_op jit(solution)/shard_map/join_outputs/pallas_call | solution.py:346
  (53 shorter events, 11.2 us)
Async XLA Ops:
  0.6 3.3 %collective-permute-start = (bf16[128,512]{1,0:T(8,128)(2,1)}, bf16[128,512]{1,0:T(8,128)(2,1)S(1)}, u32[]{:S(2)}, u32[]{:S(2)}) collective-permute-start(bf16[128,512]{1,0:T(8,128)(2,1)} %bitcast.22), channel_id=1, source_target_pairs={{0,1},{1,0},{2,3},{3,2},{4,5},{5,4},{6,7},{7,6},{8,9},{9,8},{10,11... | collective-permute-start | bytes 393224 | tf_op jit(solution)/shard_map/ppermute | solution.py:423
  4.5 15.1 %collective-permute-start.1 = (bf16[128,2048]{1,0:T(8,128)(2,1)}, bf16[128,2048]{1,0:T(8,128)(2,1)S(1)}, u32[]{:S(2)}, u32[]{:S(2)}) collective-permute-start(bf16[128,2048]{1,0:T(8,128)(2,1)} %bitcast.18), channel_id=1, source_target_pairs={{0,1},{1,0},{2,3},{3,2},{4,5},{5,4},{6,7},{7,6},{8,9},{9,8},{10,11... | collective-permute-start | bytes 1572872 | tf_op jit(solution)/shard_map/ppermute | solution.py:423
  4.6 15.0 %collective-permute-start.2 = (bf16[128,2048]{1,0:T(8,128)(2,1)}, bf16[128,2048]{1,0:T(8,128)(2,1)S(1)}, u32[]{:S(2)}, u32[]{:S(2)}) collective-permute-start(bf16[128,2048]{1,0:T(8,128)(2,1)} %bitcast.20), channel_id=1, source_target_pairs={{0,1},{1,0},{2,3},{3,2},{4,5},{5,4},{6,7},{7,6},{8,9},{9,8},{10,11... | collective-permute-start | bytes 1572872 | tf_op jit(solution)/shard_map/ppermute | solution.py:423
  5.1 8.6 %collective-permute-start.3 = (bf16[128,512]{1,0:T(8,128)(2,1)}, bf16[128,512]{1,0:T(8,128)(2,1)S(1)}, u32[]{:S(2)}, u32[]{:S(2)}) collective-permute-start(bf16[128,512]{1,0:T(8,128)(2,1)} %bitcast.23), channel_id=1, source_target_pairs={{0,1},{1,0},{2,3},{3,2},{4,5},{5,4},{6,7},{7,6},{8,9},{9,8},{10,11... | collective-permute-start | bytes 393224 | tf_op jit(solution)/shard_map/ppermute | solution.py:423
  5.2 18.7 %collective-permute-start.5 = (bf16[256,256]{1,0:T(8,128)(2,1)S(1)}, bf16[256,256]{1,0:T(8,128)(2,1)S(1)}, u32[]{:S(2)}, u32[]{:S(2)}) collective-permute-start(bf16[256,256]{1,0:T(8,128)(2,1)S(1)} %pick_keys.1.keys.k0), channel_id=1, source_target_pairs={{0,2},{2,4},{4,6},{6,8},{8,10},{10,12},{12,14},{14,16},{16,18},{18... | collective-permute-start | bytes 393224 | tf_op jit(solution)/shard_map/ppermute | solution.py:415
  14.3 9.6 %collective-permute-start.4 = (bf16[128,512]{1,0:T(8,128)(2,1)S(1)}, bf16[128,512]{1,0:T(8,128)(2,1)S(1)}, u32[]{:S(2)}, u32[]{:S(2)}) collective-permute-start(bf16[128,512]{1,0:T(8,128)(2,1)S(1)} %get-tuple-element.65), channel_id=1, source_target_pairs={{0,4},{2,6},{4,8},{6,10},{8,12},{10,14},{12,16},{14,18},{16,20},{1... | collective-permute-start | bytes 393224 | tf_op jit(solution)/shard_map/ppermute | solution.py:415
  20.4 11.1 %collective-permute-start.7 = (bf16[256,256]{1,0:T(8,128)(2,1)S(1)}, bf16[256,256]{1,0:T(8,128)(2,1)S(1)}, u32[]{:S(2)}, u32[]{:S(2)}) collective-permute-start(bf16[256,256]{1,0:T(8,128)(2,1)S(1)} %get-tuple-element.70.v0), channel_id=1, source_target_pairs={{0,2},{2,4},{4,6},{6,8},{8,10},{10,12},{12,14},{14,16},{16,18},{18... | collective-permute-start | bytes 393224 | tf_op jit(solution)/shard_map/ppermute | solution.py:415
  27.2 17.3 %collective-permute-start.6 = (bf16[256,256]{1,0:T(8,128)(2,1)S(1)}, bf16[256,256]{1,0:T(8,128)(2,1)S(1)}, u32[]{:S(2)}, u32[]{:S(2)}) collective-permute-start(bf16[256,256]{1,0:T(8,128)(2,1)S(1)} %get-tuple-element.68), channel_id=1, source_target_pairs={{2,0},{4,2},{6,4},{8,6},{10,8},{12,10},{14,12},{16,14},{18,16},{20... | collective-permute-start | bytes 393224 | tf_op jit(solution)/shard_map/ppermute | solution.py:415
  30.0 25.9 %collective-permute-start.9 = (bf16[128,1024]{1,0:T(8,128)(2,1)S(1)}, bf16[128,1024]{1,0:T(8,128)(2,1)S(1)}, u32[]{:S(2)}, u32[]{:S(2)}) collective-permute-start(bf16[128,1024]{1,0:T(8,128)(2,1)S(1)} %get-tuple-element.77), channel_id=1, source_target_pairs={{0,8},{8,16},{16,24},{24,0},{1,9},{9,17},{17,25},{25,1},{2,10},{10... | collective-permute-start | bytes 786440 | tf_op jit(solution)/shard_map/ppermute | solution.py:419
  30.0 25.8 %collective-permute-start.10 = (bf16[128,1024]{1,0:T(8,128)(2,1)S(1)}, bf16[128,1024]{1,0:T(8,128)(2,1)S(1)}, u32[]{:S(2)}, u32[]{:S(2)}) collective-permute-start(bf16[128,1024]{1,0:T(8,128)(2,1)S(1)} %get-tuple-element.78), channel_id=1, source_target_pairs={{0,16},{8,24},{16,0},{24,8},{1,17},{9,25},{17,1},{25,9},{2,18},{10... | collective-permute-start | bytes 786440 | tf_op jit(solution)/shard_map/ppermute | solution.py:419
  30.1 26.2 %collective-permute-start.11 = (bf16[128,1024]{1,0:T(8,128)(2,1)S(1)}, bf16[128,1024]{1,0:T(8,128)(2,1)S(1)}, u32[]{:S(2)}, u32[]{:S(2)}) collective-permute-start(bf16[128,1024]{1,0:T(8,128)(2,1)S(1)} %get-tuple-element.79), channel_id=1, source_target_pairs={{0,24},{8,0},{16,8},{24,16},{1,25},{9,1},{17,9},{25,17},{2,26},{10... | collective-permute-start | bytes 786440 | tf_op jit(solution)/shard_map/ppermute | solution.py:419
  31.5 15.3 %collective-permute-start.8 = (bf16[128,256]{1,0:T(8,128)(2,1)S(1)}, bf16[128,256]{1,0:T(8,128)(2,1)S(1)}, u32[]{:S(2)}, u32[]{:S(2)}) collective-permute-start(bf16[128,256]{1,0:T(8,128)(2,1)S(1)} %get-tuple-element.73), channel_id=1, source_target_pairs={{4,0},{6,2},{8,4},{10,6},{12,8},{14,10},{16,12},{18,14},{20,16},{2... | collective-permute-start | bytes 196616 | tf_op jit(solution)/shard_map/ppermute | solution.py:415
  48.2 10.2 %all-to-all-start = ((bf16[4,256,256]{2,1,0:T(8,128)(2,1)}), bf16[4,256,256]{2,1,0:T(8,128)(2,1)S(1)}, u32[]{:S(2)}, u32[]{:S(2)}) async-start(bf16[4,256,256]{2,1,0:T(8,128)(2,1)} %get-tuple-element.74), calls=%async_computation | async-start | bytes 1048576 | tf_op jit(solution)/shard_map/all_to_all | solution.py:471
  52.1 6.2 %collective-permute-start.12 = (bf16[128,1024]{1,0:T(8,128)(2,1)S(1)}, bf16[128,1024]{1,0:T(8,128)(2,1)S(1)}, u32[]{:S(2)}, u32[]{:S(2)}) collective-permute-start(bf16[128,1024]{1,0:T(8,128)(2,1)S(1)} %get-tuple-element.76.a0), channel_id=1, source_target_pairs={{0,1},{1,0},{2,3},{3,2},{4,5},{5,4},{6,7},{7,6},{8,9},{9,8},{10,11... | collective-permute-start | bytes 786440 | tf_op jit(solution)/shard_map/ppermute | solution.py:423
  55.8 2.6 %collective-permute-start.13 = (bf16[128,1024]{1,0:T(8,128)(2,1)S(1)}, bf16[128,1024]{1,0:T(8,128)(2,1)S(1)}, u32[]{:S(2)}, u32[]{:S(2)}) collective-permute-start(bf16[128,1024]{1,0:T(8,128)(2,1)S(1)} %collective-permute-done.9.a1), channel_id=1, source_target_pairs={{0,1},{1,0},{2,3},{3,2},{4,5},{5,4},{6,7},{7,6},{8,9},{9,8},{10,11... | collective-permute-start | bytes 786440 | tf_op jit(solution)/shard_map/ppermute | solution.py:423
  55.8 2.6 %collective-permute-start.14 = (bf16[128,1024]{1,0:T(8,128)(2,1)S(1)}, bf16[128,1024]{1,0:T(8,128)(2,1)S(1)}, u32[]{:S(2)}, u32[]{:S(2)}) collective-permute-start(bf16[128,1024]{1,0:T(8,128)(2,1)S(1)} %collective-permute-done.10.a2), channel_id=1, source_target_pairs={{0,1},{1,0},{2,3},{3,2},{4,5},{5,4},{6,7},{7,6},{8,9},{9,8},{10,11... | collective-permute-start | bytes 786440 | tf_op jit(solution)/shard_map/ppermute | solution.py:423
  56.4 2.1 %collective-permute-start.15 = (bf16[128,1024]{1,0:T(8,128)(2,1)S(1)}, bf16[128,1024]{1,0:T(8,128)(2,1)S(1)}, u32[]{:S(2)}, u32[]{:S(2)}) collective-permute-start(bf16[128,1024]{1,0:T(8,128)(2,1)S(1)} %collective-permute-done.11.a3), channel_id=1, source_target_pairs={{0,1},{1,0},{2,3},{3,2},{4,5},{5,4},{6,7},{7,6},{8,9},{9,8},{10,11... | collective-permute-start | bytes 786440 | tf_op jit(solution)/shard_map/ppermute | solution.py:423
  56.4 33.7 %collective-permute-start.16 = (bf16[256,256]{1,0:T(8,128)(2,1)S(1)}, bf16[256,256]{1,0:T(8,128)(2,1)S(1)}, u32[]{:S(2)}, u32[]{:S(2)}) collective-permute-start(bf16[256,256]{1,0:T(8,128)(2,1)S(1)} %get-tuple-element.82), channel_id=1, source_target_pairs={{2,0},{4,2},{6,4},{8,6},{10,8},{12,10},{14,12},{16,14},{18,16},{20... | collective-permute-start | bytes 393224 | tf_op jit(solution)/shard_map/ppermute | solution.py:415
  61.7 37.9 %all-to-all-start.1 = ((bf16[32,32,256]{2,1,0:T(8,128)(2,1)}), bf16[32,32,256]{2,1,0:T(8,128)(2,1)S(1)}, u32[]{:S(2)}, u32[]{:S(2)}) async-start(bf16[32,32,256]{2,1,0:T(8,128)(2,1)} %bitcast.11), calls=%async_computation.1 | async-start | bytes 1048576 | tf_op jit(solution)/shard_map/all_to_all | solution.py:473
  73.8 16.4 %collective-permute-start.17 = (bf16[128,256]{1,0:T(8,128)(2,1)}, bf16[128,256]{1,0:T(8,128)(2,1)S(1)}, u32[]{:S(2)}, u32[]{:S(2)}) collective-permute-start(bf16[128,256]{1,0:T(8,128)(2,1)} %copy-done.3), channel_id=1, source_target_pairs={{4,0},{6,2},{8,4},{10,6},{12,8},{14,10},{16,12},{18,14},{20,16},{2... | collective-permute-start | bytes 196616 | tf_op jit(solution)/shard_map/ppermute | solution.py:415
  90.8 7.3 %collective-permute-start.18 = (f32[224,1024]{1,0:T(8,128)}, f32[224,1024]{1,0:T(8,128)S(1)}, u32[]{:S(2)}, u32[]{:S(2)}) collective-permute-start(f32[224,1024]{1,0:T(8,128)} %copy-done.1), channel_id=1, source_target_pairs={{0,1},{1,0},{2,3},{3,2},{4,5},{5,4},{6,7},{7,6},{8,9},{9,8},{10,11... | collective-permute-start | bytes 2752520 | tf_op jit(solution)/shard_map/ppermute | solution.py:423
  95.5 2.5 %collective-permute-start.20 = (bf16[128,256]{1,0:T(8,128)(2,1)}, bf16[128,256]{1,0:T(8,128)(2,1)S(1)}, u32[]{:S(2)}, u32[]{:S(2)}) collective-permute-start(bf16[128,256]{1,0:T(8,128)(2,1)} %copy-done.2), channel_id=1, source_target_pairs={{0,1},{1,0},{2,3},{3,2},{4,5},{5,4},{6,7},{7,6},{8,9},{9,8},{10,11... | collective-permute-start | bytes 196616 | tf_op jit(solution)/shard_map/ppermute | solution.py:423
  95.6 2.4 %collective-permute-start.19 = (bf16[128,256]{1,0:T(8,128)(2,1)S(1)}, bf16[128,256]{1,0:T(8,128)(2,1)S(1)}, u32[]{:S(2)}, u32[]{:S(2)}) collective-permute-start(bf16[128,256]{1,0:T(8,128)(2,1)S(1)} %get-tuple-element.88), channel_id=1, source_target_pairs={{0,1},{1,0},{2,3},{3,2},{4,5},{5,4},{6,7},{7,6},{8,9},{9,8},{10,11... | collective-permute-start | bytes 196616 | tf_op jit(solution)/shard_map/ppermute | solution.py:423
  100.1 1.3 %collective-permute-start.21 = (f32[16,256]{1,0:T(8,128)S(1)}, f32[16,256]{1,0:T(8,128)S(1)}, u32[]{:S(2)}, u32[]{:S(2)}) collective-permute-start(f32[16,256]{1,0:T(8,128)S(1)} %get-tuple-element.97), channel_id=1, source_target_pairs={{0,1},{1,0},{2,3},{3,2},{4,5},{5,4},{6,7},{7,6},{8,9},{9,8},{10,11... | collective-permute-start | bytes 49160 | tf_op jit(solution)/shard_map/ppermute | solution.py:423
  (4 other events, 38.8 us)
